TPU v7x, 32 devices: a whole 2x2x4 slice. The times are simulated.
32 devices in a mesh: segment: 2 (over core), lon: 4 (over z), lat: 4 (over y, x).
Axes of the slice: x: 2, y: 2, z: 4, core: 2. Of those that a mesh axis runs over, the one named last changes fastest.
Arguments:
- dec_cot: bfloat16 [2, 64, 96, 128], P('segment', 'lon', 'lat'), may hold values from -6 to 6
- saved_conv: bfloat16 [2, 4, 64, 96, 256], P('segment', None, 'lon', 'lat'), may hold values from -6 to 6
- dec_weight: bfloat16 [256, 128], replicated, may hold values from -0.5 to 0.5
- w_in: bfloat16 [4, 256, 512], replicated, may hold values from -0.375 to 0.375
- w_out: bfloat16 [4, 512, 256], replicated, may hold values from -0.25 to 0.25
- conv_taps: float32 [4, 5, 256], replicated, may hold values from -3 to 3
- dilation: int32 [4], replicated, may hold values from 1 to 48, as said below
Outputs:
- in_adjoint: bfloat16 [2, 64, 96, 256], P('segment', 'lon', 'lat')
Inputs may be any that keep to these rules, and one draw needn't show every extreme that they name: Every layer's dilation lies in 1 to 48; at least one layer has exactly 48.
All inputs are finite; a program needn't handle non-finite values.
Results may differ from a plain program's by a relative error of at most 0.013.
Values may be sent and summed in bfloat16 or wider, within the bound.
No kernel may reach another device: no remote copies, remote signals or barrier semaphores. Data moves between devices by JAX's collectives and lax.ppermute only.
A program may use at most 64 MiB of HBM per device.

v0:
```python
import jax
import jax.numpy as jnp
from jax import lax
from jax.sharding import PartitionSpec as P


def with_halo(cells, sides, width):
    for axis, dim in sides:
        count = lax.axis_size(axis)
        ends = count - 1
        head = lax.slice_in_dim(cells, 0, width, axis=dim)
        tail = lax.slice_in_dim(cells, cells.shape[dim] - width, cells.shape[dim], axis=dim)
        cells = jnp.concatenate(
            [
                lax.ppermute(tail, axis, [(i, (i + 1) % count) for i in range(ends)]),
                cells,
                lax.ppermute(head, axis, [((i + 1) % count, i) for i in range(ends)]),
            ],
            axis=dim,
        )
    return cells


def from_behind(value, axis, steps):
    count = lax.axis_size(axis)
    pairs = [(source, (source + steps) % count) for source in range(count)]
    return lax.ppermute(value, axis, pairs)


def partner(block, axis, stride):
    count = lax.axis_size(axis)
    route = []
    for low in range(count):
        high = low | 1 << stride
        if high != low and high < count:
            route += [(low, high), (high, low)]
    return lax.ppermute(block, axis, route)


def gelu_slope(hidden):
    normal_cdf = 0.5 * (1.0 + jax.scipy.special.erf(hidden * 0.7071067811865476))
    density = jnp.exp(-0.5 * hidden * hidden) * 0.3989422804014327
    return normal_cdf + hidden * density


def tap_adjoint(conv_grad, taps_now, offset):
    lon_cells, lat_rows, chans = conv_grad.shape
    lat_padded = with_halo(conv_grad, (("lat", 1),), 1)
    meridional = taps_now[3] * lat_padded[:, 2:] + taps_now[4] * lat_padded[:, :-2]
    centre = taps_now[1] * conv_grad
    rim_width = 3 * lon_cells
    pieces = []
    for distance in (3, 2, 1, 0, -1, -2, -3):
        if distance == 0:
            pieces.append(conv_grad)
        else:
            pieces.append(from_behind(conv_grad, "lon", distance))
    padded = jnp.concatenate(pieces, axis=0)
    ahead_cells = lax.dynamic_slice_in_dim(padded, rim_width + offset, lon_cells, 0)
    behind = lax.dynamic_slice_in_dim(padded, rim_width - offset, lon_cells, 0)
    zonal_sum = taps_now[0] * ahead_cells + taps_now[2] * behind
    zonal_sum = lax.optimization_barrier(zonal_sum.astype(jnp.bfloat16)).astype(jnp.float32)
    return zonal_sum + centre + meridional


def per_device(dec_cot, saved_conv, dec_weight, w_in, w_out, conv_taps, dilation):
    lon_cells = saved_conv.shape[2]
    lat_rows = saved_conv.shape[3]
    chans = saved_conv.shape[4]
    layer_count = w_in.shape[0]
    own_cot = dec_cot[0].reshape(-1, dec_cot.shape[3])
    projected = jnp.einsum(
        "nv,cv->nc", own_cot, dec_weight, preferred_element_type=jnp.float32
    ).astype(jnp.bfloat16)
    handed = partner(projected, "segment", 0)
    gradient = lax.optimization_barrier(handed).astype(jnp.float32)
    for layer_index in reversed(range(layer_count)):
        conv_out = saved_conv[0, layer_index].reshape(-1, chans)
        hidden = jnp.dot(conv_out, w_in[layer_index], preferred_element_type=jnp.float32)
        cot_low = gradient.astype(jnp.bfloat16)
        act_grad = jnp.einsum(
            "nc,hc->nh", cot_low, w_out[layer_index], preferred_element_type=jnp.float32
        )
        pre_grad = (act_grad * gelu_slope(hidden)).astype(jnp.bfloat16)
        conv_grad = jnp.einsum(
            "nh,ch->nc", pre_grad, w_in[layer_index], preferred_element_type=jnp.float32
        ).astype(jnp.bfloat16)
        tapped = tap_adjoint(
            conv_grad.reshape(lon_cells, lat_rows, chans),
            conv_taps[layer_index],
            dilation[layer_index],
        )
        gradient = gradient + tapped.reshape(-1, chans)
    return gradient.reshape(1, lon_cells, lat_rows, chans).astype(jnp.bfloat16)


def solution(mesh):
    in_specs = (
        P("segment", "lon", "lat", None),
        P("segment", None, "lon", "lat", None),
        P(),
        P(),
        P(),
        P(),
        P(),
    )
    out_specs = P("segment", "lon", "lat", None)
    return jax.shard_map(
        per_device, mesh=mesh, in_specs=in_specs, out_specs=out_specs, check_vma=False
    )
```

profile of v0, /device:TPU:0, one launch (start us, length us, event | category | flops | bytes accessed | tf_op | source)
XLA Modules:
  0.0 108.8 jit_solution(3066376072981257746)
XLA Ops:
  2.5 1.4 %fusion.136 = (s32[1]{0:T(128)}, s32[1]{0:T(128)}, s32[1]{0:T(128)}, s32[1]{0:T(128)}) fusion(s32[4]{0:T(128)} %param.13), kind=kLoop, calls=%fused_computation.179 | loop fusion | bytes 32 | tf_op jit(solution)/shard_map/slice | solution.py:91
  13.7 1.3 %fusion.130 = (bf16[1,1,16,24,256]{4,3,2,1,0:T(8,128)(2,1)S(1)}, bf16[1,1,16,24,256]{4,3,2,1,0:T(8,128)(2,1)S(1)}, bf16[1,1,16,24,256]{4,3,2,1,0:T(8,128)(2,1)S(1)}, bf16[1,1,16,24,256]{4,3,2,1,0:T(8,128)(2,1)S(1)}) fusion(bf16[1,4,16,24,256]{4,3,2,1,0:T(8,128)(2,1)} %param.8), kind=kLoop, calls=%fused_computation.173 | loop fusion | bytes 1572864 | tf_op jit(solution)/shard_map/slice | solution.py:78
  15.0 1.2 %fusion.86 = f32[384,512]{1,0:T(8,128)} fusion(bf16[384,256]{1,0:T(8,128)(2,1)S(1)} %bitcast.135, bf16[4,256,512]{2,1,0:T(8,128)(2,1)S(1)} %copy-done.1), kind=kOutput, calls=%fused_computation.100 | convolution fusion | flops 100663296 | bytes 1245184 | tf_op jit(solution)/shard_map/dot_general | solution.py:79
  19.1 1.8 %fusion.8 = bf16[384,256]{1,0:T(8,128)(2,1)S(1)} fusion(bf16[384,256]{1,0:T(8,128)(2,1)S(1)} %collective-permute-done, f32[384,512]{1,0:T(8,128)} %fusion.86, bf16[4,512,256]{2,1,0:T(8,128)(2,1)} %param.11, bf16[4,256,512]{2,1,0:T(8,128)(2,1)S(1)} %copy-done.1), kind=kOutput, calls=%fused_computation.16 | convolution fusion | flops 203390976 | bytes 1703936 | tf_op jit(solution)/shard_map/nh,ch->nc/dot_general | solution.py:85
  20.9 4.7 %collective-permute-start.1 = (bf16[16,24,256]{2,1,0:T(8,128)(2,1)S(1)}, bf16[16,24,256]{2,1,0:T(8,128)(2,1)S(1)}, u32[]{:S(2)}, u32[]{:S(2)}) collective-permute-start(bf16[16,24,256]{2,1,0:T(8,128)(2,1)S(1)} %bitcast.120), channel_id=1, source_target_pairs={{0,12},{4,0},{8,4},{12,8},{1,13},{5,1},{9,5},{13,9},{2,14},{6,2},{... | collective-permute-start | bytes 589832 | tf_op jit(solution)/shard_map/ppermute | solution.py:27
  26.6 1.3 %collective-permute-start.4 = (bf16[16,1,256]{2,1,0:T(2,128)(2,1)S(1)}, bf16[16,1,256]{2,1,0:T(2,128)(2,1)S(1)}, u32[]{:S(2)}, u32[]{:S(2)}) collective-permute-start(bf16[16,1,256]{2,1,0:T(2,128)(2,1)S(1)} %get-tuple-element.15), channel_id=1, source_target_pairs={{1,0},{2,1},{3,2},{5,4},{6,5},{7,6},{9,8},{10,9},{11,10},{13,12},{... | collective-permute-start | bytes 24584 | tf_op jit(solution)/shard_map/ppermute | solution.py:17
  27.9 4.5 %collective-permute-start.5 = (bf16[16,1,256]{2,1,0:T(2,128)(2,1)S(1)}, bf16[16,1,256]{2,1,0:T(2,128)(2,1)S(1)}, u32[]{:S(2)}, u32[]{:S(2)}) collective-permute-start(bf16[16,1,256]{2,1,0:T(2,128)(2,1)S(1)} %get-tuple-element.16), channel_id=1, source_target_pairs={{0,1},{1,2},{2,3},{4,5},{5,6},{6,7},{8,9},{9,10},{10,11},{12,13},{... | collective-permute-start | bytes 24584 | tf_op jit(solution)/shard_map/ppermute | solution.py:15
  32.5 10.4 %collective-permute-done.2 = bf16[16,24,256]{2,1,0:T(8,128)(2,1)S(1)} collective-permute-done((bf16[16,24,256]{2,1,0:T(8,128)(2,1)S(1)}, bf16[16,24,256]{2,1,0:T(8,128)(2,1)S(1)}, u32[]{:S(2)}, u32[]{:S(2)}) %collective-permute-start.2) | collective-permute-done | bytes 196640 | tf_op jit(solution)/shard_map/ppermute | solution.py:27
  44.5 1.6 %fusion.9 = bf16[384,256]{1,0:T(8,128)(2,1)S(1)} fusion(bf16[384,256]{1,0:T(8,128)(2,1)} %fusion.69, f32[384,512]{1,0:T(8,128)S(1)} %fusion.81, bf16[4,512,256]{2,1,0:T(8,128)(2,1)} %param.11, bf16[4,256,512]{2,1,0:T(8,128)(2,1)S(1)} %copy-done.1), kind=kOutput, calls=%fused_computation.17 | convolution fusion | flops 203390976 | bytes 1703936 | tf_op jit(solution)/shard_map/nh,ch->nc/dot_general | solution.py:85
  46.4 2.2 %collective-permute-start.7 = (bf16[16,24,256]{2,1,0:T(8,128)(2,1)S(1)}, bf16[16,24,256]{2,1,0:T(8,128)(2,1)S(1)}, u32[]{:S(2)}, u32[]{:S(2)}) collective-permute-start(bf16[16,24,256]{2,1,0:T(8,128)(2,1)S(1)} %bitcast.115), channel_id=1, source_target_pairs={{0,8},{4,12},{8,0},{12,4},{1,9},{5,13},{9,1},{13,5},{2,10},{6,14},... | collective-permute-start | bytes 589832 | tf_op jit(solution)/shard_map/ppermute | solution.py:27
  48.6 1.9 %collective-permute-start.8 = (bf16[16,24,256]{2,1,0:T(8,128)(2,1)S(1)}, bf16[16,24,256]{2,1,0:T(8,128)(2,1)S(1)}, u32[]{:S(2)}, u32[]{:S(2)}) collective-permute-start(bf16[16,24,256]{2,1,0:T(8,128)(2,1)S(1)} %bitcast.116), channel_id=1, source_target_pairs={{0,4},{4,8},{8,12},{12,0},{1,5},{5,9},{9,13},{13,1},{2,6},{6,10},{... | collective-permute-start | bytes 589832 | tf_op jit(solution)/shard_map/ppermute | solution.py:27
  50.6 3.4 %collective-permute-start.10 = (bf16[16,1,256]{2,1,0:T(2,128)(2,1)S(1)}, bf16[16,1,256]{2,1,0:T(2,128)(2,1)S(1)}, u32[]{:S(2)}, u32[]{:S(2)}) collective-permute-start(bf16[16,1,256]{2,1,0:T(2,128)(2,1)S(1)} %get-tuple-element.14), channel_id=1, source_target_pairs={{0,1},{1,2},{2,3},{4,5},{5,6},{6,7},{8,9},{9,10},{10,11},{12,13},{... | collective-permute-start | bytes 24584 | tf_op jit(solution)/shard_map/ppermute | solution.py:15
  54.0 1.3 %collective-permute-start.9 = (bf16[16,1,256]{2,1,0:T(2,128)(2,1)S(1)}, bf16[16,1,256]{2,1,0:T(2,128)(2,1)S(1)}, u32[]{:S(2)}, u32[]{:S(2)}) collective-permute-start(bf16[16,1,256]{2,1,0:T(2,128)(2,1)S(1)} %get-tuple-element.13), channel_id=1, source_target_pairs={{1,0},{2,1},{3,2},{5,4},{6,5},{7,6},{9,8},{10,9},{11,10},{13,12},{... | collective-permute-start | bytes 24584 | tf_op jit(solution)/shard_map/ppermute | solution.py:17
  55.4 10.3 %collective-permute-done.7 = bf16[16,24,256]{2,1,0:T(8,128)(2,1)S(1)} collective-permute-done((bf16[16,24,256]{2,1,0:T(8,128)(2,1)S(1)}, bf16[16,24,256]{2,1,0:T(8,128)(2,1)S(1)}, u32[]{:S(2)}, u32[]{:S(2)}) %collective-permute-start.7) | collective-permute-done | bytes 196640 | tf_op jit(solution)/shard_map/ppermute | solution.py:27
  66.2 1.8 %fusion.10 = bf16[384,256]{1,0:T(8,128)(2,1)S(1)} fusion(f32[384,512]{1,0:T(8,128)} %fusion.76, bf16[4,512,256]{2,1,0:T(8,128)(2,1)} %param.11, bf16[4,256,512]{2,1,0:T(8,128)(2,1)S(1)} %copy-done.1, f32[384,256]{1,0:T(8,128)S(1)} %bitcast_add_fusion.2), kind=kOutput, calls=%fused_computation.18 | convolution fusion | flops 203489280 | bytes 1900544 | tf_op jit(solution)/shard_map/nh,ch->nc/dot_general | solution.py:85
  69.0 1.9 %collective-permute-start.13 = (bf16[16,24,256]{2,1,0:T(8,128)(2,1)S(1)}, bf16[16,24,256]{2,1,0:T(8,128)(2,1)S(1)}, u32[]{:S(2)}, u32[]{:S(2)}) collective-permute-start(bf16[16,24,256]{2,1,0:T(8,128)(2,1)S(1)} %bitcast.128), channel_id=1, source_target_pairs={{0,4},{4,8},{8,12},{12,0},{1,5},{5,9},{9,13},{13,1},{2,6},{6,10},{... | collective-permute-start | bytes 589832 | tf_op jit(solution)/shard_map/ppermute | solution.py:27
  70.9 1.3 %collective-permute-start.14 = (bf16[16,1,256]{2,1,0:T(2,128)(2,1)S(1)}, bf16[16,1,256]{2,1,0:T(2,128)(2,1)S(1)}, u32[]{:S(2)}, u32[]{:S(2)}) collective-permute-start(bf16[16,1,256]{2,1,0:T(2,128)(2,1)S(1)} %get-tuple-element.11), channel_id=1, source_target_pairs={{1,0},{2,1},{3,2},{5,4},{6,5},{7,6},{9,8},{10,9},{11,10},{13,12},{... | collective-permute-start | bytes 24584 | tf_op jit(solution)/shard_map/ppermute | solution.py:17
  72.2 4.5 %collective-permute-start.15 = (bf16[16,1,256]{2,1,0:T(2,128)(2,1)S(1)}, bf16[16,1,256]{2,1,0:T(2,128)(2,1)S(1)}, u32[]{:S(2)}, u32[]{:S(2)}) collective-permute-start(bf16[16,1,256]{2,1,0:T(2,128)(2,1)S(1)} %get-tuple-element.12), channel_id=1, source_target_pairs={{0,1},{1,2},{2,3},{4,5},{5,6},{6,7},{8,9},{9,10},{10,11},{12,13},{... | collective-permute-start | bytes 24584 | tf_op jit(solution)/shard_map/ppermute | solution.py:15
  76.8 9.8 %collective-permute-done.12 = bf16[16,24,256]{2,1,0:T(8,128)(2,1)S(1)} collective-permute-done((bf16[16,24,256]{2,1,0:T(8,128)(2,1)S(1)}, bf16[16,24,256]{2,1,0:T(8,128)(2,1)S(1)}, u32[]{:S(2)}, u32[]{:S(2)}) %collective-permute-start.12) | collective-permute-done | bytes 196640 | tf_op jit(solution)/shard_map/ppermute | solution.py:27
  87.1 1.5 %fusion.11 = bf16[384,256]{1,0:T(8,128)(2,1)S(1)} fusion(f32[384,512]{1,0:T(8,128)S(1)} %fusion.71, bf16[4,512,256]{2,1,0:T(8,128)(2,1)} %param.11, bf16[4,256,512]{2,1,0:T(8,128)(2,1)S(1)} %copy-done.1, bf16[384,256]{1,0:T(8,128)(2,1)S(1)} %bitcast_add_fusion.1), kind=kOutput, calls=%fused_computation.19 | convolution fusion | flops 203390976 | bytes 1703936 | tf_op jit(solution)/shard_map/nh,ch->nc/dot_general | solution.py:85
  89.6 1.9 %collective-permute-start.18 = (bf16[16,24,256]{2,1,0:T(8,128)(2,1)S(1)}, bf16[16,24,256]{2,1,0:T(8,128)(2,1)S(1)}, u32[]{:S(2)}, u32[]{:S(2)}) collective-permute-start(bf16[16,24,256]{2,1,0:T(8,128)(2,1)S(1)} %bitcast.110), channel_id=1, source_target_pairs={{0,4},{4,8},{8,12},{12,0},{1,5},{5,9},{9,13},{13,1},{2,6},{6,10},{... | collective-permute-start | bytes 589832 | tf_op jit(solution)/shard_map/ppermute | solution.py:27
  91.5 1.3 %collective-permute-start.19 = (bf16[16,1,256]{2,1,0:T(2,128)(2,1)S(1)}, bf16[16,1,256]{2,1,0:T(2,128)(2,1)S(1)}, u32[]{:S(2)}, u32[]{:S(2)}) collective-permute-start(bf16[16,1,256]{2,1,0:T(2,128)(2,1)S(1)} %get-tuple-element.9), channel_id=1, source_target_pairs={{1,0},{2,1},{3,2},{5,4},{6,5},{7,6},{9,8},{10,9},{11,10},{13,12},{... | collective-permute-start | bytes 24584 | tf_op jit(solution)/shard_map/ppermute | solution.py:17
  92.8 4.5 %collective-permute-start.20 = (bf16[16,1,256]{2,1,0:T(2,128)(2,1)S(1)}, bf16[16,1,256]{2,1,0:T(2,128)(2,1)S(1)}, u32[]{:S(2)}, u32[]{:S(2)}) collective-permute-start(bf16[16,1,256]{2,1,0:T(2,128)(2,1)S(1)} %get-tuple-element.10), channel_id=1, source_target_pairs={{0,1},{1,2},{2,3},{4,5},{5,6},{6,7},{8,9},{9,10},{10,11},{12,13},{... | collective-permute-start | bytes 24584 | tf_op jit(solution)/shard_map/ppermute | solution.py:15
  97.4 9.8 %collective-permute-done.17 = bf16[16,24,256]{2,1,0:T(8,128)(2,1)S(1)} collective-permute-done((bf16[16,24,256]{2,1,0:T(8,128)(2,1)S(1)}, bf16[16,24,256]{2,1,0:T(8,128)(2,1)S(1)}, u32[]{:S(2)}, u32[]{:S(2)}) %collective-permute-start.17) | collective-permute-done | bytes 196640 | tf_op jit(solution)/shard_map/ppermute | solution.py:27
  (97 shorter events, 12.6 us)
Async XLA Ops:
  0.0 15.0 %copy-start.1 = (bf16[4,256,512]{2,1,0:T(8,128)(2,1)S(1)}, bf16[4,256,512]{2,1,0:T(8,128)(2,1)}, u32[]{:S(2)}) copy-start(bf16[4,256,512]{2,1,0:T(8,128)(2,1)} %param.10) | copy-start | bytes 3145732
  1.9 17.2 %collective-permute-start = (bf16[384,256]{1,0:T(8,128)(2,1)S(1)}, bf16[384,256]{1,0:T(8,128)(2,1)S(1)}, u32[]{:S(2)}, u32[]{:S(2)}) collective-permute-start(bf16[384,256]{1,0:T(8,128)(2,1)S(1)} %convolution_convert_fusion), channel_id=1, source_target_pairs={{0,16},{16,0},{1,17},{17,1},{2,18},{18,2},{3,19},{19,3},{4,20},{20... | collective-permute-start | bytes 589832 | tf_op jit(solution)/shard_map/ppermute | solution.py:37
  20.9 11.6 %collective-permute-start.1 = (bf16[16,24,256]{2,1,0:T(8,128)(2,1)S(1)}, bf16[16,24,256]{2,1,0:T(8,128)(2,1)S(1)}, u32[]{:S(2)}, u32[]{:S(2)}) collective-permute-start(bf16[16,24,256]{2,1,0:T(8,128)(2,1)S(1)} %bitcast.120), channel_id=1, source_target_pairs={{0,12},{4,0},{8,4},{12,8},{1,13},{5,1},{9,5},{13,9},{2,14},{6,2},{... | collective-permute-start | bytes 589832 | tf_op jit(solution)/shard_map/ppermute | solution.py:27
  25.5 17.4 %collective-permute-start.2 = (bf16[16,24,256]{2,1,0:T(8,128)(2,1)S(1)}, bf16[16,24,256]{2,1,0:T(8,128)(2,1)S(1)}, u32[]{:S(2)}, u32[]{:S(2)}) collective-permute-start(bf16[16,24,256]{2,1,0:T(8,128)(2,1)S(1)} %bitcast.121), channel_id=1, source_target_pairs={{0,8},{4,12},{8,0},{12,4},{1,9},{5,13},{9,1},{13,5},{2,10},{6,14},... | collective-permute-start | bytes 589832 | tf_op jit(solution)/shard_map/ppermute | solution.py:27
  25.5 17.4 %collective-permute-start.3 = (bf16[16,24,256]{2,1,0:T(8,128)(2,1)S(1)}, bf16[16,24,256]{2,1,0:T(8,128)(2,1)S(1)}, u32[]{:S(2)}, u32[]{:S(2)}) collective-permute-start(bf16[16,24,256]{2,1,0:T(8,128)(2,1)S(1)} %bitcast.122), channel_id=1, source_target_pairs={{0,4},{4,8},{8,12},{12,0},{1,5},{5,9},{9,13},{13,1},{2,6},{6,10},{... | collective-permute-start | bytes 589832 | tf_op jit(solution)/shard_map/ppermute | solution.py:27
  26.6 16.6 %collective-permute-start.4 = (bf16[16,1,256]{2,1,0:T(2,128)(2,1)S(1)}, bf16[16,1,256]{2,1,0:T(2,128)(2,1)S(1)}, u32[]{:S(2)}, u32[]{:S(2)}) collective-permute-start(bf16[16,1,256]{2,1,0:T(2,128)(2,1)S(1)} %get-tuple-element.15), channel_id=1, source_target_pairs={{1,0},{2,1},{3,2},{5,4},{6,5},{7,6},{9,8},{10,9},{11,10},{13,12},{... | collective-permute-start | bytes 24584 | tf_op jit(solution)/shard_map/ppermute | solution.py:17
  27.9 15.2 %copy-start.8 = (f32[1,1,256]{2,0,1:T(1,128)S(1)}, f32[1,1,256]{2,0,1:T(1,128)}, u32[]{:S(2)}) copy-start(f32[1,1,256]{2,0,1:T(1,128)} %get-tuple-element.33) | copy-start | bytes 3076
  27.9 15.2 %copy-start.9 = (f32[1,1,256]{2,0,1:T(1,128)S(1)}, f32[1,1,256]{2,0,1:T(1,128)}, u32[]{:S(2)}) copy-start(f32[1,1,256]{2,0,1:T(1,128)} %get-tuple-element.34) | copy-start | bytes 3076
  27.9 15.3 %collective-permute-start.5 = (bf16[16,1,256]{2,1,0:T(2,128)(2,1)S(1)}, bf16[16,1,256]{2,1,0:T(2,128)(2,1)S(1)}, u32[]{:S(2)}, u32[]{:S(2)}) collective-permute-start(bf16[16,1,256]{2,1,0:T(2,128)(2,1)S(1)} %get-tuple-element.16), channel_id=1, source_target_pairs={{0,1},{1,2},{2,3},{4,5},{5,6},{6,7},{8,9},{9,10},{10,11},{12,13},{... | collective-permute-start | bytes 24584 | tf_op jit(solution)/shard_map/ppermute | solution.py:15
  46.1 9.2 %collective-permute-start.6 = (bf16[16,24,256]{2,1,0:T(8,128)(2,1)S(1)}, bf16[16,24,256]{2,1,0:T(8,128)(2,1)S(1)}, u32[]{:S(2)}, u32[]{:S(2)}) collective-permute-start(bf16[16,24,256]{2,1,0:T(8,128)(2,1)S(1)} %bitcast.114), channel_id=1, source_target_pairs={{0,12},{4,0},{8,4},{12,8},{1,13},{5,1},{9,5},{13,9},{2,14},{6,2},{... | collective-permute-start | bytes 589832 | tf_op jit(solution)/shard_map/ppermute | solution.py:27
  46.4 19.3 %collective-permute-start.7 = (bf16[16,24,256]{2,1,0:T(8,128)(2,1)S(1)}, bf16[16,24,256]{2,1,0:T(8,128)(2,1)S(1)}, u32[]{:S(2)}, u32[]{:S(2)}) collective-permute-start(bf16[16,24,256]{2,1,0:T(8,128)(2,1)S(1)} %bitcast.115), channel_id=1, source_target_pairs={{0,8},{4,12},{8,0},{12,4},{1,9},{5,13},{9,1},{13,5},{2,10},{6,14},... | collective-permute-start | bytes 589832 | tf_op jit(solution)/shard_map/ppermute | solution.py:27
  48.6 17.0 %collective-permute-start.8 = (bf16[16,24,256]{2,1,0:T(8,128)(2,1)S(1)}, bf16[16,24,256]{2,1,0:T(8,128)(2,1)S(1)}, u32[]{:S(2)}, u32[]{:S(2)}) collective-permute-start(bf16[16,24,256]{2,1,0:T(8,128)(2,1)S(1)} %bitcast.116), channel_id=1, source_target_pairs={{0,4},{4,8},{8,12},{12,0},{1,5},{5,9},{9,13},{13,1},{2,6},{6,10},{... | collective-permute-start | bytes 589832 | tf_op jit(solution)/shard_map/ppermute | solution.py:27
  50.6 15.3 %collective-permute-start.10 = (bf16[16,1,256]{2,1,0:T(2,128)(2,1)S(1)}, bf16[16,1,256]{2,1,0:T(2,128)(2,1)S(1)}, u32[]{:S(2)}, u32[]{:S(2)}) collective-permute-start(bf16[16,1,256]{2,1,0:T(2,128)(2,1)S(1)} %get-tuple-element.14), channel_id=1, source_target_pairs={{0,1},{1,2},{2,3},{4,5},{5,6},{6,7},{8,9},{9,10},{10,11},{12,13},{... | collective-permute-start | bytes 24584 | tf_op jit(solution)/shard_map/ppermute | solution.py:15
  54.0 11.9 %collective-permute-start.9 = (bf16[16,1,256]{2,1,0:T(2,128)(2,1)S(1)}, bf16[16,1,256]{2,1,0:T(2,128)(2,1)S(1)}, u32[]{:S(2)}, u32[]{:S(2)}) collective-permute-start(bf16[16,1,256]{2,1,0:T(2,128)(2,1)S(1)} %get-tuple-element.13), channel_id=1, source_target_pairs={{1,0},{2,1},{3,2},{5,4},{6,5},{7,6},{9,8},{10,9},{11,10},{13,12},{... | collective-permute-start | bytes 24584 | tf_op jit(solution)/shard_map/ppermute | solution.py:17
  68.0 8.8 %collective-permute-start.11 = (bf16[16,24,256]{2,1,0:T(8,128)(2,1)S(1)}, bf16[16,24,256]{2,1,0:T(8,128)(2,1)S(1)}, u32[]{:S(2)}, u32[]{:S(2)}) collective-permute-start(bf16[16,24,256]{2,1,0:T(8,128)(2,1)S(1)} %bitcast.126), channel_id=1, source_target_pairs={{0,12},{4,0},{8,4},{12,8},{1,13},{5,1},{9,5},{13,9},{2,14},{6,2},{... | collective-permute-start | bytes 589832 | tf_op jit(solution)/shard_map/ppermute | solution.py:27
  68.0 18.6 %collective-permute-start.12 = (bf16[16,24,256]{2,1,0:T(8,128)(2,1)S(1)}, bf16[16,24,256]{2,1,0:T(8,128)(2,1)S(1)}, u32[]{:S(2)}, u32[]{:S(2)}) collective-permute-start(bf16[16,24,256]{2,1,0:T(8,128)(2,1)S(1)} %bitcast.127), channel_id=1, source_target_pairs={{0,8},{4,12},{8,0},{12,4},{1,9},{5,13},{9,1},{13,5},{2,10},{6,14},... | collective-permute-start | bytes 589832 | tf_op jit(solution)/shard_map/ppermute | solution.py:27
  69.0 17.7 %collective-permute-start.13 = (bf16[16,24,256]{2,1,0:T(8,128)(2,1)S(1)}, bf16[16,24,256]{2,1,0:T(8,128)(2,1)S(1)}, u32[]{:S(2)}, u32[]{:S(2)}) collective-permute-start(bf16[16,24,256]{2,1,0:T(8,128)(2,1)S(1)} %bitcast.128), channel_id=1, source_target_pairs={{0,4},{4,8},{8,12},{12,0},{1,5},{5,9},{9,13},{13,1},{2,6},{6,10},{... | collective-permute-start | bytes 589832 | tf_op jit(solution)/shard_map/ppermute | solution.py:27
  70.9 15.9 %collective-permute-start.14 = (bf16[16,1,256]{2,1,0:T(2,128)(2,1)S(1)}, bf16[16,1,256]{2,1,0:T(2,128)(2,1)S(1)}, u32[]{:S(2)}, u32[]{:S(2)}) collective-permute-start(bf16[16,1,256]{2,1,0:T(2,128)(2,1)S(1)} %get-tuple-element.11), channel_id=1, source_target_pairs={{1,0},{2,1},{3,2},{5,4},{6,5},{7,6},{9,8},{10,9},{11,10},{13,12},{... | collective-permute-start | bytes 24584 | tf_op jit(solution)/shard_map/ppermute | solution.py:17
  72.2 14.6 %collective-permute-start.15 = (bf16[16,1,256]{2,1,0:T(2,128)(2,1)S(1)}, bf16[16,1,256]{2,1,0:T(2,128)(2,1)S(1)}, u32[]{:S(2)}, u32[]{:S(2)}) collective-permute-start(bf16[16,1,256]{2,1,0:T(2,128)(2,1)S(1)} %get-tuple-element.12), channel_id=1, source_target_pairs={{0,1},{1,2},{2,3},{4,5},{5,6},{6,7},{8,9},{9,10},{10,11},{12,13},{... | collective-permute-start | bytes 24584 | tf_op jit(solution)/shard_map/ppermute | solution.py:15
  88.6 8.8 %collective-permute-start.16 = (bf16[16,24,256]{2,1,0:T(8,128)(2,1)S(1)}, bf16[16,24,256]{2,1,0:T(8,128)(2,1)S(1)}, u32[]{:S(2)}, u32[]{:S(2)}) collective-permute-start(bf16[16,24,256]{2,1,0:T(8,128)(2,1)S(1)} %bitcast.108), channel_id=1, source_target_pairs={{0,12},{4,0},{8,4},{12,8},{1,13},{5,1},{9,5},{13,9},{2,14},{6,2},{... | collective-permute-start | bytes 589832 | tf_op jit(solution)/shard_map/ppermute | solution.py:27
  88.7 18.5 %collective-permute-start.17 = (bf16[16,24,256]{2,1,0:T(8,128)(2,1)S(1)}, bf16[16,24,256]{2,1,0:T(8,128)(2,1)S(1)}, u32[]{:S(2)}, u32[]{:S(2)}) collective-permute-start(bf16[16,24,256]{2,1,0:T(8,128)(2,1)S(1)} %bitcast.109), channel_id=1, source_target_pairs={{0,8},{4,12},{8,0},{12,4},{1,9},{5,13},{9,1},{13,5},{2,10},{6,14},... | collective-permute-start | bytes 589832 | tf_op jit(solution)/shard_map/ppermute | solution.py:27
  89.6 17.7 %collective-permute-start.18 = (bf16[16,24,256]{2,1,0:T(8,128)(2,1)S(1)}, bf16[16,24,256]{2,1,0:T(8,128)(2,1)S(1)}, u32[]{:S(2)}, u32[]{:S(2)}) collective-permute-start(bf16[16,24,256]{2,1,0:T(8,128)(2,1)S(1)} %bitcast.110), channel_id=1, source_target_pairs={{0,4},{4,8},{8,12},{12,0},{1,5},{5,9},{9,13},{13,1},{2,6},{6,10},{... | collective-permute-start | bytes 589832 | tf_op jit(solution)/shard_map/ppermute | solution.py:27
  91.5 15.9 %collective-permute-start.19 = (bf16[16,1,256]{2,1,0:T(2,128)(2,1)S(1)}, bf16[16,1,256]{2,1,0:T(2,128)(2,1)S(1)}, u32[]{:S(2)}, u32[]{:S(2)}) collective-permute-start(bf16[16,1,256]{2,1,0:T(2,128)(2,1)S(1)} %get-tuple-element.9), channel_id=1, source_target_pairs={{1,0},{2,1},{3,2},{5,4},{6,5},{7,6},{9,8},{10,9},{11,10},{13,12},{... | collective-permute-start | bytes 24584 | tf_op jit(solution)/shard_map/ppermute | solution.py:17
  92.8 14.6 %collective-permute-start.20 = (bf16[16,1,256]{2,1,0:T(2,128)(2,1)S(1)}, bf16[16,1,256]{2,1,0:T(2,128)(2,1)S(1)}, u32[]{:S(2)}, u32[]{:S(2)}) collective-permute-start(bf16[16,1,256]{2,1,0:T(2,128)(2,1)S(1)} %get-tuple-element.10), channel_id=1, source_target_pairs={{0,1},{1,2},{2,3},{4,5},{5,6},{6,7},{8,9},{9,10},{10,11},{12,13},{... | collective-permute-start | bytes 24584 | tf_op jit(solution)/shard_map/ppermute | solution.py:15
  (8 other events, 28.6 us)
where the time goes:
time: 109 us
  waiting for transfers between devices  40.3 us (37%)
  starting transfers between devices  38.6 us (35%)
  matrix products  10.5 us (10%)
  between operations  10.5 us (10%)
  local copies, waits for them, and re-layouts  6.2 us (6%)
  other arithmetic  2.72 us (2%)
    ppermute x12, waiting for transfers between devices, from_behind(): return lax.ppermute(value, axis, pairs)  40.2 us
    ppermute x4, starting transfers between devices, with_halo(): lax.ppermute(tail, axis, [(i, (i + 1) % count) for i in range(ends)])  17 us
    ppermute x12, starting transfers between devices, from_behind(): return lax.ppermute(value, axis, pairs)  15.9 us
    dot_general x4, matrix products, per_device(): jnp.einsum('nh,ch->nc', pre_grad, w_in[layer_index], preferred_element_ty...  6.63 us
    ppermute x4, starting transfers between devices, with_halo(): lax.ppermute(head, axis, [((i + 1) % count, i) for i in range(ends)])  5.17 us
    dot_general x4, matrix products, per_device(): jnp.dot(conv_out, w_in[layer_index], preferred_element_type=jnp.float32)  2.84 us
  transfers between devices with their start and end apart: 21, of which 4 were waited for; matrix products, arithmetic and copies ran while one was open for 7% of the time, Pallas kernels for 0%

commit v1 on v0

v1 whole, which is shorter than its diff:
```python
import functools

import jax
import jax.numpy as jnp
from jax import lax
from jax.experimental import pallas as pl
from jax.experimental.pallas import tpu as pltpu
from jax.sharding import PartitionSpec as P

AXES = ("segment", "lon", "lat")


def with_halo(cells, sides, width):
    for axis, dim in sides:
        count = lax.axis_size(axis)
        ends = count - 1
        head = lax.slice_in_dim(cells, 0, width, axis=dim)
        tail = lax.slice_in_dim(cells, cells.shape[dim] - width, cells.shape[dim], axis=dim)
        cells = jnp.concatenate(
            [
                lax.ppermute(tail, axis, [(i, (i + 1) % count) for i in range(ends)]),
                cells,
                lax.ppermute(head, axis, [((i + 1) % count, i) for i in range(ends)]),
            ],
            axis=dim,
        )
    return cells


def from_behind(value, axis, steps):
    count = lax.axis_size(axis)
    pairs = [(source, (source + steps) % count) for source in range(count)]
    return lax.ppermute(value, axis, pairs)


def partner(block, axis):
    count = lax.axis_size(axis)
    return lax.ppermute(block, axis, [(i, i ^ 1) for i in range(count) if i ^ 1 < count])


def gelu_slope(hidden):
    normal_cdf = 0.5 * (1.0 + lax.erf(hidden * 0.7071067811865476))
    density = jnp.exp(-0.5 * hidden * hidden) * 0.3989422804014327
    return normal_cdf + hidden * density


def tap_adjoint(conv_grad, taps_now, offset):
    lon_cells = conv_grad.shape[0]
    lat_padded = with_halo(conv_grad, (("lat", 1),), 1)
    meridional = taps_now[3] * lat_padded[:, 2:] + taps_now[4] * lat_padded[:, :-2]
    centre = taps_now[1] * conv_grad
    rim_width = 3 * lon_cells
    pieces = []
    for distance in (3, 2, 1, 0, -1, -2, -3):
        pieces.append(conv_grad if distance == 0 else from_behind(conv_grad, "lon", distance))
    padded = jnp.concatenate(pieces, axis=0)
    ahead_cells = lax.dynamic_slice_in_dim(padded, rim_width + offset, lon_cells, 0)
    behind = lax.dynamic_slice_in_dim(padded, rim_width - offset, lon_cells, 0)
    zonal_sum = taps_now[0] * ahead_cells + taps_now[2] * behind
    zonal_sum = lax.optimization_barrier(zonal_sum.astype(jnp.bfloat16)).astype(jnp.float32)
    return zonal_sum + centre + meridional


def by_exchange(dec_cot, saved_conv, dec_weight, w_in, w_out, conv_taps, dilation):
    lon_cells, lat_rows, chans = saved_conv.shape[2:]
    own_cot = dec_cot[0].reshape(-1, dec_cot.shape[3])
    projected = jnp.einsum(
        "nv,cv->nc", own_cot, dec_weight, preferred_element_type=jnp.float32
    ).astype(jnp.bfloat16)
    gradient = lax.optimization_barrier(partner(projected, "segment")).astype(jnp.float32)
    for layer in reversed(range(w_in.shape[0])):
        conv_out = saved_conv[0, layer].reshape(-1, chans)
        hidden = jnp.dot(conv_out, w_in[layer], preferred_element_type=jnp.float32)
        act_grad = jnp.einsum(
            "nc,hc->nh",
            gradient.astype(jnp.bfloat16),
            w_out[layer],
            preferred_element_type=jnp.float32,
        )
        pre_grad = (act_grad * gelu_slope(hidden)).astype(jnp.bfloat16)
        conv_grad = jnp.einsum(
            "nh,ch->nc", pre_grad, w_in[layer], preferred_element_type=jnp.float32
        ).astype(jnp.bfloat16)
        tapped = tap_adjoint(
            conv_grad.reshape(lon_cells, lat_rows, chans), conv_taps[layer], dilation[layer]
        )
        gradient = gradient + tapped.reshape(-1, chans)
    return gradient.reshape(1, lon_cells, lat_rows, chans).astype(jnp.bfloat16)


def routed(value, hop):
    cores, cols, rows = (lax.axis_size(a) for a in AXES)
    pairs = []
    for c in range(cores):
        for z in range(cols):
            for j in range(rows):
                to = hop(c, z, j)
                if to is not None and 0 <= to[2] < rows:
                    pairs.append(((c * cols + z) * rows + j, (to[0] * cols + to[1]) * rows + to[2]))
    return lax.ppermute(value, AXES, pairs)


def row_chunks(low, high):
    count = max(1, (high - low) // 4)
    edges = [low + (high - low) * i // count for i in range(count + 1)]
    return list(zip(edges[:-1], edges[1:]))


def layer_kernel(layer, first, last, lat_size, *refs):
    refs = list(refs)
    offset_ref, row_ref = refs[:2]
    pieces = refs[2:6]
    refs = refs[6:]
    if first:
        cots, refs = refs[:4], refs[4:]
        dec_ref, refs = refs[0], refs[1:]
    else:
        grad_in, refs = refs[0], refs[1:]
    w_in, w_out, taps = refs[:3]
    out, cg = refs[3:5]
    cells = pieces[0].shape[1]
    lon = 4 * cells
    chans = w_in.shape[0]
    halves = [(h, slice(h * 128, (h + 1) * 128)) for h in range(chans // 128)]
    window = pieces[0].shape[0]
    offset = offset_ref[0]
    if first:
        grad = refs[5]
    for r0, r1 in row_chunks(0, window):
        count = (r1 - r0) * lon
        conv_out = jnp.concatenate([p[r0:r1] for p in pieces], axis=1).reshape(count, chans)
        hidden = jnp.dot(conv_out, w_in[...], preferred_element_type=jnp.float32)
        if first:
            cot = jnp.concatenate([p[r0:r1] for p in cots], axis=1).reshape(count, -1)
            handed = lax.dot_general(
                cot, dec_ref[...], (((1,), (1,)), ((), ())), preferred_element_type=jnp.float32
            ).astype(jnp.bfloat16)
            grad[r0:r1] = handed.astype(jnp.float32).reshape(r1 - r0, lon, chans)
            low = handed
        else:
            low = grad_in[r0:r1].reshape(count, chans).astype(jnp.bfloat16)
        act = lax.dot_general(
            low, w_out[...], (((1,), (1,)), ((), ())), preferred_element_type=jnp.float32
        )
        pre = (act * gelu_slope(hidden)).astype(jnp.bfloat16)
        conv_grad = lax.dot_general(
            pre, w_in[...], (((1,), (1,)), ((), ())), preferred_element_type=jnp.float32
        ).reshape(r1 - r0, lon, chans)
        for r in range(r0, r1):
            rows_here = conv_grad[r - r0]
            if r < layer + 1 or r >= window - (layer + 1):
                place = row_ref[0] + (r - layer - 1)
                inside = jnp.where((place >= 0) & (place < lat_size), 1.0, 0.0).astype(jnp.float32)
                rows_here = rows_here * inside
            for h, lanes in halves:
                cg[r, h, 0:lon] = rows_here[:, lanes]
                cg[r, h, lon : 2 * lon] = rows_here[:, lanes]

    def tap(r, carry):
        for h, lanes in halves:
            t = [taps[k : k + 1, lanes] for k in range(5)]
            total = t[0] * cg[r, h, pl.ds(offset, lon)] + t[2] * cg[r, h, pl.ds(lon - offset, lon)]
            total += t[1] * cg[r, h, 0:lon] + t[3] * cg[r + 1, h, 0:lon] + t[4] * cg[r - 1, h, 0:lon]
            if first:
                total += grad[r, :, lanes]
            else:
                total += grad_in[r, :, lanes]
            if last:
                out[r - 1, :, lanes] = total.astype(jnp.bfloat16)
            else:
                out[r - 1, :, lanes] = total
        return carry

    lax.fori_loop(1, window - 1, tap, 0, unroll=2)


def run_layer(layer, layers, lat_size, offset, row, pieces, cots, dec_weight, gradient, w_in, w_out, taps):
    first, last = layer == layers - 1, layer == 0
    window, cells, chans = pieces[0].shape
    lon = 4 * cells
    smem = pl.BlockSpec(memory_space=pltpu.SMEM)
    vmem = pl.BlockSpec(memory_space=pltpu.VMEM)
    args = [offset, row, *pieces]
    args += [*cots, dec_weight] if first else [gradient]
    args += [w_in, w_out, taps]
    if last:
        out = jax.ShapeDtypeStruct((window - 2, lon, chans), jnp.bfloat16)
    else:
        out = jax.ShapeDtypeStruct((window - 2, lon, chans), jnp.float32)
    scratch = [pltpu.VMEM((window, chans // 128, 2 * lon, 128), jnp.float32)]
    if first:
        scratch.append(pltpu.VMEM((window, lon, chans), jnp.float32))
    work = window * lon
    return pl.pallas_call(
        functools.partial(layer_kernel, layer, first, last, lat_size),
        out_shape=out,
        in_specs=[smem, smem] + [vmem] * (len(args) - 2),
        out_specs=vmem,
        scratch_shapes=scratch,
        compiler_params=pltpu.CompilerParams(vmem_limit_bytes=40 * 2**20),
        cost_estimate=pl.CostEstimate(
            flops=6 * work * chans * w_in.shape[1],
            bytes_accessed=work * chans * 10,
            transcendentals=2 * work * w_in.shape[1],
        ),
        name=f"layer_{layer}",
    )(*args)


def by_circles(dec_cot, saved_conv, dec_weight, w_in, w_out, conv_taps, dilation):
    layers = w_in.shape[0]
    cells, rows, chans = saved_conv.shape[2:]
    lat_size = rows * lax.axis_size("lat")
    segment, lon, lat = (lax.axis_index(a) for a in AXES)

    def home(c):
        return c + 1

    def gather(value):
        found = [value]
        for k in range(1, 4):
            found.append(
                routed(value, lambda c, z, j: (c, home(c), j) if z == (home(c) + k) % 4 else None)
            )
        return found

    cot = partner(dec_cot[0], "segment").transpose(1, 0, 2)
    conv = saved_conv[0].transpose(0, 2, 1, 3)
    tops, bottoms = [], []
    for layer in range(layers):
        tops.append(conv[layer, : layer + 1])
        bottoms.append(conv[layer, rows - layer - 1 :])
    cot_top = cot[:layers]
    cot_bottom = cot[rows - layers :]
    v = cot.shape[2]
    tops.append(jnp.concatenate([cot_top[0::2], cot_top[1::2]], axis=2))
    bottoms.append(jnp.concatenate([cot_bottom[0::2], cot_bottom[1::2]], axis=2))
    below = routed(jnp.concatenate(tops, axis=0), lambda c, z, j: (c, z, j - 1))
    above = routed(jnp.concatenate(bottoms, axis=0), lambda c, z, j: (c, z, j + 1))

    def wide(layer):
        start = layer * (layer + 1) // 2
        return jnp.concatenate(
            [above[start : start + layer + 1], conv[layer], below[start : start + layer + 1]], axis=0
        )

    def cot_rows(edge):
        pair = edge[layers * (layers + 1) // 2 :]
        return jnp.stack([pair[..., :v], pair[..., v:]], axis=1).reshape(layers, cells, v)

    wide_cot = jnp.concatenate([cot_rows(above), cot, cot_rows(below)], axis=0)
    both = gather(jnp.concatenate([wide(layers - 1), wide_cot], axis=2))
    pieces = {layers - 1: [b[..., :chans] for b in both]}
    cots = [b[..., chans:] for b in both]
    for layer in reversed(range(layers - 1)):
        pieces[layer] = gather(wide(layer))

    gradient = None
    row = (lat * rows).astype(jnp.int32).reshape(1)
    for layer in reversed(range(layers)):
        gradient = run_layer(
            layer, layers, lat_size, dilation[layer].reshape(1), row, pieces[layer], cots,
            dec_weight, gradient, w_in[layer], w_out[layer], conv_taps[layer],
        )

    result = jnp.where(lon == home(segment), gradient[:, :cells], 0)
    for k in range(1, 4):
        quarter = gradient[:, k * cells : (k + 1) * cells]
        result = result + routed(
            quarter, lambda c, z, j: (c, (z + k) % 4, j) if z == home(c) else None
        )
    return result.transpose(1, 0, 2)[None]


def solution(mesh):
    in_specs = (
        P("segment", "lon", "lat", None),
        P("segment", None, "lon", "lat", None),
        P(),
        P(),
        P(),
        P(),
        P(),
    )
    out_specs = P("segment", "lon", "lat", None)
    gathers = mesh.shape["lon"] == 4 and mesh.shape["segment"] == 2
    return jax.shard_map(
        by_circles if gathers else by_exchange,
        mesh=mesh,
        in_specs=in_specs,
        out_specs=out_specs,
        check_vma=False,
    )
```

time: 109 us -> 79.2 us (0.73)
  waiting for transfers between devices: 40.3 us -> 12.9 us
  Pallas kernels: 0 us -> 17 us
  matrix products: 10.5 us -> 0 us
  between operations: 10.5 us -> 0.52 us
  starting transfers between devices: 38.6 us -> 33 us
  local copies, waits for them, and re-layouts: 6.2 us -> 11 us
  other arithmetic: 2.72 us -> 4.17 us
    ppermute x21 -> x18, waiting for transfers between devices: 40.3 us -> 12.9 us  [the longest x17 12.9 us: routed(): return lax.ppermute(value, AXES, pairs)]
    pallas_call x0 -> x4, Pallas kernels: none -> 17 us  [run_layer(): pl.pallas_call(functools.partial(layer_kernel, layer, first, last, lat_si...]
    dot_general x9 -> x0, matrix products: 10.5 us -> none  [the longest x4 6.63 us: per_device(): jnp.einsum('nh,ch->nc', pre_grad, w_in[layer_index], preferred_element_ty...]
    ppermute x21 -> x18, starting transfers between devices: 38.6 us -> 33 us  [the longest x17 32.5 us: routed(): return lax.ppermute(value, AXES, pairs)]
    concatenate x0 -> x8, other arithmetic: none -> 4.12 us  [the longest x4 1.06 us: wide(): jnp.concatenate([above[start:start + layer + 1], conv[layer], below[start...]
    squeeze x0 -> x4, local copies, waits for them, and re-layouts: none -> 3.3 us  [the longest x1 1.29 us: by_circles(): w_in[layer]]
    unnamed x46 -> x14, local copies, waits for them, and re-layouts: 2.11 us -> 5.32 us
    slice x8 -> x19, local copies, waits for them, and re-layouts: 4.04 us -> 1.63 us  [the longest x1 0.74 us: by_circles(): cot_bottom = cot[rows - layers:]]
  transfers between devices with their start and end apart: 21 -> 18, of which waited for: 4 -> 3; matrix products, arithmetic and copies ran while one was open for 7% -> 13% of each run, Pallas kernels for 0% -> 17%
where the time goes in v1:
time: 79.2 us; the launch traced here: 78.5 us
  starting transfers between devices  33 us (42%)
  Pallas kernels  17 us (21%)
  waiting for transfers between devices  12.9 us (16%)
  local copies, waits for them, and re-layouts  11 us (14%)
  other arithmetic  4.17 us (5%)
    ppermute x17, starting transfers between devices, routed(): return lax.ppermute(value, AXES, pairs)  32.5 us
    pallas_call x4, Pallas kernels, run_layer(): pl.pallas_call(functools.partial(layer_kernel, layer, first, last, lat_si...  17 us
    ppermute x17, waiting for transfers between devices, routed(): return lax.ppermute(value, AXES, pairs)  12.9 us
    unnamed x14, local copies, waits for them, and re-layouts  5.32 us
  transfers between devices with their start and end apart: 18, of which 3 were waited for; matrix products, arithmetic and copies ran while one was open for 13% of the time, Pallas kernels for 17%

profile of v1, /device:TPU:0, one launch (start us, length us, event | category | flops | bytes accessed | tf_op | source)
XLA Modules:
  0.0 78.5 jit_solution(4286308459313651023)
XLA Ops:
  0.0 1.5 %copy.36 = bf16[1,16,24,128]{3,1,2,0:T(8,128)(2,1)} copy(bf16[1,16,24,128]{3,2,1,0:T(8,128)(2,1)} %param.7) | data formatting | bytes 196608 | tf_op args[0]
  2.0 1.3 %copy.35 = bf16[1,4,16,24,256]{4,2,3,1,0:T(8,128)(2,1)S(1)} copy(bf16[1,4,16,24,256]{4,3,2,1,0:T(8,128)(2,1)} %param.8) | data formatting | bytes 1572864 | tf_op args[1]
  3.9 0.7 slice_bitcast_fusion.8
  4.6 1.3 %slice_bitcast_fusion.1 = (bf16[256,512]{1,0:T(8,128)(2,1)S(1)}, bf16[256,512]{1,0:T(8,128)(2,1)S(1)}, bf16[256,512]{1,0:T(8,128)(2,1)S(1)}, bf16[256,512]{1,0:T(8,128)(2,1)S(1)}) fusion(bf16[4,256,512]{2,1,0:T(8,128)(2,1)} %param.10), kind=kLoop, calls=%fused_computation.4 | loop fusion | bytes 2097152 | tf_op jit(solution)/shard_map/squeeze | solution.py:263
  5.9 1.3 %slice_bitcast_fusion = (bf16[512,256]{1,0:T(8,128)(2,1)S(1)}, bf16[512,256]{1,0:T(8,128)(2,1)S(1)}, bf16[512,256]{1,0:T(8,128)(2,1)S(1)}, bf16[512,256]{1,0:T(8,128)(2,1)S(1)}) fusion(bf16[4,512,256]{2,1,0:T(8,128)(2,1)} %param.11), kind=kLoop, calls=%fused_computation.3 | loop fusion | bytes 2097152 | tf_op jit(solution)/shard_map/squeeze | solution.py:263
  9.8 0.7 fusion.9
  11.2 4.4 %collective-permute-start.1 = (bf16[12,16,256]{2,1,0:T(8,128)(2,1)}, bf16[12,16,256]{2,1,0:T(8,128)(2,1)S(1)}, u32[]{:S(2)}, u32[]{:S(2)}) collective-permute-start(bf16[12,16,256]{2,1,0:T(8,128)(2,1)} %constant_dynamic-update-slice_fusion), channel_id=1, source_target_pairs={{0,1},{1,2},{2,3},{4,5},{5,6},{6,7},{8,9},{9,10},{10,11},{12,13},{... | collective-permute-start | bytes 294920 | tf_op jit(solution)/shard_map/ppermute | solution.py:100
  16.2 1.3 %collective-permute-start.2 = (bf16[12,16,256]{2,1,0:T(8,128)(2,1)}, bf16[12,16,256]{2,1,0:T(8,128)(2,1)S(1)}, u32[]{:S(2)}, u32[]{:S(2)}) collective-permute-start(bf16[12,16,256]{2,1,0:T(8,128)(2,1)} %constant_dynamic-update-slice_fusion.3), channel_id=1, source_target_pairs={{1,0},{2,1},{3,2},{5,4},{6,5},{7,6},{9,8},{10,9},{11,10},{13,12},{... | collective-permute-start | bytes 294920 | tf_op jit(solution)/shard_map/ppermute | solution.py:100
  17.4 1.1 %collective-permute-done.1 = bf16[12,16,256]{2,1,0:T(8,128)(2,1)S(1)} collective-permute-done((bf16[12,16,256]{2,1,0:T(8,128)(2,1)}, bf16[12,16,256]{2,1,0:T(8,128)(2,1)S(1)}, u32[]{:S(2)}, u32[]{:S(2)}) %collective-permute-start.1) | collective-permute-done | bytes 98336 | tf_op jit(solution)/shard_map/ppermute | solution.py:100
  18.6 4.6 %collective-permute-done.2 = bf16[12,16,256]{2,1,0:T(8,128)(2,1)S(1)} collective-permute-done((bf16[12,16,256]{2,1,0:T(8,128)(2,1)}, bf16[12,16,256]{2,1,0:T(8,128)(2,1)S(1)}, u32[]{:S(2)}, u32[]{:S(2)}) %collective-permute-start.2) | collective-permute-done | bytes 98336 | tf_op jit(solution)/shard_map/ppermute | solution.py:100
  23.2 0.9 %maximum_maximum_fusion = bf16[32,16,384]{2,1,0:T(8,128)(2,1)S(1)} fusion(bf16[4,16,128]{2,1,0:T(8,128)(2,1)S(1)} %bitcast.99, bf16[24,16,128]{2,1,0:T(8,128)(2,1)} %bitcast.9, bf16[4,16,128]{2,1,0:T(8,128)(2,1)S(1)} %bitcast.97, bf16[4,16,256]{2,1,0:T(8,128)(2,1)S(1)} %slice.251, bf16[24,16,256]{2,1,0:T(8,128)(2,1)S(1)} %get-tuple-element.16, ...), kind=kLoop, calls=%fused_computation.1 | loop fusion | flops 2359296 | bytes 786432 | tf_op jit(solution)/shard_map/concatenate | solution.py:252
  25.5 4.7 %collective-permute-start.14 = (bf16[32,16,384]{2,1,0:T(8,128)(2,1)S(1)}, bf16[32,16,384]{2,1,0:T(8,128)(2,1)S(1)}, u32[]{:S(2)}, u32[]{:S(2)}) collective-permute-start(bf16[32,16,384]{2,1,0:T(8,128)(2,1)S(1)} %maximum_maximum_fusion), channel_id=1, source_target_pairs={{0,4},{1,5},{2,6},{3,7},{20,24},{21,25},{22,26},{23,27}} | collective-permute-start | bytes 1179656 | tf_op jit(solution)/shard_map/ppermute | solution.py:100
  30.3 1.0 %pad_maximum_fusion.1.refs_2_ = bf16[30,16,256]{2,1,0:T(8,128)(2,1)S(1)} fusion(bf16[3,16,256]{2,1,0:T(8,128)(2,1)S(1)} %slice.248, bf16[24,16,256]{2,1,0:T(8,128)(2,1)} %get-tuple-element.17, bf16[3,16,256]{2,1,0:T(8,128)(2,1)S(1)} %slice.246), kind=kLoop, calls=%fused_computation.11 | loop fusion | flops 245760 | bytes 491520 | tf_op jit(solution)/shard_map/concatenate | solution.py:243
  32.0 0.8 %collective-permute-start.6 = (bf16[28,16,256]{2,1,0:T(8,128)(2,1)S(1)}, bf16[28,16,256]{2,1,0:T(8,128)(2,1)S(1)}, u32[]{:S(2)}, u32[]{:S(2)}) collective-permute-start(bf16[28,16,256]{2,1,0:T(8,128)(2,1)S(1)} %pad_maximum_fusion.2.refs_2_), channel_id=1, source_target_pairs={{8,4},{9,5},{10,6},{11,7},{28,24},{29,25},{30,26},{31,27}} | collective-permute-start | bytes 688136 | tf_op jit(solution)/shard_map/ppermute | solution.py:100
  32.9 7.2 %collective-permute-start.11 = (bf16[30,16,256]{2,1,0:T(8,128)(2,1)S(1)}, bf16[30,16,256]{2,1,0:T(8,128)(2,1)S(1)}, u32[]{:S(2)}, u32[]{:S(2)}) collective-permute-start(bf16[30,16,256]{2,1,0:T(8,128)(2,1)S(1)} %pad_maximum_fusion.1.refs_2_), channel_id=1, source_target_pairs={{0,4},{1,5},{2,6},{3,7},{20,24},{21,25},{22,26},{23,27}} | collective-permute-start | bytes 737288 | tf_op jit(solution)/shard_map/ppermute | solution.py:100
  40.8 0.9 %pad_maximum_fusion.4.refs_6_ = bf16[32,16,128]{2,1,0:T(8,128)(2,1)S(1)} fusion(bf16[4,16,128]{2,1,0:T(8,128)(2,1)S(1)} %bitcast.100, bf16[24,16,128]{2,1,0:T(8,128)(2,1)} %bitcast.9, bf16[4,16,128]{2,1,0:T(8,128)(2,1)S(1)} %bitcast.98), kind=kLoop, calls=%fused_computation.23 | loop fusion | flops 131072 | bytes 262144 | tf_op jit(solution)/shard_map/concatenate | solution.py:251
  42.6 4.0 %collective-permute-start.8 = (bf16[28,16,256]{2,1,0:T(8,128)(2,1)S(1)}, bf16[28,16,256]{2,1,0:T(8,128)(2,1)S(1)}, u32[]{:S(2)}, u32[]{:S(2)}) collective-permute-start(bf16[28,16,256]{2,1,0:T(8,128)(2,1)S(1)} %pad_maximum_fusion.2.refs_2_), channel_id=1, source_target_pairs={{0,4},{1,5},{2,6},{3,7},{20,24},{21,25},{22,26},{23,27}} | collective-permute-start | bytes 688136 | tf_op jit(solution)/shard_map/ppermute | solution.py:100
  46.7 5.1 %layer_3.1.refs_6_ = f32[30,64,256]{2,1,0:T(8,128)S(1)} custom-call(s32[1]{0:T(128)} %get-tuple-element.42.refs_0_, s32[1]{0:T(128)} %bitcast.refs_1_, bf16[32,16,256]{2,1,0:T(8,128)(2,1)S(1)} %pad_maximum_fusion.refs_2_, bf16[32,16,256]{2,1,0:T(8,128)(2,1)S(1)} %slice.256.refs_3_, bf16[32,16,256]{2,1,0:T(8,128)(2,1)S(1)} %slice.257.refs_4_, ...), custom_call_target="tpu_custom_call" | custom-call | flops 1610612736 | bytes 5242880 | tf_op jit(solution)/shard_map/layer_3/pallas_call | solution.py:194
  53.1 2.7 %collective-permute-start.5 = (bf16[26,16,256]{2,1,0:T(8,128)(2,1)S(1)}, bf16[26,16,256]{2,1,0:T(8,128)(2,1)S(1)}, u32[]{:S(2)}, u32[]{:S(2)}) collective-permute-start(bf16[26,16,256]{2,1,0:T(8,128)(2,1)S(1)} %pad_maximum_fusion.3.refs_2_), channel_id=1, source_target_pairs={{0,4},{1,5},{2,6},{3,7},{20,24},{21,25},{22,26},{23,27}} | collective-permute-start | bytes 638984 | tf_op jit(solution)/shard_map/ppermute | solution.py:100
  55.9 4.2 %layer_2.1.refs_6_ = f32[28,64,256]{2,1,0:T(8,128)S(1)} custom-call(s32[1]{0:T(128)} %get-tuple-element.45.refs_0_, s32[1]{0:T(128)} %bitcast.refs_1_, bf16[30,16,256]{2,1,0:T(8,128)(2,1)S(1)} %pad_maximum_fusion.1.refs_2_, bf16[30,16,256]{2,1,0:T(8,128)(2,1)S(1)} %collective-permute-done.9.refs_3_, ...), custom_call_target="tpu_custom_call" | custom-call | flops 1509949440 | bytes 4915200 | tf_op jit(solution)/shard_map/layer_2/pallas_call | solution.py:194
  60.1 4.0 %layer_1.1.refs_6_ = f32[26,64,256]{2,1,0:T(8,128)S(1)} custom-call(s32[1]{0:T(128)} %get-tuple-element.43.refs_0_, s32[1]{0:T(128)} %bitcast.refs_1_, bf16[28,16,256]{2,1,0:T(8,128)(2,1)S(1)} %pad_maximum_fusion.2.refs_2_, bf16[28,16,256]{2,1,0:T(8,128)(2,1)S(1)} %collective-permute-done.6.refs_3_, bf16[28,16,256]{2,1,0:T(8,128)(2,1)S(1)} %collective-permute-done.7.refs_4_, ...), custom_call_target="tpu_custom_call" | custom-call | flops 1409286144 | bytes 4587520 | tf_op jit(solution)/shard_map/layer_1/pallas_call | solution.py:194
  64.2 3.7 %layer_0.1 = bf16[24,64,256]{2,1,0:T(8,128)(2,1)S(1)} custom-call(s32[1]{0:T(128)} %get-tuple-element.44.refs_0_, s32[1]{0:T(128)} %bitcast.refs_1_, bf16[26,16,256]{2,1,0:T(8,128)(2,1)S(1)} %pad_maximum_fusion.3.refs_2_, bf16[26,16,256]{2,1,0:T(8,128)(2,1)S(1)} %collective-permute-done.3.refs_3_, bf16[26,16,256]{2,1,0:T(8,128)(2,1)S(1)} %collective-permute-done.4.refs_4_, ...), custom_call_target="tpu_custom_call" | custom-call | flops 1308622848 | bytes 4259840 | tf_op jit(solution)/shard_map/layer_0/pallas_call | solution.py:194
  69.3 1.3 %collective-permute-start.17 = (bf16[24,16,256]{2,1,0:T(8,128)(2,1)S(1)}, bf16[24,16,256]{2,1,0:T(8,128)(2,1)S(1)}, u32[]{:S(2)}, u32[]{:S(2)}) collective-permute-start(bf16[24,16,256]{2,1,0:T(8,128)(2,1)S(1)} %get-tuple-element.14), channel_id=1, source_target_pairs={{4,0},{5,1},{6,2},{7,3},{24,20},{25,21},{26,22},{27,23}} | collective-permute-start | bytes 589832 | tf_op jit(solution)/shard_map/ppermute | solution.py:100
  70.6 7.1 %collective-permute-done.17 = bf16[24,16,256]{2,1,0:T(8,128)(2,1)S(1)} collective-permute-done((bf16[24,16,256]{2,1,0:T(8,128)(2,1)S(1)}, bf16[24,16,256]{2,1,0:T(8,128)(2,1)S(1)}, u32[]{:S(2)}, u32[]{:S(2)}) %collective-permute-start.17) | collective-permute-done | bytes 196640 | tf_op jit(solution)/shard_map/ppermute | solution.py:100
  (69 shorter events, 12.1 us)
Async XLA Ops:
  1.5 8.3 %collective-permute-start = (bf16[16,24,128]{2,0,1:T(8,128)(2,1)}, bf16[16,24,128]{2,0,1:T(8,128)(2,1)}, u32[]{:S(2)}, u32[]{:S(2)}) collective-permute-start(bf16[16,24,128]{2,0,1:T(8,128)(2,1)} %bitcast.87), channel_id=1, source_target_pairs={{0,16},{16,0},{1,17},{17,1},{2,18},{18,2},{3,19},{19,3},{4,20},{20... | collective-permute-start | bytes 294920 | tf_op jit(solution)/shard_map/ppermute | solution.py:38
  4.6 2.6 %copy-start.1 = (f32[4,5,256]{2,0,1:T(4,128)S(1)}, f32[4,5,256]{2,0,1:T(4,128)}, u32[]{:S(2)}) copy-start(f32[4,5,256]{2,0,1:T(4,128)} %param.12) | copy-start | bytes 61444
  4.6 4.5 %copy-start.2 = (s32[4]{0:T(128)S(1)}, s32[4]{0:T(128)}, u32[]{:S(2)}) copy-start(s32[4]{0:T(128)} %param.13) | copy-start | bytes 52
  11.2 7.4 %collective-permute-start.1 = (bf16[12,16,256]{2,1,0:T(8,128)(2,1)}, bf16[12,16,256]{2,1,0:T(8,128)(2,1)S(1)}, u32[]{:S(2)}, u32[]{:S(2)}) collective-permute-start(bf16[12,16,256]{2,1,0:T(8,128)(2,1)} %constant_dynamic-update-slice_fusion), channel_id=1, source_target_pairs={{0,1},{1,2},{2,3},{4,5},{5,6},{6,7},{8,9},{9,10},{10,11},{12,13},{... | collective-permute-start | bytes 294920 | tf_op jit(solution)/shard_map/ppermute | solution.py:100
  16.2 7.0 %collective-permute-start.2 = (bf16[12,16,256]{2,1,0:T(8,128)(2,1)}, bf16[12,16,256]{2,1,0:T(8,128)(2,1)S(1)}, u32[]{:S(2)}, u32[]{:S(2)}) collective-permute-start(bf16[12,16,256]{2,1,0:T(8,128)(2,1)} %constant_dynamic-update-slice_fusion.3), channel_id=1, source_target_pairs={{1,0},{2,1},{3,2},{5,4},{6,5},{7,6},{9,8},{10,9},{11,10},{13,12},{... | collective-permute-start | bytes 294920 | tf_op jit(solution)/shard_map/ppermute | solution.py:100
  24.2 8.8 %collective-permute-start.12 = (bf16[32,16,384]{2,1,0:T(8,128)(2,1)S(1)}, bf16[32,16,384]{2,1,0:T(8,128)(2,1)S(1)}, u32[]{:S(2)}, u32[]{:S(2)}) collective-permute-start(bf16[32,16,384]{2,1,0:T(8,128)(2,1)S(1)} %maximum_maximum_fusion), channel_id=1, source_target_pairs={{8,4},{9,5},{10,6},{11,7},{28,24},{29,25},{30,26},{31,27}} | collective-permute-start | bytes 1179656 | tf_op jit(solution)/shard_map/ppermute | solution.py:100
  24.8 15.3 %collective-permute-start.13 = (bf16[32,16,384]{2,1,0:T(8,128)(2,1)S(1)}, bf16[32,16,384]{2,1,0:T(8,128)(2,1)S(1)}, u32[]{:S(2)}, u32[]{:S(2)}) collective-permute-start(bf16[32,16,384]{2,1,0:T(8,128)(2,1)S(1)} %maximum_maximum_fusion), channel_id=1, source_target_pairs={{12,4},{13,5},{14,6},{15,7},{16,24},{17,25},{18,26},{19,27}} | collective-permute-start | bytes 1179656 | tf_op jit(solution)/shard_map/ppermute | solution.py:100
  25.5 16.3 %collective-permute-start.14 = (bf16[32,16,384]{2,1,0:T(8,128)(2,1)S(1)}, bf16[32,16,384]{2,1,0:T(8,128)(2,1)S(1)}, u32[]{:S(2)}, u32[]{:S(2)}) collective-permute-start(bf16[32,16,384]{2,1,0:T(8,128)(2,1)S(1)} %maximum_maximum_fusion), channel_id=1, source_target_pairs={{0,4},{1,5},{2,6},{3,7},{20,24},{21,25},{22,26},{23,27}} | collective-permute-start | bytes 1179656 | tf_op jit(solution)/shard_map/ppermute | solution.py:100
  31.3 20.5 %collective-permute-start.10 = (bf16[30,16,256]{2,1,0:T(8,128)(2,1)S(1)}, bf16[30,16,256]{2,1,0:T(8,128)(2,1)S(1)}, u32[]{:S(2)}, u32[]{:S(2)}) collective-permute-start(bf16[30,16,256]{2,1,0:T(8,128)(2,1)S(1)} %pad_maximum_fusion.1.refs_2_), channel_id=1, source_target_pairs={{12,4},{13,5},{14,6},{15,7},{16,24},{17,25},{18,26},{19,27}} | collective-permute-start | bytes 737288 | tf_op jit(solution)/shard_map/ppermute | solution.py:100
  32.0 14.7 %copy-start = (bf16[256,128]{1,0:T(8,128)(2,1)S(1)}, bf16[256,128]{1,0:T(8,128)(2,1)}, u32[]{:S(2)}) copy-start(bf16[256,128]{1,0:T(8,128)(2,1)} %refs_10_.1) | copy-start | bytes 196612
  32.0 10.6 %collective-permute-start.6 = (bf16[28,16,256]{2,1,0:T(8,128)(2,1)S(1)}, bf16[28,16,256]{2,1,0:T(8,128)(2,1)S(1)}, u32[]{:S(2)}, u32[]{:S(2)}) collective-permute-start(bf16[28,16,256]{2,1,0:T(8,128)(2,1)S(1)} %pad_maximum_fusion.2.refs_2_), channel_id=1, source_target_pairs={{8,4},{9,5},{10,6},{11,7},{28,24},{29,25},{30,26},{31,27}} | collective-permute-start | bytes 688136 | tf_op jit(solution)/shard_map/ppermute | solution.py:100
  32.9 19.5 %collective-permute-start.11 = (bf16[30,16,256]{2,1,0:T(8,128)(2,1)S(1)}, bf16[30,16,256]{2,1,0:T(8,128)(2,1)S(1)}, u32[]{:S(2)}, u32[]{:S(2)}) collective-permute-start(bf16[30,16,256]{2,1,0:T(8,128)(2,1)S(1)} %pad_maximum_fusion.1.refs_2_), channel_id=1, source_target_pairs={{0,4},{1,5},{2,6},{3,7},{20,24},{21,25},{22,26},{23,27}} | collective-permute-start | bytes 737288 | tf_op jit(solution)/shard_map/ppermute | solution.py:100
  40.1 13.0 %collective-permute-start.9 = (bf16[30,16,256]{2,1,0:T(8,128)(2,1)S(1)}, bf16[30,16,256]{2,1,0:T(8,128)(2,1)S(1)}, u32[]{:S(2)}, u32[]{:S(2)}) collective-permute-start(bf16[30,16,256]{2,1,0:T(8,128)(2,1)S(1)} %pad_maximum_fusion.1.refs_2_), channel_id=1, source_target_pairs={{8,4},{9,5},{10,6},{11,7},{28,24},{29,25},{30,26},{31,27}} | collective-permute-start | bytes 737288 | tf_op jit(solution)/shard_map/ppermute | solution.py:100
  41.8 18.3 %collective-permute-start.7 = (bf16[28,16,256]{2,1,0:T(8,128)(2,1)S(1)}, bf16[28,16,256]{2,1,0:T(8,128)(2,1)S(1)}, u32[]{:S(2)}, u32[]{:S(2)}) collective-permute-start(bf16[28,16,256]{2,1,0:T(8,128)(2,1)S(1)} %pad_maximum_fusion.2.refs_2_), channel_id=1, source_target_pairs={{12,4},{13,5},{14,6},{15,7},{16,24},{17,25},{18,26},{19,27}} | collective-permute-start | bytes 688136 | tf_op jit(solution)/shard_map/ppermute | solution.py:100
  42.6 17.5 %collective-permute-start.8 = (bf16[28,16,256]{2,1,0:T(8,128)(2,1)S(1)}, bf16[28,16,256]{2,1,0:T(8,128)(2,1)S(1)}, u32[]{:S(2)}, u32[]{:S(2)}) collective-permute-start(bf16[28,16,256]{2,1,0:T(8,128)(2,1)S(1)} %pad_maximum_fusion.2.refs_2_), channel_id=1, source_target_pairs={{0,4},{1,5},{2,6},{3,7},{20,24},{21,25},{22,26},{23,27}} | collective-permute-start | bytes 688136 | tf_op jit(solution)/shard_map/ppermute | solution.py:100
  51.8 12.4 %collective-permute-start.3 = (bf16[26,16,256]{2,1,0:T(8,128)(2,1)S(1)}, bf16[26,16,256]{2,1,0:T(8,128)(2,1)S(1)}, u32[]{:S(2)}, u32[]{:S(2)}) collective-permute-start(bf16[26,16,256]{2,1,0:T(8,128)(2,1)S(1)} %pad_maximum_fusion.3.refs_2_), channel_id=1, source_target_pairs={{8,4},{9,5},{10,6},{11,7},{28,24},{29,25},{30,26},{31,27}} | collective-permute-start | bytes 638984 | tf_op jit(solution)/shard_map/ppermute | solution.py:100
  52.4 11.7 %collective-permute-start.4 = (bf16[26,16,256]{2,1,0:T(8,128)(2,1)S(1)}, bf16[26,16,256]{2,1,0:T(8,128)(2,1)S(1)}, u32[]{:S(2)}, u32[]{:S(2)}) collective-permute-start(bf16[26,16,256]{2,1,0:T(8,128)(2,1)S(1)} %pad_maximum_fusion.3.refs_2_), channel_id=1, source_target_pairs={{12,4},{13,5},{14,6},{15,7},{16,24},{17,25},{18,26},{19,27}} | collective-permute-start | bytes 638984 | tf_op jit(solution)/shard_map/ppermute | solution.py:100
  53.1 11.1 %collective-permute-start.5 = (bf16[26,16,256]{2,1,0:T(8,128)(2,1)S(1)}, bf16[26,16,256]{2,1,0:T(8,128)(2,1)S(1)}, u32[]{:S(2)}, u32[]{:S(2)}) collective-permute-start(bf16[26,16,256]{2,1,0:T(8,128)(2,1)S(1)} %pad_maximum_fusion.3.refs_2_), channel_id=1, source_target_pairs={{0,4},{1,5},{2,6},{3,7},{20,24},{21,25},{22,26},{23,27}} | collective-permute-start | bytes 638984 | tf_op jit(solution)/shard_map/ppermute | solution.py:100
  67.9 2.7 %collective-permute-start.15 = (bf16[24,16,256]{2,1,0:T(8,128)(2,1)S(1)}, bf16[24,16,256]{2,1,0:T(8,128)(2,1)S(1)}, u32[]{:S(2)}, u32[]{:S(2)}) collective-permute-start(bf16[24,16,256]{2,1,0:T(8,128)(2,1)S(1)} %get-tuple-element.13), channel_id=1, source_target_pairs={{4,8},{5,9},{6,10},{7,11},{24,28},{25,29},{26,30},{27,31}} | collective-permute-start | bytes 589832 | tf_op jit(solution)/shard_map/ppermute | solution.py:100
  68.6 2.0 %collective-permute-start.16 = (bf16[24,16,256]{2,1,0:T(8,128)(2,1)S(1)}, bf16[24,16,256]{2,1,0:T(8,128)(2,1)S(1)}, u32[]{:S(2)}, u32[]{:S(2)}) collective-permute-start(bf16[24,16,256]{2,1,0:T(8,128)(2,1)S(1)} %get-tuple-element.15), channel_id=1, source_target_pairs={{4,12},{5,13},{6,14},{7,15},{24,16},{25,17},{26,18},{27,19}} | collective-permute-start | bytes 589832 | tf_op jit(solution)/shard_map/ppermute | solution.py:100
  69.3 8.5 %collective-permute-start.17 = (bf16[24,16,256]{2,1,0:T(8,128)(2,1)S(1)}, bf16[24,16,256]{2,1,0:T(8,128)(2,1)S(1)}, u32[]{:S(2)}, u32[]{:S(2)}) collective-permute-start(bf16[24,16,256]{2,1,0:T(8,128)(2,1)S(1)} %get-tuple-element.14), channel_id=1, source_target_pairs={{4,0},{5,1},{6,2},{7,3},{24,20},{25,21},{26,22},{27,23}} | collective-permute-start | bytes 589832 | tf_op jit(solution)/shard_map/ppermute | solution.py:100

commit v2 on v1

v2 whole, which is shorter than its diff:
```python
import functools

import jax
import jax.numpy as jnp
from jax import lax
from jax.experimental import pallas as pl
from jax.experimental.pallas import tpu as pltpu
from jax.sharding import PartitionSpec as P

AXES = ("segment", "lon", "lat")


def with_halo(cells, sides, width):
    for axis, dim in sides:
        count = lax.axis_size(axis)
        ends = count - 1
        head = lax.slice_in_dim(cells, 0, width, axis=dim)
        tail = lax.slice_in_dim(cells, cells.shape[dim] - width, cells.shape[dim], axis=dim)
        cells = jnp.concatenate(
            [
                lax.ppermute(tail, axis, [(i, (i + 1) % count) for i in range(ends)]),
                cells,
                lax.ppermute(head, axis, [((i + 1) % count, i) for i in range(ends)]),
            ],
            axis=dim,
        )
    return cells


def from_behind(value, axis, steps):
    count = lax.axis_size(axis)
    pairs = [(source, (source + steps) % count) for source in range(count)]
    return lax.ppermute(value, axis, pairs)


def partner(block, axis):
    count = lax.axis_size(axis)
    return lax.ppermute(block, axis, [(i, i ^ 1) for i in range(count) if i ^ 1 < count])


def gelu_slope(hidden):
    normal_cdf = 0.5 * (1.0 + lax.erf(hidden * 0.7071067811865476))
    density = jnp.exp(-0.5 * hidden * hidden) * 0.3989422804014327
    return normal_cdf + hidden * density


def tap_adjoint(conv_grad, taps_now, offset):
    lon_cells = conv_grad.shape[0]
    lat_padded = with_halo(conv_grad, (("lat", 1),), 1)
    meridional = taps_now[3] * lat_padded[:, 2:] + taps_now[4] * lat_padded[:, :-2]
    centre = taps_now[1] * conv_grad
    rim_width = 3 * lon_cells
    pieces = []
    for distance in (3, 2, 1, 0, -1, -2, -3):
        pieces.append(conv_grad if distance == 0 else from_behind(conv_grad, "lon", distance))
    padded = jnp.concatenate(pieces, axis=0)
    ahead_cells = lax.dynamic_slice_in_dim(padded, rim_width + offset, lon_cells, 0)
    behind = lax.dynamic_slice_in_dim(padded, rim_width - offset, lon_cells, 0)
    zonal_sum = taps_now[0] * ahead_cells + taps_now[2] * behind
    zonal_sum = lax.optimization_barrier(zonal_sum.astype(jnp.bfloat16)).astype(jnp.float32)
    return zonal_sum + centre + meridional


def by_exchange(dec_cot, saved_conv, dec_weight, w_in, w_out, conv_taps, dilation):
    lon_cells, lat_rows, chans = saved_conv.shape[2:]
    own_cot = dec_cot[0].reshape(-1, dec_cot.shape[3])
    projected = jnp.einsum(
        "nv,cv->nc", own_cot, dec_weight, preferred_element_type=jnp.float32
    ).astype(jnp.bfloat16)
    gradient = lax.optimization_barrier(partner(projected, "segment")).astype(jnp.float32)
    for layer in reversed(range(w_in.shape[0])):
        conv_out = saved_conv[0, layer].reshape(-1, chans)
        hidden = jnp.dot(conv_out, w_in[layer], preferred_element_type=jnp.float32)
        act_grad = jnp.einsum(
            "nc,hc->nh",
            gradient.astype(jnp.bfloat16),
            w_out[layer],
            preferred_element_type=jnp.float32,
        )
        pre_grad = (act_grad * gelu_slope(hidden)).astype(jnp.bfloat16)
        conv_grad = jnp.einsum(
            "nh,ch->nc", pre_grad, w_in[layer], preferred_element_type=jnp.float32
        ).astype(jnp.bfloat16)
        tapped = tap_adjoint(
            conv_grad.reshape(lon_cells, lat_rows, chans), conv_taps[layer], dilation[layer]
        )
        gradient = gradient + tapped.reshape(-1, chans)
    return gradient.reshape(1, lon_cells, lat_rows, chans).astype(jnp.bfloat16)


def routed(value, hop):
    cores, cols, rows = (lax.axis_size(a) for a in AXES)
    pairs = []
    for c in range(cores):
        for z in range(cols):
            for j in range(rows):
                to = hop(c, z, j)
                if to is not None and 0 <= to[2] < rows:
                    pairs.append(((c * cols + z) * rows + j, (to[0] * cols + to[1]) * rows + to[2]))
    return lax.ppermute(value, AXES, pairs)


def row_chunks(low, high):
    count = max(1, (high - low) // 4)
    edges = [low + (high - low) * i // count for i in range(count + 1)]
    return list(zip(edges[:-1], edges[1:]))


def on_home():
    return lax.axis_index("lon") == lax.axis_index("segment") + 1


def edge_start(layer):
    return layer * (layer + 1) // 2


def edges_kernel(layers, conv, cot, first_ref, top_ref, bottom_ref):
    rows, chans, v = cot.shape[0], conv.shape[3], cot.shape[2]
    first_ref[:, :, :chans] = conv[layers - 1]
    first_ref[:, :, chans:] = cot[...]
    for layer in range(layers):
        here = slice(edge_start(layer), edge_start(layer + 1))
        top_ref[here] = conv[layer, : layer + 1]
        bottom_ref[here] = conv[layer, rows - layer - 1 :]
    for k in range(layers):
        at, lanes = edge_start(layers) + k // 2, slice(k % 2 * v, (k % 2 + 1) * v)
        top_ref[at, :, lanes] = cot[k]
        bottom_ref[at, :, lanes] = cot[rows - layers + k]


def cut_edges(conv, cot):
    layers, rows, cells, chans = conv.shape
    edge = jax.ShapeDtypeStruct((edge_start(layers) + layers // 2, cells, chans), conv.dtype)
    first = jax.ShapeDtypeStruct((rows, cells, chans + cot.shape[2]), conv.dtype)
    vmem = pl.BlockSpec(memory_space=pltpu.VMEM)
    return pl.pallas_call(
        functools.partial(edges_kernel, layers),
        out_shape=(first, edge, edge),
        in_specs=[vmem, vmem],
        out_specs=(vmem, vmem, vmem),
        compiler_params=pltpu.CompilerParams(vmem_limit_bytes=16 * 2**20),
        name="edges",
    )(conv, cot)


def layer_kernel(layer, layers, slot, *refs):
    pl.when(on_home())(functools.partial(layer_body, layer, layers, slot, *refs))


def layer_body(layer, layers, slot, *refs):
    first, last = layer == layers - 1, layer == 0
    offset_ref, refs = refs[0], refs[1:]
    mains, halos, refs = refs[:4], refs[4:8], refs[8:]
    carried, w_in, w_out, taps, refs = refs[0], refs[1], refs[2], refs[3], refs[4:]
    outs, refs = (refs[:4], refs[4:]) if last else (refs[:1], refs[1:])
    cg = refs[0]
    rows, cells = mains[0].shape[-3:-1]
    chans = halos[0].shape[2]
    v = mains[0].shape[-1] - chans
    lon, wide = 4 * cells, layer + 1
    window = rows + 2 * wide
    halves = [(h, slice(h * 128, (h + 1) * 128)) for h in range(chans // 128)]
    half_halo = halos[0].shape[0] // 2
    offset = offset_ref[layer]
    lat = lax.axis_index("lat")
    has_above = jnp.where(lat > 0, 1.0, 0.0).astype(jnp.float32)
    has_below = jnp.where(lat < lax.axis_size("lat") - 1, 1.0, 0.0).astype(jnp.float32)

    def main_row(p, r):
        return mains[p][r] if slot is None else mains[p][slot, r]

    def conv_row(r):
        if r < wide:
            return [h[edge_start(layer) + r] for h in halos]
        if r < wide + rows:
            return [main_row(p, r - wide)[:, :chans] for p in range(4)]
        return [h[half_halo + edge_start(layer) + r - wide - rows] for h in halos]

    def cot_row(r):
        if wide <= r < wide + rows:
            return [main_row(p, r - wide)[:, chans:] for p in range(4)]
        k = r if r < wide else r - wide - rows
        at = edge_start(layers) + k // 2 + (0 if r < wide else half_halo)
        return [h[at, :, k % 2 * v : (k % 2 + 1) * v] for h in halos]

    def nt(a, b):
        return lax.dot_general(a, b, (((1,), (1,)), ((), ())), preferred_element_type=jnp.float32)

    def taps_of(r):
        for h, lanes in halves:
            t = [taps[layer, k : k + 1, lanes] for k in range(5)]
            total = t[0] * cg[r, h, pl.ds(offset, lon)] + t[2] * cg[r, h, pl.ds(lon - offset, lon)]
            total += t[1] * cg[r, h, 0:lon] + t[3] * cg[r + 1, h, 0:lon] + t[4] * cg[r - 1, h, 0:lon]
            if first:
                total += refs[1][r, :, lanes].astype(jnp.float32)
            else:
                total += carried[r, :, lanes]
            if last:
                low = total.astype(jnp.bfloat16)
                for p in range(4):
                    outs[p][r - 1, :, lanes] = low[p * cells : (p + 1) * cells]
            else:
                outs[0][r - 1, :, lanes] = total

    done = 1
    for r0, r1 in row_chunks(0, window):
        count = (r1 - r0) * lon
        conv_out = jnp.concatenate(sum([conv_row(r) for r in range(r0, r1)], []), axis=0)
        hidden = jnp.dot(conv_out, w_in[layer], preferred_element_type=jnp.float32)
        if first:
            cot = jnp.concatenate(sum([cot_row(r) for r in range(r0, r1)], []), axis=0)
            low = nt(cot, carried[...]).astype(jnp.bfloat16)
        else:
            low = carried[r0:r1].reshape(count, chans).astype(jnp.bfloat16)
        pre = (nt(low, w_out[layer]) * gelu_slope(hidden)).astype(jnp.bfloat16)
        conv_grad = nt(pre, w_in[layer]).reshape(r1 - r0, lon, chans)
        while done < r0 - 1:
            taps_of(done)
            done += 1
        if first:
            refs[1][r0:r1] = low.reshape(r1 - r0, lon, chans)
        for r in range(r0, r1):
            rows_here = conv_grad[r - r0]
            if r < wide:
                rows_here = rows_here * has_above
            if r >= wide + rows:
                rows_here = rows_here * has_below
            for h, lanes in halves:
                cg[r, h, 0:lon] = rows_here[:, lanes]
                cg[r, h, lon : 2 * lon] = rows_here[:, lanes]
    while done < window - 1:
        taps_of(done)
        done += 1


def run_layer(layer, layers, slot, offsets, mains, halos, carried, w_in, w_out, taps):
    first, last = layer == layers - 1, layer == 0
    rows, cells = mains[0].shape[-3:-1]
    chans = halos[0].shape[2]
    lon = 4 * cells
    window = rows + 2 * (layer + 1)
    smem = pl.BlockSpec(memory_space=pltpu.SMEM)
    vmem = pl.BlockSpec(memory_space=pltpu.VMEM)
    args = [offsets, *mains, *halos, carried, w_in, w_out, taps]
    if last:
        out = [jax.ShapeDtypeStruct((rows, cells, chans), jnp.bfloat16)] * 4
    else:
        out = [jax.ShapeDtypeStruct((window - 2, lon, chans), jnp.float32)]
    scratch = [pltpu.VMEM((window, chans // 128, 2 * lon, 128), jnp.float32)]
    if first:
        scratch.append(pltpu.VMEM((window, lon, chans), jnp.bfloat16))
    work = window * lon
    return pl.pallas_call(
        functools.partial(layer_kernel, layer, layers, slot),
        out_shape=out,
        in_specs=[smem] + [vmem] * (len(args) - 1),
        out_specs=[vmem] * len(out),
        scratch_shapes=scratch,
        compiler_params=pltpu.CompilerParams(vmem_limit_bytes=32 * 2**20),
        cost_estimate=pl.CostEstimate(
            flops=6 * work * chans * w_in.shape[2],
            bytes_accessed=work * chans * 10,
            transcendentals=2 * work * w_in.shape[2],
        ),
        name=f"layer_{layer}",
    )(*args)


def by_circles(dec_cot, saved_conv, dec_weight, w_in, w_out, conv_taps, dilation):
    layers = w_in.shape[0]

    def home(c):
        return c + 1

    def gather(value):
        found = [value]
        for k in range(1, 4):
            found.append(
                routed(value, lambda c, z, j: (c, home(c), j) if z == (home(c) + k) % 4 else None)
            )
        return found

    cot = partner(dec_cot[0], "segment").transpose(1, 0, 2)
    conv = saved_conv[0].transpose(0, 2, 1, 3)
    message, top, bottom = cut_edges(conv, cot)
    below = routed(top, lambda c, z, j: (c, z, j - 1))
    above = routed(bottom, lambda c, z, j: (c, z, j + 1))
    mains = {layers - 1: (None, gather(message))}
    halos = gather(jnp.concatenate([above, below], axis=0))
    mains[layers - 2] = (None, gather(conv[layers - 2]))
    rest = gather(conv[: layers - 2])
    for layer in range(layers - 2):
        mains[layer] = (layer, rest)

    carried = dec_weight
    for layer in reversed(range(layers)):
        slot, pieces = mains[layer]
        found = run_layer(
            layer, layers, slot, dilation, pieces, halos, carried, w_in, w_out, conv_taps
        )
        carried = found[0]

    result = jnp.where(on_home(), found[0], 0)
    for k in range(1, 4):
        result = result + routed(
            found[k], lambda c, z, j: (c, (z + k) % 4, j) if z == home(c) else None
        )
    return result.transpose(1, 0, 2)[None]


def solution(mesh):
    in_specs = (
        P("segment", "lon", "lat", None),
        P("segment", None, "lon", "lat", None),
        P(),
        P(),
        P(),
        P(),
        P(),
    )
    out_specs = P("segment", "lon", "lat", None)
    gathers = mesh.shape["lon"] == 4 and mesh.shape["segment"] == 2
    return jax.shard_map(
        by_circles if gathers else by_exchange,
        mesh=mesh,
        in_specs=in_specs,
        out_specs=out_specs,
        check_vma=False,
    )
```

time: 79.2 us -> 72.8 us (0.919)
  waiting for transfers between devices: 12.9 us -> 36.8 us
  Pallas kernels: 17 us -> 2.47 us
  local copies, waits for them, and re-layouts: 11 us -> 3.13 us
  other arithmetic: 4.17 us -> 0.04 us
  starting transfers between devices: 33 us -> 29.5 us
    ppermute x17, waiting for transfers between devices: 12.9 us -> 36.8 us  [routed(): return lax.ppermute(value, AXES, pairs)]
    pallas_call x4 -> x5, Pallas kernels: 17 us -> 2.47 us  [the longest x4 2.42 us: run_layer(): pl.pallas_call(functools.partial(layer_kernel, layer, layers, slot), out_...]
    concatenate x8 -> x0, other arithmetic: 4.12 us -> none  [the longest x4 1.06 us: wide(): jnp.concatenate([above[start:start + layer + 1], conv[layer], below[start...]
    ppermute x17, starting transfers between devices: 32.5 us -> 29 us  [routed(): return lax.ppermute(value, AXES, pairs)]
    squeeze x4 -> x1, local copies, waits for them, and re-layouts: 3.3 us -> 0.01 us  [by_circles(): mains[layers - 2] = (None, gather(conv[layers - 2]))]
    unnamed x14, local copies, waits for them, and re-layouts: 5.32 us -> 2.34 us
    slice x19 -> x1, local copies, waits for them, and re-layouts: 1.63 us -> 0.03 us  [by_circles(): rest = gather(conv[:layers - 2])]
  transfers between devices with their start and end apart: 18 -> 18, of which waited for: 3 -> 5; matrix products, arithmetic and copies ran while one was open for 13% -> 2% of each run, Pallas kernels for 17% -> 2%
where the time goes in v2:
time: 72.8 us; the launch traced here: 72.4 us
  waiting for transfers between devices  36.8 us (51%)
  starting transfers between devices  29.5 us (41%)
  local copies, waits for them, and re-layouts  3.13 us (4%)
  Pallas kernels  2.47 us (3%)
    ppermute x17, waiting for transfers between devices, routed(): return lax.ppermute(value, AXES, pairs)  36.8 us
    ppermute x17, starting transfers between devices, routed(): return lax.ppermute(value, AXES, pairs)  29 us
    pallas_call x4, Pallas kernels, run_layer(): pl.pallas_call(functools.partial(layer_kernel, layer, layers, slot), out_...  2.42 us
    unnamed x14, local copies, waits for them, and re-layouts  2.34 us
  transfers between devices with their start and end apart: 18, of which 5 were waited for; matrix products, arithmetic and copies ran while one was open for 2% of the time, Pallas kernels for 2%

profile of v2, /device:TPU:0, one launch (start us, length us, event | category | flops | bytes accessed | tf_op | source)
XLA Modules:
  0.0 72.4 jit_solution(12359485121932937810)
XLA Ops:
  0.0 0.9 %copy.18 = bf16[1,16,24,128]{3,1,2,0:T(8,128)(2,1)S(1)} copy(bf16[1,16,24,128]{3,2,1,0:T(8,128)(2,1)} %param.7) | data formatting | bytes 196608 | tf_op args[0]
  1.5 1.4 %copy.17 = bf16[1,4,16,24,256]{4,2,3,1,0:T(8,128)(2,1)S(1)} copy(bf16[1,4,16,24,256]{4,3,2,1,0:T(8,128)(2,1)} %param.8) | data formatting | bytes 1572864 | tf_op args[1]
  2.9 4.5 %collective-permute-start.4 = (bf16[12,16,256]{2,1,0:T(8,128)(2,1)S(1)}, bf16[12,16,256]{2,1,0:T(8,128)(2,1)S(1)}, u32[]{:S(2)}, u32[]{:S(2)}) collective-permute-start(bf16[12,16,256]{2,1,0:T(8,128)(2,1)S(1)} %get-tuple-element.12), channel_id=1, source_target_pairs={{0,1},{1,2},{2,3},{4,5},{5,6},{6,7},{8,9},{9,10},{10,11},{12,13},{... | collective-permute-start | bytes 294920 | tf_op jit(solution)/shard_map/ppermute | solution.py:100
  7.4 0.7 collective-permute-start.10
  8.1 1.3 %collective-permute-start.5 = (bf16[12,16,256]{2,1,0:T(8,128)(2,1)S(1)}, bf16[12,16,256]{2,1,0:T(8,128)(2,1)S(1)}, u32[]{:S(2)}, u32[]{:S(2)}) collective-permute-start(bf16[12,16,256]{2,1,0:T(8,128)(2,1)S(1)} %get-tuple-element.13), channel_id=1, source_target_pairs={{1,0},{2,1},{3,2},{5,4},{6,5},{7,6},{9,8},{10,9},{11,10},{13,12},{... | collective-permute-start | bytes 294920 | tf_op jit(solution)/shard_map/ppermute | solution.py:100
  10.0 4.7 %collective-permute-done.5 = bf16[12,16,256]{2,1,0:T(8,128)(2,1)S(1)} collective-permute-done((bf16[12,16,256]{2,1,0:T(8,128)(2,1)S(1)}, bf16[12,16,256]{2,1,0:T(8,128)(2,1)S(1)}, u32[]{:S(2)}, u32[]{:S(2)}) %collective-permute-start.5) | collective-permute-done | bytes 98336 | tf_op jit(solution)/shard_map/ppermute | solution.py:100
  14.6 0.7 collective-permute-start.6
  15.3 0.7 collective-permute-start.12
  16.0 0.7 collective-permute-start.13
  16.7 6.0 %collective-permute-start.14 = (bf16[24,16,384]{2,1,0:T(8,128)(2,1)S(1)}, bf16[24,16,384]{2,1,0:T(8,128)(2,1)S(1)}, u32[]{:S(2)}, u32[]{:S(2)}) collective-permute-start(bf16[24,16,384]{2,1,0:T(8,128)(2,1)S(1)} %get-tuple-element.14.refs_1_), channel_id=1, source_target_pairs={{0,4},{1,5},{2,6},{3,7},{20,24},{21,25},{22,26},{23,27}} | collective-permute-start | bytes 884744 | tf_op jit(solution)/shard_map/ppermute | solution.py:100
  22.7 0.7 collective-permute-start.7
  23.4 2.9 %collective-permute-start.8 = (bf16[24,16,256]{2,1,0:T(8,128)(2,1)S(1)}, bf16[24,16,256]{2,1,0:T(8,128)(2,1)S(1)}, u32[]{:S(2)}, u32[]{:S(2)}) collective-permute-start(bf16[24,16,256]{2,1,0:T(8,128)(2,1)S(1)} %constant_dynamic-update-slice_fusion.refs_5_), channel_id=1, source_target_pairs={{0,4},{1,5},{2,6},{3,7},{20,24},{21,25},{22,26},{23,27}} | collective-permute-start | bytes 589832 | tf_op jit(solution)/shard_map/ppermute | solution.py:100
  26.3 0.7 collective-permute-start
  27.0 5.9 %collective-permute-done.8.refs_8_ = bf16[24,16,256]{2,1,0:T(8,128)(2,1)S(1)} collective-permute-done((bf16[24,16,256]{2,1,0:T(8,128)(2,1)S(1)}, bf16[24,16,256]{2,1,0:T(8,128)(2,1)S(1)}, u32[]{:S(2)}, u32[]{:S(2)}) %collective-permute-start.8) | collective-permute-done | bytes 196640 | tf_op jit(solution)/shard_map/ppermute | solution.py:100
  33.0 0.7 collective-permute-start.1
  33.7 5.0 %collective-permute-start.2 = (bf16[2,24,16,256]{3,2,1,0:T(8,128)(2,1)S(1)}, bf16[2,24,16,256]{3,2,1,0:T(8,128)(2,1)S(1)}, u32[]{:S(2)}, u32[]{:S(2)}) collective-permute-start(bf16[2,24,16,256]{3,2,1,0:T(8,128)(2,1)S(1)} %slice.8.refs_1_), channel_id=1, source_target_pairs={{0,4},{1,5},{2,6},{3,7},{20,24},{21,25},{22,26},{23,27}} | collective-permute-start | bytes 1179656 | tf_op jit(solution)/shard_map/ppermute | solution.py:100
  38.7 1.3 %collective-permute-start.11 = (bf16[24,16,256]{2,1,0:T(8,128)(2,1)S(1)}, bf16[24,16,256]{2,1,0:T(8,128)(2,1)S(1)}, u32[]{:S(2)}, u32[]{:S(2)}) collective-permute-start(bf16[24,16,256]{2,1,0:T(8,128)(2,1)S(1)} %slice_bitcast_fusion.refs_1_), channel_id=1, source_target_pairs={{0,4},{1,5},{2,6},{3,7},{20,24},{21,25},{22,26},{23,27}} | collective-permute-start | bytes 589832 | tf_op jit(solution)/shard_map/ppermute | solution.py:100
  40.0 0.7 collective-permute-start.9
  41.3 7.4 %collective-permute-done.11.refs_4_ = bf16[24,16,256]{2,1,0:T(8,128)(2,1)S(1)} collective-permute-done((bf16[24,16,256]{2,1,0:T(8,128)(2,1)S(1)}, bf16[24,16,256]{2,1,0:T(8,128)(2,1)S(1)}, u32[]{:S(2)}, u32[]{:S(2)}) %collective-permute-start.11) | collective-permute-done | bytes 196640 | tf_op jit(solution)/shard_map/ppermute | solution.py:100
  49.9 0.7 %layer_0.1 = (bf16[24,16,256]{2,1,0:T(8,128)(2,1)S(1)}, bf16[24,16,256]{2,1,0:T(8,128)(2,1)S(1)}, bf16[24,16,256]{2,1,0:T(8,128)(2,1)S(1)}, bf16[24,16,256]{2,1,0:T(8,128)(2,1)S(1)}) custom-call(s32[4]{0:T(128)S(1)} %copy-done.3, bf16[2,24,16,256]{3,2,1,0:T(8,128)(2,1)S(1)} %slice.8.refs_1_, bf16[2,24,16,256]{3,2,1,0:T(8,128)(2,1)S(1)} %collective-permute-done.refs_2_, ...), custom_call_target="tpu_custom_call" | custom-call | flops 1308622848 | bytes 4259840 | tf_op jit(solution)/shard_map/layer_0/pallas_call | solution.py:253
  50.6 0.7 collective-permute-start.15
  52.0 1.3 %collective-permute-start.17 = (bf16[24,16,256]{2,1,0:T(8,128)(2,1)S(1)}, bf16[24,16,256]{2,1,0:T(8,128)(2,1)S(1)}, u32[]{:S(2)}, u32[]{:S(2)}) collective-permute-start(bf16[24,16,256]{2,1,0:T(8,128)(2,1)S(1)} %get-tuple-element.18), channel_id=1, source_target_pairs={{4,0},{5,1},{6,2},{7,3},{24,20},{25,21},{26,22},{27,23}} | collective-permute-start | bytes 589832 | tf_op jit(solution)/shard_map/ppermute | solution.py:100
  53.3 18.3 %collective-permute-done.17 = bf16[24,16,256]{2,1,0:T(8,128)(2,1)S(1)} collective-permute-done((bf16[24,16,256]{2,1,0:T(8,128)(2,1)S(1)}, bf16[24,16,256]{2,1,0:T(8,128)(2,1)S(1)}, u32[]{:S(2)}, u32[]{:S(2)}) %collective-permute-start.17) | collective-permute-done | bytes 196640 | tf_op jit(solution)/shard_map/ppermute | solution.py:100
  71.6 0.7 %copy.14 = bf16[1,16,24,256]{3,2,1,0:T(8,128)(2,1)} copy(bf16[1,16,24,256]{3,1,2,0:T(8,128)(2,1)S(1)} %add_bitcast_fusion) | data formatting | bytes 393216 | tf_op jit(solution)/shard_map/broadcast_in_dim | solution.py:308
  (36 shorter events, 3.6 us)
Async XLA Ops:
  0.9 39.8 %copy-start.4 = (f32[4,5,256]{2,0,1:T(4,128)S(1)}, f32[4,5,256]{2,0,1:T(4,128)}, u32[]{:S(2)}) copy-start(f32[4,5,256]{2,0,1:T(4,128)} %param.12) | copy-start | bytes 61444
  0.9 39.8 %copy-start = (bf16[4,256,512]{2,1,0:T(8,128)(2,1)S(1)}, bf16[4,256,512]{2,1,0:T(8,128)(2,1)}, u32[]{:S(2)}) copy-start(bf16[4,256,512]{2,1,0:T(8,128)(2,1)} %refs_10_.7) | copy-start | bytes 3145732
  0.9 39.8 %copy-start.1 = (bf16[4,512,256]{2,1,0:T(8,128)(2,1)S(1)}, bf16[4,512,256]{2,1,0:T(8,128)(2,1)}, u32[]{:S(2)}) copy-start(bf16[4,512,256]{2,1,0:T(8,128)(2,1)} %refs_11_.7) | copy-start | bytes 3145732
  0.9 39.8 %copy-start.2 = (bf16[256,128]{1,0:T(8,128)(2,1)S(1)}, bf16[256,128]{1,0:T(8,128)(2,1)}, u32[]{:S(2)}) copy-start(bf16[256,128]{1,0:T(8,128)(2,1)} %refs_9_.1) | copy-start | bytes 196612
  1.0 39.8 %copy-start.3 = (s32[4]{0:T(128)S(1)}, s32[4]{0:T(128)}, u32[]{:S(2)}) copy-start(s32[4]{0:T(128)} %refs_0_.7) | copy-start | bytes 52
  1.0 1.9 %collective-permute-start.3 = (bf16[16,24,128]{2,0,1:T(8,128)(2,1)S(1)}, bf16[16,24,128]{2,0,1:T(8,128)(2,1)S(1)}, u32[]{:S(2)}, u32[]{:S(2)}) collective-permute-start(bf16[16,24,128]{2,0,1:T(8,128)(2,1)S(1)} %bitcast.19), channel_id=1, source_target_pairs={{0,16},{16,0},{1,17},{17,1},{2,18},{18,2},{3,19},{19,3},{4,20},{20... | collective-permute-start | bytes 294920 | tf_op jit(solution)/shard_map/ppermute | solution.py:38
  2.9 7.0 %collective-permute-start.4 = (bf16[12,16,256]{2,1,0:T(8,128)(2,1)S(1)}, bf16[12,16,256]{2,1,0:T(8,128)(2,1)S(1)}, u32[]{:S(2)}, u32[]{:S(2)}) collective-permute-start(bf16[12,16,256]{2,1,0:T(8,128)(2,1)S(1)} %get-tuple-element.12), channel_id=1, source_target_pairs={{0,1},{1,2},{2,3},{4,5},{5,6},{6,7},{8,9},{9,10},{10,11},{12,13},{... | collective-permute-start | bytes 294920 | tf_op jit(solution)/shard_map/ppermute | solution.py:100
  7.4 15.2 %collective-permute-start.10 = (bf16[24,16,256]{2,1,0:T(8,128)(2,1)S(1)}, bf16[24,16,256]{2,1,0:T(8,128)(2,1)S(1)}, u32[]{:S(2)}, u32[]{:S(2)}) collective-permute-start(bf16[24,16,256]{2,1,0:T(8,128)(2,1)S(1)} %slice_bitcast_fusion.refs_1_), channel_id=1, source_target_pairs={{12,4},{13,5},{14,6},{15,7},{16,24},{17,25},{18,26},{19,27}} | collective-permute-start | bytes 589832 | tf_op jit(solution)/shard_map/ppermute | solution.py:100
  8.1 6.5 %collective-permute-start.5 = (bf16[12,16,256]{2,1,0:T(8,128)(2,1)S(1)}, bf16[12,16,256]{2,1,0:T(8,128)(2,1)S(1)}, u32[]{:S(2)}, u32[]{:S(2)}) collective-permute-start(bf16[12,16,256]{2,1,0:T(8,128)(2,1)S(1)} %get-tuple-element.13), channel_id=1, source_target_pairs={{1,0},{2,1},{3,2},{5,4},{6,5},{7,6},{9,8},{10,9},{11,10},{13,12},{... | collective-permute-start | bytes 294920 | tf_op jit(solution)/shard_map/ppermute | solution.py:100
  14.6 8.7 %collective-permute-start.6 = (bf16[24,16,256]{2,1,0:T(8,128)(2,1)S(1)}, bf16[24,16,256]{2,1,0:T(8,128)(2,1)S(1)}, u32[]{:S(2)}, u32[]{:S(2)}) collective-permute-start(bf16[24,16,256]{2,1,0:T(8,128)(2,1)S(1)} %constant_dynamic-update-slice_fusion.refs_5_), channel_id=1, source_target_pairs={{8,4},{9,5},{10,6},{11,7},{28,24},{29,25},{30,26},{31,27}} | collective-permute-start | bytes 589832 | tf_op jit(solution)/shard_map/ppermute | solution.py:100
  15.3 18.3 %collective-permute-start.12 = (bf16[24,16,384]{2,1,0:T(8,128)(2,1)S(1)}, bf16[24,16,384]{2,1,0:T(8,128)(2,1)S(1)}, u32[]{:S(2)}, u32[]{:S(2)}) collective-permute-start(bf16[24,16,384]{2,1,0:T(8,128)(2,1)S(1)} %get-tuple-element.14.refs_1_), channel_id=1, source_target_pairs={{8,4},{9,5},{10,6},{11,7},{28,24},{29,25},{30,26},{31,27}} | collective-permute-start | bytes 884744 | tf_op jit(solution)/shard_map/ppermute | solution.py:100
  16.0 22.7 %collective-permute-start.13 = (bf16[24,16,384]{2,1,0:T(8,128)(2,1)S(1)}, bf16[24,16,384]{2,1,0:T(8,128)(2,1)S(1)}, u32[]{:S(2)}, u32[]{:S(2)}) collective-permute-start(bf16[24,16,384]{2,1,0:T(8,128)(2,1)S(1)} %get-tuple-element.14.refs_1_), channel_id=1, source_target_pairs={{12,4},{13,5},{14,6},{15,7},{16,24},{17,25},{18,26},{19,27}} | collective-permute-start | bytes 884744 | tf_op jit(solution)/shard_map/ppermute | solution.py:100
  16.7 23.3 %collective-permute-start.14 = (bf16[24,16,384]{2,1,0:T(8,128)(2,1)S(1)}, bf16[24,16,384]{2,1,0:T(8,128)(2,1)S(1)}, u32[]{:S(2)}, u32[]{:S(2)}) collective-permute-start(bf16[24,16,384]{2,1,0:T(8,128)(2,1)S(1)} %get-tuple-element.14.refs_1_), channel_id=1, source_target_pairs={{0,4},{1,5},{2,6},{3,7},{20,24},{21,25},{22,26},{23,27}} | collective-permute-start | bytes 884744 | tf_op jit(solution)/shard_map/ppermute | solution.py:100
  22.7 3.7 %collective-permute-start.7 = (bf16[24,16,256]{2,1,0:T(8,128)(2,1)S(1)}, bf16[24,16,256]{2,1,0:T(8,128)(2,1)S(1)}, u32[]{:S(2)}, u32[]{:S(2)}) collective-permute-start(bf16[24,16,256]{2,1,0:T(8,128)(2,1)S(1)} %constant_dynamic-update-slice_fusion.refs_5_), channel_id=1, source_target_pairs={{12,4},{13,5},{14,6},{15,7},{16,24},{17,25},{18,26},{19,27}} | collective-permute-start | bytes 589832 | tf_op jit(solution)/shard_map/ppermute | solution.py:100
  23.4 9.6 %collective-permute-start.8 = (bf16[24,16,256]{2,1,0:T(8,128)(2,1)S(1)}, bf16[24,16,256]{2,1,0:T(8,128)(2,1)S(1)}, u32[]{:S(2)}, u32[]{:S(2)}) collective-permute-start(bf16[24,16,256]{2,1,0:T(8,128)(2,1)S(1)} %constant_dynamic-update-slice_fusion.refs_5_), channel_id=1, source_target_pairs={{0,4},{1,5},{2,6},{3,7},{20,24},{21,25},{22,26},{23,27}} | collective-permute-start | bytes 589832 | tf_op jit(solution)/shard_map/ppermute | solution.py:100
  26.3 22.9 %collective-permute-start = (bf16[2,24,16,256]{3,2,1,0:T(8,128)(2,1)S(1)}, bf16[2,24,16,256]{3,2,1,0:T(8,128)(2,1)S(1)}, u32[]{:S(2)}, u32[]{:S(2)}) collective-permute-start(bf16[2,24,16,256]{3,2,1,0:T(8,128)(2,1)S(1)} %slice.8.refs_1_), channel_id=1, source_target_pairs={{8,4},{9,5},{10,6},{11,7},{28,24},{29,25},{30,26},{31,27}} | collective-permute-start | bytes 1179656 | tf_op jit(solution)/shard_map/ppermute | solution.py:100
  33.0 16.3 %collective-permute-start.1 = (bf16[2,24,16,256]{3,2,1,0:T(8,128)(2,1)S(1)}, bf16[2,24,16,256]{3,2,1,0:T(8,128)(2,1)S(1)}, u32[]{:S(2)}, u32[]{:S(2)}) collective-permute-start(bf16[2,24,16,256]{3,2,1,0:T(8,128)(2,1)S(1)} %slice.8.refs_1_), channel_id=1, source_target_pairs={{12,4},{13,5},{14,6},{15,7},{16,24},{17,25},{18,26},{19,27}} | collective-permute-start | bytes 1179656 | tf_op jit(solution)/shard_map/ppermute | solution.py:100
  33.7 15.6 %collective-permute-start.2 = (bf16[2,24,16,256]{3,2,1,0:T(8,128)(2,1)S(1)}, bf16[2,24,16,256]{3,2,1,0:T(8,128)(2,1)S(1)}, u32[]{:S(2)}, u32[]{:S(2)}) collective-permute-start(bf16[2,24,16,256]{3,2,1,0:T(8,128)(2,1)S(1)} %slice.8.refs_1_), channel_id=1, source_target_pairs={{0,4},{1,5},{2,6},{3,7},{20,24},{21,25},{22,26},{23,27}} | collective-permute-start | bytes 1179656 | tf_op jit(solution)/shard_map/ppermute | solution.py:100
  38.7 10.0 %collective-permute-start.11 = (bf16[24,16,256]{2,1,0:T(8,128)(2,1)S(1)}, bf16[24,16,256]{2,1,0:T(8,128)(2,1)S(1)}, u32[]{:S(2)}, u32[]{:S(2)}) collective-permute-start(bf16[24,16,256]{2,1,0:T(8,128)(2,1)S(1)} %slice_bitcast_fusion.refs_1_), channel_id=1, source_target_pairs={{0,4},{1,5},{2,6},{3,7},{20,24},{21,25},{22,26},{23,27}} | collective-permute-start | bytes 589832 | tf_op jit(solution)/shard_map/ppermute | solution.py:100
  40.0 8.7 %collective-permute-start.9 = (bf16[24,16,256]{2,1,0:T(8,128)(2,1)S(1)}, bf16[24,16,256]{2,1,0:T(8,128)(2,1)S(1)}, u32[]{:S(2)}, u32[]{:S(2)}) collective-permute-start(bf16[24,16,256]{2,1,0:T(8,128)(2,1)S(1)} %slice_bitcast_fusion.refs_1_), channel_id=1, source_target_pairs={{8,4},{9,5},{10,6},{11,7},{28,24},{29,25},{30,26},{31,27}} | collective-permute-start | bytes 589832 | tf_op jit(solution)/shard_map/ppermute | solution.py:100
  50.6 2.7 %collective-permute-start.15 = (bf16[24,16,256]{2,1,0:T(8,128)(2,1)S(1)}, bf16[24,16,256]{2,1,0:T(8,128)(2,1)S(1)}, u32[]{:S(2)}, u32[]{:S(2)}) collective-permute-start(bf16[24,16,256]{2,1,0:T(8,128)(2,1)S(1)} %get-tuple-element.16), channel_id=1, source_target_pairs={{4,8},{5,9},{6,10},{7,11},{24,28},{25,29},{26,30},{27,31}} | collective-permute-start | bytes 589832 | tf_op jit(solution)/shard_map/ppermute | solution.py:100
  51.3 2.0 %collective-permute-start.16 = (bf16[24,16,256]{2,1,0:T(8,128)(2,1)S(1)}, bf16[24,16,256]{2,1,0:T(8,128)(2,1)S(1)}, u32[]{:S(2)}, u32[]{:S(2)}) collective-permute-start(bf16[24,16,256]{2,1,0:T(8,128)(2,1)S(1)} %get-tuple-element.17), channel_id=1, source_target_pairs={{4,12},{5,13},{6,14},{7,15},{24,16},{25,17},{26,18},{27,19}} | collective-permute-start | bytes 589832 | tf_op jit(solution)/shard_map/ppermute | solution.py:100
  52.0 19.6 %collective-permute-start.17 = (bf16[24,16,256]{2,1,0:T(8,128)(2,1)S(1)}, bf16[24,16,256]{2,1,0:T(8,128)(2,1)S(1)}, u32[]{:S(2)}, u32[]{:S(2)}) collective-permute-start(bf16[24,16,256]{2,1,0:T(8,128)(2,1)S(1)} %get-tuple-element.18), channel_id=1, source_target_pairs={{4,0},{5,1},{6,2},{7,3},{24,20},{25,21},{26,22},{27,23}} | collective-permute-start | bytes 589832 | tf_op jit(solution)/shard_map/ppermute | solution.py:100

commit v3 on v2

--- a/solution.py
+++ b/solution.py
@@ -101,94 +101,151 @@
 
 
 def row_chunks(low, high):
-    count = max(1, (high - low) // 4)
+    count = max(1, round((high - low) / 7))
     edges = [low + (high - low) * i // count for i in range(count + 1)]
     return list(zip(edges[:-1], edges[1:]))
 
 
-def on_home():
-    return lax.axis_index("lon") == lax.axis_index("segment") + 1
+def home(s):
+    return s + 1
+
+
+def on_low():
+    return lax.axis_index("lon") == home(lax.axis_index("segment"))
+
+
+def on_high():
+    return lax.axis_index("lon") == home(1 - lax.axis_index("segment"))
+
+
+def to_pair(step):
+    def hop(c, z, j):
+        if z == (home(c) + step - 1) % 4:
+            return c, home(c), j
+        if z == (home(c) + step + 1) % 4:
+            return 1 - c, home(c), j
+
+    return hop
+
+
+def to_other(c, z, j):
+    return (1 - c, z, j) if z in (home(0), home(1)) else None
+
+
+def edge_to(step):
+    def hop(c, z, j):
+        if z == (home(c) + step) % 4:
+            return c, home(c), j + 1
+        if z == (home(c) + step + 2) % 4:
+            return 1 - c, home(c), j - 1
+
+    return hop
+
+
+def back_from(piece):
+    def hop(c, z, j):
+        if z == home(c):
+            return c, (home(c) - 1 + piece) % 4, j
+        if z == home(1 - c):
+            return 1 - c, (home(1 - c) + 1 + piece) % 4, j
+
+    return hop
 
 
 def edge_start(layer):
     return layer * (layer + 1) // 2
 
 
-def edges_kernel(layers, conv, cot, first_ref, top_ref, bottom_ref):
+def edges_kernel(layers, conv, cot, *outs):
+    early_ref, late_ref = outs[layers:]
     rows, chans, v = cot.shape[0], conv.shape[3], cot.shape[2]
-    first_ref[:, :, :chans] = conv[layers - 1]
-    first_ref[:, :, chans:] = cot[...]
-    for layer in range(layers):
-        here = slice(edge_start(layer), edge_start(layer + 1))
-        top_ref[here] = conv[layer, : layer + 1]
-        bottom_ref[here] = conv[layer, rows - layer - 1 :]
-    for k in range(layers):
-        at, lanes = edge_start(layers) + k // 2, slice(k % 2 * v, (k % 2 + 1) * v)
-        top_ref[at, :, lanes] = cot[k]
-        bottom_ref[at, :, lanes] = cot[rows - layers + k]
+    for layer in range(layers - 1):
+        outs[layer][...] = conv[layer]
+    outs[layers - 1][:, :, :chans] = conv[layers - 1]
+    outs[layers - 1][:, :, chans:] = cot[...]
+
+    def edges(top_ref, bottom_ref):
+        for layer in range(layers):
+            here = slice(edge_start(layer), edge_start(layer + 1))
+            top_ref[here] = conv[layer, : layer + 1]
+            bottom_ref[here] = conv[layer, rows - layer - 1 :]
+        for k in range(layers):
+            at, lanes = edge_start(layers) + k // 2, slice(k % 2 * v, (k % 2 + 1) * v)
+            top_ref[at, :, lanes] = cot[k]
+            bottom_ref[at, :, lanes] = cot[rows - layers + k]
+
+    bottom_first = (lax.axis_index("lon") - home(lax.axis_index("segment")) + 4) % 4 < 2
+    pl.when(bottom_first)(lambda: edges(late_ref, early_ref))
+    pl.when(jnp.logical_not(bottom_first))(lambda: edges(early_ref, late_ref))
 
 
 def cut_edges(conv, cot):
     layers, rows, cells, chans = conv.shape
     edge = jax.ShapeDtypeStruct((edge_start(layers) + layers // 2, cells, chans), conv.dtype)
+    plain = jax.ShapeDtypeStruct((rows, cells, chans), conv.dtype)
     first = jax.ShapeDtypeStruct((rows, cells, chans + cot.shape[2]), conv.dtype)
     vmem = pl.BlockSpec(memory_space=pltpu.VMEM)
     return pl.pallas_call(
         functools.partial(edges_kernel, layers),
-        out_shape=(first, edge, edge),
+        out_shape=[plain] * (layers - 1) + [first, edge, edge],
         in_specs=[vmem, vmem],
-        out_specs=(vmem, vmem, vmem),
+        out_specs=[vmem] * (layers + 2),
         compiler_params=pltpu.CompilerParams(vmem_limit_bytes=16 * 2**20),
         name="edges",
     )(conv, cot)
 
 
-def layer_kernel(layer, layers, slot, *refs):
-    pl.when(on_home())(functools.partial(layer_body, layer, layers, slot, *refs))
-
-
-def layer_body(layer, layers, slot, *refs):
+def layer_kernel(layer, layers, *refs):
+    pl.when(on_low() | on_high())(functools.partial(layer_body, layer, layers, *refs))
+
+
+def layer_body(layer, layers, *refs):
     first, last = layer == layers - 1, layer == 0
     offset_ref, refs = refs[0], refs[1:]
     mains, halos, refs = refs[:4], refs[4:8], refs[8:]
     carried, w_in, w_out, taps, refs = refs[0], refs[1], refs[2], refs[3], refs[4:]
     outs, refs = (refs[:4], refs[4:]) if last else (refs[:1], refs[1:])
     cg = refs[0]
-    rows, cells = mains[0].shape[-3:-1]
+    rows, cells = mains[0].shape[:2]
     chans = halos[0].shape[2]
-    v = mains[0].shape[-1] - chans
-    lon, wide = 4 * cells, layer + 1
-    window = rows + 2 * wide
+    v = mains[0].shape[2] - chans
+    lon, wide, own = 4 * cells, layer + 1, rows // 2
+    window = own + 2 * wide
     halves = [(h, slice(h * 128, (h + 1) * 128)) for h in range(chans // 128)]
-    half_halo = halos[0].shape[0] // 2
     offset = offset_ref[layer]
+    low = on_low()
     lat = lax.axis_index("lat")
-    has_above = jnp.where(lat > 0, 1.0, 0.0).astype(jnp.float32)
-    has_below = jnp.where(lat < lax.axis_size("lat") - 1, 1.0, 0.0).astype(jnp.float32)
-
-    def main_row(p, r):
-        return mains[p][r] if slot is None else mains[p][slot, r]
+    has_edge = jnp.where(low, lat > 0, lat < lax.axis_size("lat") - 1)
+    has_edge = jnp.where(has_edge, 1.0, 0.0).astype(jnp.float32)
+
+    def main_at(r):
+        return jnp.where(low, r - wide, rows - 1 - (r - wide))
 
     def conv_row(r):
         if r < wide:
-            return [h[edge_start(layer) + r] for h in halos]
-        if r < wide + rows:
-            return [main_row(p, r - wide)[:, :chans] for p in range(4)]
-        return [h[half_halo + edge_start(layer) + r - wide - rows] for h in halos]
+            at = edge_start(layer) + jnp.where(low, r, wide - 1 - r)
+            return [h[at] for h in halos]
+        return [m[main_at(r), :, :chans] for m in mains]
 
     def cot_row(r):
-        if wide <= r < wide + rows:
-            return [main_row(p, r - wide)[:, chans:] for p in range(4)]
-        k = r if r < wide else r - wide - rows
-        at = edge_start(layers) + k // 2 + (0 if r < wide else half_halo)
-        return [h[at, :, k % 2 * v : (k % 2 + 1) * v] for h in halos]
+        if r < wide:
+            base = edge_start(layers)
+            pair = jnp.where(low, r // 2, (wide - 1 - r) // 2)
+            here = [h[base + pair] for h in halos]
+            left = jnp.where(low, r % 2, (wide - 1 - r) % 2) == 0
+            return [jnp.where(left, h[:, :v], h[:, v:]) for h in here]
+        return [m[main_at(r), :, chans:] for m in mains]
 
     def nt(a, b):
         return lax.dot_general(a, b, (((1,), (1,)), ((), ())), preferred_element_type=jnp.float32)
 
+    tap = [[taps[layer, k : k + 1, lanes] for k in range(5)] for _, lanes in halves]
+    for t in tap:
+        t[3], t[4] = jnp.where(low, t[3], t[4]), jnp.where(low, t[4], t[3])
+
     def taps_of(r):
         for h, lanes in halves:
-            t = [taps[layer, k : k + 1, lanes] for k in range(5)]
+            t = tap[h]
             total = t[0] * cg[r, h, pl.ds(offset, lon)] + t[2] * cg[r, h, pl.ds(lon - offset, lon)]
             total += t[1] * cg[r, h, 0:lon] + t[3] * cg[r + 1, h, 0:lon] + t[4] * cg[r - 1, h, 0:lon]
             if first:
@@ -196,9 +253,10 @@
             else:
                 total += carried[r, :, lanes]
             if last:
-                low = total.astype(jnp.bfloat16)
+                low_bits = total.astype(jnp.bfloat16)
+                at = jnp.where(low, r - 1, own - r)
                 for p in range(4):
-                    outs[p][r - 1, :, lanes] = low[p * cells : (p + 1) * cells]
+                    outs[p][at, :, lanes] = low_bits[p * cells : (p + 1) * cells]
             else:
                 outs[0][r - 1, :, lanes] = total
 
@@ -209,22 +267,20 @@
         hidden = jnp.dot(conv_out, w_in[layer], preferred_element_type=jnp.float32)
         if first:
             cot = jnp.concatenate(sum([cot_row(r) for r in range(r0, r1)], []), axis=0)
-            low = nt(cot, carried[...]).astype(jnp.bfloat16)
+            cot_low = nt(cot, carried[...]).astype(jnp.bfloat16)
         else:
-            low = carried[r0:r1].reshape(count, chans).astype(jnp.bfloat16)
-        pre = (nt(low, w_out[layer]) * gelu_slope(hidden)).astype(jnp.bfloat16)
+            cot_low = carried[r0:r1].reshape(count, chans).astype(jnp.bfloat16)
+        pre = (nt(cot_low, w_out[layer]) * gelu_slope(hidden)).astype(jnp.bfloat16)
         conv_grad = nt(pre, w_in[layer]).reshape(r1 - r0, lon, chans)
         while done < r0 - 1:
             taps_of(done)
             done += 1
         if first:
-            refs[1][r0:r1] = low.reshape(r1 - r0, lon, chans)
+            refs[1][r0:r1] = cot_low.reshape(r1 - r0, lon, chans)
         for r in range(r0, r1):
             rows_here = conv_grad[r - r0]
             if r < wide:
-                rows_here = rows_here * has_above
-            if r >= wide + rows:
-                rows_here = rows_here * has_below
+                rows_here = rows_here * has_edge
             for h, lanes in halves:
                 cg[r, h, 0:lon] = rows_here[:, lanes]
                 cg[r, h, lon : 2 * lon] = rows_here[:, lanes]
@@ -233,17 +289,17 @@
         done += 1
 
 
-def run_layer(layer, layers, slot, offsets, mains, halos, carried, w_in, w_out, taps):
+def run_layer(layer, layers, offsets, mains, halos, carried, w_in, w_out, taps):
     first, last = layer == layers - 1, layer == 0
-    rows, cells = mains[0].shape[-3:-1]
+    rows, cells = mains[0].shape[:2]
     chans = halos[0].shape[2]
     lon = 4 * cells
-    window = rows + 2 * (layer + 1)
+    window = rows // 2 + 2 * (layer + 1)
     smem = pl.BlockSpec(memory_space=pltpu.SMEM)
     vmem = pl.BlockSpec(memory_space=pltpu.VMEM)
     args = [offsets, *mains, *halos, carried, w_in, w_out, taps]
     if last:
-        out = [jax.ShapeDtypeStruct((rows, cells, chans), jnp.bfloat16)] * 4
+        out = [jax.ShapeDtypeStruct((rows // 2, cells, chans), jnp.bfloat16)] * 4
     else:
         out = [jax.ShapeDtypeStruct((window - 2, lon, chans), jnp.float32)]
     scratch = [pltpu.VMEM((window, chans // 128, 2 * lon, 128), jnp.float32)]
@@ -251,12 +307,12 @@
         scratch.append(pltpu.VMEM((window, lon, chans), jnp.bfloat16))
     work = window * lon
     return pl.pallas_call(
-        functools.partial(layer_kernel, layer, layers, slot),
+        functools.partial(layer_kernel, layer, layers),
         out_shape=out,
         in_specs=[smem] + [vmem] * (len(args) - 1),
         out_specs=[vmem] * len(out),
         scratch_shapes=scratch,
-        compiler_params=pltpu.CompilerParams(vmem_limit_bytes=32 * 2**20),
+        compiler_params=pltpu.CompilerParams(vmem_limit_bytes=24 * 2**20),
         cost_estimate=pl.CostEstimate(
             flops=6 * work * chans * w_in.shape[2],
             bytes_accessed=work * chans * 10,
@@ -268,43 +324,28 @@
 
 def by_circles(dec_cot, saved_conv, dec_weight, w_in, w_out, conv_taps, dilation):
     layers = w_in.shape[0]
-
-    def home(c):
-        return c + 1
-
-    def gather(value):
-        found = [value]
-        for k in range(1, 4):
-            found.append(
-                routed(value, lambda c, z, j: (c, home(c), j) if z == (home(c) + k) % 4 else None)
-            )
-        return found
-
     cot = partner(dec_cot[0], "segment").transpose(1, 0, 2)
     conv = saved_conv[0].transpose(0, 2, 1, 3)
-    message, top, bottom = cut_edges(conv, cot)
-    below = routed(top, lambda c, z, j: (c, z, j - 1))
-    above = routed(bottom, lambda c, z, j: (c, z, j + 1))
-    mains = {layers - 1: (None, gather(message))}
-    halos = gather(jnp.concatenate([above, below], axis=0))
-    mains[layers - 2] = (None, gather(conv[layers - 2]))
-    rest = gather(conv[: layers - 2])
-    for layer in range(layers - 2):
-        mains[layer] = (layer, rest)
+    *messages, early, late = cut_edges(conv, cot)
+    mains = {}
+    for layer in reversed(range(layers)):
+        own = [routed(messages[layer], to_pair(step)) for step in range(2)]
+        mains[layer] = own + [routed(half, to_other) for half in own]
+        if layer == layers - 1:
+            edges = [routed(early if step < 2 else late, edge_to(step)) for step in range(4)]
+            halos = [edges[3], *edges[:3]]
 
     carried = dec_weight
     for layer in reversed(range(layers)):
-        slot, pieces = mains[layer]
         found = run_layer(
-            layer, layers, slot, dilation, pieces, halos, carried, w_in, w_out, conv_taps
+            layer, layers, dilation, mains[layer], halos, carried, w_in, w_out, conv_taps
         )
         carried = found[0]
 
-    result = jnp.where(on_home(), found[0], 0)
-    for k in range(1, 4):
-        result = result + routed(
-            found[k], lambda c, z, j: (c, (z + k) % 4, j) if z == home(c) else None
-        )
+    parts = [routed(found[p], back_from(p)) for p in range(4)]
+    before = (lax.axis_index("lon") - home(lax.axis_index("segment")) + 5) % 4 < 2
+    one, two = parts[0] + parts[1], parts[2] + parts[3]
+    result = jnp.concatenate([jnp.where(before, one, two), jnp.where(before, two, one)], axis=0)
     return result.transpose(1, 0, 2)[None]
 
 

time: 72.8 us -> 77 us (1.058)
  the two profiles are of different devices: /device:TPU:0 before, /device:TPU:30 now
where the time goes in v3:
time: 77 us; the launch traced here: 76.3 us
  starting transfers between devices  44.5 us (58%)
  waiting for transfers between devices  25.8 us (34%)
  local copies, waits for them, and re-layouts  3.1 us (4%)
  Pallas kernels  2.35 us (3%)
    ppermute x24, starting transfers between devices, routed(): return lax.ppermute(value, AXES, pairs)  44.5 us
    ppermute x24, waiting for transfers between devices, routed(): return lax.ppermute(value, AXES, pairs)  25.8 us
    unnamed x13, local copies, waits for them, and re-layouts  2.36 us
    pallas_call x4, Pallas kernels, run_layer(): pl.pallas_call(functools.partial(layer_kernel, layer, layers), out_shape=...  2.26 us
  transfers between devices with their start and end apart: 25, of which 3 were waited for; matrix products, arithmetic and copies ran while one was open for 2% of the time, Pallas kernels for 2%

profile of v3, /device:TPU:30, one launch (start us, length us, event | category | flops | bytes accessed | tf_op | source)
XLA Modules:
  0.0 76.3 jit_solution(16542183159336560439)
XLA Ops:
  0.0 0.9 %copy.18 = bf16[1,16,24,128]{3,1,2,0:T(8,128)(2,1)S(1)} copy(bf16[1,16,24,128]{3,2,1,0:T(8,128)(2,1)} %param.7) | data formatting | bytes 196608 | tf_op args[0]
  1.1 1.4 %copy.17 = bf16[1,4,16,24,256]{4,2,3,1,0:T(8,128)(2,1)S(1)} copy(bf16[1,4,16,24,256]{4,3,2,1,0:T(8,128)(2,1)} %param.8) | data formatting | bytes 1572864 | tf_op args[1]
  3.3 5.7 %collective-permute-start.6 = (bf16[12,16,256]{2,1,0:T(8,128)(2,1)S(1)}, bf16[12,16,256]{2,1,0:T(8,128)(2,1)S(1)}, u32[]{:S(2)}, u32[]{:S(2)}) collective-permute-start(bf16[12,16,256]{2,1,0:T(8,128)(2,1)S(1)} %get-tuple-element.17), channel_id=1, source_target_pairs={{4,5},{5,6},{6,7},{13,20},{14,21},{15,22},{17,8},{18,9},{19,10},{2... | collective-permute-start | bytes 294920 | tf_op jit(solution)/shard_map/ppermute | solution.py:100
  8.9 0.7 collective-permute-start.13
  10.3 0.7 collective-permute-start.17
  11.0 6.8 %collective-permute-start.18 = (bf16[24,16,384]{2,1,0:T(8,128)(2,1)S(1)}, bf16[24,16,384]{2,1,0:T(8,128)(2,1)S(1)}, u32[]{:S(2)}, u32[]{:S(2)}) collective-permute-start(bf16[24,16,384]{2,1,0:T(8,128)(2,1)S(1)} %get-tuple-element.20), channel_id=1, source_target_pairs={{4,4},{5,5},{6,6},{7,7},{12,20},{13,21},{14,22},{15,23},{16,8},{17... | collective-permute-start | bytes 884744 | tf_op jit(solution)/shard_map/ppermute | solution.py:100
  18.4 1.3 %collective-permute-start.14 = (bf16[24,16,256]{2,1,0:T(8,128)(2,1)S(1)}, bf16[24,16,256]{2,1,0:T(8,128)(2,1)S(1)}, u32[]{:S(2)}, u32[]{:S(2)}) collective-permute-start(bf16[24,16,256]{2,1,0:T(8,128)(2,1)S(1)} %get-tuple-element.19), channel_id=1, source_target_pairs={{4,4},{5,5},{6,6},{7,7},{12,20},{13,21},{14,22},{15,23},{16,8},{17... | collective-permute-start | bytes 589832 | tf_op jit(solution)/shard_map/ppermute | solution.py:100
  19.8 0.7 collective-permute-start.9
  20.5 11.2 %collective-permute-start.10 = (bf16[24,16,256]{2,1,0:T(8,128)(2,1)S(1)}, bf16[24,16,256]{2,1,0:T(8,128)(2,1)S(1)}, u32[]{:S(2)}, u32[]{:S(2)}) collective-permute-start(bf16[24,16,256]{2,1,0:T(8,128)(2,1)S(1)} %get-tuple-element.18), channel_id=1, source_target_pairs={{4,4},{5,5},{6,6},{7,7},{12,20},{13,21},{14,22},{15,23},{16,8},{17... | collective-permute-start | bytes 589832 | tf_op jit(solution)/shard_map/ppermute | solution.py:100
  31.7 0.7 collective-permute-start.1
  32.4 0.7 collective-permute-start.19
  33.1 0.7 collective-permute-start.20
  33.8 5.5 %collective-permute-start.2 = (bf16[24,16,256]{2,1,0:T(8,128)(2,1)S(1)}, bf16[24,16,256]{2,1,0:T(8,128)(2,1)S(1)}, u32[]{:S(2)}, u32[]{:S(2)}) collective-permute-start(bf16[24,16,256]{2,1,0:T(8,128)(2,1)S(1)} %get-tuple-element.15), channel_id=1, source_target_pairs={{4,4},{5,5},{6,6},{7,7},{12,20},{13,21},{14,22},{15,23},{16,8},{17... | collective-permute-start | bytes 589832 | tf_op jit(solution)/shard_map/ppermute | solution.py:100
  39.3 0.7 collective-permute-start.15
  40.0 0.7 collective-permute-start.16
  40.7 1.8 %collective-permute-done.2.refs_2_ = bf16[24,16,256]{2,1,0:T(8,128)(2,1)S(1)} collective-permute-done((bf16[24,16,256]{2,1,0:T(8,128)(2,1)S(1)}, bf16[24,16,256]{2,1,0:T(8,128)(2,1)S(1)}, u32[]{:S(2)}, u32[]{:S(2)}) %collective-permute-start.2) | collective-permute-done | bytes 196640 | tf_op jit(solution)/shard_map/ppermute | solution.py:100
  43.1 0.7 collective-permute-start.12
  43.8 0.7 collective-permute-start.3
  44.5 0.7 collective-permute-start.4
  48.3 1.3 %collective-permute-start.22 = (bf16[12,16,256]{2,1,0:T(8,128)(2,1)S(1)}, bf16[12,16,256]{2,1,0:T(8,128)(2,1)S(1)}, u32[]{:S(2)}, u32[]{:S(2)}) collective-permute-start(bf16[12,16,256]{2,1,0:T(8,128)(2,1)S(1)} %get-tuple-element.22), channel_id=1, source_target_pairs={{4,4},{5,5},{6,6},{7,7},{8,16},{9,17},{10,18},{11,19},{20,12},{21,... | collective-permute-start | bytes 294920 | tf_op jit(solution)/shard_map/ppermute | solution.py:100
  50.3 1.3 %collective-permute-start.24 = (bf16[12,16,256]{2,1,0:T(8,128)(2,1)S(1)}, bf16[12,16,256]{2,1,0:T(8,128)(2,1)S(1)}, u32[]{:S(2)}, u32[]{:S(2)}) collective-permute-start(bf16[12,16,256]{2,1,0:T(8,128)(2,1)S(1)} %get-tuple-element.24), channel_id=1, source_target_pairs={{4,12},{5,13},{6,14},{7,15},{8,24},{9,25},{10,26},{11,27},{20,4},{... | collective-permute-start | bytes 294920 | tf_op jit(solution)/shard_map/ppermute | solution.py:100
  51.6 19.6 %collective-permute-done.22 = bf16[12,16,256]{2,1,0:T(8,128)(2,1)S(1)} collective-permute-done((bf16[12,16,256]{2,1,0:T(8,128)(2,1)S(1)}, bf16[12,16,256]{2,1,0:T(8,128)(2,1)S(1)}, u32[]{:S(2)}, u32[]{:S(2)}) %collective-permute-start.22) | collective-permute-done | bytes 98336 | tf_op jit(solution)/shard_map/ppermute | solution.py:100
  71.2 4.3 %collective-permute-done.24 = bf16[12,16,256]{2,1,0:T(8,128)(2,1)S(1)} collective-permute-done((bf16[12,16,256]{2,1,0:T(8,128)(2,1)S(1)}, bf16[12,16,256]{2,1,0:T(8,128)(2,1)S(1)}, u32[]{:S(2)}, u32[]{:S(2)}) %collective-permute-start.24) | collective-permute-done | bytes 98336 | tf_op jit(solution)/shard_map/ppermute | solution.py:100
  75.6 0.7 copy.14
  (47 shorter events, 6.6 us)
Async XLA Ops:
  2.6 8.4 %collective-permute-start.5 = (bf16[12,16,256]{2,1,0:T(8,128)(2,1)S(1)}, bf16[12,16,256]{2,1,0:T(8,128)(2,1)S(1)}, u32[]{:S(2)}, u32[]{:S(2)}) collective-permute-start(bf16[12,16,256]{2,1,0:T(8,128)(2,1)S(1)} %get-tuple-element.16), channel_id=1, source_target_pairs={{0,5},{1,6},{2,7},{9,20},{10,21},{11,22},{20,25},{21,26},{22,27},{... | collective-permute-start | bytes 294920 | tf_op jit(solution)/shard_map/ppermute | solution.py:100
  3.3 14.5 %collective-permute-start.6 = (bf16[12,16,256]{2,1,0:T(8,128)(2,1)S(1)}, bf16[12,16,256]{2,1,0:T(8,128)(2,1)S(1)}, u32[]{:S(2)}, u32[]{:S(2)}) collective-permute-start(bf16[12,16,256]{2,1,0:T(8,128)(2,1)S(1)} %get-tuple-element.17), channel_id=1, source_target_pairs={{4,5},{5,6},{6,7},{13,20},{14,21},{15,22},{17,8},{18,9},{19,10},{2... | collective-permute-start | bytes 294920 | tf_op jit(solution)/shard_map/ppermute | solution.py:100
  8.9 11.5 %collective-permute-start.13 = (bf16[24,16,256]{2,1,0:T(8,128)(2,1)S(1)}, bf16[24,16,256]{2,1,0:T(8,128)(2,1)S(1)}, u32[]{:S(2)}, u32[]{:S(2)}) collective-permute-start(bf16[24,16,256]{2,1,0:T(8,128)(2,1)S(1)} %get-tuple-element.19), channel_id=1, source_target_pairs={{0,4},{1,5},{2,6},{3,7},{8,20},{9,21},{10,22},{11,23},{20,24},{21,... | collective-permute-start | bytes 589832 | tf_op jit(solution)/shard_map/ppermute | solution.py:100
  9.6 8.8 %collective-permute-start.7 = (bf16[12,16,256]{2,1,0:T(8,128)(2,1)S(1)}, bf16[12,16,256]{2,1,0:T(8,128)(2,1)S(1)}, u32[]{:S(2)}, u32[]{:S(2)}) collective-permute-start(bf16[12,16,256]{2,1,0:T(8,128)(2,1)S(1)} %get-tuple-element.17), channel_id=1, source_target_pairs={{1,20},{2,21},{3,22},{8,5},{9,6},{10,7},{21,8},{22,9},{23,10},{28,... | collective-permute-start | bytes 294920 | tf_op jit(solution)/shard_map/ppermute | solution.py:100
  10.3 22.1 %collective-permute-start.17 = (bf16[24,16,384]{2,1,0:T(8,128)(2,1)S(1)}, bf16[24,16,384]{2,1,0:T(8,128)(2,1)S(1)}, u32[]{:S(2)}, u32[]{:S(2)}) collective-permute-start(bf16[24,16,384]{2,1,0:T(8,128)(2,1)S(1)} %get-tuple-element.20), channel_id=1, source_target_pairs={{0,4},{1,5},{2,6},{3,7},{8,20},{9,21},{10,22},{11,23},{20,24},{21,... | collective-permute-start | bytes 884744 | tf_op jit(solution)/shard_map/ppermute | solution.py:100
  11.0 22.1 %collective-permute-start.18 = (bf16[24,16,384]{2,1,0:T(8,128)(2,1)S(1)}, bf16[24,16,384]{2,1,0:T(8,128)(2,1)S(1)}, u32[]{:S(2)}, u32[]{:S(2)}) collective-permute-start(bf16[24,16,384]{2,1,0:T(8,128)(2,1)S(1)} %get-tuple-element.20), channel_id=1, source_target_pairs={{4,4},{5,5},{6,6},{7,7},{12,20},{13,21},{14,22},{15,23},{16,8},{17... | collective-permute-start | bytes 884744 | tf_op jit(solution)/shard_map/ppermute | solution.py:100
  17.8 2.0 %collective-permute-start.8 = (bf16[12,16,256]{2,1,0:T(8,128)(2,1)S(1)}, bf16[12,16,256]{2,1,0:T(8,128)(2,1)S(1)}, u32[]{:S(2)}, u32[]{:S(2)}) collective-permute-start(bf16[12,16,256]{2,1,0:T(8,128)(2,1)S(1)} %get-tuple-element.16), channel_id=1, source_target_pairs={{5,20},{6,21},{7,22},{12,5},{13,6},{14,7},{16,25},{17,26},{18,27},... | collective-permute-start | bytes 294920 | tf_op jit(solution)/shard_map/ppermute | solution.py:100
  18.4 13.2 %collective-permute-start.14 = (bf16[24,16,256]{2,1,0:T(8,128)(2,1)S(1)}, bf16[24,16,256]{2,1,0:T(8,128)(2,1)S(1)}, u32[]{:S(2)}, u32[]{:S(2)}) collective-permute-start(bf16[24,16,256]{2,1,0:T(8,128)(2,1)S(1)} %get-tuple-element.19), channel_id=1, source_target_pairs={{4,4},{5,5},{6,6},{7,7},{12,20},{13,21},{14,22},{15,23},{16,8},{17... | collective-permute-start | bytes 589832 | tf_op jit(solution)/shard_map/ppermute | solution.py:100
  19.8 14.0 %collective-permute-start.9 = (bf16[24,16,256]{2,1,0:T(8,128)(2,1)S(1)}, bf16[24,16,256]{2,1,0:T(8,128)(2,1)S(1)}, u32[]{:S(2)}, u32[]{:S(2)}) collective-permute-start(bf16[24,16,256]{2,1,0:T(8,128)(2,1)S(1)} %get-tuple-element.18), channel_id=1, source_target_pairs={{0,4},{1,5},{2,6},{3,7},{8,20},{9,21},{10,22},{11,23},{20,24},{21,... | collective-permute-start | bytes 589832 | tf_op jit(solution)/shard_map/ppermute | solution.py:100
  20.5 18.8 %collective-permute-start.10 = (bf16[24,16,256]{2,1,0:T(8,128)(2,1)S(1)}, bf16[24,16,256]{2,1,0:T(8,128)(2,1)S(1)}, u32[]{:S(2)}, u32[]{:S(2)}) collective-permute-start(bf16[24,16,256]{2,1,0:T(8,128)(2,1)S(1)} %get-tuple-element.18), channel_id=1, source_target_pairs={{4,4},{5,5},{6,6},{7,7},{12,20},{13,21},{14,22},{15,23},{16,8},{17... | collective-permute-start | bytes 589832 | tf_op jit(solution)/shard_map/ppermute | solution.py:100
  31.7 8.3 %collective-permute-start.1 = (bf16[24,16,256]{2,1,0:T(8,128)(2,1)S(1)}, bf16[24,16,256]{2,1,0:T(8,128)(2,1)S(1)}, u32[]{:S(2)}, u32[]{:S(2)}) collective-permute-start(bf16[24,16,256]{2,1,0:T(8,128)(2,1)S(1)} %get-tuple-element.15), channel_id=1, source_target_pairs={{0,4},{1,5},{2,6},{3,7},{8,20},{9,21},{10,22},{11,23},{20,24},{21,... | collective-permute-start | bytes 589832 | tf_op jit(solution)/shard_map/ppermute | solution.py:100
  32.4 11.5 %collective-permute-start.19 = (bf16[24,16,384]{2,1,0:T(8,128)(2,1)S(1)}, bf16[24,16,384]{2,1,0:T(8,128)(2,1)S(1)}, u32[]{:S(2)}, u32[]{:S(2)}) collective-permute-start(bf16[24,16,384]{2,1,0:T(8,128)(2,1)S(1)} %collective-permute-done.17.refs_1_), channel_id=1, source_target_pairs={{4,20},{5,21},{6,22},{7,23},{8,24},{9,25},{10,26},{11,27},{20,4},{... | collective-permute-start | bytes 884744 | tf_op jit(solution)/shard_map/ppermute | solution.py:100
  33.1 11.5 %collective-permute-start.20 = (bf16[24,16,384]{2,1,0:T(8,128)(2,1)S(1)}, bf16[24,16,384]{2,1,0:T(8,128)(2,1)S(1)}, u32[]{:S(2)}, u32[]{:S(2)}) collective-permute-start(bf16[24,16,384]{2,1,0:T(8,128)(2,1)S(1)} %collective-permute-done.18.refs_2_), channel_id=1, source_target_pairs={{4,20},{5,21},{6,22},{7,23},{8,24},{9,25},{10,26},{11,27},{20,4},{... | collective-permute-start | bytes 884744 | tf_op jit(solution)/shard_map/ppermute | solution.py:100
  33.8 8.7 %collective-permute-start.2 = (bf16[24,16,256]{2,1,0:T(8,128)(2,1)S(1)}, bf16[24,16,256]{2,1,0:T(8,128)(2,1)S(1)}, u32[]{:S(2)}, u32[]{:S(2)}) collective-permute-start(bf16[24,16,256]{2,1,0:T(8,128)(2,1)S(1)} %get-tuple-element.15), channel_id=1, source_target_pairs={{4,4},{5,5},{6,6},{7,7},{12,20},{13,21},{14,22},{15,23},{16,8},{17... | collective-permute-start | bytes 589832 | tf_op jit(solution)/shard_map/ppermute | solution.py:100
  39.3 3.8 %collective-permute-start.15 = (bf16[24,16,256]{2,1,0:T(8,128)(2,1)S(1)}, bf16[24,16,256]{2,1,0:T(8,128)(2,1)S(1)}, u32[]{:S(2)}, u32[]{:S(2)}) collective-permute-start(bf16[24,16,256]{2,1,0:T(8,128)(2,1)S(1)} %collective-permute-done.13.refs_1_), channel_id=1, source_target_pairs={{4,20},{5,21},{6,22},{7,23},{8,24},{9,25},{10,26},{11,27},{20,4},{... | collective-permute-start | bytes 589832 | tf_op jit(solution)/shard_map/ppermute | solution.py:100
  40.0 5.8 %collective-permute-start.16 = (bf16[24,16,256]{2,1,0:T(8,128)(2,1)S(1)}, bf16[24,16,256]{2,1,0:T(8,128)(2,1)S(1)}, u32[]{:S(2)}, u32[]{:S(2)}) collective-permute-start(bf16[24,16,256]{2,1,0:T(8,128)(2,1)S(1)} %collective-permute-done.14.refs_2_), channel_id=1, source_target_pairs={{4,20},{5,21},{6,22},{7,23},{8,24},{9,25},{10,26},{11,27},{20,4},{... | collective-permute-start | bytes 589832 | tf_op jit(solution)/shard_map/ppermute | solution.py:100
  42.4 4.0 %collective-permute-start.11 = (bf16[24,16,256]{2,1,0:T(8,128)(2,1)S(1)}, bf16[24,16,256]{2,1,0:T(8,128)(2,1)S(1)}, u32[]{:S(2)}, u32[]{:S(2)}) collective-permute-start(bf16[24,16,256]{2,1,0:T(8,128)(2,1)S(1)} %collective-permute-done.9.refs_1_), channel_id=1, source_target_pairs={{4,20},{5,21},{6,22},{7,23},{8,24},{9,25},{10,26},{11,27},{20,4},{... | collective-permute-start | bytes 589832 | tf_op jit(solution)/shard_map/ppermute | solution.py:100
  43.1 3.3 %collective-permute-start.12 = (bf16[24,16,256]{2,1,0:T(8,128)(2,1)S(1)}, bf16[24,16,256]{2,1,0:T(8,128)(2,1)S(1)}, u32[]{:S(2)}, u32[]{:S(2)}) collective-permute-start(bf16[24,16,256]{2,1,0:T(8,128)(2,1)S(1)} %collective-permute-done.10.refs_2_), channel_id=1, source_target_pairs={{4,20},{5,21},{6,22},{7,23},{8,24},{9,25},{10,26},{11,27},{20,4},{... | collective-permute-start | bytes 589832 | tf_op jit(solution)/shard_map/ppermute | solution.py:100
  43.8 3.2 %collective-permute-start.3 = (bf16[24,16,256]{2,1,0:T(8,128)(2,1)S(1)}, bf16[24,16,256]{2,1,0:T(8,128)(2,1)S(1)}, u32[]{:S(2)}, u32[]{:S(2)}) collective-permute-start(bf16[24,16,256]{2,1,0:T(8,128)(2,1)S(1)} %collective-permute-done.1.refs_1_), channel_id=1, source_target_pairs={{4,20},{5,21},{6,22},{7,23},{8,24},{9,25},{10,26},{11,27},{20,4},{... | collective-permute-start | bytes 589832 | tf_op jit(solution)/shard_map/ppermute | solution.py:100
  44.5 2.5 %collective-permute-start.4 = (bf16[24,16,256]{2,1,0:T(8,128)(2,1)S(1)}, bf16[24,16,256]{2,1,0:T(8,128)(2,1)S(1)}, u32[]{:S(2)}, u32[]{:S(2)}) collective-permute-start(bf16[24,16,256]{2,1,0:T(8,128)(2,1)S(1)} %collective-permute-done.2.refs_2_), channel_id=1, source_target_pairs={{4,20},{5,21},{6,22},{7,23},{8,24},{9,25},{10,26},{11,27},{20,4},{... | collective-permute-start | bytes 589832 | tf_op jit(solution)/shard_map/ppermute | solution.py:100
  47.6 4.0 %collective-permute-start.21 = (bf16[12,16,256]{2,1,0:T(8,128)(2,1)S(1)}, bf16[12,16,256]{2,1,0:T(8,128)(2,1)S(1)}, u32[]{:S(2)}, u32[]{:S(2)}) collective-permute-start(bf16[12,16,256]{2,1,0:T(8,128)(2,1)S(1)} %get-tuple-element.21), channel_id=1, source_target_pairs={{4,0},{5,1},{6,2},{7,3},{8,28},{9,29},{10,30},{11,31},{20,8},{21,9... | collective-permute-start | bytes 294920 | tf_op jit(solution)/shard_map/ppermute | solution.py:100
  48.3 22.9 %collective-permute-start.22 = (bf16[12,16,256]{2,1,0:T(8,128)(2,1)S(1)}, bf16[12,16,256]{2,1,0:T(8,128)(2,1)S(1)}, u32[]{:S(2)}, u32[]{:S(2)}) collective-permute-start(bf16[12,16,256]{2,1,0:T(8,128)(2,1)S(1)} %get-tuple-element.22), channel_id=1, source_target_pairs={{4,4},{5,5},{6,6},{7,7},{8,16},{9,17},{10,18},{11,19},{20,12},{21,... | collective-permute-start | bytes 294920 | tf_op jit(solution)/shard_map/ppermute | solution.py:100
  49.6 21.6 %collective-permute-start.23 = (bf16[12,16,256]{2,1,0:T(8,128)(2,1)S(1)}, bf16[12,16,256]{2,1,0:T(8,128)(2,1)S(1)}, u32[]{:S(2)}, u32[]{:S(2)}) collective-permute-start(bf16[12,16,256]{2,1,0:T(8,128)(2,1)S(1)} %get-tuple-element.23), channel_id=1, source_target_pairs={{4,8},{5,9},{6,10},{7,11},{8,20},{9,21},{10,22},{11,23},{20,0},{21... | collective-permute-start | bytes 294920 | tf_op jit(solution)/shard_map/ppermute | solution.py:100
  50.3 25.3 %collective-permute-start.24 = (bf16[12,16,256]{2,1,0:T(8,128)(2,1)S(1)}, bf16[12,16,256]{2,1,0:T(8,128)(2,1)S(1)}, u32[]{:S(2)}, u32[]{:S(2)}) collective-permute-start(bf16[12,16,256]{2,1,0:T(8,128)(2,1)S(1)} %get-tuple-element.24), channel_id=1, source_target_pairs={{4,12},{5,13},{6,14},{7,15},{8,24},{9,25},{10,26},{11,27},{20,4},{... | collective-permute-start | bytes 294920 | tf_op jit(solution)/shard_map/ppermute | solution.py:100
  (6 other events, 221.6 us)

commit v4 on v2

--- a/solution.py
+++ b/solution.py
@@ -101,7 +101,7 @@
 
 
 def row_chunks(low, high):
-    count = max(1, (high - low) // 4)
+    count = max(1, round((high - low) / 7))
     edges = [low + (high - low) * i // count for i in range(count + 1)]
     return list(zip(edges[:-1], edges[1:]))
 
@@ -114,10 +114,13 @@
     return layer * (layer + 1) // 2
 
 
-def edges_kernel(layers, conv, cot, first_ref, top_ref, bottom_ref):
+def edges_kernel(layers, groups, conv, cot, *outs):
+    *messages, top_ref, bottom_ref = outs
     rows, chans, v = cot.shape[0], conv.shape[3], cot.shape[2]
-    first_ref[:, :, :chans] = conv[layers - 1]
-    first_ref[:, :, chans:] = cot[...]
+    for message, group in zip(messages, groups):
+        for k, layer in enumerate(group):
+            message[:, :, k * chans : (k + 1) * chans] = conv[layer]
+    messages[0][:, :, len(groups[0]) * chans :] = cot[...]
     for layer in range(layers):
         here = slice(edge_start(layer), edge_start(layer + 1))
         top_ref[here] = conv[layer, : layer + 1]
@@ -128,35 +131,38 @@
         bottom_ref[at, :, lanes] = cot[rows - layers + k]
 
 
-def cut_edges(conv, cot):
+def cut_edges(groups, conv, cot):
     layers, rows, cells, chans = conv.shape
     edge = jax.ShapeDtypeStruct((edge_start(layers) + layers // 2, cells, chans), conv.dtype)
-    first = jax.ShapeDtypeStruct((rows, cells, chans + cot.shape[2]), conv.dtype)
+    widths = [len(group) * chans for group in groups]
+    widths[0] += cot.shape[2]
+    messages = [jax.ShapeDtypeStruct((rows, cells, width), conv.dtype) for width in widths]
     vmem = pl.BlockSpec(memory_space=pltpu.VMEM)
     return pl.pallas_call(
-        functools.partial(edges_kernel, layers),
-        out_shape=(first, edge, edge),
+        functools.partial(edges_kernel, layers, groups),
+        out_shape=messages + [edge, edge],
         in_specs=[vmem, vmem],
-        out_specs=(vmem, vmem, vmem),
+        out_specs=[vmem] * (len(groups) + 2),
         compiler_params=pltpu.CompilerParams(vmem_limit_bytes=16 * 2**20),
         name="edges",
     )(conv, cot)
 
 
-def layer_kernel(layer, layers, slot, *refs):
-    pl.when(on_home())(functools.partial(layer_body, layer, layers, slot, *refs))
-
-
-def layer_body(layer, layers, slot, *refs):
+def layer_kernel(layer, layers, place, *refs):
+    pl.when(on_home())(functools.partial(layer_body, layer, layers, place, *refs))
+
+
+def layer_body(layer, layers, place, *refs):
     first, last = layer == layers - 1, layer == 0
     offset_ref, refs = refs[0], refs[1:]
     mains, halos, refs = refs[:4], refs[4:8], refs[8:]
     carried, w_in, w_out, taps, refs = refs[0], refs[1], refs[2], refs[3], refs[4:]
     outs, refs = (refs[:4], refs[4:]) if last else (refs[:1], refs[1:])
     cg = refs[0]
-    rows, cells = mains[0].shape[-3:-1]
+    rows, cells = mains[0].shape[:2]
     chans = halos[0].shape[2]
-    v = mains[0].shape[-1] - chans
+    convs, cots = slice(place * chans, (place + 1) * chans), slice(2 * chans, mains[0].shape[2])
+    v = cots.stop - cots.start
     lon, wide = 4 * cells, layer + 1
     window = rows + 2 * wide
     halves = [(h, slice(h * 128, (h + 1) * 128)) for h in range(chans // 128)]
@@ -166,19 +172,16 @@
     has_above = jnp.where(lat > 0, 1.0, 0.0).astype(jnp.float32)
     has_below = jnp.where(lat < lax.axis_size("lat") - 1, 1.0, 0.0).astype(jnp.float32)
 
-    def main_row(p, r):
-        return mains[p][r] if slot is None else mains[p][slot, r]
-
     def conv_row(r):
         if r < wide:
             return [h[edge_start(layer) + r] for h in halos]
         if r < wide + rows:
-            return [main_row(p, r - wide)[:, :chans] for p in range(4)]
+            return [m[r - wide, :, convs] for m in mains]
         return [h[half_halo + edge_start(layer) + r - wide - rows] for h in halos]
 
     def cot_row(r):
         if wide <= r < wide + rows:
-            return [main_row(p, r - wide)[:, chans:] for p in range(4)]
+            return [m[r - wide, :, cots] for m in mains]
         k = r if r < wide else r - wide - rows
         at = edge_start(layers) + k // 2 + (0 if r < wide else half_halo)
         return [h[at, :, k % 2 * v : (k % 2 + 1) * v] for h in halos]
@@ -233,9 +236,9 @@
         done += 1
 
 
-def run_layer(layer, layers, slot, offsets, mains, halos, carried, w_in, w_out, taps):
+def run_layer(layer, layers, place, offsets, mains, halos, carried, w_in, w_out, taps):
     first, last = layer == layers - 1, layer == 0
-    rows, cells = mains[0].shape[-3:-1]
+    rows, cells = mains[0].shape[:2]
     chans = halos[0].shape[2]
     lon = 4 * cells
     window = rows + 2 * (layer + 1)
@@ -251,7 +254,7 @@
         scratch.append(pltpu.VMEM((window, lon, chans), jnp.bfloat16))
     work = window * lon
     return pl.pallas_call(
-        functools.partial(layer_kernel, layer, layers, slot),
+        functools.partial(layer_kernel, layer, layers, place),
         out_shape=out,
         in_specs=[smem] + [vmem] * (len(args) - 1),
         out_specs=[vmem] * len(out),
@@ -282,21 +285,21 @@
 
     cot = partner(dec_cot[0], "segment").transpose(1, 0, 2)
     conv = saved_conv[0].transpose(0, 2, 1, 3)
-    message, top, bottom = cut_edges(conv, cot)
+    groups = ((3, 2), (1, 0))
+    early, late, top, bottom = cut_edges(groups, conv, cot)
     below = routed(top, lambda c, z, j: (c, z, j - 1))
     above = routed(bottom, lambda c, z, j: (c, z, j + 1))
-    mains = {layers - 1: (None, gather(message))}
+    early = gather(early)
     halos = gather(jnp.concatenate([above, below], axis=0))
-    mains[layers - 2] = (None, gather(conv[layers - 2]))
-    rest = gather(conv[: layers - 2])
-    for layer in range(layers - 2):
-        mains[layer] = (layer, rest)
+    late, *early = lax.optimization_barrier((late, *early))
+    late = gather(late)
+    mains = {3: (0, early), 2: (1, early), 1: (0, late), 0: (1, late)}
 
     carried = dec_weight
     for layer in reversed(range(layers)):
-        slot, pieces = mains[layer]
+        place, pieces = mains[layer]
         found = run_layer(
-            layer, layers, slot, dilation, pieces, halos, carried, w_in, w_out, conv_taps
+            layer, layers, place, dilation, pieces, halos, carried, w_in, w_out, conv_taps
         )
         carried = found[0]
 

time: 72.8 us -> 59 us (0.81)
  waiting for transfers between devices: 36.8 us -> 27.9 us
  starting transfers between devices: 29.5 us -> 24.8 us
    ppermute x17 -> x14, waiting for transfers between devices: 36.8 us -> 27.9 us  [routed(): return lax.ppermute(value, AXES, pairs)]
    ppermute x17 -> x14, starting transfers between devices: 29 us -> 24.2 us  [routed(): return lax.ppermute(value, AXES, pairs)]
  transfers between devices with their start and end apart: 18 -> 15, of which waited for: 5 -> 4; matrix products, arithmetic and copies ran while one was open for 2% -> 2% of each run, Pallas kernels for 2% -> 2%
where the time goes in v4:
time: 59 us; the launch traced here: 58.6 us
  waiting for transfers between devices  27.9 us (47%)
  starting transfers between devices  24.8 us (42%)
  local copies, waits for them, and re-layouts  3.12 us (5%)
  Pallas kernels  2.5 us (4%)
    ppermute x14, waiting for transfers between devices, routed(): return lax.ppermute(value, AXES, pairs)  27.9 us
    ppermute x14, starting transfers between devices, routed(): return lax.ppermute(value, AXES, pairs)  24.2 us
    pallas_call x4, Pallas kernels, run_layer(): pl.pallas_call(functools.partial(layer_kernel, layer, layers, place), out...  2.42 us
    unnamed x14, local copies, waits for them, and re-layouts  2.38 us
  transfers between devices with their start and end apart: 15, of which 4 were waited for; matrix products, arithmetic and copies ran while one was open for 2% of the time, Pallas kernels for 2%

profile of v4, /device:TPU:0, one launch (start us, length us, event | category | flops | bytes accessed | tf_op | source)
XLA Modules:
  0.0 58.6 jit_solution(11634194731396032565)
XLA Ops:
  0.0 1.1 %copy.18 = bf16[1,16,24,128]{3,1,2,0:T(8,128)(2,1)S(1)} copy(bf16[1,16,24,128]{3,2,1,0:T(8,128)(2,1)} %param.7) | data formatting | bytes 196608 | tf_op args[0]
  1.6 1.3 %copy.17 = bf16[1,4,16,24,256]{4,2,3,1,0:T(8,128)(2,1)S(1)} copy(bf16[1,4,16,24,256]{4,3,2,1,0:T(8,128)(2,1)} %param.8) | data formatting | bytes 1572864 | tf_op args[1]
  3.0 0.7 %collective-permute-start.1 = (bf16[24,16,640]{2,1,0:T(8,128)(2,1)S(1)}, bf16[24,16,640]{2,1,0:T(8,128)(2,1)S(1)}, u32[]{:S(2)}, u32[]{:S(2)}) collective-permute-start(bf16[24,16,640]{2,1,0:T(8,128)(2,1)S(1)} %get-tuple-element.23.refs_1_), channel_id=1, source_target_pairs={{8,4},{9,5},{10,6},{11,7},{28,24},{29,25},{30,26},{31,27}} | collective-permute-start | bytes 1474568 | tf_op jit(solution)/shard_map/ppermute | solution.py:100
  3.7 4.4 %collective-permute-start.7 = (bf16[12,16,256]{2,1,0:T(8,128)(2,1)S(1)}, bf16[12,16,256]{2,1,0:T(8,128)(2,1)S(1)}, u32[]{:S(2)}, u32[]{:S(2)}) collective-permute-start(bf16[12,16,256]{2,1,0:T(8,128)(2,1)S(1)} %get-tuple-element.21), channel_id=1, source_target_pairs={{0,1},{1,2},{2,3},{4,5},{5,6},{6,7},{8,9},{9,10},{10,11},{12,13},{... | collective-permute-start | bytes 294920 | tf_op jit(solution)/shard_map/ppermute | solution.py:100
  8.1 0.7 %collective-permute-start.2 = (bf16[24,16,640]{2,1,0:T(8,128)(2,1)S(1)}, bf16[24,16,640]{2,1,0:T(8,128)(2,1)S(1)}, u32[]{:S(2)}, u32[]{:S(2)}) collective-permute-start(bf16[24,16,640]{2,1,0:T(8,128)(2,1)S(1)} %get-tuple-element.23.refs_1_), channel_id=1, source_target_pairs={{12,4},{13,5},{14,6},{15,7},{16,24},{17,25},{18,26},{19,27}} | collective-permute-start | bytes 1474568 | tf_op jit(solution)/shard_map/ppermute | solution.py:100
  8.8 4.7 %collective-permute-start.3 = (bf16[24,16,640]{2,1,0:T(8,128)(2,1)S(1)}, bf16[24,16,640]{2,1,0:T(8,128)(2,1)S(1)}, u32[]{:S(2)}, u32[]{:S(2)}) collective-permute-start(bf16[24,16,640]{2,1,0:T(8,128)(2,1)S(1)} %get-tuple-element.23.refs_1_), channel_id=1, source_target_pairs={{0,4},{1,5},{2,6},{3,7},{20,24},{21,25},{22,26},{23,27}} | collective-permute-start | bytes 1474568 | tf_op jit(solution)/shard_map/ppermute | solution.py:100
  13.5 1.3 %collective-permute-start.8 = (bf16[12,16,256]{2,1,0:T(8,128)(2,1)S(1)}, bf16[12,16,256]{2,1,0:T(8,128)(2,1)S(1)}, u32[]{:S(2)}, u32[]{:S(2)}) collective-permute-start(bf16[12,16,256]{2,1,0:T(8,128)(2,1)S(1)} %get-tuple-element.22), channel_id=1, source_target_pairs={{1,0},{2,1},{3,2},{5,4},{6,5},{7,6},{9,8},{10,9},{11,10},{13,12},{... | collective-permute-start | bytes 294920 | tf_op jit(solution)/shard_map/ppermute | solution.py:100
  14.9 5.6 %collective-permute-done.8 = bf16[12,16,256]{2,1,0:T(8,128)(2,1)S(1)} collective-permute-done((bf16[12,16,256]{2,1,0:T(8,128)(2,1)S(1)}, bf16[12,16,256]{2,1,0:T(8,128)(2,1)S(1)}, u32[]{:S(2)}, u32[]{:S(2)}) %collective-permute-start.8) | collective-permute-done | bytes 98336 | tf_op jit(solution)/shard_map/ppermute | solution.py:100
  20.5 0.7 %collective-permute-start.10 = (bf16[24,16,256]{2,1,0:T(8,128)(2,1)S(1)}, bf16[24,16,256]{2,1,0:T(8,128)(2,1)S(1)}, u32[]{:S(2)}, u32[]{:S(2)}) collective-permute-start(bf16[24,16,256]{2,1,0:T(8,128)(2,1)S(1)} %constant_dynamic-update-slice_fusion.refs_5_), channel_id=1, source_target_pairs={{12,4},{13,5},{14,6},{15,7},{16,24},{17,25},{18,26},{19,27}} | collective-permute-start | bytes 589832 | tf_op jit(solution)/shard_map/ppermute | solution.py:100
  21.2 1.5 %collective-permute-start.11 = (bf16[24,16,256]{2,1,0:T(8,128)(2,1)S(1)}, bf16[24,16,256]{2,1,0:T(8,128)(2,1)S(1)}, u32[]{:S(2)}, u32[]{:S(2)}) collective-permute-start(bf16[24,16,256]{2,1,0:T(8,128)(2,1)S(1)} %constant_dynamic-update-slice_fusion.refs_5_), channel_id=1, source_target_pairs={{0,4},{1,5},{2,6},{3,7},{20,24},{21,25},{22,26},{23,27}} | collective-permute-start | bytes 589832 | tf_op jit(solution)/shard_map/ppermute | solution.py:100
  22.6 0.7 %collective-permute-start.9 = (bf16[24,16,256]{2,1,0:T(8,128)(2,1)S(1)}, bf16[24,16,256]{2,1,0:T(8,128)(2,1)S(1)}, u32[]{:S(2)}, u32[]{:S(2)}) collective-permute-start(bf16[24,16,256]{2,1,0:T(8,128)(2,1)S(1)} %constant_dynamic-update-slice_fusion.refs_5_), channel_id=1, source_target_pairs={{8,4},{9,5},{10,6},{11,7},{28,24},{29,25},{30,26},{31,27}} | collective-permute-start | bytes 589832 | tf_op jit(solution)/shard_map/ppermute | solution.py:100
  23.3 1.8 %collective-permute-done.3.refs_4_ = bf16[24,16,640]{2,1,0:T(8,128)(2,1)S(1)} collective-permute-done((bf16[24,16,640]{2,1,0:T(8,128)(2,1)S(1)}, bf16[24,16,640]{2,1,0:T(8,128)(2,1)S(1)}, u32[]{:S(2)}, u32[]{:S(2)}) %collective-permute-start.3) | collective-permute-done | bytes 491552 | tf_op jit(solution)/shard_map/ppermute | solution.py:100
  25.1 0.7 %collective-permute-start.4 = (bf16[24,16,512]{2,1,0:T(8,128)(2,1)S(1)}, bf16[24,16,512]{2,1,0:T(8,128)(2,1)S(1)}, u32[]{:S(2)}, u32[]{:S(2)}) collective-permute-start(bf16[24,16,512]{2,1,0:T(8,128)(2,1)S(1)} %get-tuple-element.20.refs_1_), channel_id=1, source_target_pairs={{8,4},{9,5},{10,6},{11,7},{28,24},{29,25},{30,26},{31,27}} | collective-permute-start | bytes 1179656 | tf_op jit(solution)/shard_map/ppermute | solution.py:100
  25.8 0.7 %collective-permute-start.5 = (bf16[24,16,512]{2,1,0:T(8,128)(2,1)S(1)}, bf16[24,16,512]{2,1,0:T(8,128)(2,1)S(1)}, u32[]{:S(2)}, u32[]{:S(2)}) collective-permute-start(bf16[24,16,512]{2,1,0:T(8,128)(2,1)S(1)} %get-tuple-element.20.refs_1_), channel_id=1, source_target_pairs={{12,4},{13,5},{14,6},{15,7},{16,24},{17,25},{18,26},{19,27}} | collective-permute-start | bytes 1179656 | tf_op jit(solution)/shard_map/ppermute | solution.py:100
  26.5 5.6 %collective-permute-start.6 = (bf16[24,16,512]{2,1,0:T(8,128)(2,1)S(1)}, bf16[24,16,512]{2,1,0:T(8,128)(2,1)S(1)}, u32[]{:S(2)}, u32[]{:S(2)}) collective-permute-start(bf16[24,16,512]{2,1,0:T(8,128)(2,1)S(1)} %get-tuple-element.20.refs_1_), channel_id=1, source_target_pairs={{0,4},{1,5},{2,6},{3,7},{20,24},{21,25},{22,26},{23,27}} | collective-permute-start | bytes 1179656 | tf_op jit(solution)/shard_map/ppermute | solution.py:100
  32.2 0.6 layer_3.1.refs_9_
  32.8 0.6 layer_2.1.refs_9_
  33.4 6.7 %collective-permute-done.6.refs_4_ = bf16[24,16,512]{2,1,0:T(8,128)(2,1)S(1)} collective-permute-done((bf16[24,16,512]{2,1,0:T(8,128)(2,1)S(1)}, bf16[24,16,512]{2,1,0:T(8,128)(2,1)S(1)}, u32[]{:S(2)}, u32[]{:S(2)}) %collective-permute-start.6) | collective-permute-done | bytes 393248 | tf_op jit(solution)/shard_map/ppermute | solution.py:100
  40.6 0.7 %layer_0.1 = (bf16[24,16,256]{2,1,0:T(8,128)(2,1)S(1)}, bf16[24,16,256]{2,1,0:T(8,128)(2,1)S(1)}, bf16[24,16,256]{2,1,0:T(8,128)(2,1)S(1)}, bf16[24,16,256]{2,1,0:T(8,128)(2,1)S(1)}) custom-call(s32[4]{0:T(128)S(1)} %copy-done.3, bf16[24,16,512]{2,1,0:T(8,128)(2,1)S(1)} %get-tuple-element.20.refs_1_, ...), custom_call_target="tpu_custom_call" | custom-call | flops 1308622848 | bytes 4259840 | tf_op jit(solution)/shard_map/layer_0/pallas_call | solution.py:256
  41.3 0.7 %collective-permute-start.12 = (bf16[24,16,256]{2,1,0:T(8,128)(2,1)S(1)}, bf16[24,16,256]{2,1,0:T(8,128)(2,1)S(1)}, u32[]{:S(2)}, u32[]{:S(2)}) collective-permute-start(bf16[24,16,256]{2,1,0:T(8,128)(2,1)S(1)} %get-tuple-element.28), channel_id=1, source_target_pairs={{4,8},{5,9},{6,10},{7,11},{24,28},{25,29},{26,30},{27,31}} | collective-permute-start | bytes 589832 | tf_op jit(solution)/shard_map/ppermute | solution.py:100
  42.0 0.7 %collective-permute-start.13 = (bf16[24,16,256]{2,1,0:T(8,128)(2,1)S(1)}, bf16[24,16,256]{2,1,0:T(8,128)(2,1)S(1)}, u32[]{:S(2)}, u32[]{:S(2)}) collective-permute-start(bf16[24,16,256]{2,1,0:T(8,128)(2,1)S(1)} %get-tuple-element.29), channel_id=1, source_target_pairs={{4,12},{5,13},{6,14},{7,15},{24,16},{25,17},{26,18},{27,19}} | collective-permute-start | bytes 589832 | tf_op jit(solution)/shard_map/ppermute | solution.py:100
  42.7 1.3 %collective-permute-start.14 = (bf16[24,16,256]{2,1,0:T(8,128)(2,1)S(1)}, bf16[24,16,256]{2,1,0:T(8,128)(2,1)S(1)}, u32[]{:S(2)}, u32[]{:S(2)}) collective-permute-start(bf16[24,16,256]{2,1,0:T(8,128)(2,1)S(1)} %get-tuple-element.30), channel_id=1, source_target_pairs={{4,0},{5,1},{6,2},{7,3},{24,20},{25,21},{26,22},{27,23}} | collective-permute-start | bytes 589832 | tf_op jit(solution)/shard_map/ppermute | solution.py:100
  44.0 13.8 %collective-permute-done.14 = bf16[24,16,256]{2,1,0:T(8,128)(2,1)S(1)} collective-permute-done((bf16[24,16,256]{2,1,0:T(8,128)(2,1)S(1)}, bf16[24,16,256]{2,1,0:T(8,128)(2,1)S(1)}, u32[]{:S(2)}, u32[]{:S(2)}) %collective-permute-start.14) | collective-permute-done | bytes 196640 | tf_op jit(solution)/shard_map/ppermute | solution.py:100
  57.9 0.7 %copy.14 = bf16[1,16,24,256]{3,2,1,0:T(8,128)(2,1)} copy(bf16[1,16,24,256]{3,1,2,0:T(8,128)(2,1)S(1)} %add_bitcast_fusion) | data formatting | bytes 393216 | tf_op jit(solution)/shard_map/broadcast_in_dim | solution.py:311
  (28 shorter events, 1.3 us)
Async XLA Ops:
  0.0 32.1 %copy-start.4 = (f32[4,5,256]{2,0,1:T(4,128)S(1)}, f32[4,5,256]{2,0,1:T(4,128)}, u32[]{:S(2)}) copy-start(f32[4,5,256]{2,0,1:T(4,128)} %param.12) | copy-start | bytes 61444
  0.0 32.2 %copy-start = (bf16[4,256,512]{2,1,0:T(8,128)(2,1)S(1)}, bf16[4,256,512]{2,1,0:T(8,128)(2,1)}, u32[]{:S(2)}) copy-start(bf16[4,256,512]{2,1,0:T(8,128)(2,1)} %refs_10_.7) | copy-start | bytes 3145732
  0.0 32.2 %copy-start.1 = (bf16[4,512,256]{2,1,0:T(8,128)(2,1)S(1)}, bf16[4,512,256]{2,1,0:T(8,128)(2,1)}, u32[]{:S(2)}) copy-start(bf16[4,512,256]{2,1,0:T(8,128)(2,1)} %refs_11_.7) | copy-start | bytes 3145732
  0.0 32.2 %copy-start.3 = (s32[4]{0:T(128)S(1)}, s32[4]{0:T(128)}, u32[]{:S(2)}) copy-start(s32[4]{0:T(128)} %refs_0_.7) | copy-start | bytes 52
  0.0 32.2 %copy-start.2 = (bf16[256,128]{1,0:T(8,128)(2,1)S(1)}, bf16[256,128]{1,0:T(8,128)(2,1)}, u32[]{:S(2)}) copy-start(bf16[256,128]{1,0:T(8,128)(2,1)} %refs_9_.1) | copy-start | bytes 196612
  1.1 1.8 %collective-permute-start = (bf16[16,24,128]{2,0,1:T(8,128)(2,1)S(1)}, bf16[16,24,128]{2,0,1:T(8,128)(2,1)S(1)}, u32[]{:S(2)}, u32[]{:S(2)}) collective-permute-start(bf16[16,24,128]{2,0,1:T(8,128)(2,1)S(1)} %bitcast.15), channel_id=1, source_target_pairs={{0,16},{16,0},{1,17},{17,1},{2,18},{18,2},{3,19},{19,3},{4,20},{20... | collective-permute-start | bytes 294920 | tf_op jit(solution)/shard_map/ppermute | solution.py:38
  3.0 19.6 %collective-permute-start.1 = (bf16[24,16,640]{2,1,0:T(8,128)(2,1)S(1)}, bf16[24,16,640]{2,1,0:T(8,128)(2,1)S(1)}, u32[]{:S(2)}, u32[]{:S(2)}) collective-permute-start(bf16[24,16,640]{2,1,0:T(8,128)(2,1)S(1)} %get-tuple-element.23.refs_1_), channel_id=1, source_target_pairs={{8,4},{9,5},{10,6},{11,7},{28,24},{29,25},{30,26},{31,27}} | collective-permute-start | bytes 1474568 | tf_op jit(solution)/shard_map/ppermute | solution.py:100
  3.7 11.1 %collective-permute-start.7 = (bf16[12,16,256]{2,1,0:T(8,128)(2,1)S(1)}, bf16[12,16,256]{2,1,0:T(8,128)(2,1)S(1)}, u32[]{:S(2)}, u32[]{:S(2)}) collective-permute-start(bf16[12,16,256]{2,1,0:T(8,128)(2,1)S(1)} %get-tuple-element.21), channel_id=1, source_target_pairs={{0,1},{1,2},{2,3},{4,5},{5,6},{6,7},{8,9},{9,10},{10,11},{12,13},{... | collective-permute-start | bytes 294920 | tf_op jit(solution)/shard_map/ppermute | solution.py:100
  8.1 15.2 %collective-permute-start.2 = (bf16[24,16,640]{2,1,0:T(8,128)(2,1)S(1)}, bf16[24,16,640]{2,1,0:T(8,128)(2,1)S(1)}, u32[]{:S(2)}, u32[]{:S(2)}) collective-permute-start(bf16[24,16,640]{2,1,0:T(8,128)(2,1)S(1)} %get-tuple-element.23.refs_1_), channel_id=1, source_target_pairs={{12,4},{13,5},{14,6},{15,7},{16,24},{17,25},{18,26},{19,27}} | collective-permute-start | bytes 1474568 | tf_op jit(solution)/shard_map/ppermute | solution.py:100
  8.8 16.3 %collective-permute-start.3 = (bf16[24,16,640]{2,1,0:T(8,128)(2,1)S(1)}, bf16[24,16,640]{2,1,0:T(8,128)(2,1)S(1)}, u32[]{:S(2)}, u32[]{:S(2)}) collective-permute-start(bf16[24,16,640]{2,1,0:T(8,128)(2,1)S(1)} %get-tuple-element.23.refs_1_), channel_id=1, source_target_pairs={{0,4},{1,5},{2,6},{3,7},{20,24},{21,25},{22,26},{23,27}} | collective-permute-start | bytes 1474568 | tf_op jit(solution)/shard_map/ppermute | solution.py:100
  13.5 6.9 %collective-permute-start.8 = (bf16[12,16,256]{2,1,0:T(8,128)(2,1)S(1)}, bf16[12,16,256]{2,1,0:T(8,128)(2,1)S(1)}, u32[]{:S(2)}, u32[]{:S(2)}) collective-permute-start(bf16[12,16,256]{2,1,0:T(8,128)(2,1)S(1)} %get-tuple-element.22), channel_id=1, source_target_pairs={{1,0},{2,1},{3,2},{5,4},{6,5},{7,6},{9,8},{10,9},{11,10},{13,12},{... | collective-permute-start | bytes 294920 | tf_op jit(solution)/shard_map/ppermute | solution.py:100
  20.5 6.0 %collective-permute-start.10 = (bf16[24,16,256]{2,1,0:T(8,128)(2,1)S(1)}, bf16[24,16,256]{2,1,0:T(8,128)(2,1)S(1)}, u32[]{:S(2)}, u32[]{:S(2)}) collective-permute-start(bf16[24,16,256]{2,1,0:T(8,128)(2,1)S(1)} %constant_dynamic-update-slice_fusion.refs_5_), channel_id=1, source_target_pairs={{12,4},{13,5},{14,6},{15,7},{16,24},{17,25},{18,26},{19,27}} | collective-permute-start | bytes 589832 | tf_op jit(solution)/shard_map/ppermute | solution.py:100
  21.2 11.0 %collective-permute-start.11 = (bf16[24,16,256]{2,1,0:T(8,128)(2,1)S(1)}, bf16[24,16,256]{2,1,0:T(8,128)(2,1)S(1)}, u32[]{:S(2)}, u32[]{:S(2)}) collective-permute-start(bf16[24,16,256]{2,1,0:T(8,128)(2,1)S(1)} %constant_dynamic-update-slice_fusion.refs_5_), channel_id=1, source_target_pairs={{0,4},{1,5},{2,6},{3,7},{20,24},{21,25},{22,26},{23,27}} | collective-permute-start | bytes 589832 | tf_op jit(solution)/shard_map/ppermute | solution.py:100
  22.6 9.5 %collective-permute-start.9 = (bf16[24,16,256]{2,1,0:T(8,128)(2,1)S(1)}, bf16[24,16,256]{2,1,0:T(8,128)(2,1)S(1)}, u32[]{:S(2)}, u32[]{:S(2)}) collective-permute-start(bf16[24,16,256]{2,1,0:T(8,128)(2,1)S(1)} %constant_dynamic-update-slice_fusion.refs_5_), channel_id=1, source_target_pairs={{8,4},{9,5},{10,6},{11,7},{28,24},{29,25},{30,26},{31,27}} | collective-permute-start | bytes 589832 | tf_op jit(solution)/shard_map/ppermute | solution.py:100
  25.1 8.2 %collective-permute-start.4 = (bf16[24,16,512]{2,1,0:T(8,128)(2,1)S(1)}, bf16[24,16,512]{2,1,0:T(8,128)(2,1)S(1)}, u32[]{:S(2)}, u32[]{:S(2)}) collective-permute-start(bf16[24,16,512]{2,1,0:T(8,128)(2,1)S(1)} %get-tuple-element.20.refs_1_), channel_id=1, source_target_pairs={{8,4},{9,5},{10,6},{11,7},{28,24},{29,25},{30,26},{31,27}} | collective-permute-start | bytes 1179656 | tf_op jit(solution)/shard_map/ppermute | solution.py:100
  25.8 7.6 %collective-permute-start.5 = (bf16[24,16,512]{2,1,0:T(8,128)(2,1)S(1)}, bf16[24,16,512]{2,1,0:T(8,128)(2,1)S(1)}, u32[]{:S(2)}, u32[]{:S(2)}) collective-permute-start(bf16[24,16,512]{2,1,0:T(8,128)(2,1)S(1)} %get-tuple-element.20.refs_1_), channel_id=1, source_target_pairs={{12,4},{13,5},{14,6},{15,7},{16,24},{17,25},{18,26},{19,27}} | collective-permute-start | bytes 1179656 | tf_op jit(solution)/shard_map/ppermute | solution.py:100
  26.5 13.5 %collective-permute-start.6 = (bf16[24,16,512]{2,1,0:T(8,128)(2,1)S(1)}, bf16[24,16,512]{2,1,0:T(8,128)(2,1)S(1)}, u32[]{:S(2)}, u32[]{:S(2)}) collective-permute-start(bf16[24,16,512]{2,1,0:T(8,128)(2,1)S(1)} %get-tuple-element.20.refs_1_), channel_id=1, source_target_pairs={{0,4},{1,5},{2,6},{3,7},{20,24},{21,25},{22,26},{23,27}} | collective-permute-start | bytes 1179656 | tf_op jit(solution)/shard_map/ppermute | solution.py:100
  41.3 2.7 %collective-permute-start.12 = (bf16[24,16,256]{2,1,0:T(8,128)(2,1)S(1)}, bf16[24,16,256]{2,1,0:T(8,128)(2,1)S(1)}, u32[]{:S(2)}, u32[]{:S(2)}) collective-permute-start(bf16[24,16,256]{2,1,0:T(8,128)(2,1)S(1)} %get-tuple-element.28), channel_id=1, source_target_pairs={{4,8},{5,9},{6,10},{7,11},{24,28},{25,29},{26,30},{27,31}} | collective-permute-start | bytes 589832 | tf_op jit(solution)/shard_map/ppermute | solution.py:100
  42.0 2.0 %collective-permute-start.13 = (bf16[24,16,256]{2,1,0:T(8,128)(2,1)S(1)}, bf16[24,16,256]{2,1,0:T(8,128)(2,1)S(1)}, u32[]{:S(2)}, u32[]{:S(2)}) collective-permute-start(bf16[24,16,256]{2,1,0:T(8,128)(2,1)S(1)} %get-tuple-element.29), channel_id=1, source_target_pairs={{4,12},{5,13},{6,14},{7,15},{24,16},{25,17},{26,18},{27,19}} | collective-permute-start | bytes 589832 | tf_op jit(solution)/shard_map/ppermute | solution.py:100
  42.7 15.1 %collective-permute-start.14 = (bf16[24,16,256]{2,1,0:T(8,128)(2,1)S(1)}, bf16[24,16,256]{2,1,0:T(8,128)(2,1)S(1)}, u32[]{:S(2)}, u32[]{:S(2)}) collective-permute-start(bf16[24,16,256]{2,1,0:T(8,128)(2,1)S(1)} %get-tuple-element.30), channel_id=1, source_target_pairs={{4,0},{5,1},{6,2},{7,3},{24,20},{25,21},{26,22},{27,23}} | collective-permute-start | bytes 589832 | tf_op jit(solution)/shard_map/ppermute | solution.py:100

commit v5 on v4

--- a/solution.py
+++ b/solution.py
@@ -148,124 +148,238 @@
     )(conv, cot)
 
 
-def layer_kernel(layer, layers, place, *refs):
-    pl.when(on_home())(functools.partial(layer_body, layer, layers, place, *refs))
-
-
-def layer_body(layer, layers, place, *refs):
+def nt(a, b):
+    return lax.dot_general(a, b, (((1,), (1,)), ((), ())), preferred_element_type=jnp.float32)
+
+
+def halves_of(chans):
+    return [(h, slice(h * 128, (h + 1) * 128)) for h in range(chans // 128)]
+
+
+def in_order(pieces):
+    upward = lax.axis_index("segment") == 0
+    own, one, two, three = pieces
+    return [own, jnp.where(upward, one, three), two, jnp.where(upward, three, one)]
+
+
+def conv_gradient(conv_out, cot_low, w_in, w_out):
+    hidden = jnp.dot(conv_out, w_in, preferred_element_type=jnp.float32)
+    pre = (nt(cot_low, w_out) * gelu_slope(hidden)).astype(jnp.bfloat16)
+    return nt(pre, w_in)
+
+
+def keep_row(cg, at, row):
+    lon = row.shape[0]
+    for h, lanes in halves_of(row.shape[1]):
+        cg[at, h, 0:lon] = row[:, lanes]
+        cg[at, h, lon : 2 * lon] = row[:, lanes]
+
+
+def tapped(cg, at, h, taps, offset):
+    lon = cg.shape[2] // 2
+    total = taps[0] * cg[at, h, pl.ds(offset, lon)] + taps[2] * cg[at, h, pl.ds(lon - offset, lon)]
+    total += taps[1] * cg[at, h, 0:lon]
+    return total + taps[3] * cg[at + 1, h, 0:lon] + taps[4] * cg[at - 1, h, 0:lon]
+
+
+def inner_kernel(layer, layers, place, *refs):
+    pl.when(on_home())(functools.partial(inner_body, layer, layers, place, *refs))
+
+
+def inner_body(layer, layers, place, *refs):
     first, last = layer == layers - 1, layer == 0
-    offset_ref, refs = refs[0], refs[1:]
-    mains, halos, refs = refs[:4], refs[4:8], refs[8:]
+    offset_ref, mains, refs = refs[0], refs[1:5], refs[5:]
     carried, w_in, w_out, taps, refs = refs[0], refs[1], refs[2], refs[3], refs[4:]
     outs, refs = (refs[:4], refs[4:]) if last else (refs[:1], refs[1:])
-    cg = refs[0]
-    rows, cells = mains[0].shape[:2]
-    chans = halos[0].shape[2]
+    cg_edges, refs = refs[0], refs[1:]
+    if first:
+        handed_edges, cg, handed = refs
+    else:
+        (cg,) = refs
+    lon, chans = cg_edges.shape[1:]
+    cells, rows = lon // 4, cg.shape[0]
+    skipped = layers - 1 - layer
     convs, cots = slice(place * chans, (place + 1) * chans), slice(2 * chans, mains[0].shape[2])
-    v = cots.stop - cots.start
-    lon, wide = 4 * cells, layer + 1
-    window = rows + 2 * wide
-    halves = [(h, slice(h * 128, (h + 1) * 128)) for h in range(chans // 128)]
-    half_halo = halos[0].shape[0] // 2
     offset = offset_ref[layer]
-    lat = lax.axis_index("lat")
-    has_above = jnp.where(lat > 0, 1.0, 0.0).astype(jnp.float32)
-    has_below = jnp.where(lat < lax.axis_size("lat") - 1, 1.0, 0.0).astype(jnp.float32)
-
-    def conv_row(r):
-        if r < wide:
-            return [h[edge_start(layer) + r] for h in halos]
-        if r < wide + rows:
-            return [m[r - wide, :, convs] for m in mains]
-        return [h[half_halo + edge_start(layer) + r - wide - rows] for h in halos]
-
-    def cot_row(r):
-        if wide <= r < wide + rows:
-            return [m[r - wide, :, cots] for m in mains]
-        k = r if r < wide else r - wide - rows
-        at = edge_start(layers) + k // 2 + (0 if r < wide else half_halo)
-        return [h[at, :, k % 2 * v : (k % 2 + 1) * v] for h in halos]
-
-    def nt(a, b):
-        return lax.dot_general(a, b, (((1,), (1,)), ((), ())), preferred_element_type=jnp.float32)
+
+    def rows_of(r0, r1, lanes):
+        found = [in_order([m[skipped + r, :, lanes] for m in mains]) for r in range(r0, r1)]
+        return jnp.concatenate(sum(found, []), axis=0)
 
     def taps_of(r):
-        for h, lanes in halves:
-            t = [taps[layer, k : k + 1, lanes] for k in range(5)]
-            total = t[0] * cg[r, h, pl.ds(offset, lon)] + t[2] * cg[r, h, pl.ds(lon - offset, lon)]
-            total += t[1] * cg[r, h, 0:lon] + t[3] * cg[r + 1, h, 0:lon] + t[4] * cg[r - 1, h, 0:lon]
-            if first:
-                total += refs[1][r, :, lanes].astype(jnp.float32)
-            else:
-                total += carried[r, :, lanes]
+        for h, lanes in halves_of(chans):
+            total = tapped(cg, r, h, [taps[layer, k : k + 1, lanes] for k in range(5)], offset)
+            total += (handed[r, :, lanes].astype(jnp.float32) if first else carried[r, :, lanes])
             if last:
                 low = total.astype(jnp.bfloat16)
+                quarters = in_order([low[p * cells : (p + 1) * cells] for p in range(4)])
                 for p in range(4):
-                    outs[p][r - 1, :, lanes] = low[p * cells : (p + 1) * cells]
+                    outs[p][r - 1, :, lanes] = quarters[p]
             else:
                 outs[0][r - 1, :, lanes] = total
 
+    edge_rows = (0, 1, rows - 2, rows - 1)
     done = 1
-    for r0, r1 in row_chunks(0, window):
-        count = (r1 - r0) * lon
-        conv_out = jnp.concatenate(sum([conv_row(r) for r in range(r0, r1)], []), axis=0)
-        hidden = jnp.dot(conv_out, w_in[layer], preferred_element_type=jnp.float32)
+    for r0, r1 in row_chunks(0, rows):
         if first:
-            cot = jnp.concatenate(sum([cot_row(r) for r in range(r0, r1)], []), axis=0)
-            low = nt(cot, carried[...]).astype(jnp.bfloat16)
+            cot_low = nt(rows_of(r0, r1, cots), carried[...]).astype(jnp.bfloat16)
         else:
-            low = carried[r0:r1].reshape(count, chans).astype(jnp.bfloat16)
-        pre = (nt(low, w_out[layer]) * gelu_slope(hidden)).astype(jnp.bfloat16)
-        conv_grad = nt(pre, w_in[layer]).reshape(r1 - r0, lon, chans)
+            cot_low = carried[r0:r1].reshape((r1 - r0) * lon, chans).astype(jnp.bfloat16)
+        conv_grad = conv_gradient(rows_of(r0, r1, convs), cot_low, w_in[layer], w_out[layer])
+        conv_grad = conv_grad.reshape(r1 - r0, lon, chans)
         while done < r0 - 1:
             taps_of(done)
             done += 1
         if first:
-            refs[1][r0:r1] = low.reshape(r1 - r0, lon, chans)
+            handed[r0:r1] = cot_low.reshape(r1 - r0, lon, chans)
         for r in range(r0, r1):
-            rows_here = conv_grad[r - r0]
-            if r < wide:
-                rows_here = rows_here * has_above
-            if r >= wide + rows:
-                rows_here = rows_here * has_below
-            for h, lanes in halves:
-                cg[r, h, 0:lon] = rows_here[:, lanes]
-                cg[r, h, lon : 2 * lon] = rows_here[:, lanes]
-    while done < window - 1:
+            keep_row(cg, r, conv_grad[r - r0])
+            if r in edge_rows:
+                cg_edges[edge_rows.index(r)] = conv_grad[r - r0]
+    while done < rows - 1:
         taps_of(done)
         done += 1
-
-
-def run_layer(layer, layers, place, offsets, mains, halos, carried, w_in, w_out, taps):
+    if first:
+        handed_edges[0] = handed[0].astype(jnp.float32)
+        handed_edges[1] = handed[rows - 1].astype(jnp.float32)
+
+
+def run_inner(layer, layers, place, offsets, mains, carried, w_in, w_out, taps):
     first, last = layer == layers - 1, layer == 0
     rows, cells = mains[0].shape[:2]
-    chans = halos[0].shape[2]
+    chans = w_in.shape[1]
     lon = 4 * cells
-    window = rows + 2 * (layer + 1)
+    rows -= 2 * (layers - 1 - layer)
     smem = pl.BlockSpec(memory_space=pltpu.SMEM)
     vmem = pl.BlockSpec(memory_space=pltpu.VMEM)
-    args = [offsets, *mains, *halos, carried, w_in, w_out, taps]
+    args = [offsets, *mains, carried, w_in, w_out, taps]
     if last:
-        out = [jax.ShapeDtypeStruct((rows, cells, chans), jnp.bfloat16)] * 4
+        out = [jax.ShapeDtypeStruct((rows - 2, cells, chans), jnp.bfloat16)] * 4
     else:
-        out = [jax.ShapeDtypeStruct((window - 2, lon, chans), jnp.float32)]
-    scratch = [pltpu.VMEM((window, chans // 128, 2 * lon, 128), jnp.float32)]
+        out = [jax.ShapeDtypeStruct((rows - 2, lon, chans), jnp.float32)]
+    out.append(jax.ShapeDtypeStruct((4, lon, chans), jnp.float32))
+    scratch = [pltpu.VMEM((rows, chans // 128, 2 * lon, 128), jnp.float32)]
     if first:
-        scratch.append(pltpu.VMEM((window, lon, chans), jnp.bfloat16))
-    work = window * lon
+        out.append(jax.ShapeDtypeStruct((2, lon, chans), jnp.float32))
+        scratch.append(pltpu.VMEM((rows, lon, chans), jnp.bfloat16))
+    work = rows * lon
     return pl.pallas_call(
-        functools.partial(layer_kernel, layer, layers, place),
+        functools.partial(inner_kernel, layer, layers, place),
         out_shape=out,
         in_specs=[smem] + [vmem] * (len(args) - 1),
         out_specs=[vmem] * len(out),
         scratch_shapes=scratch,
-        compiler_params=pltpu.CompilerParams(vmem_limit_bytes=32 * 2**20),
+        compiler_params=pltpu.CompilerParams(vmem_limit_bytes=24 * 2**20),
         cost_estimate=pl.CostEstimate(
             flops=6 * work * chans * w_in.shape[2],
             bytes_accessed=work * chans * 10,
             transcendentals=2 * work * w_in.shape[2],
         ),
-        name=f"layer_{layer}",
+        name=f"inner_{layer}",
+    )(*args)
+
+
+def outer_kernel(layers, *refs):
+    pl.when(on_home())(functools.partial(outer_body, layers, *refs))
+
+
+def outer_body(layers, *refs):
+    offset_ref, refs = refs[0], refs[1:]
+    halos, mains, refs = refs[:4], (refs[4:8], refs[8:12]), refs[12:]
+    inner, refs = refs[:4], refs[4:]
+    handed_edges, gradients, refs = refs[0], refs[1:layers], refs[layers:]
+    cg_edges, refs = refs[:layers], refs[layers:]
+    dec_weight, w_in, w_out, taps, refs = refs[0], refs[1], refs[2], refs[3], refs[4:]
+    outs, (cg, grad) = refs[:4], refs[4:]
+    rows, cells = mains[0][0].shape[:2]
+    lon, chans = cg_edges[0].shape[1:]
+    v = dec_weight.shape[1]
+    half_halo = halos[0].shape[0] // 2
+    lat = lax.axis_index("lat")
+    has_above = jnp.where(lat > 0, 1.0, 0.0).astype(jnp.float32)
+    has_below = jnp.where(lat < lax.axis_size("lat") - 1, 1.0, 0.0).astype(jnp.float32)
+
+    def conv_row(layer, r):
+        if 0 <= r < rows:
+            place = (layers - 1 - layer) % 2
+            group = mains[(layers - 1 - layer) // 2]
+            return in_order([m[r, :, place * chans : (place + 1) * chans] for m in group])
+        at = edge_start(layer) + (r + layer + 1 if r < 0 else half_halo + r - rows)
+        return in_order([h[at] for h in halos])
+
+    def cot_row(r):
+        k = r + layers if r < 0 else r - rows
+        at = edge_start(layers) + k // 2 + (0 if r < 0 else half_halo)
+        return in_order([h[at, :, k % 2 * v : (k % 2 + 1) * v] for h in halos])
+
+    for p in range(4):
+        outs[p][layers : rows - layers] = inner[p][...]
+    for layer in reversed(range(layers)):
+        shift = layers - 1 - layer
+        here = [*range(-layers + shift, shift), *range(rows - shift, rows - shift + layers)]
+        if layer == layers - 1:
+            cot = jnp.concatenate(sum([cot_row(r) for r in here], []), axis=0)
+            cot_low = nt(cot, dec_weight[...]).astype(jnp.bfloat16)
+            grad[...] = cot_low.astype(jnp.float32).reshape(grad.shape)
+            near = [handed_edges[0], handed_edges[1]]
+        else:
+            cot_low = grad[...].reshape(len(here) * lon, chans).astype(jnp.bfloat16)
+            before = gradients[layers - 2 - layer]
+            near = [before[0], before[before.shape[0] - 1]]
+        conv_out = jnp.concatenate(sum([conv_row(layer, r) for r in here], []), axis=0)
+        conv_grad = conv_gradient(conv_out, cot_low, w_in[layer], w_out[layer])
+        conv_grad = conv_grad.reshape(len(here), lon, chans)
+        edge = cg_edges[layers - 1 - layer]
+        for k, r in enumerate(here):
+            row = conv_grad[k]
+            if r < 0:
+                row = row * has_above
+            if r >= rows:
+                row = row * has_below
+            keep_row(cg, k if k < layers else k + 4, row)
+        for k in range(4):
+            keep_row(cg, layers + k, edge[k])
+        old = [grad[k] for k in range(2 * layers)]
+        old = [*old[1:layers], near[0], near[1], *old[layers:-1]]
+        places = [*range(1, layers + 1), *range(layers + 3, 2 * layers + 3)]
+        for k, at in enumerate(places):
+            for h, lanes in halves_of(chans):
+                tap = [taps[layer, n : n + 1, lanes] for n in range(5)]
+                total = old[k][:, lanes] + tapped(cg, at, h, tap, offset_ref[layer])
+                if layer:
+                    grad[k, :, lanes] = total
+                else:
+                    low = total.astype(jnp.bfloat16)
+                    quarters = in_order([low[p * cells : (p + 1) * cells] for p in range(4)])
+                    r = k if k < layers else rows - 2 * layers + k
+                    for p in range(4):
+                        outs[p][r, :, lanes] = quarters[p]
+
+
+def run_outer(layers, offsets, halos, mains, inner, handed_edges, gradients, cg_edges, weights):
+    rows, cells = mains[0][0].shape[:2]
+    lon, chans = cg_edges[0].shape[1:]
+    smem = pl.BlockSpec(memory_space=pltpu.SMEM)
+    vmem = pl.BlockSpec(memory_space=pltpu.VMEM)
+    args = [offsets, *halos, *mains[0], *mains[1], *inner, handed_edges, *gradients, *cg_edges]
+    args += weights
+    work = 2 * layers * layers * lon
+    return pl.pallas_call(
+        functools.partial(outer_kernel, layers),
+        out_shape=[jax.ShapeDtypeStruct((rows, cells, chans), jnp.bfloat16)] * 4,
+        in_specs=[smem] + [vmem] * (len(args) - 1),
+        out_specs=[vmem] * 4,
+        scratch_shapes=[
+            pltpu.VMEM((2 * layers + 4, chans // 128, 2 * lon, 128), jnp.float32),
+            pltpu.VMEM((2 * layers, lon, chans), jnp.float32),
+        ],
+        compiler_params=pltpu.CompilerParams(vmem_limit_bytes=24 * 2**20),
+        cost_estimate=pl.CostEstimate(
+            flops=6 * work * chans * weights[1].shape[2],
+            bytes_accessed=work * chans * 10,
+            transcendentals=2 * work * weights[1].shape[2],
+        ),
+        name="outer",
     )(*args)
 
 
@@ -275,38 +389,69 @@
     def home(c):
         return c + 1
 
+    def away(c, k):
+        return (home(c) + (k if c == 0 else -k)) % 4
+
+    order = (2, 1, 3)
+
     def gather(value):
-        found = [value]
-        for k in range(1, 4):
-            found.append(
-                routed(value, lambda c, z, j: (c, home(c), j) if z == (home(c) + k) % 4 else None)
+        found = {0: value}
+        for k in order:
+            found[k] = routed(
+                value, lambda c, z, j: (c, home(c), j) if z == away(c, k) else None
             )
-        return found
+        return [found[k] for k in range(4)]
+
+    def neighbours(c, z, j):
+        if z == away(c, 1):
+            return c, home(c), j
+        if z == away(c, 2):
+            return 1 - c, home(c), j
+
+    def across(c, z, j):
+        return (1 - c, z, j) if z == home(1 - c) else None
 
     cot = partner(dec_cot[0], "segment").transpose(1, 0, 2)
     conv = saved_conv[0].transpose(0, 2, 1, 3)
     groups = ((3, 2), (1, 0))
     early, late, top, bottom = cut_edges(groups, conv, cot)
+    first = gather(early)
+    second = gather(late)
     below = routed(top, lambda c, z, j: (c, z, j - 1))
     above = routed(bottom, lambda c, z, j: (c, z, j + 1))
-    early = gather(early)
-    halos = gather(jnp.concatenate([above, below], axis=0))
-    late, *early = lax.optimization_barrier((late, *early))
-    late = gather(late)
-    mains = {3: (0, early), 2: (1, early), 1: (0, late), 0: (1, late)}
-
-    carried = dec_weight
+
+    carried, gradients, cg_edges = dec_weight, [], []
     for layer in reversed(range(layers)):
-        place, pieces = mains[layer]
-        found = run_layer(
-            layer, layers, place, dilation, pieces, halos, carried, w_in, w_out, conv_taps
+        mains = first if layer > 1 else second
+        found = run_inner(
+            layer, layers, (layers - 1 - layer) % 2, dilation, mains, carried, w_in, w_out, conv_taps
         )
-        carried = found[0]
+        if layer == layers - 1:
+            carried, cg_edge, handed_edges = found
+        elif layer:
+            carried, cg_edge = found
+        else:
+            *inner, cg_edge = found
+        cg_edges.append(cg_edge)
+        if layer:
+            gradients.append(carried)
+        if layer == layers - 1:
+            edges = jnp.concatenate([above, below], axis=0)
+            edges, carried = lax.optimization_barrier((edges, carried))
+            one = routed(edges, neighbours)
+            three = routed(edges, lambda c, z, j: (c, home(c), j) if z == away(c, 3) else None)
+        if layer == 1:
+            one, carried = lax.optimization_barrier((one, carried))
+            halos = [edges, one, routed(one, across), three]
+    weights = [dec_weight, w_in, w_out, conv_taps]
+    found = run_outer(
+        layers, dilation, halos, (first, second), inner, handed_edges, gradients, cg_edges, weights
+    )
 
     result = jnp.where(on_home(), found[0], 0)
-    for k in range(1, 4):
+    for k in order:
         result = result + routed(
-            found[k], lambda c, z, j: (c, (z + k) % 4, j) if z == home(c) else None
+            found[k], lambda c, z, j: (c, away(c, k), j) if z == home(c) else None
         )
     return result.transpose(1, 0, 2)[None]
 

time: 59 us -> 55.9 us (0.947)
  waiting for transfers between devices: 27.9 us -> 23.6 us
  starting transfers between devices: 24.8 us -> 25.4 us
    ppermute x14, waiting for transfers between devices: 27.9 us -> 23.6 us  [routed(): return lax.ppermute(value, AXES, pairs)]
    ppermute x14, starting transfers between devices: 24.2 us -> 24.9 us  [routed(): return lax.ppermute(value, AXES, pairs)]
    pallas_call x4 -> x5, Pallas kernels: 2.42 us -> 2.97 us  [the longest x4 2.23 us: run_inner(): pl.pallas_call(functools.partial(inner_kernel, layer, layers, place), out...]
    unnamed x14 -> x13, local copies, waits for them, and re-layouts: 2.38 us -> 2.34 us
  transfers between devices with their start and end apart: 15 -> 15, of which waited for: 4 -> 5; matrix products, arithmetic and copies ran while one was open for 2% -> 3% of each run, Pallas kernels for 2% -> 4%
where the time goes in v5:
time: 55.9 us; the launch traced here: 55.5 us
  starting transfers between devices  25.4 us (45%)
  waiting for transfers between devices  23.6 us (42%)
  local copies, waits for them, and re-layouts  3.08 us (6%)
  Pallas kernels  3.05 us (5%)
    ppermute x14, starting transfers between devices, routed(): return lax.ppermute(value, AXES, pairs)  24.9 us
    ppermute x14, waiting for transfers between devices, routed(): return lax.ppermute(value, AXES, pairs)  23.6 us
    unnamed x13, local copies, waits for them, and re-layouts  2.34 us
    pallas_call x4, Pallas kernels, run_inner(): pl.pallas_call(functools.partial(inner_kernel, layer, layers, place), out...  2.23 us
  transfers between devices with their start and end apart: 15, of which 5 were waited for; matrix products, arithmetic and copies ran while one was open for 3% of the time, Pallas kernels for 4%

profile of v5, /device:TPU:0, one launch (start us, length us, event | category | flops | bytes accessed | tf_op | source)
XLA Modules:
  0.0 55.5 jit_solution(15317947979405422681)
XLA Ops:
  0.0 0.9 %copy.19 = bf16[1,16,24,128]{3,1,2,0:T(8,128)(2,1)S(1)} copy(bf16[1,16,24,128]{3,2,1,0:T(8,128)(2,1)} %param.7) | data formatting | bytes 196608 | tf_op args[0]
  1.5 1.4 %copy.18 = bf16[1,4,16,24,256]{4,2,3,1,0:T(8,128)(2,1)S(1)} copy(bf16[1,4,16,24,256]{4,3,2,1,0:T(8,128)(2,1)} %param.8) | data formatting | bytes 1572864 | tf_op args[1]
  3.0 0.7 %collective-permute-start.3 = (bf16[24,16,640]{2,1,0:T(8,128)(2,1)S(1)}, bf16[24,16,640]{2,1,0:T(8,128)(2,1)S(1)}, u32[]{:S(2)}, u32[]{:S(2)}) collective-permute-start(bf16[24,16,640]{2,1,0:T(8,128)(2,1)S(1)} %get-tuple-element.31.refs_1_.refs_5_), channel_id=1, source_target_pairs={{8,4},{9,5},{10,6},{11,7},{20,24},{21,25},{22,26},{23,27}} | collective-permute-start | bytes 1474568 | tf_op jit(solution)/shard_map/ppermute | solution.py:100
  3.7 0.7 %collective-permute-start.4 = (bf16[24,16,640]{2,1,0:T(8,128)(2,1)S(1)}, bf16[24,16,640]{2,1,0:T(8,128)(2,1)S(1)}, u32[]{:S(2)}, u32[]{:S(2)}) collective-permute-start(bf16[24,16,640]{2,1,0:T(8,128)(2,1)S(1)} %get-tuple-element.31.refs_1_.refs_5_), channel_id=1, source_target_pairs={{12,4},{13,5},{14,6},{15,7},{16,24},{17,25},{18,26},{19,27}} | collective-permute-start | bytes 1474568 | tf_op jit(solution)/shard_map/ppermute | solution.py:100
  4.4 5.7 %collective-permute-start.5 = (bf16[24,16,640]{2,1,0:T(8,128)(2,1)S(1)}, bf16[24,16,640]{2,1,0:T(8,128)(2,1)S(1)}, u32[]{:S(2)}, u32[]{:S(2)}) collective-permute-start(bf16[24,16,640]{2,1,0:T(8,128)(2,1)S(1)} %get-tuple-element.31.refs_1_.refs_5_), channel_id=1, source_target_pairs={{0,4},{1,5},{2,6},{3,7},{28,24},{29,25},{30,26},{31,27}} | collective-permute-start | bytes 1474568 | tf_op jit(solution)/shard_map/ppermute | solution.py:100
  10.1 3.4 %collective-permute-start.1 = (bf16[12,16,256]{2,1,0:T(8,128)(2,1)S(1)}, bf16[12,16,256]{2,1,0:T(8,128)(2,1)S(1)}, u32[]{:S(2)}, u32[]{:S(2)}) collective-permute-start(bf16[12,16,256]{2,1,0:T(8,128)(2,1)S(1)} %get-tuple-element.29), channel_id=1, source_target_pairs={{0,1},{1,2},{2,3},{4,5},{5,6},{6,7},{8,9},{9,10},{10,11},{12,13},{... | collective-permute-start | bytes 294920 | tf_op jit(solution)/shard_map/ppermute | solution.py:100
  13.5 1.3 %collective-permute-start.2 = (bf16[12,16,256]{2,1,0:T(8,128)(2,1)S(1)}, bf16[12,16,256]{2,1,0:T(8,128)(2,1)S(1)}, u32[]{:S(2)}, u32[]{:S(2)}) collective-permute-start(bf16[12,16,256]{2,1,0:T(8,128)(2,1)S(1)} %get-tuple-element.30), channel_id=1, source_target_pairs={{1,0},{2,1},{3,2},{5,4},{6,5},{7,6},{9,8},{10,9},{11,10},{13,12},{... | collective-permute-start | bytes 294920 | tf_op jit(solution)/shard_map/ppermute | solution.py:100
  14.8 1.4 %collective-permute-done.1 = bf16[12,16,256]{2,1,0:T(8,128)(2,1)S(1)} collective-permute-done((bf16[12,16,256]{2,1,0:T(8,128)(2,1)S(1)}, bf16[12,16,256]{2,1,0:T(8,128)(2,1)S(1)}, u32[]{:S(2)}, u32[]{:S(2)}) %collective-permute-start.1) | collective-permute-done | bytes 98336 | tf_op jit(solution)/shard_map/ppermute | solution.py:100
  16.2 0.7 %collective-permute-start.7 = (bf16[24,16,512]{2,1,0:T(8,128)(2,1)S(1)}, bf16[24,16,512]{2,1,0:T(8,128)(2,1)S(1)}, u32[]{:S(2)}, u32[]{:S(2)}) collective-permute-start(bf16[24,16,512]{2,1,0:T(8,128)(2,1)S(1)} %get-tuple-element.34.refs_1_.refs_9_), channel_id=1, source_target_pairs={{8,4},{9,5},{10,6},{11,7},{20,24},{21,25},{22,26},{23,27}} | collective-permute-start | bytes 1179656 | tf_op jit(solution)/shard_map/ppermute | solution.py:100
  16.9 3.4 %collective-permute-done.2 = bf16[12,16,256]{2,1,0:T(8,128)(2,1)S(1)} collective-permute-done((bf16[12,16,256]{2,1,0:T(8,128)(2,1)S(1)}, bf16[12,16,256]{2,1,0:T(8,128)(2,1)S(1)}, u32[]{:S(2)}, u32[]{:S(2)}) %collective-permute-start.2) | collective-permute-done | bytes 98336 | tf_op jit(solution)/shard_map/ppermute | solution.py:100
  20.4 0.7 %collective-permute-start.8 = (bf16[24,16,512]{2,1,0:T(8,128)(2,1)S(1)}, bf16[24,16,512]{2,1,0:T(8,128)(2,1)S(1)}, u32[]{:S(2)}, u32[]{:S(2)}) collective-permute-start(bf16[24,16,512]{2,1,0:T(8,128)(2,1)S(1)} %get-tuple-element.34.refs_1_.refs_9_), channel_id=1, source_target_pairs={{12,4},{13,5},{14,6},{15,7},{16,24},{17,25},{18,26},{19,27}} | collective-permute-start | bytes 1179656 | tf_op jit(solution)/shard_map/ppermute | solution.py:100
  21.0 2.5 %collective-permute-start.9 = (bf16[24,16,512]{2,1,0:T(8,128)(2,1)S(1)}, bf16[24,16,512]{2,1,0:T(8,128)(2,1)S(1)}, u32[]{:S(2)}, u32[]{:S(2)}) collective-permute-start(bf16[24,16,512]{2,1,0:T(8,128)(2,1)S(1)} %get-tuple-element.34.refs_1_.refs_9_), channel_id=1, source_target_pairs={{0,4},{1,5},{2,6},{3,7},{28,24},{29,25},{30,26},{31,27}} | collective-permute-start | bytes 1179656 | tf_op jit(solution)/shard_map/ppermute | solution.py:100
  23.7 0.6 %inner_3.1 = (f32[22,64,256]{2,1,0:T(8,128)S(1)}, f32[4,64,256]{2,1,0:T(8,128)S(1)}, f32[2,64,256]{2,1,0:T(8,128)S(1)}) custom-call(s32[4]{0:T(128)S(1)} %copy-done.3, bf16[24,16,640]{2,1,0:T(8,128)(2,1)S(1)} %get-tuple-element.31.refs_1_.refs_5_, bf16[24,16,640]{2,1,0:T(8,128)(2,1)S(1)} %collective-permute-done.3.refs_2_.refs_6_, ...), custom_call_target="tpu_custom_call" | custom-call | flops 1207959552 | bytes 3932160 | tf_op jit(solution)/shard_map/inner_3/pallas_call | solution.py:266
  24.2 0.7 %collective-permute-start.6 = (bf16[24,16,256]{2,1,0:T(8,128)(2,1)S(1)}, bf16[24,16,256]{2,1,0:T(8,128)(2,1)S(1)}, u32[]{:S(2)}, u32[]{:S(2)}) collective-permute-start(bf16[24,16,256]{2,1,0:T(8,128)(2,1)S(1)} %pad_maximum_fusion.refs_1_), channel_id=1, source_target_pairs={{8,4},{9,5},{10,6},{11,7},{12,20},{13,21},{14,22},{15,23},{16,8},{... | collective-permute-start | bytes 589832 | tf_op jit(solution)/shard_map/ppermute | solution.py:100
  24.9 5.2 %collective-permute-start.11 = (bf16[24,16,256]{2,1,0:T(8,128)(2,1)S(1)}, bf16[24,16,256]{2,1,0:T(8,128)(2,1)S(1)}, u32[]{:S(2)}, u32[]{:S(2)}) collective-permute-start(bf16[24,16,256]{2,1,0:T(8,128)(2,1)S(1)} %pad_maximum_fusion.refs_1_), channel_id=1, source_target_pairs={{0,4},{1,5},{2,6},{3,7},{28,24},{29,25},{30,26},{31,27}} | collective-permute-start | bytes 589832 | tf_op jit(solution)/shard_map/ppermute | solution.py:100
  30.8 1.8 %collective-permute-done.9.refs_4_.refs_12_ = bf16[24,16,512]{2,1,0:T(8,128)(2,1)S(1)} collective-permute-done((bf16[24,16,512]{2,1,0:T(8,128)(2,1)S(1)}, bf16[24,16,512]{2,1,0:T(8,128)(2,1)S(1)}, u32[]{:S(2)}, u32[]{:S(2)}) %collective-permute-start.9) | collective-permute-done | bytes 393248 | tf_op jit(solution)/shard_map/ppermute | solution.py:100
  33.1 0.7 %collective-permute-start.10 = (bf16[24,16,256]{2,1,0:T(8,128)(2,1)S(1)}, bf16[24,16,256]{2,1,0:T(8,128)(2,1)S(1)}, u32[]{:S(2)}, u32[]{:S(2)}) collective-permute-start(bf16[24,16,256]{2,1,0:T(8,128)(2,1)S(1)} %collective-permute-done.6.refs_2_), channel_id=1, source_target_pairs={{8,24},{9,25},{10,26},{11,27},{20,4},{21,5},{22,6},{23,7}} | collective-permute-start | bytes 589832 | tf_op jit(solution)/shard_map/ppermute | solution.py:100
  33.8 0.6 %inner_0.1 = (bf16[16,16,256]{2,1,0:T(8,128)(2,1)S(1)}, bf16[16,16,256]{2,1,0:T(8,128)(2,1)S(1)}, bf16[16,16,256]{2,1,0:T(8,128)(2,1)S(1)}, bf16[16,16,256]{2,1,0:T(8,128)(2,1)S(1)}, f32[4,64,256]{2,1,0:T(8,128)S(1)}) custom-call(s32[4]{0:T(128)S(1)} %copy-done.3, bf16[24,16,512]{2,1,0:T(8,128)(2,1)S(1)} %get-tuple-element.34.refs_1_.refs_9_, ...), custom_call_target="tpu_custom_call" | custom-call | flops 905969664 | bytes 2949120 | tf_op jit(solution)/shard_map/inner_0/pallas_call | solution.py:266
  34.6 0.7 %outer.1 = (bf16[24,16,256]{2,1,0:T(8,128)(2,1)S(1)}, bf16[24,16,256]{2,1,0:T(8,128)(2,1)S(1)}, bf16[24,16,256]{2,1,0:T(8,128)(2,1)S(1)}, bf16[24,16,256]{2,1,0:T(8,128)(2,1)S(1)}) custom-call(s32[4]{0:T(128)S(1)} %copy-done.3, bf16[24,16,256]{2,1,0:T(8,128)(2,1)S(1)} %pad_maximum_fusion.refs_1_, bf16[24,16,256]{2,1,0:T(8,128)(2,1)S(1)} %collective-permute-done.6.refs_2_, ...), custom_call_target="tpu_custom_call" | custom-call | flops 1610612736 | bytes 5242880 | tf_op jit(solution)/shard_map/outer/pallas_call | solution.py:367
  35.4 0.7 %collective-permute-start.12 = (bf16[24,16,256]{2,1,0:T(8,128)(2,1)S(1)}, bf16[24,16,256]{2,1,0:T(8,128)(2,1)S(1)}, u32[]{:S(2)}, u32[]{:S(2)}) collective-permute-start(bf16[24,16,256]{2,1,0:T(8,128)(2,1)S(1)} %get-tuple-element.50), channel_id=1, source_target_pairs={{4,12},{5,13},{6,14},{7,15},{24,16},{25,17},{26,18},{27,19}} | collective-permute-start | bytes 589832 | tf_op jit(solution)/shard_map/ppermute | solution.py:100
  36.1 0.7 %collective-permute-start.13 = (bf16[24,16,256]{2,1,0:T(8,128)(2,1)S(1)}, bf16[24,16,256]{2,1,0:T(8,128)(2,1)S(1)}, u32[]{:S(2)}, u32[]{:S(2)}) collective-permute-start(bf16[24,16,256]{2,1,0:T(8,128)(2,1)S(1)} %get-tuple-element.51), channel_id=1, source_target_pairs={{4,8},{5,9},{6,10},{7,11},{24,20},{25,21},{26,22},{27,23}} | collective-permute-start | bytes 589832 | tf_op jit(solution)/shard_map/ppermute | solution.py:100
  36.7 1.3 %collective-permute-start.14 = (bf16[24,16,256]{2,1,0:T(8,128)(2,1)S(1)}, bf16[24,16,256]{2,1,0:T(8,128)(2,1)S(1)}, u32[]{:S(2)}, u32[]{:S(2)}) collective-permute-start(bf16[24,16,256]{2,1,0:T(8,128)(2,1)S(1)} %get-tuple-element.52), channel_id=1, source_target_pairs={{4,0},{5,1},{6,2},{7,3},{24,28},{25,29},{26,30},{27,31}} | collective-permute-start | bytes 589832 | tf_op jit(solution)/shard_map/ppermute | solution.py:100
  38.1 16.6 %collective-permute-done.14 = bf16[24,16,256]{2,1,0:T(8,128)(2,1)S(1)} collective-permute-done((bf16[24,16,256]{2,1,0:T(8,128)(2,1)S(1)}, bf16[24,16,256]{2,1,0:T(8,128)(2,1)S(1)}, u32[]{:S(2)}, u32[]{:S(2)}) %collective-permute-start.14) | collective-permute-done | bytes 196640 | tf_op jit(solution)/shard_map/ppermute | solution.py:100
  54.8 0.7 %copy.15 = bf16[1,16,24,256]{3,2,1,0:T(8,128)(2,1)} copy(bf16[1,16,24,256]{3,1,2,0:T(8,128)(2,1)S(1)} %add_bitcast_fusion) | data formatting | bytes 393216 | tf_op jit(solution)/shard_map/broadcast_in_dim | solution.py:456
  (28 shorter events, 2.1 us)
Async XLA Ops:
  0.0 23.6 %copy-start.4 = (f32[4,5,256]{2,0,1:T(4,128)S(1)}, f32[4,5,256]{2,0,1:T(4,128)}, u32[]{:S(2)}) copy-start(f32[4,5,256]{2,0,1:T(4,128)} %param.12) | copy-start | bytes 61444
  0.9 22.7 %copy-start = (bf16[4,256,512]{2,1,0:T(8,128)(2,1)S(1)}, bf16[4,256,512]{2,1,0:T(8,128)(2,1)}, u32[]{:S(2)}) copy-start(bf16[4,256,512]{2,1,0:T(8,128)(2,1)} %refs_26_.1) | copy-start | bytes 3145732
  0.9 22.7 %copy-start.1 = (bf16[4,512,256]{2,1,0:T(8,128)(2,1)S(1)}, bf16[4,512,256]{2,1,0:T(8,128)(2,1)}, u32[]{:S(2)}) copy-start(bf16[4,512,256]{2,1,0:T(8,128)(2,1)} %refs_27_.1) | copy-start | bytes 3145732
  0.9 22.7 %copy-start.2 = (bf16[256,128]{1,0:T(8,128)(2,1)S(1)}, bf16[256,128]{1,0:T(8,128)(2,1)}, u32[]{:S(2)}) copy-start(bf16[256,128]{1,0:T(8,128)(2,1)} %refs_25_.1) | copy-start | bytes 196612
  1.0 22.7 %copy-start.3 = (s32[4]{0:T(128)S(1)}, s32[4]{0:T(128)}, u32[]{:S(2)}) copy-start(s32[4]{0:T(128)} %refs_0_.9) | copy-start | bytes 52
  1.0 1.9 %collective-permute-start = (bf16[16,24,128]{2,0,1:T(8,128)(2,1)S(1)}, bf16[16,24,128]{2,0,1:T(8,128)(2,1)S(1)}, u32[]{:S(2)}, u32[]{:S(2)}) collective-permute-start(bf16[16,24,128]{2,0,1:T(8,128)(2,1)S(1)} %bitcast.15), channel_id=1, source_target_pairs={{0,16},{16,0},{1,17},{17,1},{2,18},{18,2},{3,19},{19,3},{4,20},{20... | collective-permute-start | bytes 294920 | tf_op jit(solution)/shard_map/ppermute | solution.py:38
  3.0 18.1 %collective-permute-start.3 = (bf16[24,16,640]{2,1,0:T(8,128)(2,1)S(1)}, bf16[24,16,640]{2,1,0:T(8,128)(2,1)S(1)}, u32[]{:S(2)}, u32[]{:S(2)}) collective-permute-start(bf16[24,16,640]{2,1,0:T(8,128)(2,1)S(1)} %get-tuple-element.31.refs_1_.refs_5_), channel_id=1, source_target_pairs={{8,4},{9,5},{10,6},{11,7},{20,24},{21,25},{22,26},{23,27}} | collective-permute-start | bytes 1474568 | tf_op jit(solution)/shard_map/ppermute | solution.py:100
  3.7 19.9 %collective-permute-start.4 = (bf16[24,16,640]{2,1,0:T(8,128)(2,1)S(1)}, bf16[24,16,640]{2,1,0:T(8,128)(2,1)S(1)}, u32[]{:S(2)}, u32[]{:S(2)}) collective-permute-start(bf16[24,16,640]{2,1,0:T(8,128)(2,1)S(1)} %get-tuple-element.31.refs_1_.refs_5_), channel_id=1, source_target_pairs={{12,4},{13,5},{14,6},{15,7},{16,24},{17,25},{18,26},{19,27}} | collective-permute-start | bytes 1474568 | tf_op jit(solution)/shard_map/ppermute | solution.py:100
  4.4 19.2 %collective-permute-start.5 = (bf16[24,16,640]{2,1,0:T(8,128)(2,1)S(1)}, bf16[24,16,640]{2,1,0:T(8,128)(2,1)S(1)}, u32[]{:S(2)}, u32[]{:S(2)}) collective-permute-start(bf16[24,16,640]{2,1,0:T(8,128)(2,1)S(1)} %get-tuple-element.31.refs_1_.refs_5_), channel_id=1, source_target_pairs={{0,4},{1,5},{2,6},{3,7},{28,24},{29,25},{30,26},{31,27}} | collective-permute-start | bytes 1474568 | tf_op jit(solution)/shard_map/ppermute | solution.py:100
  10.1 6.1 %collective-permute-start.1 = (bf16[12,16,256]{2,1,0:T(8,128)(2,1)S(1)}, bf16[12,16,256]{2,1,0:T(8,128)(2,1)S(1)}, u32[]{:S(2)}, u32[]{:S(2)}) collective-permute-start(bf16[12,16,256]{2,1,0:T(8,128)(2,1)S(1)} %get-tuple-element.29), channel_id=1, source_target_pairs={{0,1},{1,2},{2,3},{4,5},{5,6},{6,7},{8,9},{9,10},{10,11},{12,13},{... | collective-permute-start | bytes 294920 | tf_op jit(solution)/shard_map/ppermute | solution.py:100
  13.5 6.8 %collective-permute-start.2 = (bf16[12,16,256]{2,1,0:T(8,128)(2,1)S(1)}, bf16[12,16,256]{2,1,0:T(8,128)(2,1)S(1)}, u32[]{:S(2)}, u32[]{:S(2)}) collective-permute-start(bf16[12,16,256]{2,1,0:T(8,128)(2,1)S(1)} %get-tuple-element.30), channel_id=1, source_target_pairs={{1,0},{2,1},{3,2},{5,4},{6,5},{7,6},{9,8},{10,9},{11,10},{13,12},{... | collective-permute-start | bytes 294920 | tf_op jit(solution)/shard_map/ppermute | solution.py:100
  16.2 14.5 %collective-permute-start.7 = (bf16[24,16,512]{2,1,0:T(8,128)(2,1)S(1)}, bf16[24,16,512]{2,1,0:T(8,128)(2,1)S(1)}, u32[]{:S(2)}, u32[]{:S(2)}) collective-permute-start(bf16[24,16,512]{2,1,0:T(8,128)(2,1)S(1)} %get-tuple-element.34.refs_1_.refs_9_), channel_id=1, source_target_pairs={{8,4},{9,5},{10,6},{11,7},{20,24},{21,25},{22,26},{23,27}} | collective-permute-start | bytes 1179656 | tf_op jit(solution)/shard_map/ppermute | solution.py:100
  20.4 10.4 %collective-permute-start.8 = (bf16[24,16,512]{2,1,0:T(8,128)(2,1)S(1)}, bf16[24,16,512]{2,1,0:T(8,128)(2,1)S(1)}, u32[]{:S(2)}, u32[]{:S(2)}) collective-permute-start(bf16[24,16,512]{2,1,0:T(8,128)(2,1)S(1)} %get-tuple-element.34.refs_1_.refs_9_), channel_id=1, source_target_pairs={{12,4},{13,5},{14,6},{15,7},{16,24},{17,25},{18,26},{19,27}} | collective-permute-start | bytes 1179656 | tf_op jit(solution)/shard_map/ppermute | solution.py:100
  21.0 11.5 %collective-permute-start.9 = (bf16[24,16,512]{2,1,0:T(8,128)(2,1)S(1)}, bf16[24,16,512]{2,1,0:T(8,128)(2,1)S(1)}, u32[]{:S(2)}, u32[]{:S(2)}) collective-permute-start(bf16[24,16,512]{2,1,0:T(8,128)(2,1)S(1)} %get-tuple-element.34.refs_1_.refs_9_), channel_id=1, source_target_pairs={{0,4},{1,5},{2,6},{3,7},{28,24},{29,25},{30,26},{31,27}} | collective-permute-start | bytes 1179656 | tf_op jit(solution)/shard_map/ppermute | solution.py:100
  24.2 8.9 %collective-permute-start.6 = (bf16[24,16,256]{2,1,0:T(8,128)(2,1)S(1)}, bf16[24,16,256]{2,1,0:T(8,128)(2,1)S(1)}, u32[]{:S(2)}, u32[]{:S(2)}) collective-permute-start(bf16[24,16,256]{2,1,0:T(8,128)(2,1)S(1)} %pad_maximum_fusion.refs_1_), channel_id=1, source_target_pairs={{8,4},{9,5},{10,6},{11,7},{12,20},{13,21},{14,22},{15,23},{16,8},{... | collective-permute-start | bytes 589832 | tf_op jit(solution)/shard_map/ppermute | solution.py:100
  24.9 9.7 %collective-permute-start.11 = (bf16[24,16,256]{2,1,0:T(8,128)(2,1)S(1)}, bf16[24,16,256]{2,1,0:T(8,128)(2,1)S(1)}, u32[]{:S(2)}, u32[]{:S(2)}) collective-permute-start(bf16[24,16,256]{2,1,0:T(8,128)(2,1)S(1)} %pad_maximum_fusion.refs_1_), channel_id=1, source_target_pairs={{0,4},{1,5},{2,6},{3,7},{28,24},{29,25},{30,26},{31,27}} | collective-permute-start | bytes 589832 | tf_op jit(solution)/shard_map/ppermute | solution.py:100
  33.1 1.5 %collective-permute-start.10 = (bf16[24,16,256]{2,1,0:T(8,128)(2,1)S(1)}, bf16[24,16,256]{2,1,0:T(8,128)(2,1)S(1)}, u32[]{:S(2)}, u32[]{:S(2)}) collective-permute-start(bf16[24,16,256]{2,1,0:T(8,128)(2,1)S(1)} %collective-permute-done.6.refs_2_), channel_id=1, source_target_pairs={{8,24},{9,25},{10,26},{11,27},{20,4},{21,5},{22,6},{23,7}} | collective-permute-start | bytes 589832 | tf_op jit(solution)/shard_map/ppermute | solution.py:100
  35.4 2.7 %collective-permute-start.12 = (bf16[24,16,256]{2,1,0:T(8,128)(2,1)S(1)}, bf16[24,16,256]{2,1,0:T(8,128)(2,1)S(1)}, u32[]{:S(2)}, u32[]{:S(2)}) collective-permute-start(bf16[24,16,256]{2,1,0:T(8,128)(2,1)S(1)} %get-tuple-element.50), channel_id=1, source_target_pairs={{4,12},{5,13},{6,14},{7,15},{24,16},{25,17},{26,18},{27,19}} | collective-permute-start | bytes 589832 | tf_op jit(solution)/shard_map/ppermute | solution.py:100
  36.1 2.0 %collective-permute-start.13 = (bf16[24,16,256]{2,1,0:T(8,128)(2,1)S(1)}, bf16[24,16,256]{2,1,0:T(8,128)(2,1)S(1)}, u32[]{:S(2)}, u32[]{:S(2)}) collective-permute-start(bf16[24,16,256]{2,1,0:T(8,128)(2,1)S(1)} %get-tuple-element.51), channel_id=1, source_target_pairs={{4,8},{5,9},{6,10},{7,11},{24,20},{25,21},{26,22},{27,23}} | collective-permute-start | bytes 589832 | tf_op jit(solution)/shard_map/ppermute | solution.py:100
  36.7 18.0 %collective-permute-start.14 = (bf16[24,16,256]{2,1,0:T(8,128)(2,1)S(1)}, bf16[24,16,256]{2,1,0:T(8,128)(2,1)S(1)}, u32[]{:S(2)}, u32[]{:S(2)}) collective-permute-start(bf16[24,16,256]{2,1,0:T(8,128)(2,1)S(1)} %get-tuple-element.52), channel_id=1, source_target_pairs={{4,0},{5,1},{6,2},{7,3},{24,28},{25,29},{26,30},{27,31}} | collective-permute-start | bytes 589832 | tf_op jit(solution)/shard_map/ppermute | solution.py:100

commit v6 on v5

--- a/solution.py
+++ b/solution.py
@@ -110,17 +110,22 @@
     return lax.axis_index("lon") == lax.axis_index("segment") + 1
 
 
+GROUPS = ((3, 2), (1, 0))
+MESSAGE = {layer: (g, k) for g, group in enumerate(GROUPS) for k, layer in enumerate(group)}
+
+
 def edge_start(layer):
     return layer * (layer + 1) // 2
 
 
 def edges_kernel(layers, groups, conv, cot, *outs):
     *messages, top_ref, bottom_ref = outs
+    cot = jnp.swapaxes(cot[...].astype(jnp.float32), 0, 1).astype(conv.dtype)
     rows, chans, v = cot.shape[0], conv.shape[3], cot.shape[2]
     for message, group in zip(messages, groups):
         for k, layer in enumerate(group):
             message[:, :, k * chans : (k + 1) * chans] = conv[layer]
-    messages[0][:, :, len(groups[0]) * chans :] = cot[...]
+    messages[0][:, :, len(groups[0]) * chans :] = cot
     for layer in range(layers):
         here = slice(edge_start(layer), edge_start(layer + 1))
         top_ref[here] = conv[layer, : layer + 1]
@@ -199,7 +204,7 @@
     lon, chans = cg_edges.shape[1:]
     cells, rows = lon // 4, cg.shape[0]
     skipped = layers - 1 - layer
-    convs, cots = slice(place * chans, (place + 1) * chans), slice(2 * chans, mains[0].shape[2])
+    convs, cots = slice(place * chans, (place + 1) * chans), slice(len(GROUPS[0]) * chans, mains[0].shape[2])
     offset = offset_ref[layer]
 
     def rows_of(r0, r1, lanes):
@@ -219,7 +224,6 @@
                 outs[0][r - 1, :, lanes] = total
 
     edge_rows = (0, 1, rows - 2, rows - 1)
-    done = 1
     for r0, r1 in row_chunks(0, rows):
         if first:
             cot_low = nt(rows_of(r0, r1, cots), carried[...]).astype(jnp.bfloat16)
@@ -227,18 +231,20 @@
             cot_low = carried[r0:r1].reshape((r1 - r0) * lon, chans).astype(jnp.bfloat16)
         conv_grad = conv_gradient(rows_of(r0, r1, convs), cot_low, w_in[layer], w_out[layer])
         conv_grad = conv_grad.reshape(r1 - r0, lon, chans)
-        while done < r0 - 1:
-            taps_of(done)
-            done += 1
         if first:
             handed[r0:r1] = cot_low.reshape(r1 - r0, lon, chans)
         for r in range(r0, r1):
             keep_row(cg, r, conv_grad[r - r0])
             if r in edge_rows:
                 cg_edges[edge_rows.index(r)] = conv_grad[r - r0]
-    while done < rows - 1:
-        taps_of(done)
-        done += 1
+    half = (rows - 2) // 2
+
+    def taps_of_half(k, carry):
+        for r in range(half):
+            taps_of(1 + k * half + r)
+        return carry
+
+    lax.fori_loop(0, 2, taps_of_half, 0)
     if first:
         handed_edges[0] = handed[0].astype(jnp.float32)
         handed_edges[1] = handed[rows - 1].astype(jnp.float32)
@@ -301,9 +307,8 @@
 
     def conv_row(layer, r):
         if 0 <= r < rows:
-            place = (layers - 1 - layer) % 2
-            group = mains[(layers - 1 - layer) // 2]
-            return in_order([m[r, :, place * chans : (place + 1) * chans] for m in group])
+            group, place = MESSAGE[layer]
+            return in_order([m[r, :, place * chans : (place + 1) * chans] for m in mains[group]])
         at = edge_start(layer) + (r + layer + 1 if r < 0 else half_halo + r - rows)
         return in_order([h[at] for h in halos])
 
@@ -392,7 +397,7 @@
     def away(c, k):
         return (home(c) + (k if c == 0 else -k)) % 4
 
-    order = (2, 1, 3)
+    order = (3, 1, 2)
 
     def gather(value):
         found = {0: value}
@@ -411,20 +416,25 @@
     def across(c, z, j):
         return (1 - c, z, j) if z == home(1 - c) else None
 
-    cot = partner(dec_cot[0], "segment").transpose(1, 0, 2)
+    cot = partner(dec_cot[0], "segment")
     conv = saved_conv[0].transpose(0, 2, 1, 3)
-    groups = ((3, 2), (1, 0))
-    early, late, top, bottom = cut_edges(groups, conv, cot)
+    early, late, top, bottom = cut_edges(GROUPS, conv, cot)
     first = gather(early)
-    second = gather(late)
     below = routed(top, lambda c, z, j: (c, z, j - 1))
     above = routed(bottom, lambda c, z, j: (c, z, j + 1))
 
+    two = routed(late, lambda c, z, j: (c, home(c), j) if z == away(c, 2) else None)
+    sides, above, below = lax.optimization_barrier((late, above, below))
+    one = routed(sides, lambda c, z, j: (c, home(c), j) if z == away(c, 1) else None)
+    three = routed(sides, lambda c, z, j: (c, home(c), j) if z == away(c, 3) else None)
+    second = [late, one, two, three]
+
     carried, gradients, cg_edges = dec_weight, [], []
     for layer in reversed(range(layers)):
-        mains = first if layer > 1 else second
+        group, place = MESSAGE[layer]
+        mains = (first, second)[group]
         found = run_inner(
-            layer, layers, (layers - 1 - layer) % 2, dilation, mains, carried, w_in, w_out, conv_taps
+            layer, layers, place, dilation, mains, carried, w_in, w_out, conv_taps
         )
         if layer == layers - 1:
             carried, cg_edge, handed_edges = found

time: 55.9 us -> 53.4 us (0.955)
  the two profiles are of different devices: /device:TPU:0 before, /device:TPU:1 now
where the time goes in v6:
time: 53.4 us; the launch traced here: 53.1 us
  starting transfers between devices  24.6 us (46%)
  waiting for transfers between devices  22.8 us (43%)
  Pallas kernels  3.12 us (6%)
  local copies, waits for them, and re-layouts  2.18 us (4%)
    ppermute x14, starting transfers between devices, routed(): return lax.ppermute(value, AXES, pairs)  24.5 us
    ppermute x14, waiting for transfers between devices, routed(): return lax.ppermute(value, AXES, pairs)  22.7 us
    pallas_call x4, Pallas kernels, run_inner(): pl.pallas_call(functools.partial(inner_kernel, layer, layers, place), out...  2.24 us
    unnamed x12, local copies, waits for them, and re-layouts  1.44 us
  transfers between devices with their start and end apart: 15, of which 5 were waited for; matrix products, arithmetic and copies ran while one was open for 3% of the time, Pallas kernels for 4%

profile of v6, /device:TPU:1, one launch (start us, length us, event | category | flops | bytes accessed | tf_op | source)
XLA Modules:
  0.0 53.1 jit_solution(11452773548597653061)
XLA Ops:
  0.1 1.4 %copy.16 = bf16[1,4,16,24,256]{4,2,3,1,0:T(8,128)(2,1)S(1)} copy(bf16[1,4,16,24,256]{4,3,2,1,0:T(8,128)(2,1)} %param.8) | data formatting | bytes 1572864 | tf_op args[1]
  1.7 0.7 %collective-permute-start.3 = (bf16[24,16,640]{2,1,0:T(8,128)(2,1)S(1)}, bf16[24,16,640]{2,1,0:T(8,128)(2,1)S(1)}, u32[]{:S(2)}, u32[]{:S(2)}) collective-permute-start(bf16[24,16,640]{2,1,0:T(8,128)(2,1)S(1)} %get-tuple-element.37.refs_1_.refs_5_), channel_id=1, source_target_pairs={{8,4},{9,5},{10,6},{11,7},{20,24},{21,25},{22,26},{23,27}} | collective-permute-start | bytes 1474568 | tf_op jit(solution)/shard_map/ppermute | solution.py:100
  2.4 6.1 %collective-permute-start.4 = (bf16[24,16,640]{2,1,0:T(8,128)(2,1)S(1)}, bf16[24,16,640]{2,1,0:T(8,128)(2,1)S(1)}, u32[]{:S(2)}, u32[]{:S(2)}) collective-permute-start(bf16[24,16,640]{2,1,0:T(8,128)(2,1)S(1)} %get-tuple-element.37.refs_1_.refs_5_), channel_id=1, source_target_pairs={{12,4},{13,5},{14,6},{15,7},{16,24},{17,25},{18,26},{19,27}} | collective-permute-start | bytes 1474568 | tf_op jit(solution)/shard_map/ppermute | solution.py:100
  8.6 0.7 %collective-permute-start.5 = (bf16[24,16,640]{2,1,0:T(8,128)(2,1)S(1)}, bf16[24,16,640]{2,1,0:T(8,128)(2,1)S(1)}, u32[]{:S(2)}, u32[]{:S(2)}) collective-permute-start(bf16[24,16,640]{2,1,0:T(8,128)(2,1)S(1)} %get-tuple-element.37.refs_1_.refs_5_), channel_id=1, source_target_pairs={{0,4},{1,5},{2,6},{3,7},{28,24},{29,25},{30,26},{31,27}} | collective-permute-start | bytes 1474568 | tf_op jit(solution)/shard_map/ppermute | solution.py:100
  9.3 3.1 %collective-permute-start.1 = (bf16[12,16,256]{2,1,0:T(8,128)(2,1)S(1)}, bf16[12,16,256]{2,1,0:T(8,128)(2,1)S(1)}, u32[]{:S(2)}, u32[]{:S(2)}) collective-permute-start(bf16[12,16,256]{2,1,0:T(8,128)(2,1)S(1)} %get-tuple-element.33), channel_id=1, source_target_pairs={{0,1},{1,2},{2,3},{4,5},{5,6},{6,7},{8,9},{9,10},{10,11},{12,13},{... | collective-permute-start | bytes 294920 | tf_op jit(solution)/shard_map/ppermute | solution.py:100
  12.4 1.3 %collective-permute-start.2 = (bf16[12,16,256]{2,1,0:T(8,128)(2,1)S(1)}, bf16[12,16,256]{2,1,0:T(8,128)(2,1)S(1)}, u32[]{:S(2)}, u32[]{:S(2)}) collective-permute-start(bf16[12,16,256]{2,1,0:T(8,128)(2,1)S(1)} %get-tuple-element.34), channel_id=1, source_target_pairs={{1,0},{2,1},{3,2},{5,4},{6,5},{7,6},{9,8},{10,9},{11,10},{13,12},{... | collective-permute-start | bytes 294920 | tf_op jit(solution)/shard_map/ppermute | solution.py:100
  13.7 0.8 %collective-permute-done.1 = bf16[12,16,256]{2,1,0:T(8,128)(2,1)S(1)} collective-permute-done((bf16[12,16,256]{2,1,0:T(8,128)(2,1)S(1)}, bf16[12,16,256]{2,1,0:T(8,128)(2,1)S(1)}, u32[]{:S(2)}, u32[]{:S(2)}) %collective-permute-start.1) | collective-permute-done | bytes 98336 | tf_op jit(solution)/shard_map/ppermute | solution.py:100
  14.5 1.9 %collective-permute-start.8 = (bf16[24,16,512]{2,1,0:T(8,128)(2,1)S(1)}, bf16[24,16,512]{2,1,0:T(8,128)(2,1)S(1)}, u32[]{:S(2)}, u32[]{:S(2)}) collective-permute-start(bf16[24,16,512]{2,1,0:T(8,128)(2,1)S(1)} %get-tuple-element.40.refs_1_.refs_9_), channel_id=1, source_target_pairs={{12,4},{13,5},{14,6},{15,7},{16,24},{17,25},{18,26},{19,27}} | collective-permute-start | bytes 1179656 | tf_op jit(solution)/shard_map/ppermute | solution.py:100
  16.4 1.9 %collective-permute-done.2 = bf16[12,16,256]{2,1,0:T(8,128)(2,1)S(1)} collective-permute-done((bf16[12,16,256]{2,1,0:T(8,128)(2,1)S(1)}, bf16[12,16,256]{2,1,0:T(8,128)(2,1)S(1)}, u32[]{:S(2)}, u32[]{:S(2)}) %collective-permute-start.2) | collective-permute-done | bytes 98336 | tf_op jit(solution)/shard_map/ppermute | solution.py:100
  18.3 0.7 %collective-permute-start.7 = (bf16[24,16,512]{2,1,0:T(8,128)(2,1)S(1)}, bf16[24,16,512]{2,1,0:T(8,128)(2,1)S(1)}, u32[]{:S(2)}, u32[]{:S(2)}) collective-permute-start(bf16[24,16,512]{2,1,0:T(8,128)(2,1)S(1)} %get-tuple-element.40.refs_1_.refs_9_), channel_id=1, source_target_pairs={{8,4},{9,5},{10,6},{11,7},{20,24},{21,25},{22,26},{23,27}} | collective-permute-start | bytes 1179656 | tf_op jit(solution)/shard_map/ppermute | solution.py:100
  19.0 0.7 %collective-permute-start.9 = (bf16[24,16,512]{2,1,0:T(8,128)(2,1)S(1)}, bf16[24,16,512]{2,1,0:T(8,128)(2,1)S(1)}, u32[]{:S(2)}, u32[]{:S(2)}) collective-permute-start(bf16[24,16,512]{2,1,0:T(8,128)(2,1)S(1)} %get-tuple-element.40.refs_1_.refs_9_), channel_id=1, source_target_pairs={{0,4},{1,5},{2,6},{3,7},{28,24},{29,25},{30,26},{31,27}} | collective-permute-start | bytes 1179656 | tf_op jit(solution)/shard_map/ppermute | solution.py:100
  19.8 0.6 %inner_3.1 = (f32[22,64,256]{2,1,0:T(8,128)S(1)}, f32[4,64,256]{2,1,0:T(8,128)S(1)}, f32[2,64,256]{2,1,0:T(8,128)S(1)}) custom-call(s32[4]{0:T(128)S(1)} %copy-done.3, bf16[24,16,640]{2,1,0:T(8,128)(2,1)S(1)} %get-tuple-element.37.refs_1_.refs_5_, bf16[24,16,640]{2,1,0:T(8,128)(2,1)S(1)} %collective-permute-done.3.refs_2_.refs_6_, ...), custom_call_target="tpu_custom_call" | custom-call | flops 1207959552 | bytes 3932160 | tf_op jit(solution)/shard_map/inner_3/pallas_call | solution.py:272
  20.4 5.3 %collective-permute-start.6 = (bf16[24,16,256]{2,1,0:T(8,128)(2,1)S(1)}, bf16[24,16,256]{2,1,0:T(8,128)(2,1)S(1)}, u32[]{:S(2)}, u32[]{:S(2)}) collective-permute-start(bf16[24,16,256]{2,1,0:T(8,128)(2,1)S(1)} %pad_maximum_fusion.refs_1_), channel_id=1, source_target_pairs={{8,4},{9,5},{10,6},{11,7},{12,20},{13,21},{14,22},{15,23},{16,8},{... | collective-permute-start | bytes 589832 | tf_op jit(solution)/shard_map/ppermute | solution.py:100
  25.8 0.7 %collective-permute-start.11 = (bf16[24,16,256]{2,1,0:T(8,128)(2,1)S(1)}, bf16[24,16,256]{2,1,0:T(8,128)(2,1)S(1)}, u32[]{:S(2)}, u32[]{:S(2)}) collective-permute-start(bf16[24,16,256]{2,1,0:T(8,128)(2,1)S(1)} %pad_maximum_fusion.refs_1_), channel_id=1, source_target_pairs={{0,4},{1,5},{2,6},{3,7},{28,24},{29,25},{30,26},{31,27}} | collective-permute-start | bytes 589832 | tf_op jit(solution)/shard_map/ppermute | solution.py:100
  27.0 0.6 %inner_1.1 = (f32[18,64,256]{2,1,0:T(8,128)S(1)}, f32[4,64,256]{2,1,0:T(8,128)S(1)}) custom-call(s32[4]{0:T(128)S(1)} %copy-done.3, bf16[24,16,512]{2,1,0:T(8,128)(2,1)S(1)} %get-tuple-element.40.refs_1_.refs_9_, bf16[24,16,512]{2,1,0:T(8,128)(2,1)S(1)} %collective-permute-done.7.refs_2_.refs_10_, ...), custom_call_target="tpu_custom_call" | custom-call | flops 1006632960 | bytes 3276800 | tf_op jit(solution)/shard_map/inner_1/pallas_call | solution.py:272
  27.6 2.5 %collective-permute-done.6.refs_2_ = bf16[24,16,256]{2,1,0:T(8,128)(2,1)S(1)} collective-permute-done((bf16[24,16,256]{2,1,0:T(8,128)(2,1)S(1)}, bf16[24,16,256]{2,1,0:T(8,128)(2,1)S(1)}, u32[]{:S(2)}, u32[]{:S(2)}) %collective-permute-start.6) | collective-permute-done | bytes 196640 | tf_op jit(solution)/shard_map/ppermute | solution.py:100
  30.1 0.7 %collective-permute-start.10 = (bf16[24,16,256]{2,1,0:T(8,128)(2,1)S(1)}, bf16[24,16,256]{2,1,0:T(8,128)(2,1)S(1)}, u32[]{:S(2)}, u32[]{:S(2)}) collective-permute-start(bf16[24,16,256]{2,1,0:T(8,128)(2,1)S(1)} %collective-permute-done.6.refs_2_), channel_id=1, source_target_pairs={{8,24},{9,25},{10,26},{11,27},{20,4},{21,5},{22,6},{23,7}} | collective-permute-start | bytes 589832 | tf_op jit(solution)/shard_map/ppermute | solution.py:100
  30.8 0.6 %inner_0.1 = (bf16[16,16,256]{2,1,0:T(8,128)(2,1)S(1)}, bf16[16,16,256]{2,1,0:T(8,128)(2,1)S(1)}, bf16[16,16,256]{2,1,0:T(8,128)(2,1)S(1)}, bf16[16,16,256]{2,1,0:T(8,128)(2,1)S(1)}, f32[4,64,256]{2,1,0:T(8,128)S(1)}) custom-call(s32[4]{0:T(128)S(1)} %copy-done.3, bf16[24,16,512]{2,1,0:T(8,128)(2,1)S(1)} %get-tuple-element.40.refs_1_.refs_9_, ...), custom_call_target="tpu_custom_call" | custom-call | flops 905969664 | bytes 2949120 | tf_op jit(solution)/shard_map/inner_0/pallas_call | solution.py:272
  31.4 0.8 %outer.1 = (bf16[24,16,256]{2,1,0:T(8,128)(2,1)S(1)}, bf16[24,16,256]{2,1,0:T(8,128)(2,1)S(1)}, bf16[24,16,256]{2,1,0:T(8,128)(2,1)S(1)}, bf16[24,16,256]{2,1,0:T(8,128)(2,1)S(1)}) custom-call(s32[4]{0:T(128)S(1)} %copy-done.3, bf16[24,16,256]{2,1,0:T(8,128)(2,1)S(1)} %pad_maximum_fusion.refs_1_, bf16[24,16,256]{2,1,0:T(8,128)(2,1)S(1)} %collective-permute-done.6.refs_2_, ...), custom_call_target="tpu_custom_call" | custom-call | flops 1610612736 | bytes 5242880 | tf_op jit(solution)/shard_map/outer/pallas_call | solution.py:372
  32.2 0.7 %collective-permute-start.12 = (bf16[24,16,256]{2,1,0:T(8,128)(2,1)S(1)}, bf16[24,16,256]{2,1,0:T(8,128)(2,1)S(1)}, u32[]{:S(2)}, u32[]{:S(2)}) collective-permute-start(bf16[24,16,256]{2,1,0:T(8,128)(2,1)S(1)} %get-tuple-element.56), channel_id=1, source_target_pairs={{4,0},{5,1},{6,2},{7,3},{24,28},{25,29},{26,30},{27,31}} | collective-permute-start | bytes 589832 | tf_op jit(solution)/shard_map/ppermute | solution.py:100
  32.8 0.7 %collective-permute-start.13 = (bf16[24,16,256]{2,1,0:T(8,128)(2,1)S(1)}, bf16[24,16,256]{2,1,0:T(8,128)(2,1)S(1)}, u32[]{:S(2)}, u32[]{:S(2)}) collective-permute-start(bf16[24,16,256]{2,1,0:T(8,128)(2,1)S(1)} %get-tuple-element.57), channel_id=1, source_target_pairs={{4,8},{5,9},{6,10},{7,11},{24,20},{25,21},{26,22},{27,23}} | collective-permute-start | bytes 589832 | tf_op jit(solution)/shard_map/ppermute | solution.py:100
  33.5 1.3 %collective-permute-start.14 = (bf16[24,16,256]{2,1,0:T(8,128)(2,1)S(1)}, bf16[24,16,256]{2,1,0:T(8,128)(2,1)S(1)}, u32[]{:S(2)}, u32[]{:S(2)}) collective-permute-start(bf16[24,16,256]{2,1,0:T(8,128)(2,1)S(1)} %get-tuple-element.58), channel_id=1, source_target_pairs={{4,12},{5,13},{6,14},{7,15},{24,16},{25,17},{26,18},{27,19}} | collective-permute-start | bytes 589832 | tf_op jit(solution)/shard_map/ppermute | solution.py:100
  34.9 17.4 %collective-permute-done.14 = bf16[24,16,256]{2,1,0:T(8,128)(2,1)S(1)} collective-permute-done((bf16[24,16,256]{2,1,0:T(8,128)(2,1)S(1)}, bf16[24,16,256]{2,1,0:T(8,128)(2,1)S(1)}, u32[]{:S(2)}, u32[]{:S(2)}) %collective-permute-start.14) | collective-permute-done | bytes 196640 | tf_op jit(solution)/shard_map/ppermute | solution.py:100
  52.3 0.7 %copy.14 = bf16[1,16,24,256]{3,2,1,0:T(8,128)(2,1)} copy(bf16[1,16,24,256]{3,1,2,0:T(8,128)(2,1)S(1)} %add_bitcast_fusion) | data formatting | bytes 393216 | tf_op jit(solution)/shard_map/broadcast_in_dim | solution.py:466
  (27 shorter events, 0.9 us)
Async XLA Ops:
  0.0 19.7 %copy-start.4 = (f32[4,5,256]{2,0,1:T(4,128)S(1)}, f32[4,5,256]{2,0,1:T(4,128)}, u32[]{:S(2)}) copy-start(f32[4,5,256]{2,0,1:T(4,128)} %param.12) | copy-start | bytes 61444
  0.0 19.8 %copy-start = (bf16[4,256,512]{2,1,0:T(8,128)(2,1)S(1)}, bf16[4,256,512]{2,1,0:T(8,128)(2,1)}, u32[]{:S(2)}) copy-start(bf16[4,256,512]{2,1,0:T(8,128)(2,1)} %refs_26_.1) | copy-start | bytes 3145732
  0.0 19.8 %copy-start.1 = (bf16[4,512,256]{2,1,0:T(8,128)(2,1)S(1)}, bf16[4,512,256]{2,1,0:T(8,128)(2,1)}, u32[]{:S(2)}) copy-start(bf16[4,512,256]{2,1,0:T(8,128)(2,1)} %refs_27_.1) | copy-start | bytes 3145732
  0.0 19.8 %copy-start.2 = (bf16[256,128]{1,0:T(8,128)(2,1)S(1)}, bf16[256,128]{1,0:T(8,128)(2,1)}, u32[]{:S(2)}) copy-start(bf16[256,128]{1,0:T(8,128)(2,1)} %refs_25_.1) | copy-start | bytes 196612
  0.0 19.8 %copy-start.3 = (s32[4]{0:T(128)S(1)}, s32[4]{0:T(128)}, u32[]{:S(2)}) copy-start(s32[4]{0:T(128)} %refs_0_.9) | copy-start | bytes 52
  0.0 1.6 %collective-permute-start = (bf16[16,24,128]{2,1,0:T(8,128)(2,1)}, bf16[16,24,128]{2,1,0:T(8,128)(2,1)S(1)}, u32[]{:S(2)}, u32[]{:S(2)}) collective-permute-start(bf16[16,24,128]{2,1,0:T(8,128)(2,1)} %bitcast.11), channel_id=1, source_target_pairs={{0,16},{16,0},{1,17},{17,1},{2,18},{18,2},{3,19},{19,3},{4,20},{20... | collective-permute-start | bytes 294920 | tf_op jit(solution)/shard_map/ppermute | solution.py:38
  1.7 17.3 %collective-permute-start.3 = (bf16[24,16,640]{2,1,0:T(8,128)(2,1)S(1)}, bf16[24,16,640]{2,1,0:T(8,128)(2,1)S(1)}, u32[]{:S(2)}, u32[]{:S(2)}) collective-permute-start(bf16[24,16,640]{2,1,0:T(8,128)(2,1)S(1)} %get-tuple-element.37.refs_1_.refs_5_), channel_id=1, source_target_pairs={{8,4},{9,5},{10,6},{11,7},{20,24},{21,25},{22,26},{23,27}} | collective-permute-start | bytes 1474568 | tf_op jit(solution)/shard_map/ppermute | solution.py:100
  2.4 17.4 %collective-permute-start.4 = (bf16[24,16,640]{2,1,0:T(8,128)(2,1)S(1)}, bf16[24,16,640]{2,1,0:T(8,128)(2,1)S(1)}, u32[]{:S(2)}, u32[]{:S(2)}) collective-permute-start(bf16[24,16,640]{2,1,0:T(8,128)(2,1)S(1)} %get-tuple-element.37.refs_1_.refs_5_), channel_id=1, source_target_pairs={{12,4},{13,5},{14,6},{15,7},{16,24},{17,25},{18,26},{19,27}} | collective-permute-start | bytes 1474568 | tf_op jit(solution)/shard_map/ppermute | solution.py:100
  8.6 11.2 %collective-permute-start.5 = (bf16[24,16,640]{2,1,0:T(8,128)(2,1)S(1)}, bf16[24,16,640]{2,1,0:T(8,128)(2,1)S(1)}, u32[]{:S(2)}, u32[]{:S(2)}) collective-permute-start(bf16[24,16,640]{2,1,0:T(8,128)(2,1)S(1)} %get-tuple-element.37.refs_1_.refs_5_), channel_id=1, source_target_pairs={{0,4},{1,5},{2,6},{3,7},{28,24},{29,25},{30,26},{31,27}} | collective-permute-start | bytes 1474568 | tf_op jit(solution)/shard_map/ppermute | solution.py:100
  9.3 5.3 %collective-permute-start.1 = (bf16[12,16,256]{2,1,0:T(8,128)(2,1)S(1)}, bf16[12,16,256]{2,1,0:T(8,128)(2,1)S(1)}, u32[]{:S(2)}, u32[]{:S(2)}) collective-permute-start(bf16[12,16,256]{2,1,0:T(8,128)(2,1)S(1)} %get-tuple-element.33), channel_id=1, source_target_pairs={{0,1},{1,2},{2,3},{4,5},{5,6},{6,7},{8,9},{9,10},{10,11},{12,13},{... | collective-permute-start | bytes 294920 | tf_op jit(solution)/shard_map/ppermute | solution.py:100
  12.4 5.9 %collective-permute-start.2 = (bf16[12,16,256]{2,1,0:T(8,128)(2,1)S(1)}, bf16[12,16,256]{2,1,0:T(8,128)(2,1)S(1)}, u32[]{:S(2)}, u32[]{:S(2)}) collective-permute-start(bf16[12,16,256]{2,1,0:T(8,128)(2,1)S(1)} %get-tuple-element.34), channel_id=1, source_target_pairs={{1,0},{2,1},{3,2},{5,4},{6,5},{7,6},{9,8},{10,9},{11,10},{13,12},{... | collective-permute-start | bytes 294920 | tf_op jit(solution)/shard_map/ppermute | solution.py:100
  14.5 12.5 %collective-permute-start.8 = (bf16[24,16,512]{2,1,0:T(8,128)(2,1)S(1)}, bf16[24,16,512]{2,1,0:T(8,128)(2,1)S(1)}, u32[]{:S(2)}, u32[]{:S(2)}) collective-permute-start(bf16[24,16,512]{2,1,0:T(8,128)(2,1)S(1)} %get-tuple-element.40.refs_1_.refs_9_), channel_id=1, source_target_pairs={{12,4},{13,5},{14,6},{15,7},{16,24},{17,25},{18,26},{19,27}} | collective-permute-start | bytes 1179656 | tf_op jit(solution)/shard_map/ppermute | solution.py:100
  18.3 8.7 %collective-permute-start.7 = (bf16[24,16,512]{2,1,0:T(8,128)(2,1)S(1)}, bf16[24,16,512]{2,1,0:T(8,128)(2,1)S(1)}, u32[]{:S(2)}, u32[]{:S(2)}) collective-permute-start(bf16[24,16,512]{2,1,0:T(8,128)(2,1)S(1)} %get-tuple-element.40.refs_1_.refs_9_), channel_id=1, source_target_pairs={{8,4},{9,5},{10,6},{11,7},{20,24},{21,25},{22,26},{23,27}} | collective-permute-start | bytes 1179656 | tf_op jit(solution)/shard_map/ppermute | solution.py:100
  19.0 8.0 %collective-permute-start.9 = (bf16[24,16,512]{2,1,0:T(8,128)(2,1)S(1)}, bf16[24,16,512]{2,1,0:T(8,128)(2,1)S(1)}, u32[]{:S(2)}, u32[]{:S(2)}) collective-permute-start(bf16[24,16,512]{2,1,0:T(8,128)(2,1)S(1)} %get-tuple-element.40.refs_1_.refs_9_), channel_id=1, source_target_pairs={{0,4},{1,5},{2,6},{3,7},{28,24},{29,25},{30,26},{31,27}} | collective-permute-start | bytes 1179656 | tf_op jit(solution)/shard_map/ppermute | solution.py:100
  20.4 9.7 %collective-permute-start.6 = (bf16[24,16,256]{2,1,0:T(8,128)(2,1)S(1)}, bf16[24,16,256]{2,1,0:T(8,128)(2,1)S(1)}, u32[]{:S(2)}, u32[]{:S(2)}) collective-permute-start(bf16[24,16,256]{2,1,0:T(8,128)(2,1)S(1)} %pad_maximum_fusion.refs_1_), channel_id=1, source_target_pairs={{8,4},{9,5},{10,6},{11,7},{12,20},{13,21},{14,22},{15,23},{16,8},{... | collective-permute-start | bytes 589832 | tf_op jit(solution)/shard_map/ppermute | solution.py:100
  25.8 5.6 %collective-permute-start.11 = (bf16[24,16,256]{2,1,0:T(8,128)(2,1)S(1)}, bf16[24,16,256]{2,1,0:T(8,128)(2,1)S(1)}, u32[]{:S(2)}, u32[]{:S(2)}) collective-permute-start(bf16[24,16,256]{2,1,0:T(8,128)(2,1)S(1)} %pad_maximum_fusion.refs_1_), channel_id=1, source_target_pairs={{0,4},{1,5},{2,6},{3,7},{28,24},{29,25},{30,26},{31,27}} | collective-permute-start | bytes 589832 | tf_op jit(solution)/shard_map/ppermute | solution.py:100
  30.1 1.2 %collective-permute-start.10 = (bf16[24,16,256]{2,1,0:T(8,128)(2,1)S(1)}, bf16[24,16,256]{2,1,0:T(8,128)(2,1)S(1)}, u32[]{:S(2)}, u32[]{:S(2)}) collective-permute-start(bf16[24,16,256]{2,1,0:T(8,128)(2,1)S(1)} %collective-permute-done.6.refs_2_), channel_id=1, source_target_pairs={{8,24},{9,25},{10,26},{11,27},{20,4},{21,5},{22,6},{23,7}} | collective-permute-start | bytes 589832 | tf_op jit(solution)/shard_map/ppermute | solution.py:100
  32.2 2.7 %collective-permute-start.12 = (bf16[24,16,256]{2,1,0:T(8,128)(2,1)S(1)}, bf16[24,16,256]{2,1,0:T(8,128)(2,1)S(1)}, u32[]{:S(2)}, u32[]{:S(2)}) collective-permute-start(bf16[24,16,256]{2,1,0:T(8,128)(2,1)S(1)} %get-tuple-element.56), channel_id=1, source_target_pairs={{4,0},{5,1},{6,2},{7,3},{24,28},{25,29},{26,30},{27,31}} | collective-permute-start | bytes 589832 | tf_op jit(solution)/shard_map/ppermute | solution.py:100
  32.8 2.0 %collective-permute-start.13 = (bf16[24,16,256]{2,1,0:T(8,128)(2,1)S(1)}, bf16[24,16,256]{2,1,0:T(8,128)(2,1)S(1)}, u32[]{:S(2)}, u32[]{:S(2)}) collective-permute-start(bf16[24,16,256]{2,1,0:T(8,128)(2,1)S(1)} %get-tuple-element.57), channel_id=1, source_target_pairs={{4,8},{5,9},{6,10},{7,11},{24,20},{25,21},{26,22},{27,23}} | collective-permute-start | bytes 589832 | tf_op jit(solution)/shard_map/ppermute | solution.py:100
  33.5 18.8 %collective-permute-start.14 = (bf16[24,16,256]{2,1,0:T(8,128)(2,1)S(1)}, bf16[24,16,256]{2,1,0:T(8,128)(2,1)S(1)}, u32[]{:S(2)}, u32[]{:S(2)}) collective-permute-start(bf16[24,16,256]{2,1,0:T(8,128)(2,1)S(1)} %get-tuple-element.58), channel_id=1, source_target_pairs={{4,12},{5,13},{6,14},{7,15},{24,16},{25,17},{26,18},{27,19}} | collective-permute-start | bytes 589832 | tf_op jit(solution)/shard_map/ppermute | solution.py:100

commit v7 on v6

--- a/solution.py
+++ b/solution.py
@@ -296,7 +296,7 @@
     handed_edges, gradients, refs = refs[0], refs[1:layers], refs[layers:]
     cg_edges, refs = refs[:layers], refs[layers:]
     dec_weight, w_in, w_out, taps, refs = refs[0], refs[1], refs[2], refs[3], refs[4:]
-    outs, (cg, grad) = refs[:4], refs[4:]
+    outs, cg, grad = refs[:4], refs[4:6], refs[6:8]
     rows, cells = mains[0][0].shape[:2]
     lon, chans = cg_edges[0].shape[1:]
     v = dec_weight.shape[1]
@@ -317,48 +317,61 @@
         at = edge_start(layers) + k // 2 + (0 if r < 0 else half_halo)
         return in_order([h[at, :, k % 2 * v : (k % 2 + 1) * v] for h in halos])
 
-    for p in range(4):
-        outs[p][layers : rows - layers] = inner[p][...]
-    for layer in reversed(range(layers)):
+    def gradient_rows(layer, side):
         shift = layers - 1 - layer
-        here = [*range(-layers + shift, shift), *range(rows - shift, rows - shift + layers)]
+        here = range(-layers + shift, shift) if side == 0 else range(rows - shift, rows - shift + layers)
         if layer == layers - 1:
             cot = jnp.concatenate(sum([cot_row(r) for r in here], []), axis=0)
             cot_low = nt(cot, dec_weight[...]).astype(jnp.bfloat16)
-            grad[...] = cot_low.astype(jnp.float32).reshape(grad.shape)
-            near = [handed_edges[0], handed_edges[1]]
+            grad[side][...] = cot_low.astype(jnp.float32).reshape(grad[side].shape)
         else:
-            cot_low = grad[...].reshape(len(here) * lon, chans).astype(jnp.bfloat16)
-            before = gradients[layers - 2 - layer]
-            near = [before[0], before[before.shape[0] - 1]]
+            cot_low = grad[side][...].reshape(layers * lon, chans).astype(jnp.bfloat16)
         conv_out = jnp.concatenate(sum([conv_row(layer, r) for r in here], []), axis=0)
-        conv_grad = conv_gradient(conv_out, cot_low, w_in[layer], w_out[layer])
-        conv_grad = conv_grad.reshape(len(here), lon, chans)
+        found = conv_gradient(conv_out, cot_low, w_in[layer], w_out[layer])
+        found = found.reshape(layers, lon, chans)
         edge = cg_edges[layers - 1 - layer]
         for k, r in enumerate(here):
-            row = conv_grad[k]
+            row = found[k]
             if r < 0:
                 row = row * has_above
             if r >= rows:
                 row = row * has_below
-            keep_row(cg, k if k < layers else k + 4, row)
-        for k in range(4):
-            keep_row(cg, layers + k, edge[k])
-        old = [grad[k] for k in range(2 * layers)]
-        old = [*old[1:layers], near[0], near[1], *old[layers:-1]]
-        places = [*range(1, layers + 1), *range(layers + 3, 2 * layers + 3)]
-        for k, at in enumerate(places):
+            keep_row(cg[side], k if side == 0 else k + 2, row)
+        for k in range(2):
+            keep_row(cg[side], layers + k if side == 0 else k, edge[k + 2 * side])
+
+    def gradient_taps(layer, side):
+        if layer == layers - 1:
+            near = handed_edges[side]
+        else:
+            before = gradients[layers - 2 - layer]
+            near = before[0 if side == 0 else before.shape[0] - 1]
+        old = [grad[side][k] for k in range(layers)]
+        old = [*old[1:], near] if side == 0 else [near, *old[:-1]]
+        for k in range(layers):
             for h, lanes in halves_of(chans):
                 tap = [taps[layer, n : n + 1, lanes] for n in range(5)]
-                total = old[k][:, lanes] + tapped(cg, at, h, tap, offset_ref[layer])
+                total = old[k][:, lanes] + tapped(cg[side], k + 1, h, tap, offset_ref[layer])
                 if layer:
-                    grad[k, :, lanes] = total
+                    grad[side][k, :, lanes] = total
                 else:
-                    low = total.astype(jnp.bfloat16)
-                    quarters = in_order([low[p * cells : (p + 1) * cells] for p in range(4)])
-                    r = k if k < layers else rows - 2 * layers + k
+                    quarters = quarters_of(total.astype(jnp.bfloat16))
+                    r = k if side == 0 else rows - layers + k
                     for p in range(4):
                         outs[p][r, :, lanes] = quarters[p]
+
+    def quarters_of(row):
+        return in_order([row[p * cells : (p + 1) * cells] for p in range(4)])
+
+    for p in range(4):
+        outs[p][layers : rows - layers] = inner[p][...]
+    gradient_rows(layers - 1, 0)
+    for layer in reversed(range(layers)):
+        gradient_rows(layer, 1)
+        gradient_taps(layer, 0)
+        if layer:
+            gradient_rows(layer - 1, 0)
+        gradient_taps(layer, 1)
 
 
 def run_outer(layers, offsets, halos, mains, inner, handed_edges, gradients, cg_edges, weights):
@@ -375,8 +388,8 @@
         in_specs=[smem] + [vmem] * (len(args) - 1),
         out_specs=[vmem] * 4,
         scratch_shapes=[
-            pltpu.VMEM((2 * layers + 4, chans // 128, 2 * lon, 128), jnp.float32),
-            pltpu.VMEM((2 * layers, lon, chans), jnp.float32),
+            *[pltpu.VMEM((layers + 2, chans // 128, 2 * lon, 128), jnp.float32)] * 2,
+            *[pltpu.VMEM((layers, lon, chans), jnp.float32)] * 2,
         ],
         compiler_params=pltpu.CompilerParams(vmem_limit_bytes=24 * 2**20),
         cost_estimate=pl.CostEstimate(
@@ -459,7 +472,7 @@
     )
 
     result = jnp.where(on_home(), found[0], 0)
-    for k in order:
+    for k in (2, 3, 1):
         result = result + routed(
             found[k], lambda c, z, j: (c, away(c, k), j) if z == home(c) else None
         )

time: 53.4 us -> 52.5 us (0.983)
  the two profiles are of different devices: /device:TPU:1 before, /device:TPU:0 now
where the time goes in v7:
time: 52.5 us; the launch traced here: 52.1 us
  starting transfers between devices  26.2 us (50%)
  waiting for transfers between devices  20.3 us (39%)
  Pallas kernels  3.08 us (6%)
  local copies, waits for them, and re-layouts  2.18 us (4%)
    ppermute x14, starting transfers between devices, routed(): return lax.ppermute(value, AXES, pairs)  25.7 us
    ppermute x14, waiting for transfers between devices, routed(): return lax.ppermute(value, AXES, pairs)  20.3 us
    pallas_call x4, Pallas kernels, run_inner(): pl.pallas_call(functools.partial(inner_kernel, layer, layers, place), out...  2.24 us
    unnamed x12, local copies, waits for them, and re-layouts  1.45 us
  transfers between devices with their start and end apart: 15, of which 4 were waited for; matrix products, arithmetic and copies ran while one was open for 3% of the time, Pallas kernels for 4%

profile of v7, /device:TPU:0, one launch (start us, length us, event | category | flops | bytes accessed | tf_op | source)
XLA Modules:
  0.0 52.1 jit_solution(15875556907636539797)
XLA Ops:
  0.5 1.4 %copy.16 = bf16[1,4,16,24,256]{4,2,3,1,0:T(8,128)(2,1)S(1)} copy(bf16[1,4,16,24,256]{4,3,2,1,0:T(8,128)(2,1)} %param.8) | data formatting | bytes 1572864 | tf_op args[1]
  2.1 0.7 %collective-permute-start.3 = (bf16[24,16,640]{2,1,0:T(8,128)(2,1)S(1)}, bf16[24,16,640]{2,1,0:T(8,128)(2,1)S(1)}, u32[]{:S(2)}, u32[]{:S(2)}) collective-permute-start(bf16[24,16,640]{2,1,0:T(8,128)(2,1)S(1)} %get-tuple-element.37.refs_1_.refs_5_), channel_id=1, source_target_pairs={{8,4},{9,5},{10,6},{11,7},{20,24},{21,25},{22,26},{23,27}} | collective-permute-start | bytes 1474568 | tf_op jit(solution)/shard_map/ppermute | solution.py:100
  2.8 0.7 %collective-permute-start.4 = (bf16[24,16,640]{2,1,0:T(8,128)(2,1)S(1)}, bf16[24,16,640]{2,1,0:T(8,128)(2,1)S(1)}, u32[]{:S(2)}, u32[]{:S(2)}) collective-permute-start(bf16[24,16,640]{2,1,0:T(8,128)(2,1)S(1)} %get-tuple-element.37.refs_1_.refs_5_), channel_id=1, source_target_pairs={{12,4},{13,5},{14,6},{15,7},{16,24},{17,25},{18,26},{19,27}} | collective-permute-start | bytes 1474568 | tf_op jit(solution)/shard_map/ppermute | solution.py:100
  3.5 5.8 %collective-permute-start.5 = (bf16[24,16,640]{2,1,0:T(8,128)(2,1)S(1)}, bf16[24,16,640]{2,1,0:T(8,128)(2,1)S(1)}, u32[]{:S(2)}, u32[]{:S(2)}) collective-permute-start(bf16[24,16,640]{2,1,0:T(8,128)(2,1)S(1)} %get-tuple-element.37.refs_1_.refs_5_), channel_id=1, source_target_pairs={{0,4},{1,5},{2,6},{3,7},{28,24},{29,25},{30,26},{31,27}} | collective-permute-start | bytes 1474568 | tf_op jit(solution)/shard_map/ppermute | solution.py:100
  9.3 3.4 %collective-permute-start.1 = (bf16[12,16,256]{2,1,0:T(8,128)(2,1)S(1)}, bf16[12,16,256]{2,1,0:T(8,128)(2,1)S(1)}, u32[]{:S(2)}, u32[]{:S(2)}) collective-permute-start(bf16[12,16,256]{2,1,0:T(8,128)(2,1)S(1)} %get-tuple-element.33), channel_id=1, source_target_pairs={{0,1},{1,2},{2,3},{4,5},{5,6},{6,7},{8,9},{9,10},{10,11},{12,13},{... | collective-permute-start | bytes 294920 | tf_op jit(solution)/shard_map/ppermute | solution.py:100
  12.7 1.3 %collective-permute-start.2 = (bf16[12,16,256]{2,1,0:T(8,128)(2,1)S(1)}, bf16[12,16,256]{2,1,0:T(8,128)(2,1)S(1)}, u32[]{:S(2)}, u32[]{:S(2)}) collective-permute-start(bf16[12,16,256]{2,1,0:T(8,128)(2,1)S(1)} %get-tuple-element.34), channel_id=1, source_target_pairs={{1,0},{2,1},{3,2},{5,4},{6,5},{7,6},{9,8},{10,9},{11,10},{13,12},{... | collective-permute-start | bytes 294920 | tf_op jit(solution)/shard_map/ppermute | solution.py:100
  14.0 1.3 %collective-permute-done.1 = bf16[12,16,256]{2,1,0:T(8,128)(2,1)S(1)} collective-permute-done((bf16[12,16,256]{2,1,0:T(8,128)(2,1)S(1)}, bf16[12,16,256]{2,1,0:T(8,128)(2,1)S(1)}, u32[]{:S(2)}, u32[]{:S(2)}) %collective-permute-start.1) | collective-permute-done | bytes 98336 | tf_op jit(solution)/shard_map/ppermute | solution.py:100
  15.3 0.7 %collective-permute-start.8 = (bf16[24,16,512]{2,1,0:T(8,128)(2,1)S(1)}, bf16[24,16,512]{2,1,0:T(8,128)(2,1)S(1)}, u32[]{:S(2)}, u32[]{:S(2)}) collective-permute-start(bf16[24,16,512]{2,1,0:T(8,128)(2,1)S(1)} %get-tuple-element.40.refs_1_.refs_9_), channel_id=1, source_target_pairs={{12,4},{13,5},{14,6},{15,7},{16,24},{17,25},{18,26},{19,27}} | collective-permute-start | bytes 1179656 | tf_op jit(solution)/shard_map/ppermute | solution.py:100
  16.0 3.4 %collective-permute-done.2 = bf16[12,16,256]{2,1,0:T(8,128)(2,1)S(1)} collective-permute-done((bf16[12,16,256]{2,1,0:T(8,128)(2,1)S(1)}, bf16[12,16,256]{2,1,0:T(8,128)(2,1)S(1)}, u32[]{:S(2)}, u32[]{:S(2)}) %collective-permute-start.2) | collective-permute-done | bytes 98336 | tf_op jit(solution)/shard_map/ppermute | solution.py:100
  19.5 0.7 %collective-permute-start.7 = (bf16[24,16,512]{2,1,0:T(8,128)(2,1)S(1)}, bf16[24,16,512]{2,1,0:T(8,128)(2,1)S(1)}, u32[]{:S(2)}, u32[]{:S(2)}) collective-permute-start(bf16[24,16,512]{2,1,0:T(8,128)(2,1)S(1)} %get-tuple-element.40.refs_1_.refs_9_), channel_id=1, source_target_pairs={{8,4},{9,5},{10,6},{11,7},{20,24},{21,25},{22,26},{23,27}} | collective-permute-start | bytes 1179656 | tf_op jit(solution)/shard_map/ppermute | solution.py:100
  20.1 2.5 %collective-permute-start.9 = (bf16[24,16,512]{2,1,0:T(8,128)(2,1)S(1)}, bf16[24,16,512]{2,1,0:T(8,128)(2,1)S(1)}, u32[]{:S(2)}, u32[]{:S(2)}) collective-permute-start(bf16[24,16,512]{2,1,0:T(8,128)(2,1)S(1)} %get-tuple-element.40.refs_1_.refs_9_), channel_id=1, source_target_pairs={{0,4},{1,5},{2,6},{3,7},{28,24},{29,25},{30,26},{31,27}} | collective-permute-start | bytes 1179656 | tf_op jit(solution)/shard_map/ppermute | solution.py:100
  22.8 0.6 %inner_3.1 = (f32[22,64,256]{2,1,0:T(8,128)S(1)}, f32[4,64,256]{2,1,0:T(8,128)S(1)}, f32[2,64,256]{2,1,0:T(8,128)S(1)}) custom-call(s32[4]{0:T(128)S(1)} %copy-done.3, bf16[24,16,640]{2,1,0:T(8,128)(2,1)S(1)} %get-tuple-element.37.refs_1_.refs_5_, bf16[24,16,640]{2,1,0:T(8,128)(2,1)S(1)} %collective-permute-done.3.refs_2_.refs_6_, ...), custom_call_target="tpu_custom_call" | custom-call | flops 1207959552 | bytes 3932160 | tf_op jit(solution)/shard_map/inner_3/pallas_call | solution.py:272
  23.3 0.7 %collective-permute-start.6 = (bf16[24,16,256]{2,1,0:T(8,128)(2,1)S(1)}, bf16[24,16,256]{2,1,0:T(8,128)(2,1)S(1)}, u32[]{:S(2)}, u32[]{:S(2)}) collective-permute-start(bf16[24,16,256]{2,1,0:T(8,128)(2,1)S(1)} %pad_maximum_fusion.refs_1_), channel_id=1, source_target_pairs={{8,4},{9,5},{10,6},{11,7},{12,20},{13,21},{14,22},{15,23},{16,8},{... | collective-permute-start | bytes 589832 | tf_op jit(solution)/shard_map/ppermute | solution.py:100
  24.0 6.0 %collective-permute-start.11 = (bf16[24,16,256]{2,1,0:T(8,128)(2,1)S(1)}, bf16[24,16,256]{2,1,0:T(8,128)(2,1)S(1)}, u32[]{:S(2)}, u32[]{:S(2)}) collective-permute-start(bf16[24,16,256]{2,1,0:T(8,128)(2,1)S(1)} %pad_maximum_fusion.refs_1_), channel_id=1, source_target_pairs={{0,4},{1,5},{2,6},{3,7},{28,24},{29,25},{30,26},{31,27}} | collective-permute-start | bytes 589832 | tf_op jit(solution)/shard_map/ppermute | solution.py:100
  30.0 0.6 %inner_2.1 = (f32[20,64,256]{2,1,0:T(8,128)S(1)}, f32[4,64,256]{2,1,0:T(8,128)S(1)}) custom-call(s32[4]{0:T(128)S(1)} %copy-done.3, bf16[24,16,640]{2,1,0:T(8,128)(2,1)S(1)} %get-tuple-element.37.refs_1_.refs_5_, bf16[24,16,640]{2,1,0:T(8,128)(2,1)S(1)} %collective-permute-done.3.refs_2_.refs_6_, ...), custom_call_target="tpu_custom_call" | custom-call | flops 1107296256 | bytes 3604480 | tf_op jit(solution)/shard_map/inner_2/pallas_call | solution.py:272
  31.2 0.7 %collective-permute-start.10 = (bf16[24,16,256]{2,1,0:T(8,128)(2,1)S(1)}, bf16[24,16,256]{2,1,0:T(8,128)(2,1)S(1)}, u32[]{:S(2)}, u32[]{:S(2)}) collective-permute-start(bf16[24,16,256]{2,1,0:T(8,128)(2,1)S(1)} %collective-permute-done.6.refs_2_), channel_id=1, source_target_pairs={{8,24},{9,25},{10,26},{11,27},{20,4},{21,5},{22,6},{23,7}} | collective-permute-start | bytes 589832 | tf_op jit(solution)/shard_map/ppermute | solution.py:100
  31.9 0.6 %inner_0.1 = (bf16[16,16,256]{2,1,0:T(8,128)(2,1)S(1)}, bf16[16,16,256]{2,1,0:T(8,128)(2,1)S(1)}, bf16[16,16,256]{2,1,0:T(8,128)(2,1)S(1)}, bf16[16,16,256]{2,1,0:T(8,128)(2,1)S(1)}, f32[4,64,256]{2,1,0:T(8,128)S(1)}) custom-call(s32[4]{0:T(128)S(1)} %copy-done.3, bf16[24,16,512]{2,1,0:T(8,128)(2,1)S(1)} %get-tuple-element.40.refs_1_.refs_9_, ...), custom_call_target="tpu_custom_call" | custom-call | flops 905969664 | bytes 2949120 | tf_op jit(solution)/shard_map/inner_0/pallas_call | solution.py:272
  32.5 0.7 %collective-permute-done.11.refs_4_ = bf16[24,16,256]{2,1,0:T(8,128)(2,1)S(1)} collective-permute-done((bf16[24,16,256]{2,1,0:T(8,128)(2,1)S(1)}, bf16[24,16,256]{2,1,0:T(8,128)(2,1)S(1)}, u32[]{:S(2)}, u32[]{:S(2)}) %collective-permute-start.11) | collective-permute-done | bytes 196640 | tf_op jit(solution)/shard_map/ppermute | solution.py:100
  33.2 0.7 %outer.1 = (bf16[24,16,256]{2,1,0:T(8,128)(2,1)S(1)}, bf16[24,16,256]{2,1,0:T(8,128)(2,1)S(1)}, bf16[24,16,256]{2,1,0:T(8,128)(2,1)S(1)}, bf16[24,16,256]{2,1,0:T(8,128)(2,1)S(1)}) custom-call(s32[4]{0:T(128)S(1)} %copy-done.3, bf16[24,16,256]{2,1,0:T(8,128)(2,1)S(1)} %pad_maximum_fusion.refs_1_, bf16[24,16,256]{2,1,0:T(8,128)(2,1)S(1)} %collective-permute-done.6.refs_2_, ...), custom_call_target="tpu_custom_call" | custom-call | flops 1610612736 | bytes 5242880 | tf_op jit(solution)/shard_map/outer/pallas_call | solution.py:385
  33.9 0.7 %collective-permute-start.12 = (bf16[24,16,256]{2,1,0:T(8,128)(2,1)S(1)}, bf16[24,16,256]{2,1,0:T(8,128)(2,1)S(1)}, u32[]{:S(2)}, u32[]{:S(2)}) collective-permute-start(bf16[24,16,256]{2,1,0:T(8,128)(2,1)S(1)} %get-tuple-element.56), channel_id=1, source_target_pairs={{4,12},{5,13},{6,14},{7,15},{24,16},{25,17},{26,18},{27,19}} | collective-permute-start | bytes 589832 | tf_op jit(solution)/shard_map/ppermute | solution.py:100
  34.6 1.3 %collective-permute-start.13 = (bf16[24,16,256]{2,1,0:T(8,128)(2,1)S(1)}, bf16[24,16,256]{2,1,0:T(8,128)(2,1)S(1)}, u32[]{:S(2)}, u32[]{:S(2)}) collective-permute-start(bf16[24,16,256]{2,1,0:T(8,128)(2,1)S(1)} %get-tuple-element.57), channel_id=1, source_target_pairs={{4,0},{5,1},{6,2},{7,3},{24,28},{25,29},{26,30},{27,31}} | collective-permute-start | bytes 589832 | tf_op jit(solution)/shard_map/ppermute | solution.py:100
  35.9 0.7 %collective-permute-start.14 = (bf16[24,16,256]{2,1,0:T(8,128)(2,1)S(1)}, bf16[24,16,256]{2,1,0:T(8,128)(2,1)S(1)}, u32[]{:S(2)}, u32[]{:S(2)}) collective-permute-start(bf16[24,16,256]{2,1,0:T(8,128)(2,1)S(1)} %get-tuple-element.58), channel_id=1, source_target_pairs={{4,8},{5,9},{6,10},{7,11},{24,20},{25,21},{26,22},{27,23}} | collective-permute-start | bytes 589832 | tf_op jit(solution)/shard_map/ppermute | solution.py:100
  36.6 14.7 %collective-permute-done.13 = bf16[24,16,256]{2,1,0:T(8,128)(2,1)S(1)} collective-permute-done((bf16[24,16,256]{2,1,0:T(8,128)(2,1)S(1)}, bf16[24,16,256]{2,1,0:T(8,128)(2,1)S(1)}, u32[]{:S(2)}, u32[]{:S(2)}) %collective-permute-start.13) | collective-permute-done | bytes 196640 | tf_op jit(solution)/shard_map/ppermute | solution.py:100
  51.4 0.7 %copy.14 = bf16[1,16,24,256]{3,2,1,0:T(8,128)(2,1)} copy(bf16[1,16,24,256]{3,1,2,0:T(8,128)(2,1)S(1)} %add_bitcast_fusion) | data formatting | bytes 393216 | tf_op jit(solution)/shard_map/broadcast_in_dim | solution.py:479
  (27 shorter events, 1.3 us)
Async XLA Ops:
  0.0 22.6 %copy-start.4 = (f32[4,5,256]{2,0,1:T(4,128)S(1)}, f32[4,5,256]{2,0,1:T(4,128)}, u32[]{:S(2)}) copy-start(f32[4,5,256]{2,0,1:T(4,128)} %param.12) | copy-start | bytes 61444
  0.0 22.7 %copy-start = (bf16[4,256,512]{2,1,0:T(8,128)(2,1)S(1)}, bf16[4,256,512]{2,1,0:T(8,128)(2,1)}, u32[]{:S(2)}) copy-start(bf16[4,256,512]{2,1,0:T(8,128)(2,1)} %refs_26_.1) | copy-start | bytes 3145732
  0.0 22.7 %copy-start.1 = (bf16[4,512,256]{2,1,0:T(8,128)(2,1)S(1)}, bf16[4,512,256]{2,1,0:T(8,128)(2,1)}, u32[]{:S(2)}) copy-start(bf16[4,512,256]{2,1,0:T(8,128)(2,1)} %refs_27_.1) | copy-start | bytes 3145732
  0.0 22.7 %copy-start.2 = (bf16[256,128]{1,0:T(8,128)(2,1)S(1)}, bf16[256,128]{1,0:T(8,128)(2,1)}, u32[]{:S(2)}) copy-start(bf16[256,128]{1,0:T(8,128)(2,1)} %refs_25_.1) | copy-start | bytes 196612
  0.0 22.7 %copy-start.3 = (s32[4]{0:T(128)S(1)}, s32[4]{0:T(128)}, u32[]{:S(2)}) copy-start(s32[4]{0:T(128)} %refs_0_.9) | copy-start | bytes 52
  0.0 2.0 %collective-permute-start = (bf16[16,24,128]{2,1,0:T(8,128)(2,1)}, bf16[16,24,128]{2,1,0:T(8,128)(2,1)S(1)}, u32[]{:S(2)}, u32[]{:S(2)}) collective-permute-start(bf16[16,24,128]{2,1,0:T(8,128)(2,1)} %bitcast.11), channel_id=1, source_target_pairs={{0,16},{16,0},{1,17},{17,1},{2,18},{18,2},{3,19},{19,3},{4,20},{20... | collective-permute-start | bytes 294920 | tf_op jit(solution)/shard_map/ppermute | solution.py:38
  2.1 18.0 %collective-permute-start.3 = (bf16[24,16,640]{2,1,0:T(8,128)(2,1)S(1)}, bf16[24,16,640]{2,1,0:T(8,128)(2,1)S(1)}, u32[]{:S(2)}, u32[]{:S(2)}) collective-permute-start(bf16[24,16,640]{2,1,0:T(8,128)(2,1)S(1)} %get-tuple-element.37.refs_1_.refs_5_), channel_id=1, source_target_pairs={{8,4},{9,5},{10,6},{11,7},{20,24},{21,25},{22,26},{23,27}} | collective-permute-start | bytes 1474568 | tf_op jit(solution)/shard_map/ppermute | solution.py:100
  2.8 19.9 %collective-permute-start.4 = (bf16[24,16,640]{2,1,0:T(8,128)(2,1)S(1)}, bf16[24,16,640]{2,1,0:T(8,128)(2,1)S(1)}, u32[]{:S(2)}, u32[]{:S(2)}) collective-permute-start(bf16[24,16,640]{2,1,0:T(8,128)(2,1)S(1)} %get-tuple-element.37.refs_1_.refs_5_), channel_id=1, source_target_pairs={{12,4},{13,5},{14,6},{15,7},{16,24},{17,25},{18,26},{19,27}} | collective-permute-start | bytes 1474568 | tf_op jit(solution)/shard_map/ppermute | solution.py:100
  3.5 19.2 %collective-permute-start.5 = (bf16[24,16,640]{2,1,0:T(8,128)(2,1)S(1)}, bf16[24,16,640]{2,1,0:T(8,128)(2,1)S(1)}, u32[]{:S(2)}, u32[]{:S(2)}) collective-permute-start(bf16[24,16,640]{2,1,0:T(8,128)(2,1)S(1)} %get-tuple-element.37.refs_1_.refs_5_), channel_id=1, source_target_pairs={{0,4},{1,5},{2,6},{3,7},{28,24},{29,25},{30,26},{31,27}} | collective-permute-start | bytes 1474568 | tf_op jit(solution)/shard_map/ppermute | solution.py:100
  9.3 6.0 %collective-permute-start.1 = (bf16[12,16,256]{2,1,0:T(8,128)(2,1)S(1)}, bf16[12,16,256]{2,1,0:T(8,128)(2,1)S(1)}, u32[]{:S(2)}, u32[]{:S(2)}) collective-permute-start(bf16[12,16,256]{2,1,0:T(8,128)(2,1)S(1)} %get-tuple-element.33), channel_id=1, source_target_pairs={{0,1},{1,2},{2,3},{4,5},{5,6},{6,7},{8,9},{9,10},{10,11},{12,13},{... | collective-permute-start | bytes 294920 | tf_op jit(solution)/shard_map/ppermute | solution.py:100
  12.7 6.8 %collective-permute-start.2 = (bf16[12,16,256]{2,1,0:T(8,128)(2,1)S(1)}, bf16[12,16,256]{2,1,0:T(8,128)(2,1)S(1)}, u32[]{:S(2)}, u32[]{:S(2)}) collective-permute-start(bf16[12,16,256]{2,1,0:T(8,128)(2,1)S(1)} %get-tuple-element.34), channel_id=1, source_target_pairs={{1,0},{2,1},{3,2},{5,4},{6,5},{7,6},{9,8},{10,9},{11,10},{13,12},{... | collective-permute-start | bytes 294920 | tf_op jit(solution)/shard_map/ppermute | solution.py:100
  15.3 15.3 %collective-permute-start.8 = (bf16[24,16,512]{2,1,0:T(8,128)(2,1)S(1)}, bf16[24,16,512]{2,1,0:T(8,128)(2,1)S(1)}, u32[]{:S(2)}, u32[]{:S(2)}) collective-permute-start(bf16[24,16,512]{2,1,0:T(8,128)(2,1)S(1)} %get-tuple-element.40.refs_1_.refs_9_), channel_id=1, source_target_pairs={{12,4},{13,5},{14,6},{15,7},{16,24},{17,25},{18,26},{19,27}} | collective-permute-start | bytes 1179656 | tf_op jit(solution)/shard_map/ppermute | solution.py:100
  19.5 11.2 %collective-permute-start.7 = (bf16[24,16,512]{2,1,0:T(8,128)(2,1)S(1)}, bf16[24,16,512]{2,1,0:T(8,128)(2,1)S(1)}, u32[]{:S(2)}, u32[]{:S(2)}) collective-permute-start(bf16[24,16,512]{2,1,0:T(8,128)(2,1)S(1)} %get-tuple-element.40.refs_1_.refs_9_), channel_id=1, source_target_pairs={{8,4},{9,5},{10,6},{11,7},{20,24},{21,25},{22,26},{23,27}} | collective-permute-start | bytes 1179656 | tf_op jit(solution)/shard_map/ppermute | solution.py:100
  20.1 10.5 %collective-permute-start.9 = (bf16[24,16,512]{2,1,0:T(8,128)(2,1)S(1)}, bf16[24,16,512]{2,1,0:T(8,128)(2,1)S(1)}, u32[]{:S(2)}, u32[]{:S(2)}) collective-permute-start(bf16[24,16,512]{2,1,0:T(8,128)(2,1)S(1)} %get-tuple-element.40.refs_1_.refs_9_), channel_id=1, source_target_pairs={{0,4},{1,5},{2,6},{3,7},{28,24},{29,25},{30,26},{31,27}} | collective-permute-start | bytes 1179656 | tf_op jit(solution)/shard_map/ppermute | solution.py:100
  23.3 7.9 %collective-permute-start.6 = (bf16[24,16,256]{2,1,0:T(8,128)(2,1)S(1)}, bf16[24,16,256]{2,1,0:T(8,128)(2,1)S(1)}, u32[]{:S(2)}, u32[]{:S(2)}) collective-permute-start(bf16[24,16,256]{2,1,0:T(8,128)(2,1)S(1)} %pad_maximum_fusion.refs_1_), channel_id=1, source_target_pairs={{8,4},{9,5},{10,6},{11,7},{12,20},{13,21},{14,22},{15,23},{16,8},{... | collective-permute-start | bytes 589832 | tf_op jit(solution)/shard_map/ppermute | solution.py:100
  24.0 9.2 %collective-permute-start.11 = (bf16[24,16,256]{2,1,0:T(8,128)(2,1)S(1)}, bf16[24,16,256]{2,1,0:T(8,128)(2,1)S(1)}, u32[]{:S(2)}, u32[]{:S(2)}) collective-permute-start(bf16[24,16,256]{2,1,0:T(8,128)(2,1)S(1)} %pad_maximum_fusion.refs_1_), channel_id=1, source_target_pairs={{0,4},{1,5},{2,6},{3,7},{28,24},{29,25},{30,26},{31,27}} | collective-permute-start | bytes 589832 | tf_op jit(solution)/shard_map/ppermute | solution.py:100
  31.2 2.0 %collective-permute-start.10 = (bf16[24,16,256]{2,1,0:T(8,128)(2,1)S(1)}, bf16[24,16,256]{2,1,0:T(8,128)(2,1)S(1)}, u32[]{:S(2)}, u32[]{:S(2)}) collective-permute-start(bf16[24,16,256]{2,1,0:T(8,128)(2,1)S(1)} %collective-permute-done.6.refs_2_), channel_id=1, source_target_pairs={{8,24},{9,25},{10,26},{11,27},{20,4},{21,5},{22,6},{23,7}} | collective-permute-start | bytes 589832 | tf_op jit(solution)/shard_map/ppermute | solution.py:100
  33.9 2.7 %collective-permute-start.12 = (bf16[24,16,256]{2,1,0:T(8,128)(2,1)S(1)}, bf16[24,16,256]{2,1,0:T(8,128)(2,1)S(1)}, u32[]{:S(2)}, u32[]{:S(2)}) collective-permute-start(bf16[24,16,256]{2,1,0:T(8,128)(2,1)S(1)} %get-tuple-element.56), channel_id=1, source_target_pairs={{4,12},{5,13},{6,14},{7,15},{24,16},{25,17},{26,18},{27,19}} | collective-permute-start | bytes 589832 | tf_op jit(solution)/shard_map/ppermute | solution.py:100
  34.6 16.7 %collective-permute-start.13 = (bf16[24,16,256]{2,1,0:T(8,128)(2,1)S(1)}, bf16[24,16,256]{2,1,0:T(8,128)(2,1)S(1)}, u32[]{:S(2)}, u32[]{:S(2)}) collective-permute-start(bf16[24,16,256]{2,1,0:T(8,128)(2,1)S(1)} %get-tuple-element.57), channel_id=1, source_target_pairs={{4,0},{5,1},{6,2},{7,3},{24,28},{25,29},{26,30},{27,31}} | collective-permute-start | bytes 589832 | tf_op jit(solution)/shard_map/ppermute | solution.py:100
  35.9 15.4 %collective-permute-start.14 = (bf16[24,16,256]{2,1,0:T(8,128)(2,1)S(1)}, bf16[24,16,256]{2,1,0:T(8,128)(2,1)S(1)}, u32[]{:S(2)}, u32[]{:S(2)}) collective-permute-start(bf16[24,16,256]{2,1,0:T(8,128)(2,1)S(1)} %get-tuple-element.58), channel_id=1, source_target_pairs={{4,8},{5,9},{6,10},{7,11},{24,20},{25,21},{26,22},{27,23}} | collective-permute-start | bytes 589832 | tf_op jit(solution)/shard_map/ppermute | solution.py:100

commit v8 on v7

--- a/solution.py
+++ b/solution.py
@@ -193,7 +193,7 @@
 
 def inner_body(layer, layers, place, *refs):
     first, last = layer == layers - 1, layer == 0
-    offset_ref, mains, refs = refs[0], refs[1:5], refs[5:]
+    offset_ref, mains, refs = refs[0], [refs[1 + k] for k in (3, 1, 0, 2)], refs[5:]
     carried, w_in, w_out, taps, refs = refs[0], refs[1], refs[2], refs[3], refs[4:]
     outs, refs = (refs[:4], refs[4:]) if last else (refs[:1], refs[1:])
     cg_edges, refs = refs[0], refs[1:]
@@ -258,7 +258,7 @@
     rows -= 2 * (layers - 1 - layer)
     smem = pl.BlockSpec(memory_space=pltpu.SMEM)
     vmem = pl.BlockSpec(memory_space=pltpu.VMEM)
-    args = [offsets, *mains, carried, w_in, w_out, taps]
+    args = [offsets, *(mains[k] for k in (2, 1, 3, 0)), carried, w_in, w_out, taps]
     if last:
         out = [jax.ShapeDtypeStruct((rows - 2, cells, chans), jnp.bfloat16)] * 4
     else:

time: 52.5 us -> 51.6 us (0.983)
  waiting for transfers between devices: 20.3 us -> 19.6 us
    ppermute x14, waiting for transfers between devices: 20.3 us -> 19.6 us  [routed(): return lax.ppermute(value, AXES, pairs)]
where the time goes in v8:
time: 51.6 us; the launch traced here: 51.3 us
  starting transfers between devices  26 us (50%)
  waiting for transfers between devices  19.6 us (38%)
  Pallas kernels  3.08 us (6%)
  local copies, waits for them, and re-layouts  2.18 us (4%)
    ppermute x14, starting transfers between devices, routed(): return lax.ppermute(value, AXES, pairs)  25.5 us
    ppermute x14, waiting for transfers between devices, routed(): return lax.ppermute(value, AXES, pairs)  19.6 us
    pallas_call x4, Pallas kernels, run_inner(): pl.pallas_call(functools.partial(inner_kernel, layer, layers, place), out...  2.24 us
    unnamed x12, local copies, waits for them, and re-layouts  1.45 us
  transfers between devices with their start and end apart: 15, of which 4 were waited for; matrix products, arithmetic and copies ran while one was open for 3% of the time, Pallas kernels for 4%

profile of v8, /device:TPU:0, one launch (start us, length us, event | category | flops | bytes accessed | tf_op | source)
XLA Modules:
  0.0 51.3 jit_solution(4236067625339395292)
XLA Ops:
  0.5 1.4 %copy.16 = bf16[1,4,16,24,256]{4,2,3,1,0:T(8,128)(2,1)S(1)} copy(bf16[1,4,16,24,256]{4,3,2,1,0:T(8,128)(2,1)} %param.8) | data formatting | bytes 1572864 | tf_op args[1]
  2.1 0.7 %collective-permute-start.3 = (bf16[24,16,640]{2,1,0:T(8,128)(2,1)S(1)}, bf16[24,16,640]{2,1,0:T(8,128)(2,1)S(1)}, u32[]{:S(2)}, u32[]{:S(2)}) collective-permute-start(bf16[24,16,640]{2,1,0:T(8,128)(2,1)S(1)} %get-tuple-element.37.refs_4_.refs_5_), channel_id=1, source_target_pairs={{12,4},{13,5},{14,6},{15,7},{16,24},{17,25},{18,26},{19,27}} | collective-permute-start | bytes 1474568 | tf_op jit(solution)/shard_map/ppermute | solution.py:100
  2.8 0.7 %collective-permute-start.4 = (bf16[24,16,640]{2,1,0:T(8,128)(2,1)S(1)}, bf16[24,16,640]{2,1,0:T(8,128)(2,1)S(1)}, u32[]{:S(2)}, u32[]{:S(2)}) collective-permute-start(bf16[24,16,640]{2,1,0:T(8,128)(2,1)S(1)} %get-tuple-element.37.refs_4_.refs_5_), channel_id=1, source_target_pairs={{8,4},{9,5},{10,6},{11,7},{20,24},{21,25},{22,26},{23,27}} | collective-permute-start | bytes 1474568 | tf_op jit(solution)/shard_map/ppermute | solution.py:100
  3.5 5.8 %collective-permute-start.5 = (bf16[24,16,640]{2,1,0:T(8,128)(2,1)S(1)}, bf16[24,16,640]{2,1,0:T(8,128)(2,1)S(1)}, u32[]{:S(2)}, u32[]{:S(2)}) collective-permute-start(bf16[24,16,640]{2,1,0:T(8,128)(2,1)S(1)} %get-tuple-element.37.refs_4_.refs_5_), channel_id=1, source_target_pairs={{0,4},{1,5},{2,6},{3,7},{28,24},{29,25},{30,26},{31,27}} | collective-permute-start | bytes 1474568 | tf_op jit(solution)/shard_map/ppermute | solution.py:100
  9.3 3.4 %collective-permute-start.1 = (bf16[12,16,256]{2,1,0:T(8,128)(2,1)S(1)}, bf16[12,16,256]{2,1,0:T(8,128)(2,1)S(1)}, u32[]{:S(2)}, u32[]{:S(2)}) collective-permute-start(bf16[12,16,256]{2,1,0:T(8,128)(2,1)S(1)} %get-tuple-element.33), channel_id=1, source_target_pairs={{0,1},{1,2},{2,3},{4,5},{5,6},{6,7},{8,9},{9,10},{10,11},{12,13},{... | collective-permute-start | bytes 294920 | tf_op jit(solution)/shard_map/ppermute | solution.py:100
  12.7 1.3 %collective-permute-start.2 = (bf16[12,16,256]{2,1,0:T(8,128)(2,1)S(1)}, bf16[12,16,256]{2,1,0:T(8,128)(2,1)S(1)}, u32[]{:S(2)}, u32[]{:S(2)}) collective-permute-start(bf16[12,16,256]{2,1,0:T(8,128)(2,1)S(1)} %get-tuple-element.34), channel_id=1, source_target_pairs={{1,0},{2,1},{3,2},{5,4},{6,5},{7,6},{9,8},{10,9},{11,10},{13,12},{... | collective-permute-start | bytes 294920 | tf_op jit(solution)/shard_map/ppermute | solution.py:100
  14.0 0.9 %collective-permute-done.1 = bf16[12,16,256]{2,1,0:T(8,128)(2,1)S(1)} collective-permute-done((bf16[12,16,256]{2,1,0:T(8,128)(2,1)S(1)}, bf16[12,16,256]{2,1,0:T(8,128)(2,1)S(1)}, u32[]{:S(2)}, u32[]{:S(2)}) %collective-permute-start.1) | collective-permute-done | bytes 98336 | tf_op jit(solution)/shard_map/ppermute | solution.py:100
  14.9 0.7 %collective-permute-start.7 = (bf16[24,16,512]{2,1,0:T(8,128)(2,1)S(1)}, bf16[24,16,512]{2,1,0:T(8,128)(2,1)S(1)}, u32[]{:S(2)}, u32[]{:S(2)}) collective-permute-start(bf16[24,16,512]{2,1,0:T(8,128)(2,1)S(1)} %get-tuple-element.40.refs_4_.refs_9_), channel_id=1, source_target_pairs={{12,4},{13,5},{14,6},{15,7},{16,24},{17,25},{18,26},{19,27}} | collective-permute-start | bytes 1179656 | tf_op jit(solution)/shard_map/ppermute | solution.py:100
  15.6 3.6 %collective-permute-done.2 = bf16[12,16,256]{2,1,0:T(8,128)(2,1)S(1)} collective-permute-done((bf16[12,16,256]{2,1,0:T(8,128)(2,1)S(1)}, bf16[12,16,256]{2,1,0:T(8,128)(2,1)S(1)}, u32[]{:S(2)}, u32[]{:S(2)}) %collective-permute-start.2) | collective-permute-done | bytes 98336 | tf_op jit(solution)/shard_map/ppermute | solution.py:100
  19.2 0.7 %collective-permute-start.8 = (bf16[24,16,512]{2,1,0:T(8,128)(2,1)S(1)}, bf16[24,16,512]{2,1,0:T(8,128)(2,1)S(1)}, u32[]{:S(2)}, u32[]{:S(2)}) collective-permute-start(bf16[24,16,512]{2,1,0:T(8,128)(2,1)S(1)} %get-tuple-element.40.refs_4_.refs_9_), channel_id=1, source_target_pairs={{8,4},{9,5},{10,6},{11,7},{20,24},{21,25},{22,26},{23,27}} | collective-permute-start | bytes 1179656 | tf_op jit(solution)/shard_map/ppermute | solution.py:100
  19.9 2.6 %collective-permute-start.9 = (bf16[24,16,512]{2,1,0:T(8,128)(2,1)S(1)}, bf16[24,16,512]{2,1,0:T(8,128)(2,1)S(1)}, u32[]{:S(2)}, u32[]{:S(2)}) collective-permute-start(bf16[24,16,512]{2,1,0:T(8,128)(2,1)S(1)} %get-tuple-element.40.refs_4_.refs_9_), channel_id=1, source_target_pairs={{0,4},{1,5},{2,6},{3,7},{28,24},{29,25},{30,26},{31,27}} | collective-permute-start | bytes 1179656 | tf_op jit(solution)/shard_map/ppermute | solution.py:100
  22.7 0.6 %inner_3.1 = (f32[22,64,256]{2,1,0:T(8,128)S(1)}, f32[4,64,256]{2,1,0:T(8,128)S(1)}, f32[2,64,256]{2,1,0:T(8,128)S(1)}) custom-call(s32[4]{0:T(128)S(1)} %copy-done.3, bf16[24,16,640]{2,1,0:T(8,128)(2,1)S(1)} %collective-permute-done.3.refs_1_.refs_7_, bf16[24,16,640]{2,1,0:T(8,128)(2,1)S(1)} %collective-permute-done.4.refs_2_.refs_6_, ...), custom_call_target="tpu_custom_call" | custom-call | flops 1207959552 | bytes 3932160 | tf_op jit(solution)/shard_map/inner_3/pallas_call | solution.py:272
  23.2 0.7 %collective-permute-start.6 = (bf16[24,16,256]{2,1,0:T(8,128)(2,1)S(1)}, bf16[24,16,256]{2,1,0:T(8,128)(2,1)S(1)}, u32[]{:S(2)}, u32[]{:S(2)}) collective-permute-start(bf16[24,16,256]{2,1,0:T(8,128)(2,1)S(1)} %pad_maximum_fusion.refs_1_), channel_id=1, source_target_pairs={{8,4},{9,5},{10,6},{11,7},{12,20},{13,21},{14,22},{15,23},{16,8},{... | collective-permute-start | bytes 589832 | tf_op jit(solution)/shard_map/ppermute | solution.py:100
  23.9 5.7 %collective-permute-start.11 = (bf16[24,16,256]{2,1,0:T(8,128)(2,1)S(1)}, bf16[24,16,256]{2,1,0:T(8,128)(2,1)S(1)}, u32[]{:S(2)}, u32[]{:S(2)}) collective-permute-start(bf16[24,16,256]{2,1,0:T(8,128)(2,1)S(1)} %pad_maximum_fusion.refs_1_), channel_id=1, source_target_pairs={{0,4},{1,5},{2,6},{3,7},{28,24},{29,25},{30,26},{31,27}} | collective-permute-start | bytes 589832 | tf_op jit(solution)/shard_map/ppermute | solution.py:100
  29.6 0.6 %inner_2.1 = (f32[20,64,256]{2,1,0:T(8,128)S(1)}, f32[4,64,256]{2,1,0:T(8,128)S(1)}) custom-call(s32[4]{0:T(128)S(1)} %copy-done.3, bf16[24,16,640]{2,1,0:T(8,128)(2,1)S(1)} %collective-permute-done.3.refs_1_.refs_7_, bf16[24,16,640]{2,1,0:T(8,128)(2,1)S(1)} %collective-permute-done.4.refs_2_.refs_6_, ...), custom_call_target="tpu_custom_call" | custom-call | flops 1107296256 | bytes 3604480 | tf_op jit(solution)/shard_map/inner_2/pallas_call | solution.py:272
  30.8 0.7 %collective-permute-start.10 = (bf16[24,16,256]{2,1,0:T(8,128)(2,1)S(1)}, bf16[24,16,256]{2,1,0:T(8,128)(2,1)S(1)}, u32[]{:S(2)}, u32[]{:S(2)}) collective-permute-start(bf16[24,16,256]{2,1,0:T(8,128)(2,1)S(1)} %collective-permute-done.6.refs_2_), channel_id=1, source_target_pairs={{8,24},{9,25},{10,26},{11,27},{20,4},{21,5},{22,6},{23,7}} | collective-permute-start | bytes 589832 | tf_op jit(solution)/shard_map/ppermute | solution.py:100
  31.4 0.6 %inner_0.1 = (bf16[16,16,256]{2,1,0:T(8,128)(2,1)S(1)}, bf16[16,16,256]{2,1,0:T(8,128)(2,1)S(1)}, bf16[16,16,256]{2,1,0:T(8,128)(2,1)S(1)}, bf16[16,16,256]{2,1,0:T(8,128)(2,1)S(1)}, f32[4,64,256]{2,1,0:T(8,128)S(1)}) custom-call(s32[4]{0:T(128)S(1)} %copy-done.3, bf16[24,16,512]{2,1,0:T(8,128)(2,1)S(1)} %collective-permute-done.7.refs_1_.refs_11_, ...), custom_call_target="tpu_custom_call" | custom-call | flops 905969664 | bytes 2949120 | tf_op jit(solution)/shard_map/inner_0/pallas_call | solution.py:272
  32.0 0.7 %collective-permute-done.11.refs_4_ = bf16[24,16,256]{2,1,0:T(8,128)(2,1)S(1)} collective-permute-done((bf16[24,16,256]{2,1,0:T(8,128)(2,1)S(1)}, bf16[24,16,256]{2,1,0:T(8,128)(2,1)S(1)}, u32[]{:S(2)}, u32[]{:S(2)}) %collective-permute-start.11) | collective-permute-done | bytes 196640 | tf_op jit(solution)/shard_map/ppermute | solution.py:100
  32.8 0.7 %outer.1 = (bf16[24,16,256]{2,1,0:T(8,128)(2,1)S(1)}, bf16[24,16,256]{2,1,0:T(8,128)(2,1)S(1)}, bf16[24,16,256]{2,1,0:T(8,128)(2,1)S(1)}, bf16[24,16,256]{2,1,0:T(8,128)(2,1)S(1)}) custom-call(s32[4]{0:T(128)S(1)} %copy-done.3, bf16[24,16,256]{2,1,0:T(8,128)(2,1)S(1)} %pad_maximum_fusion.refs_1_, bf16[24,16,256]{2,1,0:T(8,128)(2,1)S(1)} %collective-permute-done.6.refs_2_, ...), custom_call_target="tpu_custom_call" | custom-call | flops 1610612736 | bytes 5242880 | tf_op jit(solution)/shard_map/outer/pallas_call | solution.py:385
  33.5 0.7 %collective-permute-start.12 = (bf16[24,16,256]{2,1,0:T(8,128)(2,1)S(1)}, bf16[24,16,256]{2,1,0:T(8,128)(2,1)S(1)}, u32[]{:S(2)}, u32[]{:S(2)}) collective-permute-start(bf16[24,16,256]{2,1,0:T(8,128)(2,1)S(1)} %get-tuple-element.56), channel_id=1, source_target_pairs={{4,12},{5,13},{6,14},{7,15},{24,16},{25,17},{26,18},{27,19}} | collective-permute-start | bytes 589832 | tf_op jit(solution)/shard_map/ppermute | solution.py:100
  34.2 1.3 %collective-permute-start.13 = (bf16[24,16,256]{2,1,0:T(8,128)(2,1)S(1)}, bf16[24,16,256]{2,1,0:T(8,128)(2,1)S(1)}, u32[]{:S(2)}, u32[]{:S(2)}) collective-permute-start(bf16[24,16,256]{2,1,0:T(8,128)(2,1)S(1)} %get-tuple-element.57), channel_id=1, source_target_pairs={{4,0},{5,1},{6,2},{7,3},{24,28},{25,29},{26,30},{27,31}} | collective-permute-start | bytes 589832 | tf_op jit(solution)/shard_map/ppermute | solution.py:100
  35.5 0.7 %collective-permute-start.14 = (bf16[24,16,256]{2,1,0:T(8,128)(2,1)S(1)}, bf16[24,16,256]{2,1,0:T(8,128)(2,1)S(1)}, u32[]{:S(2)}, u32[]{:S(2)}) collective-permute-start(bf16[24,16,256]{2,1,0:T(8,128)(2,1)S(1)} %get-tuple-element.58), channel_id=1, source_target_pairs={{4,8},{5,9},{6,10},{7,11},{24,20},{25,21},{26,22},{27,23}} | collective-permute-start | bytes 589832 | tf_op jit(solution)/shard_map/ppermute | solution.py:100
  36.2 14.3 %collective-permute-done.13 = bf16[24,16,256]{2,1,0:T(8,128)(2,1)S(1)} collective-permute-done((bf16[24,16,256]{2,1,0:T(8,128)(2,1)S(1)}, bf16[24,16,256]{2,1,0:T(8,128)(2,1)S(1)}, u32[]{:S(2)}, u32[]{:S(2)}) %collective-permute-start.13) | collective-permute-done | bytes 196640 | tf_op jit(solution)/shard_map/ppermute | solution.py:100
  50.6 0.7 %copy.14 = bf16[1,16,24,256]{3,2,1,0:T(8,128)(2,1)} copy(bf16[1,16,24,256]{3,1,2,0:T(8,128)(2,1)S(1)} %add_bitcast_fusion) | data formatting | bytes 393216 | tf_op jit(solution)/shard_map/broadcast_in_dim | solution.py:479
  (27 shorter events, 1.3 us)
Async XLA Ops:
  0.0 22.5 %copy-start.4 = (f32[4,5,256]{2,0,1:T(4,128)S(1)}, f32[4,5,256]{2,0,1:T(4,128)}, u32[]{:S(2)}) copy-start(f32[4,5,256]{2,0,1:T(4,128)} %param.12) | copy-start | bytes 61444
  0.0 22.6 %copy-start = (bf16[4,256,512]{2,1,0:T(8,128)(2,1)S(1)}, bf16[4,256,512]{2,1,0:T(8,128)(2,1)}, u32[]{:S(2)}) copy-start(bf16[4,256,512]{2,1,0:T(8,128)(2,1)} %refs_26_.1) | copy-start | bytes 3145732
  0.0 22.6 %copy-start.1 = (bf16[4,512,256]{2,1,0:T(8,128)(2,1)S(1)}, bf16[4,512,256]{2,1,0:T(8,128)(2,1)}, u32[]{:S(2)}) copy-start(bf16[4,512,256]{2,1,0:T(8,128)(2,1)} %refs_27_.1) | copy-start | bytes 3145732
  0.0 22.6 %copy-start.2 = (bf16[256,128]{1,0:T(8,128)(2,1)S(1)}, bf16[256,128]{1,0:T(8,128)(2,1)}, u32[]{:S(2)}) copy-start(bf16[256,128]{1,0:T(8,128)(2,1)} %refs_25_.1) | copy-start | bytes 196612
  0.0 22.6 %copy-start.3 = (s32[4]{0:T(128)S(1)}, s32[4]{0:T(128)}, u32[]{:S(2)}) copy-start(s32[4]{0:T(128)} %refs_0_.9) | copy-start | bytes 52
  0.0 2.0 %collective-permute-start = (bf16[16,24,128]{2,1,0:T(8,128)(2,1)}, bf16[16,24,128]{2,1,0:T(8,128)(2,1)S(1)}, u32[]{:S(2)}, u32[]{:S(2)}) collective-permute-start(bf16[16,24,128]{2,1,0:T(8,128)(2,1)} %bitcast.11), channel_id=1, source_target_pairs={{0,16},{16,0},{1,17},{17,1},{2,18},{18,2},{3,19},{19,3},{4,20},{20... | collective-permute-start | bytes 294920 | tf_op jit(solution)/shard_map/ppermute | solution.py:38
  2.1 17.8 %collective-permute-start.3 = (bf16[24,16,640]{2,1,0:T(8,128)(2,1)S(1)}, bf16[24,16,640]{2,1,0:T(8,128)(2,1)S(1)}, u32[]{:S(2)}, u32[]{:S(2)}) collective-permute-start(bf16[24,16,640]{2,1,0:T(8,128)(2,1)S(1)} %get-tuple-element.37.refs_4_.refs_5_), channel_id=1, source_target_pairs={{12,4},{13,5},{14,6},{15,7},{16,24},{17,25},{18,26},{19,27}} | collective-permute-start | bytes 1474568 | tf_op jit(solution)/shard_map/ppermute | solution.py:100
  2.8 19.8 %collective-permute-start.4 = (bf16[24,16,640]{2,1,0:T(8,128)(2,1)S(1)}, bf16[24,16,640]{2,1,0:T(8,128)(2,1)S(1)}, u32[]{:S(2)}, u32[]{:S(2)}) collective-permute-start(bf16[24,16,640]{2,1,0:T(8,128)(2,1)S(1)} %get-tuple-element.37.refs_4_.refs_5_), channel_id=1, source_target_pairs={{8,4},{9,5},{10,6},{11,7},{20,24},{21,25},{22,26},{23,27}} | collective-permute-start | bytes 1474568 | tf_op jit(solution)/shard_map/ppermute | solution.py:100
  3.5 19.1 %collective-permute-start.5 = (bf16[24,16,640]{2,1,0:T(8,128)(2,1)S(1)}, bf16[24,16,640]{2,1,0:T(8,128)(2,1)S(1)}, u32[]{:S(2)}, u32[]{:S(2)}) collective-permute-start(bf16[24,16,640]{2,1,0:T(8,128)(2,1)S(1)} %get-tuple-element.37.refs_4_.refs_5_), channel_id=1, source_target_pairs={{0,4},{1,5},{2,6},{3,7},{28,24},{29,25},{30,26},{31,27}} | collective-permute-start | bytes 1474568 | tf_op jit(solution)/shard_map/ppermute | solution.py:100
  9.3 5.6 %collective-permute-start.1 = (bf16[12,16,256]{2,1,0:T(8,128)(2,1)S(1)}, bf16[12,16,256]{2,1,0:T(8,128)(2,1)S(1)}, u32[]{:S(2)}, u32[]{:S(2)}) collective-permute-start(bf16[12,16,256]{2,1,0:T(8,128)(2,1)S(1)} %get-tuple-element.33), channel_id=1, source_target_pairs={{0,1},{1,2},{2,3},{4,5},{5,6},{6,7},{8,9},{9,10},{10,11},{12,13},{... | collective-permute-start | bytes 294920 | tf_op jit(solution)/shard_map/ppermute | solution.py:100
  12.7 6.5 %collective-permute-start.2 = (bf16[12,16,256]{2,1,0:T(8,128)(2,1)S(1)}, bf16[12,16,256]{2,1,0:T(8,128)(2,1)S(1)}, u32[]{:S(2)}, u32[]{:S(2)}) collective-permute-start(bf16[12,16,256]{2,1,0:T(8,128)(2,1)S(1)} %get-tuple-element.34), channel_id=1, source_target_pairs={{1,0},{2,1},{3,2},{5,4},{6,5},{7,6},{9,8},{10,9},{11,10},{13,12},{... | collective-permute-start | bytes 294920 | tf_op jit(solution)/shard_map/ppermute | solution.py:100
  14.9 15.3 %collective-permute-start.7 = (bf16[24,16,512]{2,1,0:T(8,128)(2,1)S(1)}, bf16[24,16,512]{2,1,0:T(8,128)(2,1)S(1)}, u32[]{:S(2)}, u32[]{:S(2)}) collective-permute-start(bf16[24,16,512]{2,1,0:T(8,128)(2,1)S(1)} %get-tuple-element.40.refs_4_.refs_9_), channel_id=1, source_target_pairs={{12,4},{13,5},{14,6},{15,7},{16,24},{17,25},{18,26},{19,27}} | collective-permute-start | bytes 1179656 | tf_op jit(solution)/shard_map/ppermute | solution.py:100
  19.2 11.0 %collective-permute-start.8 = (bf16[24,16,512]{2,1,0:T(8,128)(2,1)S(1)}, bf16[24,16,512]{2,1,0:T(8,128)(2,1)S(1)}, u32[]{:S(2)}, u32[]{:S(2)}) collective-permute-start(bf16[24,16,512]{2,1,0:T(8,128)(2,1)S(1)} %get-tuple-element.40.refs_4_.refs_9_), channel_id=1, source_target_pairs={{8,4},{9,5},{10,6},{11,7},{20,24},{21,25},{22,26},{23,27}} | collective-permute-start | bytes 1179656 | tf_op jit(solution)/shard_map/ppermute | solution.py:100
  19.9 10.3 %collective-permute-start.9 = (bf16[24,16,512]{2,1,0:T(8,128)(2,1)S(1)}, bf16[24,16,512]{2,1,0:T(8,128)(2,1)S(1)}, u32[]{:S(2)}, u32[]{:S(2)}) collective-permute-start(bf16[24,16,512]{2,1,0:T(8,128)(2,1)S(1)} %get-tuple-element.40.refs_4_.refs_9_), channel_id=1, source_target_pairs={{0,4},{1,5},{2,6},{3,7},{28,24},{29,25},{30,26},{31,27}} | collective-permute-start | bytes 1179656 | tf_op jit(solution)/shard_map/ppermute | solution.py:100
  23.2 7.5 %collective-permute-start.6 = (bf16[24,16,256]{2,1,0:T(8,128)(2,1)S(1)}, bf16[24,16,256]{2,1,0:T(8,128)(2,1)S(1)}, u32[]{:S(2)}, u32[]{:S(2)}) collective-permute-start(bf16[24,16,256]{2,1,0:T(8,128)(2,1)S(1)} %pad_maximum_fusion.refs_1_), channel_id=1, source_target_pairs={{8,4},{9,5},{10,6},{11,7},{12,20},{13,21},{14,22},{15,23},{16,8},{... | collective-permute-start | bytes 589832 | tf_op jit(solution)/shard_map/ppermute | solution.py:100
  23.9 8.8 %collective-permute-start.11 = (bf16[24,16,256]{2,1,0:T(8,128)(2,1)S(1)}, bf16[24,16,256]{2,1,0:T(8,128)(2,1)S(1)}, u32[]{:S(2)}, u32[]{:S(2)}) collective-permute-start(bf16[24,16,256]{2,1,0:T(8,128)(2,1)S(1)} %pad_maximum_fusion.refs_1_), channel_id=1, source_target_pairs={{0,4},{1,5},{2,6},{3,7},{28,24},{29,25},{30,26},{31,27}} | collective-permute-start | bytes 589832 | tf_op jit(solution)/shard_map/ppermute | solution.py:100
  30.8 2.0 %collective-permute-start.10 = (bf16[24,16,256]{2,1,0:T(8,128)(2,1)S(1)}, bf16[24,16,256]{2,1,0:T(8,128)(2,1)S(1)}, u32[]{:S(2)}, u32[]{:S(2)}) collective-permute-start(bf16[24,16,256]{2,1,0:T(8,128)(2,1)S(1)} %collective-permute-done.6.refs_2_), channel_id=1, source_target_pairs={{8,24},{9,25},{10,26},{11,27},{20,4},{21,5},{22,6},{23,7}} | collective-permute-start | bytes 589832 | tf_op jit(solution)/shard_map/ppermute | solution.py:100
  33.5 2.7 %collective-permute-start.12 = (bf16[24,16,256]{2,1,0:T(8,128)(2,1)S(1)}, bf16[24,16,256]{2,1,0:T(8,128)(2,1)S(1)}, u32[]{:S(2)}, u32[]{:S(2)}) collective-permute-start(bf16[24,16,256]{2,1,0:T(8,128)(2,1)S(1)} %get-tuple-element.56), channel_id=1, source_target_pairs={{4,12},{5,13},{6,14},{7,15},{24,16},{25,17},{26,18},{27,19}} | collective-permute-start | bytes 589832 | tf_op jit(solution)/shard_map/ppermute | solution.py:100
  34.2 16.3 %collective-permute-start.13 = (bf16[24,16,256]{2,1,0:T(8,128)(2,1)S(1)}, bf16[24,16,256]{2,1,0:T(8,128)(2,1)S(1)}, u32[]{:S(2)}, u32[]{:S(2)}) collective-permute-start(bf16[24,16,256]{2,1,0:T(8,128)(2,1)S(1)} %get-tuple-element.57), channel_id=1, source_target_pairs={{4,0},{5,1},{6,2},{7,3},{24,28},{25,29},{26,30},{27,31}} | collective-permute-start | bytes 589832 | tf_op jit(solution)/shard_map/ppermute | solution.py:100
  35.5 15.0 %collective-permute-start.14 = (bf16[24,16,256]{2,1,0:T(8,128)(2,1)S(1)}, bf16[24,16,256]{2,1,0:T(8,128)(2,1)S(1)}, u32[]{:S(2)}, u32[]{:S(2)}) collective-permute-start(bf16[24,16,256]{2,1,0:T(8,128)(2,1)S(1)} %get-tuple-element.58), channel_id=1, source_target_pairs={{4,8},{5,9},{6,10},{7,11},{24,20},{25,21},{26,22},{27,23}} | collective-permute-start | bytes 589832 | tf_op jit(solution)/shard_map/ppermute | solution.py:100

commit v9 on v8

--- a/solution.py
+++ b/solution.py
@@ -101,7 +101,7 @@
 
 
 def row_chunks(low, high):
-    count = max(1, round((high - low) / 7))
+    count = max(1, round((high - low) / 11))
     edges = [low + (high - low) * i // count for i in range(count + 1)]
     return list(zip(edges[:-1], edges[1:]))
 

time: 51.6 us -> 51.7 us (level)
  no operation moved by 1% of the time
where the time goes in v9:
time: 51.7 us; the launch traced here: 51.4 us
  starting transfers between devices  26.2 us (51%)
  waiting for transfers between devices  19.6 us (38%)
  Pallas kernels  3.08 us (6%)
  local copies, waits for them, and re-layouts  2.18 us (4%)
    ppermute x14, starting transfers between devices, routed(): return lax.ppermute(value, AXES, pairs)  25.6 us
    ppermute x14, waiting for transfers between devices, routed(): return lax.ppermute(value, AXES, pairs)  19.6 us
    pallas_call x4, Pallas kernels, run_inner(): pl.pallas_call(functools.partial(inner_kernel, layer, layers, place), out...  2.24 us
    unnamed x12, local copies, waits for them, and re-layouts  1.45 us
  transfers between devices with their start and end apart: 15, of which 4 were waited for; matrix products, arithmetic and copies ran while one was open for 3% of the time, Pallas kernels for 4%

profile of v9, /device:TPU:0, one launch (start us, length us, event | category | flops | bytes accessed | tf_op | source)
XLA Modules:
  0.0 51.4 jit_solution(4402014079625999611)
XLA Ops:
  0.5 1.4 %copy.16 = bf16[1,4,16,24,256]{4,2,3,1,0:T(8,128)(2,1)S(1)} copy(bf16[1,4,16,24,256]{4,3,2,1,0:T(8,128)(2,1)} %param.8) | data formatting | bytes 1572864 | tf_op args[1]
  2.1 0.7 %collective-permute-start.3 = (bf16[24,16,640]{2,1,0:T(8,128)(2,1)S(1)}, bf16[24,16,640]{2,1,0:T(8,128)(2,1)S(1)}, u32[]{:S(2)}, u32[]{:S(2)}) collective-permute-start(bf16[24,16,640]{2,1,0:T(8,128)(2,1)S(1)} %get-tuple-element.37.refs_4_.refs_5_), channel_id=1, source_target_pairs={{12,4},{13,5},{14,6},{15,7},{16,24},{17,25},{18,26},{19,27}} | collective-permute-start | bytes 1474568 | tf_op jit(solution)/shard_map/ppermute | solution.py:100
  2.8 0.7 %collective-permute-start.4 = (bf16[24,16,640]{2,1,0:T(8,128)(2,1)S(1)}, bf16[24,16,640]{2,1,0:T(8,128)(2,1)S(1)}, u32[]{:S(2)}, u32[]{:S(2)}) collective-permute-start(bf16[24,16,640]{2,1,0:T(8,128)(2,1)S(1)} %get-tuple-element.37.refs_4_.refs_5_), channel_id=1, source_target_pairs={{8,4},{9,5},{10,6},{11,7},{20,24},{21,25},{22,26},{23,27}} | collective-permute-start | bytes 1474568 | tf_op jit(solution)/shard_map/ppermute | solution.py:100
  3.5 5.8 %collective-permute-start.5 = (bf16[24,16,640]{2,1,0:T(8,128)(2,1)S(1)}, bf16[24,16,640]{2,1,0:T(8,128)(2,1)S(1)}, u32[]{:S(2)}, u32[]{:S(2)}) collective-permute-start(bf16[24,16,640]{2,1,0:T(8,128)(2,1)S(1)} %get-tuple-element.37.refs_4_.refs_5_), channel_id=1, source_target_pairs={{0,4},{1,5},{2,6},{3,7},{28,24},{29,25},{30,26},{31,27}} | collective-permute-start | bytes 1474568 | tf_op jit(solution)/shard_map/ppermute | solution.py:100
  9.3 3.4 %collective-permute-start.1 = (bf16[12,16,256]{2,1,0:T(8,128)(2,1)S(1)}, bf16[12,16,256]{2,1,0:T(8,128)(2,1)S(1)}, u32[]{:S(2)}, u32[]{:S(2)}) collective-permute-start(bf16[12,16,256]{2,1,0:T(8,128)(2,1)S(1)} %get-tuple-element.33), channel_id=1, source_target_pairs={{0,1},{1,2},{2,3},{4,5},{5,6},{6,7},{8,9},{9,10},{10,11},{12,13},{... | collective-permute-start | bytes 294920 | tf_op jit(solution)/shard_map/ppermute | solution.py:100
  12.7 1.3 %collective-permute-start.2 = (bf16[12,16,256]{2,1,0:T(8,128)(2,1)S(1)}, bf16[12,16,256]{2,1,0:T(8,128)(2,1)S(1)}, u32[]{:S(2)}, u32[]{:S(2)}) collective-permute-start(bf16[12,16,256]{2,1,0:T(8,128)(2,1)S(1)} %get-tuple-element.34), channel_id=1, source_target_pairs={{1,0},{2,1},{3,2},{5,4},{6,5},{7,6},{9,8},{10,9},{11,10},{13,12},{... | collective-permute-start | bytes 294920 | tf_op jit(solution)/shard_map/ppermute | solution.py:100
  14.0 0.9 %collective-permute-done.1 = bf16[12,16,256]{2,1,0:T(8,128)(2,1)S(1)} collective-permute-done((bf16[12,16,256]{2,1,0:T(8,128)(2,1)S(1)}, bf16[12,16,256]{2,1,0:T(8,128)(2,1)S(1)}, u32[]{:S(2)}, u32[]{:S(2)}) %collective-permute-start.1) | collective-permute-done | bytes 98336 | tf_op jit(solution)/shard_map/ppermute | solution.py:100
  14.9 0.7 %collective-permute-start.7 = (bf16[24,16,512]{2,1,0:T(8,128)(2,1)S(1)}, bf16[24,16,512]{2,1,0:T(8,128)(2,1)S(1)}, u32[]{:S(2)}, u32[]{:S(2)}) collective-permute-start(bf16[24,16,512]{2,1,0:T(8,128)(2,1)S(1)} %get-tuple-element.40.refs_4_.refs_9_), channel_id=1, source_target_pairs={{12,4},{13,5},{14,6},{15,7},{16,24},{17,25},{18,26},{19,27}} | collective-permute-start | bytes 1179656 | tf_op jit(solution)/shard_map/ppermute | solution.py:100
  15.6 3.6 %collective-permute-done.2 = bf16[12,16,256]{2,1,0:T(8,128)(2,1)S(1)} collective-permute-done((bf16[12,16,256]{2,1,0:T(8,128)(2,1)S(1)}, bf16[12,16,256]{2,1,0:T(8,128)(2,1)S(1)}, u32[]{:S(2)}, u32[]{:S(2)}) %collective-permute-start.2) | collective-permute-done | bytes 98336 | tf_op jit(solution)/shard_map/ppermute | solution.py:100
  19.2 0.7 %collective-permute-start.8 = (bf16[24,16,512]{2,1,0:T(8,128)(2,1)S(1)}, bf16[24,16,512]{2,1,0:T(8,128)(2,1)S(1)}, u32[]{:S(2)}, u32[]{:S(2)}) collective-permute-start(bf16[24,16,512]{2,1,0:T(8,128)(2,1)S(1)} %get-tuple-element.40.refs_4_.refs_9_), channel_id=1, source_target_pairs={{8,4},{9,5},{10,6},{11,7},{20,24},{21,25},{22,26},{23,27}} | collective-permute-start | bytes 1179656 | tf_op jit(solution)/shard_map/ppermute | solution.py:100
  19.9 2.6 %collective-permute-start.9 = (bf16[24,16,512]{2,1,0:T(8,128)(2,1)S(1)}, bf16[24,16,512]{2,1,0:T(8,128)(2,1)S(1)}, u32[]{:S(2)}, u32[]{:S(2)}) collective-permute-start(bf16[24,16,512]{2,1,0:T(8,128)(2,1)S(1)} %get-tuple-element.40.refs_4_.refs_9_), channel_id=1, source_target_pairs={{0,4},{1,5},{2,6},{3,7},{28,24},{29,25},{30,26},{31,27}} | collective-permute-start | bytes 1179656 | tf_op jit(solution)/shard_map/ppermute | solution.py:100
  22.7 0.6 %inner_3.1 = (f32[22,64,256]{2,1,0:T(8,128)S(1)}, f32[4,64,256]{2,1,0:T(8,128)S(1)}, f32[2,64,256]{2,1,0:T(8,128)S(1)}) custom-call(s32[4]{0:T(128)S(1)} %copy-done.3, bf16[24,16,640]{2,1,0:T(8,128)(2,1)S(1)} %collective-permute-done.3.refs_1_.refs_7_, bf16[24,16,640]{2,1,0:T(8,128)(2,1)S(1)} %collective-permute-done.4.refs_2_.refs_6_, ...), custom_call_target="tpu_custom_call" | custom-call | flops 1207959552 | bytes 3932160 | tf_op jit(solution)/shard_map/inner_3/pallas_call | solution.py:272
  23.2 0.7 %collective-permute-start.6 = (bf16[24,16,256]{2,1,0:T(8,128)(2,1)S(1)}, bf16[24,16,256]{2,1,0:T(8,128)(2,1)S(1)}, u32[]{:S(2)}, u32[]{:S(2)}) collective-permute-start(bf16[24,16,256]{2,1,0:T(8,128)(2,1)S(1)} %pad_maximum_fusion.refs_1_), channel_id=1, source_target_pairs={{8,4},{9,5},{10,6},{11,7},{12,20},{13,21},{14,22},{15,23},{16,8},{... | collective-permute-start | bytes 589832 | tf_op jit(solution)/shard_map/ppermute | solution.py:100
  23.9 5.8 %collective-permute-start.11 = (bf16[24,16,256]{2,1,0:T(8,128)(2,1)S(1)}, bf16[24,16,256]{2,1,0:T(8,128)(2,1)S(1)}, u32[]{:S(2)}, u32[]{:S(2)}) collective-permute-start(bf16[24,16,256]{2,1,0:T(8,128)(2,1)S(1)} %pad_maximum_fusion.refs_1_), channel_id=1, source_target_pairs={{0,4},{1,5},{2,6},{3,7},{28,24},{29,25},{30,26},{31,27}} | collective-permute-start | bytes 589832 | tf_op jit(solution)/shard_map/ppermute | solution.py:100
  29.7 0.6 %inner_2.1 = (f32[20,64,256]{2,1,0:T(8,128)S(1)}, f32[4,64,256]{2,1,0:T(8,128)S(1)}) custom-call(s32[4]{0:T(128)S(1)} %copy-done.3, bf16[24,16,640]{2,1,0:T(8,128)(2,1)S(1)} %collective-permute-done.3.refs_1_.refs_7_, bf16[24,16,640]{2,1,0:T(8,128)(2,1)S(1)} %collective-permute-done.4.refs_2_.refs_6_, ...), custom_call_target="tpu_custom_call" | custom-call | flops 1107296256 | bytes 3604480 | tf_op jit(solution)/shard_map/inner_2/pallas_call | solution.py:272
  30.9 0.7 %collective-permute-start.10 = (bf16[24,16,256]{2,1,0:T(8,128)(2,1)S(1)}, bf16[24,16,256]{2,1,0:T(8,128)(2,1)S(1)}, u32[]{:S(2)}, u32[]{:S(2)}) collective-permute-start(bf16[24,16,256]{2,1,0:T(8,128)(2,1)S(1)} %collective-permute-done.6.refs_2_), channel_id=1, source_target_pairs={{8,24},{9,25},{10,26},{11,27},{20,4},{21,5},{22,6},{23,7}} | collective-permute-start | bytes 589832 | tf_op jit(solution)/shard_map/ppermute | solution.py:100
  31.6 0.6 %inner_0.1 = (bf16[16,16,256]{2,1,0:T(8,128)(2,1)S(1)}, bf16[16,16,256]{2,1,0:T(8,128)(2,1)S(1)}, bf16[16,16,256]{2,1,0:T(8,128)(2,1)S(1)}, bf16[16,16,256]{2,1,0:T(8,128)(2,1)S(1)}, f32[4,64,256]{2,1,0:T(8,128)S(1)}) custom-call(s32[4]{0:T(128)S(1)} %copy-done.3, bf16[24,16,512]{2,1,0:T(8,128)(2,1)S(1)} %collective-permute-done.7.refs_1_.refs_11_, ...), custom_call_target="tpu_custom_call" | custom-call | flops 905969664 | bytes 2949120 | tf_op jit(solution)/shard_map/inner_0/pallas_call | solution.py:272
  32.2 0.7 %collective-permute-done.11.refs_4_ = bf16[24,16,256]{2,1,0:T(8,128)(2,1)S(1)} collective-permute-done((bf16[24,16,256]{2,1,0:T(8,128)(2,1)S(1)}, bf16[24,16,256]{2,1,0:T(8,128)(2,1)S(1)}, u32[]{:S(2)}, u32[]{:S(2)}) %collective-permute-start.11) | collective-permute-done | bytes 196640 | tf_op jit(solution)/shard_map/ppermute | solution.py:100
  32.9 0.7 %outer.1 = (bf16[24,16,256]{2,1,0:T(8,128)(2,1)S(1)}, bf16[24,16,256]{2,1,0:T(8,128)(2,1)S(1)}, bf16[24,16,256]{2,1,0:T(8,128)(2,1)S(1)}, bf16[24,16,256]{2,1,0:T(8,128)(2,1)S(1)}) custom-call(s32[4]{0:T(128)S(1)} %copy-done.3, bf16[24,16,256]{2,1,0:T(8,128)(2,1)S(1)} %pad_maximum_fusion.refs_1_, bf16[24,16,256]{2,1,0:T(8,128)(2,1)S(1)} %collective-permute-done.6.refs_2_, ...), custom_call_target="tpu_custom_call" | custom-call | flops 1610612736 | bytes 5242880 | tf_op jit(solution)/shard_map/outer/pallas_call | solution.py:385
  33.6 0.7 %collective-permute-start.12 = (bf16[24,16,256]{2,1,0:T(8,128)(2,1)S(1)}, bf16[24,16,256]{2,1,0:T(8,128)(2,1)S(1)}, u32[]{:S(2)}, u32[]{:S(2)}) collective-permute-start(bf16[24,16,256]{2,1,0:T(8,128)(2,1)S(1)} %get-tuple-element.56), channel_id=1, source_target_pairs={{4,12},{5,13},{6,14},{7,15},{24,16},{25,17},{26,18},{27,19}} | collective-permute-start | bytes 589832 | tf_op jit(solution)/shard_map/ppermute | solution.py:100
  34.3 1.3 %collective-permute-start.13 = (bf16[24,16,256]{2,1,0:T(8,128)(2,1)S(1)}, bf16[24,16,256]{2,1,0:T(8,128)(2,1)S(1)}, u32[]{:S(2)}, u32[]{:S(2)}) collective-permute-start(bf16[24,16,256]{2,1,0:T(8,128)(2,1)S(1)} %get-tuple-element.57), channel_id=1, source_target_pairs={{4,0},{5,1},{6,2},{7,3},{24,28},{25,29},{26,30},{27,31}} | collective-permute-start | bytes 589832 | tf_op jit(solution)/shard_map/ppermute | solution.py:100
  35.6 0.7 %collective-permute-start.14 = (bf16[24,16,256]{2,1,0:T(8,128)(2,1)S(1)}, bf16[24,16,256]{2,1,0:T(8,128)(2,1)S(1)}, u32[]{:S(2)}, u32[]{:S(2)}) collective-permute-start(bf16[24,16,256]{2,1,0:T(8,128)(2,1)S(1)} %get-tuple-element.58), channel_id=1, source_target_pairs={{4,8},{5,9},{6,10},{7,11},{24,20},{25,21},{26,22},{27,23}} | collective-permute-start | bytes 589832 | tf_op jit(solution)/shard_map/ppermute | solution.py:100
  36.3 14.3 %collective-permute-done.13 = bf16[24,16,256]{2,1,0:T(8,128)(2,1)S(1)} collective-permute-done((bf16[24,16,256]{2,1,0:T(8,128)(2,1)S(1)}, bf16[24,16,256]{2,1,0:T(8,128)(2,1)S(1)}, u32[]{:S(2)}, u32[]{:S(2)}) %collective-permute-start.13) | collective-permute-done | bytes 196640 | tf_op jit(solution)/shard_map/ppermute | solution.py:100
  50.7 0.7 %copy.14 = bf16[1,16,24,256]{3,2,1,0:T(8,128)(2,1)} copy(bf16[1,16,24,256]{3,1,2,0:T(8,128)(2,1)S(1)} %add_bitcast_fusion) | data formatting | bytes 393216 | tf_op jit(solution)/shard_map/broadcast_in_dim | solution.py:479
  (27 shorter events, 1.3 us)
Async XLA Ops:
  0.0 22.5 %copy-start.4 = (f32[4,5,256]{2,0,1:T(4,128)S(1)}, f32[4,5,256]{2,0,1:T(4,128)}, u32[]{:S(2)}) copy-start(f32[4,5,256]{2,0,1:T(4,128)} %param.12) | copy-start | bytes 61444
  0.0 22.6 %copy-start = (bf16[4,256,512]{2,1,0:T(8,128)(2,1)S(1)}, bf16[4,256,512]{2,1,0:T(8,128)(2,1)}, u32[]{:S(2)}) copy-start(bf16[4,256,512]{2,1,0:T(8,128)(2,1)} %refs_26_.1) | copy-start | bytes 3145732
  0.0 22.6 %copy-start.1 = (bf16[4,512,256]{2,1,0:T(8,128)(2,1)S(1)}, bf16[4,512,256]{2,1,0:T(8,128)(2,1)}, u32[]{:S(2)}) copy-start(bf16[4,512,256]{2,1,0:T(8,128)(2,1)} %refs_27_.1) | copy-start | bytes 3145732
  0.0 22.6 %copy-start.2 = (bf16[256,128]{1,0:T(8,128)(2,1)S(1)}, bf16[256,128]{1,0:T(8,128)(2,1)}, u32[]{:S(2)}) copy-start(bf16[256,128]{1,0:T(8,128)(2,1)} %refs_25_.1) | copy-start | bytes 196612
  0.0 22.6 %copy-start.3 = (s32[4]{0:T(128)S(1)}, s32[4]{0:T(128)}, u32[]{:S(2)}) copy-start(s32[4]{0:T(128)} %refs_0_.9) | copy-start | bytes 52
  0.0 2.0 %collective-permute-start = (bf16[16,24,128]{2,1,0:T(8,128)(2,1)}, bf16[16,24,128]{2,1,0:T(8,128)(2,1)S(1)}, u32[]{:S(2)}, u32[]{:S(2)}) collective-permute-start(bf16[16,24,128]{2,1,0:T(8,128)(2,1)} %bitcast.11), channel_id=1, source_target_pairs={{0,16},{16,0},{1,17},{17,1},{2,18},{18,2},{3,19},{19,3},{4,20},{20... | collective-permute-start | bytes 294920 | tf_op jit(solution)/shard_map/ppermute | solution.py:38
  2.1 17.8 %collective-permute-start.3 = (bf16[24,16,640]{2,1,0:T(8,128)(2,1)S(1)}, bf16[24,16,640]{2,1,0:T(8,128)(2,1)S(1)}, u32[]{:S(2)}, u32[]{:S(2)}) collective-permute-start(bf16[24,16,640]{2,1,0:T(8,128)(2,1)S(1)} %get-tuple-element.37.refs_4_.refs_5_), channel_id=1, source_target_pairs={{12,4},{13,5},{14,6},{15,7},{16,24},{17,25},{18,26},{19,27}} | collective-permute-start | bytes 1474568 | tf_op jit(solution)/shard_map/ppermute | solution.py:100
  2.8 19.8 %collective-permute-start.4 = (bf16[24,16,640]{2,1,0:T(8,128)(2,1)S(1)}, bf16[24,16,640]{2,1,0:T(8,128)(2,1)S(1)}, u32[]{:S(2)}, u32[]{:S(2)}) collective-permute-start(bf16[24,16,640]{2,1,0:T(8,128)(2,1)S(1)} %get-tuple-element.37.refs_4_.refs_5_), channel_id=1, source_target_pairs={{8,4},{9,5},{10,6},{11,7},{20,24},{21,25},{22,26},{23,27}} | collective-permute-start | bytes 1474568 | tf_op jit(solution)/shard_map/ppermute | solution.py:100
  3.5 19.1 %collective-permute-start.5 = (bf16[24,16,640]{2,1,0:T(8,128)(2,1)S(1)}, bf16[24,16,640]{2,1,0:T(8,128)(2,1)S(1)}, u32[]{:S(2)}, u32[]{:S(2)}) collective-permute-start(bf16[24,16,640]{2,1,0:T(8,128)(2,1)S(1)} %get-tuple-element.37.refs_4_.refs_5_), channel_id=1, source_target_pairs={{0,4},{1,5},{2,6},{3,7},{28,24},{29,25},{30,26},{31,27}} | collective-permute-start | bytes 1474568 | tf_op jit(solution)/shard_map/ppermute | solution.py:100
  9.3 5.6 %collective-permute-start.1 = (bf16[12,16,256]{2,1,0:T(8,128)(2,1)S(1)}, bf16[12,16,256]{2,1,0:T(8,128)(2,1)S(1)}, u32[]{:S(2)}, u32[]{:S(2)}) collective-permute-start(bf16[12,16,256]{2,1,0:T(8,128)(2,1)S(1)} %get-tuple-element.33), channel_id=1, source_target_pairs={{0,1},{1,2},{2,3},{4,5},{5,6},{6,7},{8,9},{9,10},{10,11},{12,13},{... | collective-permute-start | bytes 294920 | tf_op jit(solution)/shard_map/ppermute | solution.py:100
  12.7 6.5 %collective-permute-start.2 = (bf16[12,16,256]{2,1,0:T(8,128)(2,1)S(1)}, bf16[12,16,256]{2,1,0:T(8,128)(2,1)S(1)}, u32[]{:S(2)}, u32[]{:S(2)}) collective-permute-start(bf16[12,16,256]{2,1,0:T(8,128)(2,1)S(1)} %get-tuple-element.34), channel_id=1, source_target_pairs={{1,0},{2,1},{3,2},{5,4},{6,5},{7,6},{9,8},{10,9},{11,10},{13,12},{... | collective-permute-start | bytes 294920 | tf_op jit(solution)/shard_map/ppermute | solution.py:100
  14.9 15.4 %collective-permute-start.7 = (bf16[24,16,512]{2,1,0:T(8,128)(2,1)S(1)}, bf16[24,16,512]{2,1,0:T(8,128)(2,1)S(1)}, u32[]{:S(2)}, u32[]{:S(2)}) collective-permute-start(bf16[24,16,512]{2,1,0:T(8,128)(2,1)S(1)} %get-tuple-element.40.refs_4_.refs_9_), channel_id=1, source_target_pairs={{12,4},{13,5},{14,6},{15,7},{16,24},{17,25},{18,26},{19,27}} | collective-permute-start | bytes 1179656 | tf_op jit(solution)/shard_map/ppermute | solution.py:100
  19.2 11.1 %collective-permute-start.8 = (bf16[24,16,512]{2,1,0:T(8,128)(2,1)S(1)}, bf16[24,16,512]{2,1,0:T(8,128)(2,1)S(1)}, u32[]{:S(2)}, u32[]{:S(2)}) collective-permute-start(bf16[24,16,512]{2,1,0:T(8,128)(2,1)S(1)} %get-tuple-element.40.refs_4_.refs_9_), channel_id=1, source_target_pairs={{8,4},{9,5},{10,6},{11,7},{20,24},{21,25},{22,26},{23,27}} | collective-permute-start | bytes 1179656 | tf_op jit(solution)/shard_map/ppermute | solution.py:100
  19.9 10.4 %collective-permute-start.9 = (bf16[24,16,512]{2,1,0:T(8,128)(2,1)S(1)}, bf16[24,16,512]{2,1,0:T(8,128)(2,1)S(1)}, u32[]{:S(2)}, u32[]{:S(2)}) collective-permute-start(bf16[24,16,512]{2,1,0:T(8,128)(2,1)S(1)} %get-tuple-element.40.refs_4_.refs_9_), channel_id=1, source_target_pairs={{0,4},{1,5},{2,6},{3,7},{28,24},{29,25},{30,26},{31,27}} | collective-permute-start | bytes 1179656 | tf_op jit(solution)/shard_map/ppermute | solution.py:100
  23.2 7.7 %collective-permute-start.6 = (bf16[24,16,256]{2,1,0:T(8,128)(2,1)S(1)}, bf16[24,16,256]{2,1,0:T(8,128)(2,1)S(1)}, u32[]{:S(2)}, u32[]{:S(2)}) collective-permute-start(bf16[24,16,256]{2,1,0:T(8,128)(2,1)S(1)} %pad_maximum_fusion.refs_1_), channel_id=1, source_target_pairs={{8,4},{9,5},{10,6},{11,7},{12,20},{13,21},{14,22},{15,23},{16,8},{... | collective-permute-start | bytes 589832 | tf_op jit(solution)/shard_map/ppermute | solution.py:100
  23.9 9.0 %collective-permute-start.11 = (bf16[24,16,256]{2,1,0:T(8,128)(2,1)S(1)}, bf16[24,16,256]{2,1,0:T(8,128)(2,1)S(1)}, u32[]{:S(2)}, u32[]{:S(2)}) collective-permute-start(bf16[24,16,256]{2,1,0:T(8,128)(2,1)S(1)} %pad_maximum_fusion.refs_1_), channel_id=1, source_target_pairs={{0,4},{1,5},{2,6},{3,7},{28,24},{29,25},{30,26},{31,27}} | collective-permute-start | bytes 589832 | tf_op jit(solution)/shard_map/ppermute | solution.py:100
  30.9 2.0 %collective-permute-start.10 = (bf16[24,16,256]{2,1,0:T(8,128)(2,1)S(1)}, bf16[24,16,256]{2,1,0:T(8,128)(2,1)S(1)}, u32[]{:S(2)}, u32[]{:S(2)}) collective-permute-start(bf16[24,16,256]{2,1,0:T(8,128)(2,1)S(1)} %collective-permute-done.6.refs_2_), channel_id=1, source_target_pairs={{8,24},{9,25},{10,26},{11,27},{20,4},{21,5},{22,6},{23,7}} | collective-permute-start | bytes 589832 | tf_op jit(solution)/shard_map/ppermute | solution.py:100
  33.6 2.7 %collective-permute-start.12 = (bf16[24,16,256]{2,1,0:T(8,128)(2,1)S(1)}, bf16[24,16,256]{2,1,0:T(8,128)(2,1)S(1)}, u32[]{:S(2)}, u32[]{:S(2)}) collective-permute-start(bf16[24,16,256]{2,1,0:T(8,128)(2,1)S(1)} %get-tuple-element.56), channel_id=1, source_target_pairs={{4,12},{5,13},{6,14},{7,15},{24,16},{25,17},{26,18},{27,19}} | collective-permute-start | bytes 589832 | tf_op jit(solution)/shard_map/ppermute | solution.py:100
  34.3 16.3 %collective-permute-start.13 = (bf16[24,16,256]{2,1,0:T(8,128)(2,1)S(1)}, bf16[24,16,256]{2,1,0:T(8,128)(2,1)S(1)}, u32[]{:S(2)}, u32[]{:S(2)}) collective-permute-start(bf16[24,16,256]{2,1,0:T(8,128)(2,1)S(1)} %get-tuple-element.57), channel_id=1, source_target_pairs={{4,0},{5,1},{6,2},{7,3},{24,28},{25,29},{26,30},{27,31}} | collective-permute-start | bytes 589832 | tf_op jit(solution)/shard_map/ppermute | solution.py:100
  35.6 15.0 %collective-permute-start.14 = (bf16[24,16,256]{2,1,0:T(8,128)(2,1)S(1)}, bf16[24,16,256]{2,1,0:T(8,128)(2,1)S(1)}, u32[]{:S(2)}, u32[]{:S(2)}) collective-permute-start(bf16[24,16,256]{2,1,0:T(8,128)(2,1)S(1)} %get-tuple-element.58), channel_id=1, source_target_pairs={{4,8},{5,9},{6,10},{7,11},{24,20},{25,21},{26,22},{27,23}} | collective-permute-start | bytes 589832 | tf_op jit(solution)/shard_map/ppermute | solution.py:100

commit v10 on v9

--- a/solution.py
+++ b/solution.py
@@ -101,7 +101,7 @@
 
 
 def row_chunks(low, high):
-    count = max(1, round((high - low) / 11))
+    count = max(1, round((high - low) / 24))
     edges = [low + (high - low) * i // count for i in range(count + 1)]
     return list(zip(edges[:-1], edges[1:]))
 

time: 51.7 us -> 51.1 us (0.988)
  no operation moved by 1% of the time
where the time goes in v10:
time: 51.1 us; the launch traced here: 50.7 us
  starting transfers between devices  25.9 us (51%)
  waiting for transfers between devices  19.1 us (37%)
  Pallas kernels  3.08 us (6%)
  local copies, waits for them, and re-layouts  2.18 us (4%)
    ppermute x14, starting transfers between devices, routed(): return lax.ppermute(value, AXES, pairs)  25.4 us
    ppermute x14, waiting for transfers between devices, routed(): return lax.ppermute(value, AXES, pairs)  19.1 us
    pallas_call x4, Pallas kernels, run_inner(): pl.pallas_call(functools.partial(inner_kernel, layer, layers, place), out...  2.24 us
    unnamed x12, local copies, waits for them, and re-layouts  1.45 us
  transfers between devices with their start and end apart: 15, of which 4 were waited for; matrix products, arithmetic and copies ran while one was open for 3% of the time, Pallas kernels for 4%

profile of v10, /device:TPU:0, one launch (start us, length us, event | category | flops | bytes accessed | tf_op | source)
XLA Modules:
  0.0 50.7 jit_solution(17943020836638855457)
XLA Ops:
  0.5 1.4 %copy.16 = bf16[1,4,16,24,256]{4,2,3,1,0:T(8,128)(2,1)S(1)} copy(bf16[1,4,16,24,256]{4,3,2,1,0:T(8,128)(2,1)} %param.8) | data formatting | bytes 1572864 | tf_op args[1]
  2.1 0.7 %collective-permute-start.3 = (bf16[24,16,640]{2,1,0:T(8,128)(2,1)S(1)}, bf16[24,16,640]{2,1,0:T(8,128)(2,1)S(1)}, u32[]{:S(2)}, u32[]{:S(2)}) collective-permute-start(bf16[24,16,640]{2,1,0:T(8,128)(2,1)S(1)} %get-tuple-element.37.refs_4_.refs_5_), channel_id=1, source_target_pairs={{12,4},{13,5},{14,6},{15,7},{16,24},{17,25},{18,26},{19,27}} | collective-permute-start | bytes 1474568 | tf_op jit(solution)/shard_map/ppermute | solution.py:100
  2.8 0.7 %collective-permute-start.4 = (bf16[24,16,640]{2,1,0:T(8,128)(2,1)S(1)}, bf16[24,16,640]{2,1,0:T(8,128)(2,1)S(1)}, u32[]{:S(2)}, u32[]{:S(2)}) collective-permute-start(bf16[24,16,640]{2,1,0:T(8,128)(2,1)S(1)} %get-tuple-element.37.refs_4_.refs_5_), channel_id=1, source_target_pairs={{8,4},{9,5},{10,6},{11,7},{20,24},{21,25},{22,26},{23,27}} | collective-permute-start | bytes 1474568 | tf_op jit(solution)/shard_map/ppermute | solution.py:100
  3.5 5.8 %collective-permute-start.5 = (bf16[24,16,640]{2,1,0:T(8,128)(2,1)S(1)}, bf16[24,16,640]{2,1,0:T(8,128)(2,1)S(1)}, u32[]{:S(2)}, u32[]{:S(2)}) collective-permute-start(bf16[24,16,640]{2,1,0:T(8,128)(2,1)S(1)} %get-tuple-element.37.refs_4_.refs_5_), channel_id=1, source_target_pairs={{0,4},{1,5},{2,6},{3,7},{28,24},{29,25},{30,26},{31,27}} | collective-permute-start | bytes 1474568 | tf_op jit(solution)/shard_map/ppermute | solution.py:100
  9.3 3.4 %collective-permute-start.1 = (bf16[12,16,256]{2,1,0:T(8,128)(2,1)S(1)}, bf16[12,16,256]{2,1,0:T(8,128)(2,1)S(1)}, u32[]{:S(2)}, u32[]{:S(2)}) collective-permute-start(bf16[12,16,256]{2,1,0:T(8,128)(2,1)S(1)} %get-tuple-element.33), channel_id=1, source_target_pairs={{0,1},{1,2},{2,3},{4,5},{5,6},{6,7},{8,9},{9,10},{10,11},{12,13},{... | collective-permute-start | bytes 294920 | tf_op jit(solution)/shard_map/ppermute | solution.py:100
  12.7 1.3 %collective-permute-start.2 = (bf16[12,16,256]{2,1,0:T(8,128)(2,1)S(1)}, bf16[12,16,256]{2,1,0:T(8,128)(2,1)S(1)}, u32[]{:S(2)}, u32[]{:S(2)}) collective-permute-start(bf16[12,16,256]{2,1,0:T(8,128)(2,1)S(1)} %get-tuple-element.34), channel_id=1, source_target_pairs={{1,0},{2,1},{3,2},{5,4},{6,5},{7,6},{9,8},{10,9},{11,10},{13,12},{... | collective-permute-start | bytes 294920 | tf_op jit(solution)/shard_map/ppermute | solution.py:100
  14.0 0.9 %collective-permute-done.1 = bf16[12,16,256]{2,1,0:T(8,128)(2,1)S(1)} collective-permute-done((bf16[12,16,256]{2,1,0:T(8,128)(2,1)S(1)}, bf16[12,16,256]{2,1,0:T(8,128)(2,1)S(1)}, u32[]{:S(2)}, u32[]{:S(2)}) %collective-permute-start.1) | collective-permute-done | bytes 98336 | tf_op jit(solution)/shard_map/ppermute | solution.py:100
  14.9 0.7 %collective-permute-start.7 = (bf16[24,16,512]{2,1,0:T(8,128)(2,1)S(1)}, bf16[24,16,512]{2,1,0:T(8,128)(2,1)S(1)}, u32[]{:S(2)}, u32[]{:S(2)}) collective-permute-start(bf16[24,16,512]{2,1,0:T(8,128)(2,1)S(1)} %get-tuple-element.40.refs_4_.refs_9_), channel_id=1, source_target_pairs={{12,4},{13,5},{14,6},{15,7},{16,24},{17,25},{18,26},{19,27}} | collective-permute-start | bytes 1179656 | tf_op jit(solution)/shard_map/ppermute | solution.py:100
  15.6 3.6 %collective-permute-done.2 = bf16[12,16,256]{2,1,0:T(8,128)(2,1)S(1)} collective-permute-done((bf16[12,16,256]{2,1,0:T(8,128)(2,1)S(1)}, bf16[12,16,256]{2,1,0:T(8,128)(2,1)S(1)}, u32[]{:S(2)}, u32[]{:S(2)}) %collective-permute-start.2) | collective-permute-done | bytes 98336 | tf_op jit(solution)/shard_map/ppermute | solution.py:100
  19.2 0.7 %collective-permute-start.8 = (bf16[24,16,512]{2,1,0:T(8,128)(2,1)S(1)}, bf16[24,16,512]{2,1,0:T(8,128)(2,1)S(1)}, u32[]{:S(2)}, u32[]{:S(2)}) collective-permute-start(bf16[24,16,512]{2,1,0:T(8,128)(2,1)S(1)} %get-tuple-element.40.refs_4_.refs_9_), channel_id=1, source_target_pairs={{8,4},{9,5},{10,6},{11,7},{20,24},{21,25},{22,26},{23,27}} | collective-permute-start | bytes 1179656 | tf_op jit(solution)/shard_map/ppermute | solution.py:100
  19.9 2.6 %collective-permute-start.9 = (bf16[24,16,512]{2,1,0:T(8,128)(2,1)S(1)}, bf16[24,16,512]{2,1,0:T(8,128)(2,1)S(1)}, u32[]{:S(2)}, u32[]{:S(2)}) collective-permute-start(bf16[24,16,512]{2,1,0:T(8,128)(2,1)S(1)} %get-tuple-element.40.refs_4_.refs_9_), channel_id=1, source_target_pairs={{0,4},{1,5},{2,6},{3,7},{28,24},{29,25},{30,26},{31,27}} | collective-permute-start | bytes 1179656 | tf_op jit(solution)/shard_map/ppermute | solution.py:100
  22.7 0.6 %inner_3.1 = (f32[22,64,256]{2,1,0:T(8,128)S(1)}, f32[4,64,256]{2,1,0:T(8,128)S(1)}, f32[2,64,256]{2,1,0:T(8,128)S(1)}) custom-call(s32[4]{0:T(128)S(1)} %copy-done.3, bf16[24,16,640]{2,1,0:T(8,128)(2,1)S(1)} %collective-permute-done.3.refs_1_.refs_7_, bf16[24,16,640]{2,1,0:T(8,128)(2,1)S(1)} %collective-permute-done.4.refs_2_.refs_6_, ...), custom_call_target="tpu_custom_call" | custom-call | flops 1207959552 | bytes 3932160 | tf_op jit(solution)/shard_map/inner_3/pallas_call | solution.py:272
  23.2 0.7 %collective-permute-start.6 = (bf16[24,16,256]{2,1,0:T(8,128)(2,1)S(1)}, bf16[24,16,256]{2,1,0:T(8,128)(2,1)S(1)}, u32[]{:S(2)}, u32[]{:S(2)}) collective-permute-start(bf16[24,16,256]{2,1,0:T(8,128)(2,1)S(1)} %pad_maximum_fusion.refs_1_), channel_id=1, source_target_pairs={{8,4},{9,5},{10,6},{11,7},{12,20},{13,21},{14,22},{15,23},{16,8},{... | collective-permute-start | bytes 589832 | tf_op jit(solution)/shard_map/ppermute | solution.py:100
  23.9 5.5 %collective-permute-start.11 = (bf16[24,16,256]{2,1,0:T(8,128)(2,1)S(1)}, bf16[24,16,256]{2,1,0:T(8,128)(2,1)S(1)}, u32[]{:S(2)}, u32[]{:S(2)}) collective-permute-start(bf16[24,16,256]{2,1,0:T(8,128)(2,1)S(1)} %pad_maximum_fusion.refs_1_), channel_id=1, source_target_pairs={{0,4},{1,5},{2,6},{3,7},{28,24},{29,25},{30,26},{31,27}} | collective-permute-start | bytes 589832 | tf_op jit(solution)/shard_map/ppermute | solution.py:100
  30.1 0.6 %inner_1.1 = (f32[18,64,256]{2,1,0:T(8,128)S(1)}, f32[4,64,256]{2,1,0:T(8,128)S(1)}) custom-call(s32[4]{0:T(128)S(1)} %copy-done.3, bf16[24,16,512]{2,1,0:T(8,128)(2,1)S(1)} %collective-permute-done.7.refs_1_.refs_11_, bf16[24,16,512]{2,1,0:T(8,128)(2,1)S(1)} %collective-permute-done.8.refs_2_.refs_10_, ...), custom_call_target="tpu_custom_call" | custom-call | flops 1006632960 | bytes 3276800 | tf_op jit(solution)/shard_map/inner_1/pallas_call | solution.py:272
  30.6 0.7 %collective-permute-start.10 = (bf16[24,16,256]{2,1,0:T(8,128)(2,1)S(1)}, bf16[24,16,256]{2,1,0:T(8,128)(2,1)S(1)}, u32[]{:S(2)}, u32[]{:S(2)}) collective-permute-start(bf16[24,16,256]{2,1,0:T(8,128)(2,1)S(1)} %collective-permute-done.6.refs_2_), channel_id=1, source_target_pairs={{8,24},{9,25},{10,26},{11,27},{20,4},{21,5},{22,6},{23,7}} | collective-permute-start | bytes 589832 | tf_op jit(solution)/shard_map/ppermute | solution.py:100
  31.3 0.6 %inner_0.1 = (bf16[16,16,256]{2,1,0:T(8,128)(2,1)S(1)}, bf16[16,16,256]{2,1,0:T(8,128)(2,1)S(1)}, bf16[16,16,256]{2,1,0:T(8,128)(2,1)S(1)}, bf16[16,16,256]{2,1,0:T(8,128)(2,1)S(1)}, f32[4,64,256]{2,1,0:T(8,128)S(1)}) custom-call(s32[4]{0:T(128)S(1)} %copy-done.3, bf16[24,16,512]{2,1,0:T(8,128)(2,1)S(1)} %collective-permute-done.7.refs_1_.refs_11_, ...), custom_call_target="tpu_custom_call" | custom-call | flops 905969664 | bytes 2949120 | tf_op jit(solution)/shard_map/inner_0/pallas_call | solution.py:272
  31.9 0.7 %collective-permute-done.11.refs_4_ = bf16[24,16,256]{2,1,0:T(8,128)(2,1)S(1)} collective-permute-done((bf16[24,16,256]{2,1,0:T(8,128)(2,1)S(1)}, bf16[24,16,256]{2,1,0:T(8,128)(2,1)S(1)}, u32[]{:S(2)}, u32[]{:S(2)}) %collective-permute-start.11) | collective-permute-done | bytes 196640 | tf_op jit(solution)/shard_map/ppermute | solution.py:100
  32.6 0.7 %outer.1 = (bf16[24,16,256]{2,1,0:T(8,128)(2,1)S(1)}, bf16[24,16,256]{2,1,0:T(8,128)(2,1)S(1)}, bf16[24,16,256]{2,1,0:T(8,128)(2,1)S(1)}, bf16[24,16,256]{2,1,0:T(8,128)(2,1)S(1)}) custom-call(s32[4]{0:T(128)S(1)} %copy-done.3, bf16[24,16,256]{2,1,0:T(8,128)(2,1)S(1)} %pad_maximum_fusion.refs_1_, bf16[24,16,256]{2,1,0:T(8,128)(2,1)S(1)} %collective-permute-done.6.refs_2_, ...), custom_call_target="tpu_custom_call" | custom-call | flops 1610612736 | bytes 5242880 | tf_op jit(solution)/shard_map/outer/pallas_call | solution.py:385
  33.4 0.7 %collective-permute-start.12 = (bf16[24,16,256]{2,1,0:T(8,128)(2,1)S(1)}, bf16[24,16,256]{2,1,0:T(8,128)(2,1)S(1)}, u32[]{:S(2)}, u32[]{:S(2)}) collective-permute-start(bf16[24,16,256]{2,1,0:T(8,128)(2,1)S(1)} %get-tuple-element.56), channel_id=1, source_target_pairs={{4,12},{5,13},{6,14},{7,15},{24,16},{25,17},{26,18},{27,19}} | collective-permute-start | bytes 589832 | tf_op jit(solution)/shard_map/ppermute | solution.py:100
  34.0 1.3 %collective-permute-start.13 = (bf16[24,16,256]{2,1,0:T(8,128)(2,1)S(1)}, bf16[24,16,256]{2,1,0:T(8,128)(2,1)S(1)}, u32[]{:S(2)}, u32[]{:S(2)}) collective-permute-start(bf16[24,16,256]{2,1,0:T(8,128)(2,1)S(1)} %get-tuple-element.57), channel_id=1, source_target_pairs={{4,0},{5,1},{6,2},{7,3},{24,28},{25,29},{26,30},{27,31}} | collective-permute-start | bytes 589832 | tf_op jit(solution)/shard_map/ppermute | solution.py:100
  35.3 0.7 %collective-permute-start.14 = (bf16[24,16,256]{2,1,0:T(8,128)(2,1)S(1)}, bf16[24,16,256]{2,1,0:T(8,128)(2,1)S(1)}, u32[]{:S(2)}, u32[]{:S(2)}) collective-permute-start(bf16[24,16,256]{2,1,0:T(8,128)(2,1)S(1)} %get-tuple-element.58), channel_id=1, source_target_pairs={{4,8},{5,9},{6,10},{7,11},{24,20},{25,21},{26,22},{27,23}} | collective-permute-start | bytes 589832 | tf_op jit(solution)/shard_map/ppermute | solution.py:100
  36.0 13.8 %collective-permute-done.13 = bf16[24,16,256]{2,1,0:T(8,128)(2,1)S(1)} collective-permute-done((bf16[24,16,256]{2,1,0:T(8,128)(2,1)S(1)}, bf16[24,16,256]{2,1,0:T(8,128)(2,1)S(1)}, u32[]{:S(2)}, u32[]{:S(2)}) %collective-permute-start.13) | collective-permute-done | bytes 196640 | tf_op jit(solution)/shard_map/ppermute | solution.py:100
  49.9 0.7 %copy.14 = bf16[1,16,24,256]{3,2,1,0:T(8,128)(2,1)} copy(bf16[1,16,24,256]{3,1,2,0:T(8,128)(2,1)S(1)} %add_bitcast_fusion) | data formatting | bytes 393216 | tf_op jit(solution)/shard_map/broadcast_in_dim | solution.py:479
  (27 shorter events, 1.3 us)
Async XLA Ops:
  0.0 22.5 %copy-start.4 = (f32[4,5,256]{2,0,1:T(4,128)S(1)}, f32[4,5,256]{2,0,1:T(4,128)}, u32[]{:S(2)}) copy-start(f32[4,5,256]{2,0,1:T(4,128)} %param.12) | copy-start | bytes 61444
  0.0 22.6 %copy-start = (bf16[4,256,512]{2,1,0:T(8,128)(2,1)S(1)}, bf16[4,256,512]{2,1,0:T(8,128)(2,1)}, u32[]{:S(2)}) copy-start(bf16[4,256,512]{2,1,0:T(8,128)(2,1)} %refs_26_.1) | copy-start | bytes 3145732
  0.0 22.6 %copy-start.1 = (bf16[4,512,256]{2,1,0:T(8,128)(2,1)S(1)}, bf16[4,512,256]{2,1,0:T(8,128)(2,1)}, u32[]{:S(2)}) copy-start(bf16[4,512,256]{2,1,0:T(8,128)(2,1)} %refs_27_.1) | copy-start | bytes 3145732
  0.0 22.6 %copy-start.2 = (bf16[256,128]{1,0:T(8,128)(2,1)S(1)}, bf16[256,128]{1,0:T(8,128)(2,1)}, u32[]{:S(2)}) copy-start(bf16[256,128]{1,0:T(8,128)(2,1)} %refs_25_.1) | copy-start | bytes 196612
  0.0 22.6 %copy-start.3 = (s32[4]{0:T(128)S(1)}, s32[4]{0:T(128)}, u32[]{:S(2)}) copy-start(s32[4]{0:T(128)} %refs_0_.9) | copy-start | bytes 52
  0.0 2.0 %collective-permute-start = (bf16[16,24,128]{2,1,0:T(8,128)(2,1)}, bf16[16,24,128]{2,1,0:T(8,128)(2,1)S(1)}, u32[]{:S(2)}, u32[]{:S(2)}) collective-permute-start(bf16[16,24,128]{2,1,0:T(8,128)(2,1)} %bitcast.11), channel_id=1, source_target_pairs={{0,16},{16,0},{1,17},{17,1},{2,18},{18,2},{3,19},{19,3},{4,20},{20... | collective-permute-start | bytes 294920 | tf_op jit(solution)/shard_map/ppermute | solution.py:38
  2.1 17.8 %collective-permute-start.3 = (bf16[24,16,640]{2,1,0:T(8,128)(2,1)S(1)}, bf16[24,16,640]{2,1,0:T(8,128)(2,1)S(1)}, u32[]{:S(2)}, u32[]{:S(2)}) collective-permute-start(bf16[24,16,640]{2,1,0:T(8,128)(2,1)S(1)} %get-tuple-element.37.refs_4_.refs_5_), channel_id=1, source_target_pairs={{12,4},{13,5},{14,6},{15,7},{16,24},{17,25},{18,26},{19,27}} | collective-permute-start | bytes 1474568 | tf_op jit(solution)/shard_map/ppermute | solution.py:100
  2.8 19.8 %collective-permute-start.4 = (bf16[24,16,640]{2,1,0:T(8,128)(2,1)S(1)}, bf16[24,16,640]{2,1,0:T(8,128)(2,1)S(1)}, u32[]{:S(2)}, u32[]{:S(2)}) collective-permute-start(bf16[24,16,640]{2,1,0:T(8,128)(2,1)S(1)} %get-tuple-element.37.refs_4_.refs_5_), channel_id=1, source_target_pairs={{8,4},{9,5},{10,6},{11,7},{20,24},{21,25},{22,26},{23,27}} | collective-permute-start | bytes 1474568 | tf_op jit(solution)/shard_map/ppermute | solution.py:100
  3.5 19.1 %collective-permute-start.5 = (bf16[24,16,640]{2,1,0:T(8,128)(2,1)S(1)}, bf16[24,16,640]{2,1,0:T(8,128)(2,1)S(1)}, u32[]{:S(2)}, u32[]{:S(2)}) collective-permute-start(bf16[24,16,640]{2,1,0:T(8,128)(2,1)S(1)} %get-tuple-element.37.refs_4_.refs_5_), channel_id=1, source_target_pairs={{0,4},{1,5},{2,6},{3,7},{28,24},{29,25},{30,26},{31,27}} | collective-permute-start | bytes 1474568 | tf_op jit(solution)/shard_map/ppermute | solution.py:100
  9.3 5.6 %collective-permute-start.1 = (bf16[12,16,256]{2,1,0:T(8,128)(2,1)S(1)}, bf16[12,16,256]{2,1,0:T(8,128)(2,1)S(1)}, u32[]{:S(2)}, u32[]{:S(2)}) collective-permute-start(bf16[12,16,256]{2,1,0:T(8,128)(2,1)S(1)} %get-tuple-element.33), channel_id=1, source_target_pairs={{0,1},{1,2},{2,3},{4,5},{5,6},{6,7},{8,9},{9,10},{10,11},{12,13},{... | collective-permute-start | bytes 294920 | tf_op jit(solution)/shard_map/ppermute | solution.py:100
  12.7 6.5 %collective-permute-start.2 = (bf16[12,16,256]{2,1,0:T(8,128)(2,1)S(1)}, bf16[12,16,256]{2,1,0:T(8,128)(2,1)S(1)}, u32[]{:S(2)}, u32[]{:S(2)}) collective-permute-start(bf16[12,16,256]{2,1,0:T(8,128)(2,1)S(1)} %get-tuple-element.34), channel_id=1, source_target_pairs={{1,0},{2,1},{3,2},{5,4},{6,5},{7,6},{9,8},{10,9},{11,10},{13,12},{... | collective-permute-start | bytes 294920 | tf_op jit(solution)/shard_map/ppermute | solution.py:100
  14.9 15.1 %collective-permute-start.7 = (bf16[24,16,512]{2,1,0:T(8,128)(2,1)S(1)}, bf16[24,16,512]{2,1,0:T(8,128)(2,1)S(1)}, u32[]{:S(2)}, u32[]{:S(2)}) collective-permute-start(bf16[24,16,512]{2,1,0:T(8,128)(2,1)S(1)} %get-tuple-element.40.refs_4_.refs_9_), channel_id=1, source_target_pairs={{12,4},{13,5},{14,6},{15,7},{16,24},{17,25},{18,26},{19,27}} | collective-permute-start | bytes 1179656 | tf_op jit(solution)/shard_map/ppermute | solution.py:100
  19.2 10.8 %collective-permute-start.8 = (bf16[24,16,512]{2,1,0:T(8,128)(2,1)S(1)}, bf16[24,16,512]{2,1,0:T(8,128)(2,1)S(1)}, u32[]{:S(2)}, u32[]{:S(2)}) collective-permute-start(bf16[24,16,512]{2,1,0:T(8,128)(2,1)S(1)} %get-tuple-element.40.refs_4_.refs_9_), channel_id=1, source_target_pairs={{8,4},{9,5},{10,6},{11,7},{20,24},{21,25},{22,26},{23,27}} | collective-permute-start | bytes 1179656 | tf_op jit(solution)/shard_map/ppermute | solution.py:100
  19.9 10.2 %collective-permute-start.9 = (bf16[24,16,512]{2,1,0:T(8,128)(2,1)S(1)}, bf16[24,16,512]{2,1,0:T(8,128)(2,1)S(1)}, u32[]{:S(2)}, u32[]{:S(2)}) collective-permute-start(bf16[24,16,512]{2,1,0:T(8,128)(2,1)S(1)} %get-tuple-element.40.refs_4_.refs_9_), channel_id=1, source_target_pairs={{0,4},{1,5},{2,6},{3,7},{28,24},{29,25},{30,26},{31,27}} | collective-permute-start | bytes 1179656 | tf_op jit(solution)/shard_map/ppermute | solution.py:100
  23.2 7.4 %collective-permute-start.6 = (bf16[24,16,256]{2,1,0:T(8,128)(2,1)S(1)}, bf16[24,16,256]{2,1,0:T(8,128)(2,1)S(1)}, u32[]{:S(2)}, u32[]{:S(2)}) collective-permute-start(bf16[24,16,256]{2,1,0:T(8,128)(2,1)S(1)} %pad_maximum_fusion.refs_1_), channel_id=1, source_target_pairs={{8,4},{9,5},{10,6},{11,7},{12,20},{13,21},{14,22},{15,23},{16,8},{... | collective-permute-start | bytes 589832 | tf_op jit(solution)/shard_map/ppermute | solution.py:100
  23.9 8.7 %collective-permute-start.11 = (bf16[24,16,256]{2,1,0:T(8,128)(2,1)S(1)}, bf16[24,16,256]{2,1,0:T(8,128)(2,1)S(1)}, u32[]{:S(2)}, u32[]{:S(2)}) collective-permute-start(bf16[24,16,256]{2,1,0:T(8,128)(2,1)S(1)} %pad_maximum_fusion.refs_1_), channel_id=1, source_target_pairs={{0,4},{1,5},{2,6},{3,7},{28,24},{29,25},{30,26},{31,27}} | collective-permute-start | bytes 589832 | tf_op jit(solution)/shard_map/ppermute | solution.py:100
  30.6 2.0 %collective-permute-start.10 = (bf16[24,16,256]{2,1,0:T(8,128)(2,1)S(1)}, bf16[24,16,256]{2,1,0:T(8,128)(2,1)S(1)}, u32[]{:S(2)}, u32[]{:S(2)}) collective-permute-start(bf16[24,16,256]{2,1,0:T(8,128)(2,1)S(1)} %collective-permute-done.6.refs_2_), channel_id=1, source_target_pairs={{8,24},{9,25},{10,26},{11,27},{20,4},{21,5},{22,6},{23,7}} | collective-permute-start | bytes 589832 | tf_op jit(solution)/shard_map/ppermute | solution.py:100
  33.4 2.7 %collective-permute-start.12 = (bf16[24,16,256]{2,1,0:T(8,128)(2,1)S(1)}, bf16[24,16,256]{2,1,0:T(8,128)(2,1)S(1)}, u32[]{:S(2)}, u32[]{:S(2)}) collective-permute-start(bf16[24,16,256]{2,1,0:T(8,128)(2,1)S(1)} %get-tuple-element.56), channel_id=1, source_target_pairs={{4,12},{5,13},{6,14},{7,15},{24,16},{25,17},{26,18},{27,19}} | collective-permute-start | bytes 589832 | tf_op jit(solution)/shard_map/ppermute | solution.py:100
  34.0 15.8 %collective-permute-start.13 = (bf16[24,16,256]{2,1,0:T(8,128)(2,1)S(1)}, bf16[24,16,256]{2,1,0:T(8,128)(2,1)S(1)}, u32[]{:S(2)}, u32[]{:S(2)}) collective-permute-start(bf16[24,16,256]{2,1,0:T(8,128)(2,1)S(1)} %get-tuple-element.57), channel_id=1, source_target_pairs={{4,0},{5,1},{6,2},{7,3},{24,28},{25,29},{26,30},{27,31}} | collective-permute-start | bytes 589832 | tf_op jit(solution)/shard_map/ppermute | solution.py:100
  35.3 14.6 %collective-permute-start.14 = (bf16[24,16,256]{2,1,0:T(8,128)(2,1)S(1)}, bf16[24,16,256]{2,1,0:T(8,128)(2,1)S(1)}, u32[]{:S(2)}, u32[]{:S(2)}) collective-permute-start(bf16[24,16,256]{2,1,0:T(8,128)(2,1)S(1)} %get-tuple-element.58), channel_id=1, source_target_pairs={{4,8},{5,9},{6,10},{7,11},{24,20},{25,21},{26,22},{27,23}} | collective-permute-start | bytes 589832 | tf_op jit(solution)/shard_map/ppermute | solution.py:100

commit v11 on v10

--- a/solution.py
+++ b/solution.py
@@ -211,10 +211,14 @@
         found = [in_order([m[skipped + r, :, lanes] for m in mains]) for r in range(r0, r1)]
         return jnp.concatenate(sum(found, []), axis=0)
 
-    def taps_of(r):
-        for h, lanes in halves_of(chans):
-            total = tapped(cg, r, h, [taps[layer, k : k + 1, lanes] for k in range(5)], offset)
-            total += (handed[r, :, lanes].astype(jnp.float32) if first else carried[r, :, lanes])
+    def taps_of(at):
+        found = []
+        for r in at:
+            for h, lanes in halves_of(chans):
+                total = tapped(cg, r, h, [taps[layer, k : k + 1, lanes] for k in range(5)], offset)
+                before = handed[r, :, lanes].astype(jnp.float32) if first else carried[r, :, lanes]
+                found.append((r, lanes, total + before))
+        for r, lanes, total in found:
             if last:
                 low = total.astype(jnp.bfloat16)
                 quarters = in_order([low[p * cells : (p + 1) * cells] for p in range(4)])
@@ -240,8 +244,8 @@
     half = (rows - 2) // 2
 
     def taps_of_half(k, carry):
-        for r in range(half):
-            taps_of(1 + k * half + r)
+        for r in range(0, half, 2):
+            taps_of([1 + k * half + n for n in range(r, min(r + 2, half))])
         return carry
 
     lax.fori_loop(0, 2, taps_of_half, 0)

time: 51.1 us -> 51.3 us (level)
  no operation moved by 1% of the time
where the time goes in v11:
time: 51.3 us; the launch traced here: 50.9 us
  starting transfers between devices  26 us (51%)
  waiting for transfers between devices  19.3 us (38%)
  Pallas kernels  3.08 us (6%)
  local copies, waits for them, and re-layouts  2.18 us (4%)
    ppermute x14, starting transfers between devices, routed(): return lax.ppermute(value, AXES, pairs)  25.4 us
    ppermute x14, waiting for transfers between devices, routed(): return lax.ppermute(value, AXES, pairs)  19.3 us
    pallas_call x4, Pallas kernels, run_inner(): pl.pallas_call(functools.partial(inner_kernel, layer, layers, place), out...  2.24 us
    unnamed x12, local copies, waits for them, and re-layouts  1.45 us
  transfers between devices with their start and end apart: 15, of which 4 were waited for; matrix products, arithmetic and copies ran while one was open for 3% of the time, Pallas kernels for 4%

profile of v11, /device:TPU:0, one launch (start us, length us, event | category | flops | bytes accessed | tf_op | source)
XLA Modules:
  0.0 50.9 jit_solution(5090485728221379266)
XLA Ops:
  0.5 1.4 %copy.16 = bf16[1,4,16,24,256]{4,2,3,1,0:T(8,128)(2,1)S(1)} copy(bf16[1,4,16,24,256]{4,3,2,1,0:T(8,128)(2,1)} %param.8) | data formatting | bytes 1572864 | tf_op args[1]
  2.1 0.7 %collective-permute-start.3 = (bf16[24,16,640]{2,1,0:T(8,128)(2,1)S(1)}, bf16[24,16,640]{2,1,0:T(8,128)(2,1)S(1)}, u32[]{:S(2)}, u32[]{:S(2)}) collective-permute-start(bf16[24,16,640]{2,1,0:T(8,128)(2,1)S(1)} %get-tuple-element.37.refs_4_.refs_5_), channel_id=1, source_target_pairs={{12,4},{13,5},{14,6},{15,7},{16,24},{17,25},{18,26},{19,27}} | collective-permute-start | bytes 1474568 | tf_op jit(solution)/shard_map/ppermute | solution.py:100
  2.8 0.7 %collective-permute-start.4 = (bf16[24,16,640]{2,1,0:T(8,128)(2,1)S(1)}, bf16[24,16,640]{2,1,0:T(8,128)(2,1)S(1)}, u32[]{:S(2)}, u32[]{:S(2)}) collective-permute-start(bf16[24,16,640]{2,1,0:T(8,128)(2,1)S(1)} %get-tuple-element.37.refs_4_.refs_5_), channel_id=1, source_target_pairs={{8,4},{9,5},{10,6},{11,7},{20,24},{21,25},{22,26},{23,27}} | collective-permute-start | bytes 1474568 | tf_op jit(solution)/shard_map/ppermute | solution.py:100
  3.5 5.8 %collective-permute-start.5 = (bf16[24,16,640]{2,1,0:T(8,128)(2,1)S(1)}, bf16[24,16,640]{2,1,0:T(8,128)(2,1)S(1)}, u32[]{:S(2)}, u32[]{:S(2)}) collective-permute-start(bf16[24,16,640]{2,1,0:T(8,128)(2,1)S(1)} %get-tuple-element.37.refs_4_.refs_5_), channel_id=1, source_target_pairs={{0,4},{1,5},{2,6},{3,7},{28,24},{29,25},{30,26},{31,27}} | collective-permute-start | bytes 1474568 | tf_op jit(solution)/shard_map/ppermute | solution.py:100
  9.3 3.4 %collective-permute-start.1 = (bf16[12,16,256]{2,1,0:T(8,128)(2,1)S(1)}, bf16[12,16,256]{2,1,0:T(8,128)(2,1)S(1)}, u32[]{:S(2)}, u32[]{:S(2)}) collective-permute-start(bf16[12,16,256]{2,1,0:T(8,128)(2,1)S(1)} %get-tuple-element.33), channel_id=1, source_target_pairs={{0,1},{1,2},{2,3},{4,5},{5,6},{6,7},{8,9},{9,10},{10,11},{12,13},{... | collective-permute-start | bytes 294920 | tf_op jit(solution)/shard_map/ppermute | solution.py:100
  12.7 1.3 %collective-permute-start.2 = (bf16[12,16,256]{2,1,0:T(8,128)(2,1)S(1)}, bf16[12,16,256]{2,1,0:T(8,128)(2,1)S(1)}, u32[]{:S(2)}, u32[]{:S(2)}) collective-permute-start(bf16[12,16,256]{2,1,0:T(8,128)(2,1)S(1)} %get-tuple-element.34), channel_id=1, source_target_pairs={{1,0},{2,1},{3,2},{5,4},{6,5},{7,6},{9,8},{10,9},{11,10},{13,12},{... | collective-permute-start | bytes 294920 | tf_op jit(solution)/shard_map/ppermute | solution.py:100
  14.0 0.9 %collective-permute-done.1 = bf16[12,16,256]{2,1,0:T(8,128)(2,1)S(1)} collective-permute-done((bf16[12,16,256]{2,1,0:T(8,128)(2,1)S(1)}, bf16[12,16,256]{2,1,0:T(8,128)(2,1)S(1)}, u32[]{:S(2)}, u32[]{:S(2)}) %collective-permute-start.1) | collective-permute-done | bytes 98336 | tf_op jit(solution)/shard_map/ppermute | solution.py:100
  14.9 0.7 %collective-permute-start.7 = (bf16[24,16,512]{2,1,0:T(8,128)(2,1)S(1)}, bf16[24,16,512]{2,1,0:T(8,128)(2,1)S(1)}, u32[]{:S(2)}, u32[]{:S(2)}) collective-permute-start(bf16[24,16,512]{2,1,0:T(8,128)(2,1)S(1)} %get-tuple-element.40.refs_4_.refs_9_), channel_id=1, source_target_pairs={{12,4},{13,5},{14,6},{15,7},{16,24},{17,25},{18,26},{19,27}} | collective-permute-start | bytes 1179656 | tf_op jit(solution)/shard_map/ppermute | solution.py:100
  15.6 3.6 %collective-permute-done.2 = bf16[12,16,256]{2,1,0:T(8,128)(2,1)S(1)} collective-permute-done((bf16[12,16,256]{2,1,0:T(8,128)(2,1)S(1)}, bf16[12,16,256]{2,1,0:T(8,128)(2,1)S(1)}, u32[]{:S(2)}, u32[]{:S(2)}) %collective-permute-start.2) | collective-permute-done | bytes 98336 | tf_op jit(solution)/shard_map/ppermute | solution.py:100
  19.2 0.7 %collective-permute-start.8 = (bf16[24,16,512]{2,1,0:T(8,128)(2,1)S(1)}, bf16[24,16,512]{2,1,0:T(8,128)(2,1)S(1)}, u32[]{:S(2)}, u32[]{:S(2)}) collective-permute-start(bf16[24,16,512]{2,1,0:T(8,128)(2,1)S(1)} %get-tuple-element.40.refs_4_.refs_9_), channel_id=1, source_target_pairs={{8,4},{9,5},{10,6},{11,7},{20,24},{21,25},{22,26},{23,27}} | collective-permute-start | bytes 1179656 | tf_op jit(solution)/shard_map/ppermute | solution.py:100
  19.9 2.6 %collective-permute-start.9 = (bf16[24,16,512]{2,1,0:T(8,128)(2,1)S(1)}, bf16[24,16,512]{2,1,0:T(8,128)(2,1)S(1)}, u32[]{:S(2)}, u32[]{:S(2)}) collective-permute-start(bf16[24,16,512]{2,1,0:T(8,128)(2,1)S(1)} %get-tuple-element.40.refs_4_.refs_9_), channel_id=1, source_target_pairs={{0,4},{1,5},{2,6},{3,7},{28,24},{29,25},{30,26},{31,27}} | collective-permute-start | bytes 1179656 | tf_op jit(solution)/shard_map/ppermute | solution.py:100
  22.7 0.6 %inner_3.1 = (f32[22,64,256]{2,1,0:T(8,128)S(1)}, f32[4,64,256]{2,1,0:T(8,128)S(1)}, f32[2,64,256]{2,1,0:T(8,128)S(1)}) custom-call(s32[4]{0:T(128)S(1)} %copy-done.3, bf16[24,16,640]{2,1,0:T(8,128)(2,1)S(1)} %collective-permute-done.3.refs_1_.refs_7_, bf16[24,16,640]{2,1,0:T(8,128)(2,1)S(1)} %collective-permute-done.4.refs_2_.refs_6_, ...), custom_call_target="tpu_custom_call" | custom-call | flops 1207959552 | bytes 3932160 | tf_op jit(solution)/shard_map/inner_3/pallas_call | solution.py:276
  23.2 0.7 %collective-permute-start.6 = (bf16[24,16,256]{2,1,0:T(8,128)(2,1)S(1)}, bf16[24,16,256]{2,1,0:T(8,128)(2,1)S(1)}, u32[]{:S(2)}, u32[]{:S(2)}) collective-permute-start(bf16[24,16,256]{2,1,0:T(8,128)(2,1)S(1)} %pad_maximum_fusion.refs_1_), channel_id=1, source_target_pairs={{8,4},{9,5},{10,6},{11,7},{12,20},{13,21},{14,22},{15,23},{16,8},{... | collective-permute-start | bytes 589832 | tf_op jit(solution)/shard_map/ppermute | solution.py:100
  23.9 5.6 %collective-permute-start.11 = (bf16[24,16,256]{2,1,0:T(8,128)(2,1)S(1)}, bf16[24,16,256]{2,1,0:T(8,128)(2,1)S(1)}, u32[]{:S(2)}, u32[]{:S(2)}) collective-permute-start(bf16[24,16,256]{2,1,0:T(8,128)(2,1)S(1)} %pad_maximum_fusion.refs_1_), channel_id=1, source_target_pairs={{0,4},{1,5},{2,6},{3,7},{28,24},{29,25},{30,26},{31,27}} | collective-permute-start | bytes 589832 | tf_op jit(solution)/shard_map/ppermute | solution.py:100
  30.1 0.6 %inner_1.1 = (f32[18,64,256]{2,1,0:T(8,128)S(1)}, f32[4,64,256]{2,1,0:T(8,128)S(1)}) custom-call(s32[4]{0:T(128)S(1)} %copy-done.3, bf16[24,16,512]{2,1,0:T(8,128)(2,1)S(1)} %collective-permute-done.7.refs_1_.refs_11_, bf16[24,16,512]{2,1,0:T(8,128)(2,1)S(1)} %collective-permute-done.8.refs_2_.refs_10_, ...), custom_call_target="tpu_custom_call" | custom-call | flops 1006632960 | bytes 3276800 | tf_op jit(solution)/shard_map/inner_1/pallas_call | solution.py:276
  30.7 0.7 %collective-permute-start.10 = (bf16[24,16,256]{2,1,0:T(8,128)(2,1)S(1)}, bf16[24,16,256]{2,1,0:T(8,128)(2,1)S(1)}, u32[]{:S(2)}, u32[]{:S(2)}) collective-permute-start(bf16[24,16,256]{2,1,0:T(8,128)(2,1)S(1)} %collective-permute-done.6.refs_2_), channel_id=1, source_target_pairs={{8,24},{9,25},{10,26},{11,27},{20,4},{21,5},{22,6},{23,7}} | collective-permute-start | bytes 589832 | tf_op jit(solution)/shard_map/ppermute | solution.py:100
  31.4 0.6 %inner_0.1 = (bf16[16,16,256]{2,1,0:T(8,128)(2,1)S(1)}, bf16[16,16,256]{2,1,0:T(8,128)(2,1)S(1)}, bf16[16,16,256]{2,1,0:T(8,128)(2,1)S(1)}, bf16[16,16,256]{2,1,0:T(8,128)(2,1)S(1)}, f32[4,64,256]{2,1,0:T(8,128)S(1)}) custom-call(s32[4]{0:T(128)S(1)} %copy-done.3, bf16[24,16,512]{2,1,0:T(8,128)(2,1)S(1)} %collective-permute-done.7.refs_1_.refs_11_, ...), custom_call_target="tpu_custom_call" | custom-call | flops 905969664 | bytes 2949120 | tf_op jit(solution)/shard_map/inner_0/pallas_call | solution.py:276
  31.9 0.7 %collective-permute-done.11.refs_4_ = bf16[24,16,256]{2,1,0:T(8,128)(2,1)S(1)} collective-permute-done((bf16[24,16,256]{2,1,0:T(8,128)(2,1)S(1)}, bf16[24,16,256]{2,1,0:T(8,128)(2,1)S(1)}, u32[]{:S(2)}, u32[]{:S(2)}) %collective-permute-start.11) | collective-permute-done | bytes 196640 | tf_op jit(solution)/shard_map/ppermute | solution.py:100
  32.7 0.7 %outer.1 = (bf16[24,16,256]{2,1,0:T(8,128)(2,1)S(1)}, bf16[24,16,256]{2,1,0:T(8,128)(2,1)S(1)}, bf16[24,16,256]{2,1,0:T(8,128)(2,1)S(1)}, bf16[24,16,256]{2,1,0:T(8,128)(2,1)S(1)}) custom-call(s32[4]{0:T(128)S(1)} %copy-done.3, bf16[24,16,256]{2,1,0:T(8,128)(2,1)S(1)} %pad_maximum_fusion.refs_1_, bf16[24,16,256]{2,1,0:T(8,128)(2,1)S(1)} %collective-permute-done.6.refs_2_, ...), custom_call_target="tpu_custom_call" | custom-call | flops 1610612736 | bytes 5242880 | tf_op jit(solution)/shard_map/outer/pallas_call | solution.py:389
  33.4 0.7 %collective-permute-start.12 = (bf16[24,16,256]{2,1,0:T(8,128)(2,1)S(1)}, bf16[24,16,256]{2,1,0:T(8,128)(2,1)S(1)}, u32[]{:S(2)}, u32[]{:S(2)}) collective-permute-start(bf16[24,16,256]{2,1,0:T(8,128)(2,1)S(1)} %get-tuple-element.56), channel_id=1, source_target_pairs={{4,12},{5,13},{6,14},{7,15},{24,16},{25,17},{26,18},{27,19}} | collective-permute-start | bytes 589832 | tf_op jit(solution)/shard_map/ppermute | solution.py:100
  34.1 1.3 %collective-permute-start.13 = (bf16[24,16,256]{2,1,0:T(8,128)(2,1)S(1)}, bf16[24,16,256]{2,1,0:T(8,128)(2,1)S(1)}, u32[]{:S(2)}, u32[]{:S(2)}) collective-permute-start(bf16[24,16,256]{2,1,0:T(8,128)(2,1)S(1)} %get-tuple-element.57), channel_id=1, source_target_pairs={{4,0},{5,1},{6,2},{7,3},{24,28},{25,29},{26,30},{27,31}} | collective-permute-start | bytes 589832 | tf_op jit(solution)/shard_map/ppermute | solution.py:100
  35.4 0.7 %collective-permute-start.14 = (bf16[24,16,256]{2,1,0:T(8,128)(2,1)S(1)}, bf16[24,16,256]{2,1,0:T(8,128)(2,1)S(1)}, u32[]{:S(2)}, u32[]{:S(2)}) collective-permute-start(bf16[24,16,256]{2,1,0:T(8,128)(2,1)S(1)} %get-tuple-element.58), channel_id=1, source_target_pairs={{4,8},{5,9},{6,10},{7,11},{24,20},{25,21},{26,22},{27,23}} | collective-permute-start | bytes 589832 | tf_op jit(solution)/shard_map/ppermute | solution.py:100
  36.1 14.0 %collective-permute-done.13 = bf16[24,16,256]{2,1,0:T(8,128)(2,1)S(1)} collective-permute-done((bf16[24,16,256]{2,1,0:T(8,128)(2,1)S(1)}, bf16[24,16,256]{2,1,0:T(8,128)(2,1)S(1)}, u32[]{:S(2)}, u32[]{:S(2)}) %collective-permute-start.13) | collective-permute-done | bytes 196640 | tf_op jit(solution)/shard_map/ppermute | solution.py:100
  50.1 0.7 %copy.14 = bf16[1,16,24,256]{3,2,1,0:T(8,128)(2,1)} copy(bf16[1,16,24,256]{3,1,2,0:T(8,128)(2,1)S(1)} %add_bitcast_fusion) | data formatting | bytes 393216 | tf_op jit(solution)/shard_map/broadcast_in_dim | solution.py:483
  (27 shorter events, 1.3 us)
Async XLA Ops:
  0.0 22.5 %copy-start.4 = (f32[4,5,256]{2,0,1:T(4,128)S(1)}, f32[4,5,256]{2,0,1:T(4,128)}, u32[]{:S(2)}) copy-start(f32[4,5,256]{2,0,1:T(4,128)} %param.12) | copy-start | bytes 61444
  0.0 22.6 %copy-start = (bf16[4,256,512]{2,1,0:T(8,128)(2,1)S(1)}, bf16[4,256,512]{2,1,0:T(8,128)(2,1)}, u32[]{:S(2)}) copy-start(bf16[4,256,512]{2,1,0:T(8,128)(2,1)} %refs_26_.1) | copy-start | bytes 3145732
  0.0 22.6 %copy-start.1 = (bf16[4,512,256]{2,1,0:T(8,128)(2,1)S(1)}, bf16[4,512,256]{2,1,0:T(8,128)(2,1)}, u32[]{:S(2)}) copy-start(bf16[4,512,256]{2,1,0:T(8,128)(2,1)} %refs_27_.1) | copy-start | bytes 3145732
  0.0 22.6 %copy-start.2 = (bf16[256,128]{1,0:T(8,128)(2,1)S(1)}, bf16[256,128]{1,0:T(8,128)(2,1)}, u32[]{:S(2)}) copy-start(bf16[256,128]{1,0:T(8,128)(2,1)} %refs_25_.1) | copy-start | bytes 196612
  0.0 22.6 %copy-start.3 = (s32[4]{0:T(128)S(1)}, s32[4]{0:T(128)}, u32[]{:S(2)}) copy-start(s32[4]{0:T(128)} %refs_0_.9) | copy-start | bytes 52
  0.0 2.0 %collective-permute-start = (bf16[16,24,128]{2,1,0:T(8,128)(2,1)}, bf16[16,24,128]{2,1,0:T(8,128)(2,1)S(1)}, u32[]{:S(2)}, u32[]{:S(2)}) collective-permute-start(bf16[16,24,128]{2,1,0:T(8,128)(2,1)} %bitcast.11), channel_id=1, source_target_pairs={{0,16},{16,0},{1,17},{17,1},{2,18},{18,2},{3,19},{19,3},{4,20},{20... | collective-permute-start | bytes 294920 | tf_op jit(solution)/shard_map/ppermute | solution.py:38
  2.1 17.8 %collective-permute-start.3 = (bf16[24,16,640]{2,1,0:T(8,128)(2,1)S(1)}, bf16[24,16,640]{2,1,0:T(8,128)(2,1)S(1)}, u32[]{:S(2)}, u32[]{:S(2)}) collective-permute-start(bf16[24,16,640]{2,1,0:T(8,128)(2,1)S(1)} %get-tuple-element.37.refs_4_.refs_5_), channel_id=1, source_target_pairs={{12,4},{13,5},{14,6},{15,7},{16,24},{17,25},{18,26},{19,27}} | collective-permute-start | bytes 1474568 | tf_op jit(solution)/shard_map/ppermute | solution.py:100
  2.8 19.8 %collective-permute-start.4 = (bf16[24,16,640]{2,1,0:T(8,128)(2,1)S(1)}, bf16[24,16,640]{2,1,0:T(8,128)(2,1)S(1)}, u32[]{:S(2)}, u32[]{:S(2)}) collective-permute-start(bf16[24,16,640]{2,1,0:T(8,128)(2,1)S(1)} %get-tuple-element.37.refs_4_.refs_5_), channel_id=1, source_target_pairs={{8,4},{9,5},{10,6},{11,7},{20,24},{21,25},{22,26},{23,27}} | collective-permute-start | bytes 1474568 | tf_op jit(solution)/shard_map/ppermute | solution.py:100
  3.5 19.1 %collective-permute-start.5 = (bf16[24,16,640]{2,1,0:T(8,128)(2,1)S(1)}, bf16[24,16,640]{2,1,0:T(8,128)(2,1)S(1)}, u32[]{:S(2)}, u32[]{:S(2)}) collective-permute-start(bf16[24,16,640]{2,1,0:T(8,128)(2,1)S(1)} %get-tuple-element.37.refs_4_.refs_5_), channel_id=1, source_target_pairs={{0,4},{1,5},{2,6},{3,7},{28,24},{29,25},{30,26},{31,27}} | collective-permute-start | bytes 1474568 | tf_op jit(solution)/shard_map/ppermute | solution.py:100
  9.3 5.6 %collective-permute-start.1 = (bf16[12,16,256]{2,1,0:T(8,128)(2,1)S(1)}, bf16[12,16,256]{2,1,0:T(8,128)(2,1)S(1)}, u32[]{:S(2)}, u32[]{:S(2)}) collective-permute-start(bf16[12,16,256]{2,1,0:T(8,128)(2,1)S(1)} %get-tuple-element.33), channel_id=1, source_target_pairs={{0,1},{1,2},{2,3},{4,5},{5,6},{6,7},{8,9},{9,10},{10,11},{12,13},{... | collective-permute-start | bytes 294920 | tf_op jit(solution)/shard_map/ppermute | solution.py:100
  12.7 6.5 %collective-permute-start.2 = (bf16[12,16,256]{2,1,0:T(8,128)(2,1)S(1)}, bf16[12,16,256]{2,1,0:T(8,128)(2,1)S(1)}, u32[]{:S(2)}, u32[]{:S(2)}) collective-permute-start(bf16[12,16,256]{2,1,0:T(8,128)(2,1)S(1)} %get-tuple-element.34), channel_id=1, source_target_pairs={{1,0},{2,1},{3,2},{5,4},{6,5},{7,6},{9,8},{10,9},{11,10},{13,12},{... | collective-permute-start | bytes 294920 | tf_op jit(solution)/shard_map/ppermute | solution.py:100
  14.9 15.2 %collective-permute-start.7 = (bf16[24,16,512]{2,1,0:T(8,128)(2,1)S(1)}, bf16[24,16,512]{2,1,0:T(8,128)(2,1)S(1)}, u32[]{:S(2)}, u32[]{:S(2)}) collective-permute-start(bf16[24,16,512]{2,1,0:T(8,128)(2,1)S(1)} %get-tuple-element.40.refs_4_.refs_9_), channel_id=1, source_target_pairs={{12,4},{13,5},{14,6},{15,7},{16,24},{17,25},{18,26},{19,27}} | collective-permute-start | bytes 1179656 | tf_op jit(solution)/shard_map/ppermute | solution.py:100
  19.2 10.9 %collective-permute-start.8 = (bf16[24,16,512]{2,1,0:T(8,128)(2,1)S(1)}, bf16[24,16,512]{2,1,0:T(8,128)(2,1)S(1)}, u32[]{:S(2)}, u32[]{:S(2)}) collective-permute-start(bf16[24,16,512]{2,1,0:T(8,128)(2,1)S(1)} %get-tuple-element.40.refs_4_.refs_9_), channel_id=1, source_target_pairs={{8,4},{9,5},{10,6},{11,7},{20,24},{21,25},{22,26},{23,27}} | collective-permute-start | bytes 1179656 | tf_op jit(solution)/shard_map/ppermute | solution.py:100
  19.9 10.2 %collective-permute-start.9 = (bf16[24,16,512]{2,1,0:T(8,128)(2,1)S(1)}, bf16[24,16,512]{2,1,0:T(8,128)(2,1)S(1)}, u32[]{:S(2)}, u32[]{:S(2)}) collective-permute-start(bf16[24,16,512]{2,1,0:T(8,128)(2,1)S(1)} %get-tuple-element.40.refs_4_.refs_9_), channel_id=1, source_target_pairs={{0,4},{1,5},{2,6},{3,7},{28,24},{29,25},{30,26},{31,27}} | collective-permute-start | bytes 1179656 | tf_op jit(solution)/shard_map/ppermute | solution.py:100
  23.2 7.5 %collective-permute-start.6 = (bf16[24,16,256]{2,1,0:T(8,128)(2,1)S(1)}, bf16[24,16,256]{2,1,0:T(8,128)(2,1)S(1)}, u32[]{:S(2)}, u32[]{:S(2)}) collective-permute-start(bf16[24,16,256]{2,1,0:T(8,128)(2,1)S(1)} %pad_maximum_fusion.refs_1_), channel_id=1, source_target_pairs={{8,4},{9,5},{10,6},{11,7},{12,20},{13,21},{14,22},{15,23},{16,8},{... | collective-permute-start | bytes 589832 | tf_op jit(solution)/shard_map/ppermute | solution.py:100
  23.9 8.8 %collective-permute-start.11 = (bf16[24,16,256]{2,1,0:T(8,128)(2,1)S(1)}, bf16[24,16,256]{2,1,0:T(8,128)(2,1)S(1)}, u32[]{:S(2)}, u32[]{:S(2)}) collective-permute-start(bf16[24,16,256]{2,1,0:T(8,128)(2,1)S(1)} %pad_maximum_fusion.refs_1_), channel_id=1, source_target_pairs={{0,4},{1,5},{2,6},{3,7},{28,24},{29,25},{30,26},{31,27}} | collective-permute-start | bytes 589832 | tf_op jit(solution)/shard_map/ppermute | solution.py:100
  30.7 2.0 %collective-permute-start.10 = (bf16[24,16,256]{2,1,0:T(8,128)(2,1)S(1)}, bf16[24,16,256]{2,1,0:T(8,128)(2,1)S(1)}, u32[]{:S(2)}, u32[]{:S(2)}) collective-permute-start(bf16[24,16,256]{2,1,0:T(8,128)(2,1)S(1)} %collective-permute-done.6.refs_2_), channel_id=1, source_target_pairs={{8,24},{9,25},{10,26},{11,27},{20,4},{21,5},{22,6},{23,7}} | collective-permute-start | bytes 589832 | tf_op jit(solution)/shard_map/ppermute | solution.py:100
  33.4 2.7 %collective-permute-start.12 = (bf16[24,16,256]{2,1,0:T(8,128)(2,1)S(1)}, bf16[24,16,256]{2,1,0:T(8,128)(2,1)S(1)}, u32[]{:S(2)}, u32[]{:S(2)}) collective-permute-start(bf16[24,16,256]{2,1,0:T(8,128)(2,1)S(1)} %get-tuple-element.56), channel_id=1, source_target_pairs={{4,12},{5,13},{6,14},{7,15},{24,16},{25,17},{26,18},{27,19}} | collective-permute-start | bytes 589832 | tf_op jit(solution)/shard_map/ppermute | solution.py:100
  34.1 16.0 %collective-permute-start.13 = (bf16[24,16,256]{2,1,0:T(8,128)(2,1)S(1)}, bf16[24,16,256]{2,1,0:T(8,128)(2,1)S(1)}, u32[]{:S(2)}, u32[]{:S(2)}) collective-permute-start(bf16[24,16,256]{2,1,0:T(8,128)(2,1)S(1)} %get-tuple-element.57), channel_id=1, source_target_pairs={{4,0},{5,1},{6,2},{7,3},{24,28},{25,29},{26,30},{27,31}} | collective-permute-start | bytes 589832 | tf_op jit(solution)/shard_map/ppermute | solution.py:100
  35.4 14.7 %collective-permute-start.14 = (bf16[24,16,256]{2,1,0:T(8,128)(2,1)S(1)}, bf16[24,16,256]{2,1,0:T(8,128)(2,1)S(1)}, u32[]{:S(2)}, u32[]{:S(2)}) collective-permute-start(bf16[24,16,256]{2,1,0:T(8,128)(2,1)S(1)} %get-tuple-element.58), channel_id=1, source_target_pairs={{4,8},{5,9},{6,10},{7,11},{24,20},{25,21},{26,22},{27,23}} | collective-permute-start | bytes 589832 | tf_op jit(solution)/shard_map/ppermute | solution.py:100
